TPU v7x, 128 devices: a whole 4x4x4 slice. The times are simulated.
128 devices in a mesh: gx: 16 (over z, x), gy: 8 (over y, core).
Axes of the slice: x: 4, y: 4, z: 4, core: 2. Of those that a mesh axis runs over, the one named last changes fastest.
Arguments:
- activations: bfloat16 [768, 14848], P('gx', 'gy'), may hold values from -6 to 6
- norm_gain: float32 [14848], P('gy'), may hold values from 0.5 to 1.5
- norm_bias: float32 [14848], P('gy'), may hold values from -3 to 3
- input_outliers: int32 [32], P('gy'), may hold values from 0 to 1855, as said below
- query_int: bfloat16 [14848, 14336], P('gy', 'gx'), may hold values from -127 to 127, as said below
- query_scale: float32 [14336], P('gx'), as said below
- keyvalue_int: bfloat16 [14848, 1024], P('gy'), may hold values from -127 to 127, as said below
- keyvalue_scale: float32 [1024], replicated, as said below
- query_float: float32 [32, 14336], P('gy', 'gx'), may hold values from -1 to 1
- keyvalue_float: float32 [32, 1024], P('gy'), may hold values from -1 to 1
- key_cache: bfloat16 [384, 2048, 512], P(('gx', 'gy')), may hold values from -80 to 80
- value_cache: bfloat16 [384, 2048, 512], P(('gx', 'gy')), may hold values from -6 to 6
- lengths: int32 [384], P(('gx', 'gy')), may hold values from 1 to 2048, as said below
- middle_outliers: int32 [64], replicated, may hold values from 0 to 895, as said below
- output_int: bfloat16 [14336, 14848], P('gx', 'gy'), may hold values from -127 to 127, as said below
- output_scale: float32 [14848], P('gy'), as said below
- output_float: float32 [64, 14848], P('gx', 'gy'), may hold values from -0.75 to 0.75
Outputs:
- attention_out: bfloat16 [768, 14848], P('gx', 'gy')
Inputs may be any that keep to these rules, and one draw needn't show every extreme that they name: `input_outliers`: within each shard the 4 positions are distinct. `middle_outliers`: within each shard the 4 positions are distinct. `query_int`: Integers. `keyvalue_int`: Integers. `output_int`: Integers. `query_scale`: Positive. `keyvalue_scale`: Positive. `output_scale`: Positive. `lengths`: some request has exactly 2048 and some exactly 1.
All inputs are finite; a program needn't handle non-finite values.
Results may differ from a plain program's by a relative error of at most 0.012.
The roundings to bfloat16 on the way count: a program that leaves them out, or rounds other values in their place, can miss the bound.
Values may be sent and summed in bfloat16 or wider, within the bound.
No kernel may reach another device: no remote copies, remote signals or barrier semaphores. Data moves between devices by JAX's collectives and lax.ppermute only.
A program may use at most 128 MiB of HBM per device.

v0:
```python
import math

import jax
import jax.numpy as jnp
from jax import lax
from jax.sharding import PartitionSpec as P

D = 14848
HEAD = 64
KV = 8
GROUP = 28
OUTL = 4


epsilon = 1e-05
rope_base = 10000.0


def rotate(values, positions):
    dimension = values.shape[-1]
    halfway = dimension // 2
    frequency = jnp.exp(
        jnp.arange(halfway, dtype=jnp.float32) * (-2.0 * math.log(rope_base) / dimension)
    )
    angles = positions.astype(jnp.float32)[:, :, None] * frequency[None, None, :]
    cosine = jnp.cos(angles)[:, :, None, :]
    sine_part = jnp.sin(angles)[:, :, None, :]
    leading = values[..., :halfway]
    trailing = values[..., halfway:]
    return jnp.concatenate(
        [leading * cosine - trailing * sine_part, trailing * cosine + leading * sine_part], axis=-1
    )


def attend(queries, fresh_keys, fresh_values, cached_keys, cached_values, lengths):
    score_scale = 1.0 / math.sqrt(queries.shape[-1])
    window = cached_keys.shape[1]
    fresh = fresh_keys.shape[1]
    cache_scores = (
        jnp.einsum("rtkgd,rlkd->rkgtl", queries, cached_keys, preferred_element_type=jnp.float32)
        * score_scale
    )
    fresh_scores = (
        jnp.einsum("rtkgd,rukd->rkgtu", queries, fresh_keys, preferred_element_type=jnp.float32)
        * score_scale
    )
    active = jnp.arange(window, dtype=jnp.int32)[None, :] < lengths[:, None]
    cache_scores = jnp.where(active[:, None, None, None, :], cache_scores, -jnp.inf)
    causal = (
        jnp.arange(fresh, dtype=jnp.int32)[None, :] <= jnp.arange(fresh, dtype=jnp.int32)[:, None]
    )
    fresh_scores = jnp.where(causal, fresh_scores, -jnp.inf)
    highest = jnp.maximum(jnp.max(cache_scores, axis=-1), jnp.max(fresh_scores, axis=-1))[..., None]
    cache_weights = jnp.exp(cache_scores - highest)
    fresh_weights = jnp.exp(fresh_scores - highest)
    denominator = jnp.sum(cache_weights, axis=-1, keepdims=True) + jnp.sum(
        fresh_weights, axis=-1, keepdims=True
    )
    cache_probs = (cache_weights / denominator).astype(jnp.bfloat16)
    fresh_probs = (fresh_weights / denominator).astype(jnp.bfloat16)
    result = jnp.einsum(
        "rkgtl,rlkd->rtkgd", cache_probs, cached_values, preferred_element_type=jnp.float32
    )
    result = result + jnp.einsum(
        "rkgtu,rukd->rtkgd", fresh_probs, fresh_values, preferred_element_type=jnp.float32
    )
    return result.reshape(result.shape[0], result.shape[1], -1)


def regroup(matrix, outer, inner):
    columns = matrix.shape[-1]
    return matrix.reshape(outer, inner, -1, columns).transpose(1, 0, 2, 3).reshape(-1, columns)


def block_term(regular_rows, outlier_rows, weight_int, weight_scale, weight_float):
    outlier_block = outlier_rows.astype(jnp.float32)
    term = jnp.dot(regular_rows, weight_int, preferred_element_type=jnp.float32) * weight_scale
    return term + jnp.dot(outlier_block, weight_float, precision=lax.Precision.HIGHEST)


def on_device(
    activations,
    norm_gain,
    norm_bias,
    input_outliers,
    query_int,
    query_scale,
    keyvalue_int,
    keyvalue_scale,
    query_float,
    keyvalue_float,
    key_cache,
    value_cache,
    lengths,
    middle_outliers,
    output_int,
    output_scale,
    output_float,
):
    count_gx = lax.axis_size("gx")
    count_gy = lax.axis_size("gy")
    block_rows, features = activations.shape
    requests = lengths.shape[0]
    owned_rows = block_rows // count_gy
    widened = activations.astype(jnp.float32)
    row_sum, row_squares = lax.psum(
        (jnp.sum(widened, axis=1), jnp.sum(widened * widened, axis=1)), "gy"
    )
    average = row_sum / D
    variance = row_squares / D - average * average
    normed = (widened - average[:, None]) * lax.rsqrt(
        variance[:, None] + epsilon
    ) * norm_gain + norm_bias
    picked = (jnp.arange(features, dtype=jnp.int32)[:, None] == input_outliers[None, :]).astype(
        jnp.float32
    )
    is_outlier = jnp.sum(picked, axis=1) > 0.0
    rounded = normed.astype(jnp.bfloat16)
    regular = jnp.where(is_outlier[None, :], jnp.zeros_like(rounded), rounded)
    outlier_vals = jnp.dot(normed, picked, precision=lax.Precision.HIGHEST).astype(jnp.bfloat16)
    gathered_regular, gathered_outlier = (
        lax.all_gather(regular, "gx", axis=0, tiled=True),
        lax.all_gather(outlier_vals, "gx", axis=0, tiled=True),
    )
    regular_rows = regroup(gathered_regular, count_gx, count_gy)
    outlier_rows = regroup(gathered_outlier, count_gx, count_gy)
    fresh_pairs = lax.psum_scatter(
        block_term(regular, outlier_vals, keyvalue_int, keyvalue_scale, keyvalue_float),
        "gy",
        scatter_dimension=0,
        tiled=True,
    ).astype(jnp.bfloat16)
    summed = lax.psum_scatter(
        block_term(regular_rows, outlier_rows, query_int, query_scale, query_float),
        "gy",
        scatter_dimension=0,
        tiled=True,
    )
    queries = lax.all_to_all(
        summed.astype(jnp.bfloat16), "gx", split_axis=0, concat_axis=1, tiled=True
    )
    fresh = owned_rows // requests
    positions = lengths[:, None] + jnp.arange(fresh, dtype=jnp.int32)[None, :]
    query_heads = queries.astype(jnp.float32).reshape(requests, fresh, KV * GROUP, HEAD)
    query_rot = (
        rotate(query_heads, positions)
        .astype(jnp.bfloat16)
        .reshape(requests, fresh, KV, GROUP, HEAD)
    )
    pair_heads = fresh_pairs.reshape(requests, fresh, 2, KV, HEAD)
    fresh_keys = rotate(pair_heads[:, :, 0].astype(jnp.float32), positions).astype(jnp.bfloat16)
    fresh_values = pair_heads[:, :, 1]
    cached_keys = key_cache.reshape(requests, key_cache.shape[1], KV, HEAD)
    cached_values = value_cache.reshape(requests, value_cache.shape[1], KV, HEAD)
    attended = attend(
        query_rot, fresh_keys, fresh_values, cached_keys, cached_values, lengths
    ).reshape(owned_rows, -1)
    shard_cols = attended.shape[1] // count_gx
    middle_cols = (
        jnp.arange(middle_outliers.shape[0], dtype=jnp.int32) // OUTL * shard_cols + middle_outliers
    )
    chosen = (
        jnp.arange(attended.shape[1], dtype=jnp.int32)[:, None] == middle_cols[None, :]
    ).astype(jnp.float32)
    attended_round = attended.astype(jnp.bfloat16)
    middle_regular = jnp.where(
        (jnp.sum(chosen, axis=1) > 0.0)[None, :], jnp.zeros_like(attended_round), attended_round
    )
    middle_outlier = jnp.dot(attended, chosen, precision=lax.Precision.HIGHEST).astype(jnp.bfloat16)
    back_regular, back_outlier = (
        lax.all_to_all(middle_regular, "gx", split_axis=1, concat_axis=0, tiled=True),
        lax.all_to_all(middle_outlier, "gx", split_axis=1, concat_axis=0, tiled=True),
    )
    all_regular, all_outlier = (
        lax.all_gather(back_regular, "gy", axis=0, tiled=True),
        lax.all_gather(back_outlier, "gy", axis=0, tiled=True),
    )
    token_regular = regroup(all_regular, count_gy, count_gx)
    token_outlier = regroup(all_outlier, count_gy, count_gx)
    result = lax.psum_scatter(
        block_term(token_regular, token_outlier, output_int, output_scale, output_float),
        "gx",
        scatter_dimension=0,
        tiled=True,
    )
    return result.astype(jnp.bfloat16)


def solution(mesh):
    placed = (
        P("gx", "gy"),
        P("gy"),
        P("gy"),
        P("gy"),
        P("gy", "gx"),
        P("gx"),
        P("gy", None),
        P(),
        P("gy", "gx"),
        P("gy", None),
        P(("gx", "gy"), None, None),
        P(("gx", "gy"), None, None),
        P(("gx", "gy")),
        P(),
        P("gx", "gy"),
        P("gy"),
        P("gx", "gy"),
    )
    return jax.shard_map(
        on_device, mesh=mesh, in_specs=placed, out_specs=P("gx", "gy"), check_vma=False
    )
```

profile of v0, /device:TPU:1, one launch (start us, length us, event | category | flops | bytes accessed | tf_op | source)
XLA Modules:
  0.0 336.9 jit_solution(6165911726707391658)
XLA Ops:
  6.5 1.2 convert_reduce_fusion.1
  8.5 13.5 %all-reduce.3 = (f32[48]{0:T(128)S(1)}, f32[48]{0:T(128)S(1)}) all-reduce(f32[48]{0:T(128)S(1)} %get-tuple-element.6, f32[48]{0:T(128)S(1)} %get-tuple-element.5), channel_id=1, replica_groups=mesh['gx'=16,'gy'=8] {'gy'}, use_global_device_ids=true, to_apply=%region_5.6 | all-reduce | flops 96 | bytes 768 | tf_op jit(solution)/shard_map/psum | solution.py:106
  22.0 1.8 fusion.18
  23.8 1.3 convolution_convert_fusion
  25.2 19.5 %all-gather = bf16[16,48,4]{1,2,0:T(4,128)(2,1)S(1)} all-gather(bf16[1,48,4]{1,2,0:T(4,128)(2,1)S(1)} %bitcast.104), channel_id=1, replica_groups=mesh['gx'=16,'gy'=8] {'gx'}, dimensions={0}, use_global_device_ids=true | all-gather | bytes 6528 | tf_op jit(solution)/shard_map/all_gather | solution.py:123
  45.3 27.8 %all-gather.5.cloned.1.call-done = bf16[768,1856]{1,0:T(8,128)(2,1)} async-done(((bf16[48,1856]{1,0:T(8,128)(2,1)}), bf16[768,1856]{1,0:T(8,128)(2,1)}) %all-gather.5.cloned.1.call-update) | async-done | bytes 2850832 | tf_op jit(solution)/shard_map/all_gather | solution.py:122
  73.2 6.4 %reshape.136 = bf16[16,8,6,1856]{3,2,1,0:T(8,128)(2,1)} reshape(bf16[768,1856]{1,0:T(8,128)(2,1)} %all-gather.5.cloned.1.call-done) | data formatting | bytes 5701632 | tf_op jit(solution)/shard_map/reshape | solution.py:72
  79.6 4.5 %copy.99 = bf16[8,16,6,1856]{3,2,1,0:T(8,128)(2,1)} copy(bf16[8,16,6,1856]{3,2,0,1:T(8,128)(2,1)} %bitcast.96) | data formatting | bytes 5701632 | tf_op jit(solution)/shard_map/transpose | solution.py:72
  84.1 6.6 %reshape.137 = bf16[768,1856]{1,0:T(8,128)(2,1)} reshape(bf16[8,16,6,1856]{3,2,1,0:T(8,128)(2,1)} %copy.99) | data formatting | bytes 5701632 | tf_op jit(solution)/shard_map/reshape | solution.py:72
  90.7 6.2 %fusion.39 = f32[768,896]{1,0:T(8,128)S(1)} fusion(bf16[768,1856]{1,0:T(8,128)(2,1)} %reshape.137, bf16[1856,896]{1,0:T(8,128)(2,1)} %param.21), kind=kOutput, calls=%fused_computation.82 | convolution fusion | flops 2554331136 | bytes 8929280 | tf_op jit(solution)/shard_map/dot_general | solution.py:77
  96.9 2.9 multiply_add_fusion.1
  99.9 2.9 convolution_multiply_fusion
  103.1 15.7 %fusion = f32[8,1024]{1,0:T(8,128)S(1)} fusion(f32[48,1024]{1,0:T(8,128)S(1)} %convolution_add_fusion), kind=kCustom, calls=%all-reduce-scatter | all-reduce-scatter fusion | flops 65537 | bytes 229888
  118.7 2.2 collective-permute-start
  121.0 2.7 collective-permute-start.1
  127.0 1.3 iota_compare_fusion.4
  128.8 8.8 %copy.107 = bf16[3,2048,512]{1,2,0:T(8,128)(2,1)} copy(bf16[3,2048,512]{2,1,0:T(8,128)(2,1)} %param.27) | data formatting | bytes 12582912 | tf_op args[10]
  137.6 8.9 %copy.109 = bf16[3,2048,512]{1,2,0:T(8,128)(2,1)} copy(bf16[3,2048,512]{2,1,0:T(8,128)(2,1)} %param.28) | data formatting | bytes 12582912 | tf_op args[11]
  150.0 1.0 convert_element_type.75
  151.8 3.5 %all-to-all-start = ((bf16[16,6,896]{2,1,0:T(8,128)(2,1)}), bf16[16,6,896]{2,1,0:T(8,128)(2,1)S(1)}, u32[]{:S(2)}, u32[]{:S(2)}) async-start(bf16[16,6,896]{2,1,0:T(8,128)(2,1)} %all_to_all.36), calls=%async_computation.1 | async-start | bytes 458752 | tf_op jit(solution)/shard_map/all_to_all | solution.py:139
  155.5 1.5 subtract_convert_fusion.1
  157.1 5.7 %all-to-all-done = bf16[16,6,896]{2,1,0:T(8,128)(2,1)S(1)} async-done(((bf16[16,6,896]{2,1,0:T(8,128)(2,1)}), bf16[16,6,896]{2,1,0:T(8,128)(2,1)S(1)}, u32[]{:S(2)}, u32[]{:S(2)}) %all-to-all-start) | async-done | bytes 172064 | tf_op jit(solution)/shard_map/all_to_all | solution.py:139
  162.8 0.8 copy.102
  163.6 2.0 reshape.147
  165.6 2.5 subtract_convert_fusion
  168.1 1.8 reshape.160
  169.9 1.9 reshape.161
  171.8 1.3 pad_maximum_fusion
  173.2 4.2 %bitcast_reduce_fusion = (f32[3,8,28,2]{2,3,1,0:T(2,128)S(1)}, f32[3,8,2,28,2048]{4,3,2,1,0:T(8,128)S(1)}) fusion(pred[3,2048]{1,0:T(4,128)(4,1)S(1)} %copy-done.2, bf16[3,2048,8,64,1]{1,3,4,2,0:T(8,128)(2,1)} %bitcast.95, bf16[3,2,8,28,64]{4,3,2,1,0:T(8,128)(2,1)S(1)} %pad_maximum_fusion), kind=kOutput, calls=%fused_computation.1 | convolution fusion | flops 360577728 | bytes 17485056 | tf_op jit(solution)/shard_map/rtkgd,rlkd->rkgtl/dot_general | solution.py:40
  178.3 3.0 fusion.2
  181.3 5.6 %fusion.3 = f32[3,8,28,2,64]{4,2,3,1,0:T(8,128)S(1)} fusion(bf16[3,2048,8,64,1]{1,3,4,2,0:T(8,128)(2,1)} %bitcast.98, f32[3,8,2,28,2048]{4,3,2,1,0:T(8,128)S(1)} %get-tuple-element.22, f32[3,8,28,2]{2,3,1,0:T(2,128)S(1)} %add.84, f32[3,8,28,2]{2,3,1,0:T(2,128)S(1)} %max.7, pred[3,2048]{1,0:T(4,128)(4,1)S(1)} %copy-done.2), kind=kOutput, calls=%fused_computation.6 | convolution fusion | flops 366084096 | bytes 17662464 | tf_op jit(solution)/shard_map/rkgtl,rlkd->rtkgd/dot_general | solution.py:61
  187.3 1.9 fusion.36
  189.1 0.8 copy.113
  190.0 1.3 convert_element_type.86
  191.4 10.2 %all_to_all.48 = bf16[6,16,896]{2,0,1:T(8,128)(2,1)S(1)} all-to-all(bf16[6,16,896]{2,0,1:T(8,128)(2,1)S(1)} %copy.114), channel_id=1, replica_groups=mesh['gx'=16,'gy'=8] {'gx'}, dimensions={1} | all-to-all | bytes 344064 | tf_op jit(solution)/shard_map/all_to_all | solution.py:171
  202.4 2.1 copy.116
  204.5 2.2 reshape_reshape.3
  206.7 2.9 fusion.8
  209.7 9.4 %all_to_all.49 = bf16[6,16,4]{0,2,1:T(4,128)(2,1)S(1)} all-to-all(bf16[6,16,4]{0,2,1:T(4,128)(2,1)S(1)} %bitcast.102), channel_id=1, replica_groups=mesh['gx'=16,'gy'=8] {'gx'}, dimensions={1} | all-to-all | bytes 1536 | tf_op jit(solution)/shard_map/all_to_all | solution.py:172
  219.2 13.3 %all-gather.1 = bf16[8,96,4]{1,2,0:T(4,128)(2,1)S(1)} all-gather(bf16[1,96,4]{1,2,0:T(4,128)(2,1)S(1)} %reshape.151), channel_id=1, replica_groups=mesh['gx'=16,'gy'=8] {'gy'}, dimensions={0}, use_global_device_ids=true | all-gather | bytes 6912 | tf_op jit(solution)/shard_map/all_gather | solution.py:176
  233.3 1.1 reshape.146
  234.4 3.5 %reshape.143 = bf16[8,16,6,896]{3,2,1,0:T(8,128)(2,1)} reshape(bf16[768,896]{1,0:T(8,128)(2,1)} %all-gather.7.cloned.1.call-done) | data formatting | bytes 2752512 | tf_op jit(solution)/shard_map/reshape | solution.py:72
  237.9 3.0 copy.115
  241.0 3.6 %reshape.144 = bf16[768,896]{1,0:T(8,128)(2,1)} reshape(bf16[16,8,6,896]{3,2,1,0:T(8,128)(2,1)} %copy.115) | data formatting | bytes 2752512 | tf_op jit(solution)/shard_map/reshape | solution.py:72
  244.5 4.7 %fusion.40 = f32[768,1856]{1,0:T(8,128)S(1)} fusion(bf16[768,896]{1,0:T(8,128)(2,1)} %reshape.144, bf16[896,1856]{0,1:T(8,128)(2,1)S(1)} %copy-done), kind=kOutput, calls=%fused_computation.83 | convolution fusion | flops 2554331136 | bytes 10403840 | tf_op jit(solution)/shard_map/dot_general | solution.py:77
  249.3 4.5 %multiply_add_fusion = f32[768,1856]{1,0:T(8,128)} fusion(f32[768,1856]{1,0:T(8,128)S(1)} %fusion.40, bf16[768,4]{0,1:T(4,128)(2,1)S(1)} %reshape.146, f32[4,1856]{1,0:T(4,128)S(1)} %copy-done.5, f32[1856]{0:T(1024)S(1)} %copy-done.10), kind=kOutput, calls=%fused_computation.7 | convolution fusion | flops 71270400 | bytes 11446528 | tf_op jit(solution)/shard_map/dot_general | solution.py:78
  253.8 74.9 %reduce-scatter.9.cloned.1.call-done = f32[48,1856]{1,0:T(8,128)} async-done(((f32[768,1856]{1,0:T(8,128)}), f32[48,1856]{1,0:T(8,128)}) %reduce-scatter.9.cloned.1.call-update) | async-done | bytes 356368
  328.7 1.7 convert_element_type.88
  (83 shorter events, 12.5 us)
Async XLA Ops:
  6.5 238.0 %copy-start = (bf16[896,1856]{0,1:T(8,128)(2,1)S(1)}, bf16[896,1856]{0,1:T(8,128)(2,1)}, u32[]{:S(2)}) copy-start(bf16[896,1856]{0,1:T(8,128)(2,1)} %param.31) | copy-start | bytes 9977860
  6.5 66.6 %all-gather.5.cloned.1.call-start = ((), (), s32[]{:S(2)}) async-start(), calls=%async_computation.5 | async-start | bytes 3133440 | tf_op jit(solution)/shard_map/all_gather | solution.py:122
  23.8 126.2 %reduce-scatter.7.cloned.1.call-start = ((), (), s32[]{:S(2)}) async-start(), calls=%async_computation.6 | async-start | bytes 3096576 | tf_op jit(solution)/shard_map/reduce_scatter | solution.py:133
  90.7 6.2 %copy-start.7 = (f32[4,896]{1,0:T(4,128)S(1)}, f32[4,896]{1,0:T(4,128)}, u32[]{:S(2)}) copy-start(f32[4,896]{1,0:T(4,128)} %param.25) | copy-start | bytes 43012
  90.7 6.2 %copy-start.11 = (f32[896]{0:T(1024)S(1)}, f32[896]{0:T(1024)}, u32[]{:S(2)}) copy-start(f32[896]{0:T(1024)} %param.22) | copy-start | bytes 10756
  96.9 3.0 copy-start.1
  96.9 3.0 copy-start.12
  96.9 5.9 %copy-start.6 = (f32[4,1024]{1,0:T(4,128)S(1)}, f32[4,1024]{1,0:T(4,128)}, u32[]{:S(2)}) copy-start(f32[4,1024]{1,0:T(4,128)} %param.26) | copy-start | bytes 49156
  118.7 29.7 %collective-permute-start = (bf16[8,1024]{1,0:T(8,128)(2,1)S(1)}, bf16[8,1024]{1,0:T(8,128)(2,1)S(1)}, u32[]{:S(2)}, u32[]{:S(2)}) collective-permute-start(bf16[8,1024]{1,0:T(8,128)(2,1)S(1)} %convert.27), channel_id=1, source_target_pairs={{0,1},{1,2},{2,3},{3,4},{4,5},{5,6},{6,7},{8,9},{9,10},{10,11},{11... | collective-permute-start | bytes 49160
  121.0 27.4 %collective-permute-start.1 = (bf16[6,1024]{1,0:T(8,128)(2,1)S(1)}, bf16[6,1024]{1,0:T(8,128)(2,1)S(1)}, u32[]{:S(2)}, u32[]{:S(2)}) collective-permute-start(bf16[6,1024]{1,0:T(8,128)(2,1)S(1)} %slice.30), channel_id=1, source_target_pairs={{0,2},{1,3},{2,4},{3,5},{4,6},{5,7},{8,10},{9,11},{10,12},{11,13},... | collective-permute-start | bytes 36872
  124.4 0.5 copy-start.13
  137.6 9.5 %copy-start.14 = (u32[128]{0:T(128)S(1)}, u32[128]{0:T(128)}, u32[]{:S(2)}) copy-start(u32[128]{0:T(128)} %constant.49) | copy-start | bytes 1540
  151.8 11.0 %all-to-all-start = ((bf16[16,6,896]{2,1,0:T(8,128)(2,1)}), bf16[16,6,896]{2,1,0:T(8,128)(2,1)S(1)}, u32[]{:S(2)}, u32[]{:S(2)}) async-start(bf16[16,6,896]{2,1,0:T(8,128)(2,1)} %all_to_all.36), calls=%async_computation.1 | async-start | bytes 458752 | tf_op jit(solution)/shard_map/all_to_all | solution.py:139
  155.3 79.1 %all-gather.7.cloned.1.call-start = ((), (), s32[]{:S(2)}) async-start(), calls=%async_computation.7 | async-start | bytes 1548288 | tf_op jit(solution)/shard_map/all_gather | solution.py:175
  162.8 10.4 %copy-start.2 = (pred[3,2048]{1,0:T(4,128)(4,1)S(1)}, pred[3,2048]{1,0:T(4,128)(4,1)}, u32[]{:S(2)}) copy-start(pred[3,2048]{1,0:T(4,128)(4,1)} %iota_compare_fusion.4) | copy-start | bytes 18436
  173.2 4.2 %copy-start.8 = (bf16[3,2,8,32]{3,1,2,0:T(2,128)(2,1)S(1)}, bf16[3,2,8,32]{3,1,2,0:T(2,128)(2,1)}, u32[]{:S(2)}) copy-start(bf16[3,2,8,32]{3,1,2,0:T(2,128)(2,1)} %get-tuple-element.13) | copy-start | bytes 9220
  173.2 4.2 %copy-start.9 = (bf16[3,2,8,32]{3,1,2,0:T(2,128)(2,1)S(1)}, bf16[3,2,8,32]{3,1,2,0:T(2,128)(2,1)}, u32[]{:S(2)}) copy-start(bf16[3,2,8,32]{3,1,2,0:T(2,128)(2,1)} %get-tuple-element.14) | copy-start | bytes 9220
  173.2 4.2 %copy-start.15 = (pred[2,2]{1,0:T(4,128)(4,1)S(1)}, pred[2,2]{1,0:T(4,128)(4,1)}, u32[]{:S(2)}) copy-start(pred[2,2]{1,0:T(4,128)(4,1)} %iota_compare_fusion.7) | copy-start | bytes 16
  181.3 5.7 %copy-start.4 = (bf16[3,2,1,8,64]{4,3,2,1,0:T(8,128)(2,1)S(1)}, bf16[3,2,1,8,64]{4,3,2,1,0:T(8,128)(2,1)}, u32[]{:S(2)}) copy-start(bf16[3,2,1,8,64]{4,3,2,1,0:T(8,128)(2,1)} %get-tuple-element.15) | copy-start | bytes 18436
  181.3 10.0 %copy-start.3 = (pred[16,896]{1,0:T(8,128)(4,1)S(1)}, pred[16,896]{1,0:T(8,128)(4,1)}, u32[]{:S(2)}) copy-start(pred[16,896]{1,0:T(8,128)(4,1)} %gt.25) | copy-start | bytes 43012
  202.4 126.3 %reduce-scatter.9.cloned.1.call-start = ((), (), s32[]{:S(2)}) async-start(), calls=%async_computation.8 | async-start | bytes 6266880
  244.5 4.7 %copy-start.5 = (f32[4,1856]{1,0:T(4,128)S(1)}, f32[4,1856]{1,0:T(4,128)}, u32[]{:S(2)}) copy-start(f32[4,1856]{1,0:T(4,128)} %param.33) | copy-start | bytes 89092
  244.5 4.8 %copy-start.10 = (f32[1856]{0:T(1024)S(1)}, f32[1856]{0:T(1024)}, u32[]{:S(2)}) copy-start(f32[1856]{0:T(1024)} %param.32) | copy-start | bytes 22276
Sparse Core Ops, SparseCore 0:
  23.9 49.1 all-gather.4
  100.0 31.5 reduce-scatter.6
  202.5 24.3 all-gather.6
  253.9 74.6 reduce-scatter.8
where the time goes:
time: 339 us; the launch traced here: 337 us
  waiting for transfers between devices  108 us (32%)
  blocking collectives  81.6 us (24%)
  local copies, waits for them, and re-layouts  65.3 us (19%)
  matrix products  36.5 us (11%)
  other arithmetic  22.1 us (7%)
  between operations  14.2 us (4%)
  starting transfers between devices  8.8 us (3%)
    unnamed x7, waiting for transfers between devices  74.9 us
    all_gather x1, waiting for transfers between devices, on_device(): lax.all_gather(regular, 'gx', axis=0, tiled=True)  27.8 us
    reshape x7, local copies, waits for them, and re-layouts, regroup(): matrix.reshape(outer, inner, -1, columns).transpose(1, 0, 2, 3)  21.5 us
    all_gather x1, blocking collectives, on_device(): lax.all_gather(outlier_vals, 'gx', axis=0, tiled=True)  19.5 us
    unnamed x38, local copies, waits for them, and re-layouts  19.2 us
    unnamed x1, blocking collectives  15.7 us
    dot_general x3, matrix products, block_term(): jnp.dot(regular_rows, weight_int, preferred_element_type=jnp.float32)  13.8 us
    psum x1, blocking collectives, on_device(): lax.psum((jnp.sum(widened, axis=1), jnp.sum(widened * widened, axis=1)),...  13.5 us
  transfers between devices with their start and end apart: 7, of which 3 were waited for; matrix products, arithmetic and copies ran while one was open for 17% of the time, Pallas kernels for 0%

commit v1 on v0

v1 whole, which is shorter than its diff:
```python
import functools
import math

import jax
import jax.numpy as jnp
from jax import lax
from jax.experimental import pallas as pl
from jax.experimental.pallas import tpu as pltpu
from jax.sharding import PartitionSpec as P

D = 14848
HEAD = 64
KV = 8
GROUP = 28
OUTL = 4
NEW = 2
N_Y = 4
LOCAL_HEADS = 14
CHUNK = 512

epsilon = 1e-05
rope_base = 10000.0
BF = jnp.bfloat16
F32 = jnp.float32
MIB = 1024 * 1024


def lanes_of(columns):
    return [(n, slice(128 * n, min(128 * n + 128, columns))) for n in range((columns + 127) // 128)]


def put(ref, rows, values):
    for n, lanes in lanes_of(values.shape[1]):
        ref[n, rows, 0 : lanes.stop - lanes.start] = values[:, lanes]


def whole(shape):
    return pl.BlockSpec(shape, lambda *_: (0,) * len(shape))


def query_kernel(
    place, x, stats, gain, bias, gain_out, bias_out, scale, extra, weight, pairs, keep, send, acc
):
    step = pl.program_id(0)
    rows = x.shape[0]
    average = stats[:, 0:1] / D
    variance = stats[:, 1:2] / D - average * average
    inverse = lax.rsqrt(variance + epsilon)
    regular = ((x[...].astype(F32) - average) * inverse * gain[...] + bias[...]).astype(BF)
    term = jnp.dot(regular, weight[...], preferred_element_type=F32) * scale[...]
    for k in range(OUTL):
        value = (stats[:, 2 + k : 3 + k] - average) * inverse * gain_out[:, k : k + 1]
        value = (value + bias_out[:, k : k + 1]).astype(BF).astype(F32)
        term = term + value * extra[k : k + 1, :]
    put(acc, pl.ds(pl.multiple_of(step * rows, rows), rows), term)

    @pl.when(step == pl.num_programs(0) - 1)
    def _():
        y = place[0]
        c = place[1]
        for out, core in ((keep, c), (send, 1 - c)):
            for d in range(N_Y):
                j = 2 * lax.rem(y + d, N_Y) + core
                for k in range(6):
                    for n, lanes in lanes_of(896):
                        out[d, 16 * k : 16 * k + 16, lanes] = acc[n, pl.ds(6 * j + k, 16, stride=48), :].astype(BF)
                out[d, 96:112, 0:512] = pairs[j].astype(BF)
                out[d, 96:112, 512:896] = jnp.zeros((16, 384), BF)


def add_kernel(keep, received, o0, o1, o2, o3):
    for d, out in enumerate((o0, o1, o2, o3)):
        out[...] = (keep[d].astype(F32) + received[d].astype(F32)).astype(BF)


def collect_kernel(a, b, c, d, query_out, pair_out, acc):
    total = (a[...].astype(F32) + b[...].astype(F32)) + (c[...].astype(F32) + d[...].astype(F32))
    put(acc, slice(0, 112), total)
    for i in range(16):
        for n, lanes in lanes_of(896):
            query_out[i, :, lanes] = acc[n, pl.ds(i, 6, stride=16), :].astype(BF)
    pair_out[...] = total[96:112, 0:512]


def rotate_lanes(values, cosine, sine):
    lane = lax.broadcasted_iota(jnp.int32, values.shape, 1)
    partner = jnp.where(
        lane % 64 < 32, pltpu.roll(values, 96, axis=1), pltpu.roll(values, 32, axis=1)
    )
    return values * cosine + partner * sine


def attend_kernel(
    lengths, queries, pairs, cosine, sine, keys, values, out,
    staged, rotated, fresh_key, fresh_value, block0, block1, result,
):
    r = pl.program_id(0)
    length = lengths[r]

    @pl.when(r == 0)
    def _():
        for i in range(16):
            put(staged, slice(8 * i, 8 * i + 6), queries[i].astype(F32))
        for k in range(6):
            for col in range(7):
                lanes = slice(128 * col, 128 * col + 128)
                part = staged[col, pl.ds(k, 16, stride=8), :]
                turned = rotate_lanes(part, cosine[k : k + 1, :], sine[k : k + 1, :])
                rotated[16 * k : 16 * k + 16, lanes] = turned.astype(BF).astype(F32) * 0.125
        fresh_key[...] = jnp.zeros_like(fresh_key)
        fresh_value[...] = jnp.zeros_like(fresh_value)
        rounded = pairs[...].astype(BF).astype(F32)
        for col in range(4):
            lanes = slice(128 * col, 128 * col + 128)
            fresh_key[0:6, lanes] = rotate_lanes(rounded[0:6, lanes], cosine[0:6, :], sine[0:6, :])
        fresh_value[0:6, :] = rounded[6:12, :]

    sub = lax.broadcasted_iota(jnp.int32, (8, 256), 0)
    lane = lax.broadcasted_iota(jnp.int32, (8, 256), 1)
    own = sub // 2 == lane // 64
    low = lax.broadcasted_iota(jnp.int32, (8, 128), 1) < 64
    for g, block in enumerate((block0, block1)):
        for t in range(NEW):
            start = pl.multiple_of((NEW * r + t) * 16 + 8 * g, 8)
            for col in range(7):
                part = rotated[pl.ds(start, 8), 128 * col : 128 * col + 128]
                other = pltpu.roll(part, 64, axis=1)
                for half in range(2):
                    both = jnp.where(low, part, other) if half == 0 else jnp.where(low, other, part)
                    both = jnp.concatenate([both, both], axis=1)
                    at = (2 * col + half) * 16 + t * 8
                    block[at : at + 8, :] = jnp.where(own, both, 0.0)

    rows = LOCAL_HEADS * 16
    nt = (((1,), (1,)), ((), ()))
    row = lax.broadcasted_iota(jnp.int32, (rows, 128), 0)
    column = lax.broadcasted_iota(jnp.int32, (rows, 128), 1)
    token = (row // 8) % 2
    visible = (column // 2 == r) & (column % 2 <= token)
    state = []
    grouped = []
    for g, block in enumerate((block0, block1)):
        side = slice(256 * g, 256 * g + 256)
        query = block[...].astype(BF)
        grouped.append(query)
        scores = lax.dot_general(query, fresh_key[:, side].astype(BF), nt, preferred_element_type=F32)
        scores = jnp.where(visible, scores, -jnp.inf)
        top = jnp.max(scores, axis=1, keepdims=True)
        prob = jnp.exp(scores - top)
        total = jnp.sum(prob, axis=1, keepdims=True)
        mixed = jnp.dot(prob.astype(BF), fresh_value[:, side].astype(BF), preferred_element_type=F32)
        state.append((top, total, mixed))

    place = lax.broadcasted_iota(jnp.int32, (rows, CHUNK), 1)

    def body(n, state):
        at = pl.multiple_of(n * CHUNK, CHUNK)
        active = place < length - at
        new = []
        for g in range(2):
            top, total, mixed = state[g]
            side = slice(256 * g, 256 * g + 256)
            key = keys[0, pl.ds(at, CHUNK), side]
            value = values[0, pl.ds(at, CHUNK), side]
            scores = lax.dot_general(grouped[g], key, nt, preferred_element_type=F32)
            scores = jnp.where(active, scores, -jnp.inf)
            higher = jnp.maximum(top, jnp.max(scores, axis=1, keepdims=True))
            shrink = jnp.exp(top - higher)
            prob = jnp.exp(scores - higher)
            total = total * shrink + jnp.sum(prob, axis=1, keepdims=True)
            mixed = mixed * shrink + jnp.dot(prob.astype(BF), value, preferred_element_type=F32)
            new.append((higher, total, mixed))
        return tuple(new)

    state = lax.fori_loop(0, (length + CHUNK - 1) // CHUNK, body, tuple(state))
    for g in range(2):
        top, total, mixed = state[g]
        block0[...] = mixed / total
        for t in range(NEW):
            start = pl.multiple_of((NEW * r + t) * 16 + 8 * g, 8)
            for col in range(7):
                folded = []
                for half in range(2):
                    at = (2 * col + half) * 16 + t * 8
                    part = jnp.where(own, block0[at : at + 8, :], 0.0)
                    part = part[:, 0:128] + part[:, 128:256]
                    folded.append(part + pltpu.roll(part, 64, axis=1))
                result[col, pl.ds(start, 8), :] = jnp.where(low, folded[0], folded[1])

    @pl.when(r == pl.num_programs(0) - 1)
    def _():
        for i in range(16):
            for n, lanes in lanes_of(896):
                out[i, :, lanes] = result[n, pl.ds(i, 6, stride=16), :].astype(BF)


def repack_kernel(block, out, staged):
    for i in range(16):
        put(staged, slice(8 * i, 8 * i + 6), block[i].astype(F32))
    for k in range(6):
        for n, lanes in lanes_of(896):
            out[16 * k : 16 * k + 16, lanes] = staged[n, pl.ds(k, 16, stride=8), :].astype(BF)


def output_kernel(place, b0, b1, b2, b3, s0, s1, s2, s3, chosen, plain, scale, extra, weight, out, left, acc):
    y = place[0]
    c = place[1]
    for blocks, core in (((b0, b1, b2, b3), c), ((s0, s1, s2, s3), 1 - c)):
        for d, block in enumerate(blocks):
            j = 2 * lax.rem(y + N_Y - d, N_Y) + core
            left[pl.ds(pl.multiple_of(96 * j, 96), 96), :] = block[...]
    step = 192
    for n in range(768 // step):
        rows = slice(n * step, n * step + step)
        part = left[rows, :]
        picked = jnp.dot(part, chosen[...], preferred_element_type=F32)
        term = jnp.dot(part * plain[...], weight[...], preferred_element_type=F32) * scale[...]
        for k in range(OUTL):
            term = term + picked[:, k : k + 1] * extra[k : k + 1, :]
        put(acc, rows, term)
    for i in range(16):
        for n, lanes in lanes_of(out.shape[2]):
            got = acc[n, pl.ds(i, 48, stride=16), :].astype(BF)
            out[i, :, lanes] = got[:, 0 : lanes.stop - lanes.start]


def total_kernel(parts, out):
    total = parts[0].astype(F32)
    for i in range(1, 16):
        total = total + parts[i].astype(F32)
    out[...] = total.astype(BF)


def params(mib=48):
    return pltpu.CompilerParams(vmem_limit_bytes=mib * MIB)


def over_y(shift):
    return [(2 * y + c, 2 * ((y + shift) % N_Y) + c) for y in range(N_Y) for c in range(2)]


SIBLING = [(j, j ^ 1) for j in range(2 * N_Y)]


def on_device(
    activations,
    norm_gain,
    norm_bias,
    input_outliers,
    query_int,
    query_scale,
    keyvalue_int,
    keyvalue_scale,
    query_float,
    keyvalue_float,
    key_cache,
    value_cache,
    lengths,
    middle_outliers,
    output_int,
    output_scale,
    output_float,
):
    block_rows, features = activations.shape
    tokens = block_rows * 16
    columns = query_int.shape[1]
    out_columns = output_int.shape[1]
    me_x = lax.axis_index("gx")
    me_y = lax.axis_index("gy")
    place = jnp.stack([me_y // 2, me_y % 2]).astype(jnp.int32)

    gathered = lax.all_gather(activations, "gx", axis=0, tiled=True)

    widened = activations.astype(F32)
    sums = lax.psum(
        jnp.stack([jnp.sum(widened, axis=1), jnp.sum(widened * widened, axis=1)], axis=1), "gy"
    )
    picked = jnp.arange(features, dtype=jnp.int32)[:, None] == input_outliers[None, :]
    raw = jnp.dot(activations, picked.astype(BF), preferred_element_type=F32)
    stats = lax.all_gather(jnp.concatenate([sums, raw], axis=1), "gx", axis=0, tiled=True)

    is_outlier = jnp.any(picked, axis=1)
    gain_regular = jnp.where(is_outlier, 0.0, norm_gain)
    bias_regular = jnp.where(is_outlier, 0.0, norm_bias)
    gain_out = jnp.sum(jnp.where(picked, norm_gain[:, None], 0.0), axis=0)
    bias_out = jnp.sum(jnp.where(picked, norm_bias[:, None], 0.0), axis=0)

    average = sums[:, 0:1] / D
    inverse = lax.rsqrt(sums[:, 1:2] / D - average * average + epsilon)
    own_regular = ((widened - average) * inverse * gain_regular + bias_regular).astype(BF)
    own_outlier = ((raw - average) * inverse * gain_out + bias_out).astype(BF)
    pairs = jnp.dot(own_regular, keyvalue_int, preferred_element_type=F32) * keyvalue_scale
    pairs = pairs + jnp.dot(own_outlier.astype(F32), keyvalue_float, precision=lax.Precision.HIGHEST)
    pairs = pairs.reshape(8, 6, 2, 512).transpose(0, 2, 1, 3).reshape(8, 12, 512)
    pairs = jnp.pad(pairs, ((0, 0), (0, 4), (0, 0)))

    part_rows = tokens // 4
    smem = pl.BlockSpec(memory_space=pltpu.SMEM)
    keep, send = pl.pallas_call(
        query_kernel,
        grid=(4,),
        in_specs=[
            smem,
            pl.BlockSpec((part_rows, features), lambda n: (n, 0)),
            pl.BlockSpec((part_rows, 6), lambda n: (n, 0)),
            whole((1, features)),
            whole((1, features)),
            whole((1, OUTL)),
            whole((1, OUTL)),
            whole((1, columns)),
            whole((OUTL, columns)),
            whole((features, columns)),
            whole((8, 16, 512)),
        ],
        out_specs=[whole((N_Y, 112, columns))] * 2,
        out_shape=[jax.ShapeDtypeStruct((N_Y, 112, columns), BF)] * 2,
        scratch_shapes=[pltpu.VMEM((7, tokens, 128), F32)],
        compiler_params=params(),
        name="query_projection",
    )(
        place, gathered, stats, gain_regular[None], bias_regular[None], gain_out[None], bias_out[None],
        query_scale[None], query_float, query_int, pairs,
    )
    received = lax.ppermute(send, "gy", SIBLING)
    piece = jax.ShapeDtypeStruct((112, columns), BF)
    mine, to1, to2, to3 = pl.pallas_call(
        add_kernel, out_shape=[piece] * 4, compiler_params=params(), name="add_cores"
    )(keep, received)
    from1 = lax.ppermute(to1, "gy", over_y(1))
    from3 = lax.ppermute(to3, "gy", over_y(3))
    from2 = lax.ppermute(to2, "gy", over_y(2))
    summed, pair_sums = pl.pallas_call(
        collect_kernel,
        out_shape=[
            jax.ShapeDtypeStruct((16, 6, columns), BF),
            jax.ShapeDtypeStruct((16, 512), F32),
        ],
        scratch_shapes=[pltpu.VMEM((7, 112, 128), F32)],
        compiler_params=params(),
        name="collect",
    )(mine, from1, from2, from3)
    queries = lax.all_to_all(summed, "gx", split_axis=0, concat_axis=0, tiled=True)

    positions = (lengths[:, None] + jnp.arange(NEW, dtype=jnp.int32)[None, :]).reshape(6, 1)
    frequency = jnp.exp(jnp.arange(32, dtype=F32) * (-2.0 * math.log(rope_base) / HEAD))
    angles = positions.astype(F32) * frequency[None, :]
    cosine = jnp.tile(jnp.cos(angles), (1, 4))
    sine = jnp.sin(angles)
    sine = jnp.concatenate([-sine, sine, -sine, sine], axis=1)
    cosine = jnp.pad(cosine, ((0, 2), (0, 0)))
    sine = jnp.pad(sine, ((0, 2), (0, 0)))

    window = key_cache.shape[1]
    attended = pl.pallas_call(
        attend_kernel,
        grid=(3,),
        in_specs=[
            smem,
            whole((16, 6, columns)),
            whole((16, 512)),
            whole((8, 128)),
            whole((8, 128)),
            pl.BlockSpec((1, window, 512), lambda n: (n, 0, 0)),
            pl.BlockSpec((1, window, 512), lambda n: (n, 0, 0)),
        ],
        out_specs=whole((16, 6, columns)),
        out_shape=jax.ShapeDtypeStruct((16, 6, columns), BF),
        scratch_shapes=[
            pltpu.VMEM((7, 128, 128), F32),
            pltpu.VMEM((96, columns), F32),
            pltpu.VMEM((128, 512), F32),
            pltpu.VMEM((128, 512), F32),
            pltpu.VMEM((224, 256), F32),
            pltpu.VMEM((224, 256), F32),
            pltpu.VMEM((7, 96, 128), F32),
        ],
        compiler_params=params(),
        name="attention",
    )(lengths, queries, pair_sums, cosine, sine, key_cache, value_cache)

    back = lax.all_to_all(attended, "gx", split_axis=0, concat_axis=0, tiled=True)
    mine = pl.pallas_call(
        repack_kernel,
        out_shape=jax.ShapeDtypeStruct((96, columns), BF),
        scratch_shapes=[pltpu.VMEM((7, 128, 128), F32)],
        compiler_params=params(),
        name="repack",
    )(back)
    blocks = [mine] + [lax.ppermute(mine, "gy", over_y(d)) for d in (1, 2, 3)]
    blocks = blocks + [lax.ppermute(b, "gy", SIBLING) for b in blocks]

    middle = lax.dynamic_slice(middle_outliers, (me_x * OUTL,), (OUTL,))
    chosen = jnp.arange(columns, dtype=jnp.int32)[:, None] == middle[None, :]
    plain = jnp.where(jnp.any(chosen, axis=1), 0.0, 1.0).astype(BF)[None]
    chosen = jnp.pad(chosen.astype(BF), ((0, 0), (0, 128 - OUTL)))
    vmem = pl.BlockSpec(memory_space=pltpu.VMEM)
    partial = pl.pallas_call(
        output_kernel,
        in_specs=[smem] + [vmem] * 13,
        out_specs=vmem,
        out_shape=jax.ShapeDtypeStruct((16, block_rows, out_columns), BF),
        scratch_shapes=[pltpu.VMEM((tokens, columns), BF), pltpu.VMEM((15, tokens, 128), F32)],
        compiler_params=params(),
        name="output_projection",
    )(place, *blocks, chosen, plain, output_scale[None], output_float, output_int)
    parts = lax.all_to_all(partial, "gx", split_axis=0, concat_axis=0, tiled=True)
    return pl.pallas_call(
        total_kernel,
        out_shape=jax.ShapeDtypeStruct((block_rows, out_columns), BF),
        compiler_params=params(),
        name="total",
    )(parts)


def solution(mesh):
    placed = (
        P("gx", "gy"),
        P("gy"),
        P("gy"),
        P("gy"),
        P("gy", "gx"),
        P("gx"),
        P("gy", None),
        P(),
        P("gy", "gx"),
        P("gy", None),
        P(("gx", "gy"), None, None),
        P(("gx", "gy"), None, None),
        P(("gx", "gy")),
        P(),
        P("gx", "gy"),
        P("gy"),
        P("gx", "gy"),
    )
    return jax.shard_map(
        on_device, mesh=mesh, in_specs=placed, out_specs=P("gx", "gy"), check_vma=False
    )
```

time: 339 us -> 200 us (0.59)
  waiting for transfers between devices: 108 us -> 34.3 us
  local copies, waits for them, and re-layouts: 65.3 us -> 9.21 us
  matrix products: 36.5 us -> 4.44 us
  Pallas kernels: 0 us -> 29.9 us
  starting transfers between devices: 8.8 us -> 29.3 us
  other arithmetic: 22.1 us -> 4.16 us
  blocking collectives: 81.6 us -> 73.8 us
    unnamed x7 -> x1, waiting for transfers between devices: 74.9 us -> 0.71 us
    dot_general x12 -> x3, matrix products: 36.5 us -> 4.44 us  [the longest x1 2.92 us: on_device(): jnp.dot(own_regular, keyvalue_int, preferred_element_type=F32)]
    pallas_call x0 -> x7, Pallas kernels: none -> 29.9 us  [the longest x1 10.9 us: on_device(): pl.pallas_call(attend_kernel, grid=(3,), in_specs=[smem, whole((16, 6, co...]
    ppermute x0 -> x11, starting transfers between devices: none -> 21.5 us  [the longest x4 9.93 us: on_device(): blocks = blocks + [lax.ppermute(b, 'gy', SIBLING) for b in blocks]]
    reshape x8 -> x3, local copies, waits for them, and re-layouts: 21.6 us -> 0.35 us  [on_device(): pairs.reshape(8, 6, 2, 512).transpose(0, 2, 1, 3).reshape(8, 12, 512)]
    all_to_all x2 -> x1, blocking collectives: 19.6 us -> 39.9 us  [on_device(): lax.all_to_all(partial, 'gx', split_axis=0, concat_axis=0, tiled=True)]
    all_gather x2 -> x1, waiting for transfers between devices: 27.8 us -> 9.57 us  [on_device(): gathered = lax.all_gather(activations, 'gx', axis=0, tiled=True)]
    unnamed x1 -> x0, blocking collectives: 15.7 us -> none
  transfers between devices with their start and end apart: 7 -> 14, of which waited for: 3 -> 6; matrix products, arithmetic and copies ran while one was open for 17% -> 8% of each run, Pallas kernels for 0% -> 0%
where the time goes in v1:
time: 200 us; the launch traced here: 199 us
  blocking collectives  73.8 us (37%)
  waiting for transfers between devices  34.3 us (17%)
  Pallas kernels  29.9 us (15%)
  starting transfers between devices  29.3 us (15%)
  between operations  13.6 us (7%)
  local copies, waits for them, and re-layouts  9.21 us (5%)
  matrix products  4.44 us (2%)
  other arithmetic  4.16 us (2%)
    all_to_all x1, blocking collectives, on_device(): lax.all_to_all(partial, 'gx', split_axis=0, concat_axis=0, tiled=True)  39.9 us
    all_gather x1, blocking collectives, on_device(): lax.all_gather(jnp.concatenate([sums, raw], axis=1), 'gx', axis=0, tiled=...  20.4 us
    psum x1, blocking collectives, on_device(): lax.psum(jnp.stack([jnp.sum(widened, axis=1), jnp.sum(widened * widened,...  13.5 us
    pallas_call x1, Pallas kernels, on_device(): pl.pallas_call(attend_kernel, grid=(3,), in_specs=[smem, whole((16, 6, co...  10.9 us
    ppermute x4, starting transfers between devices, on_device(): blocks = blocks + [lax.ppermute(b, 'gy', SIBLING) for b in blocks]  9.93 us
    all_gather x1, waiting for transfers between devices, on_device(): gathered = lax.all_gather(activations, 'gx', axis=0, tiled=True)  9.57 us
    pallas_call x1, Pallas kernels, on_device(): pl.pallas_call(output_kernel, in_specs=[smem] + [vmem] * 13, out_specs=vm...  8.66 us
    pallas_call x1, Pallas kernels, on_device(): pl.pallas_call(query_kernel, grid=(4,), in_specs=[smem, pl.BlockSpec((par...  8.06 us
  transfers between devices with their start and end apart: 14, of which 6 were waited for; matrix products, arithmetic and copies ran while one was open for 8% of the time, Pallas kernels for 0%

profile of v1, /device:TPU:1, one launch (start us, length us, event | category | flops | bytes accessed | tf_op | source)
XLA Modules:
  0.0 198.8 jit_solution(17649369958173904842)
XLA Ops:
  6.5 0.7 all-gather.3.cloned.1.call-update
  7.3 0.7 broadcast_in_dim.72.scale
  8.0 0.8 fusion.10
  8.7 0.7 broadcast_select_fusion
  9.5 1.1 convert_reduce_fusion
  10.6 13.5 %psum.7 = f32[48,2]{0,1:T(2,128)S(1)} all-reduce(f32[48,2]{0,1:T(2,128)S(1)} %pad_maximum_fusion), channel_id=1, replica_groups=mesh['gx'=16,'gy'=8] {'gy'}, use_global_device_ids=true, to_apply=%region_2.3 | all-reduce | flops 96 | bytes 768 | tf_op jit(solution)/shard_map/psum | solution.py:275
  24.0 1.0 select_reduce_fusion
  25.0 1.2 convolution_bitcast_fusion
  26.2 2.9 %convolution_multiply_fusion = f32[48,1024]{1,0:T(8,128)S(1)} fusion(bf16[1856,1024]{1,0:T(8,128)(2,1)} %param.23, bf16[48,1856]{1,0:T(8,128)(2,1)} %param.17, f32[1856]{0:T(1024)S(1)} %get-tuple-element.25, f32[1856]{0:T(1024)S(1)} %get-tuple-element.26, f32[48]{0:T(128)S(1)} %get-tuple-element.31, f32[48]{0:T(128)S(1)} %get-tuple-element.30, f32[1024]{0:T(1024)} %param.24), kind=kOutput, calls=%fused_computation.1 | convolution fusion | flops 183035904 | bytes 4195200 | tf_op jit(solution)/shard_map/dot_general | solution.py:292
  29.1 0.4 convolution_add_fusion
  29.5 0.2 reshape.82
  29.7 0.1 copy.31
  29.8 20.4 %all-gather = f32[16,48,6]{1,2,0:T(8,128)S(1)} all-gather(f32[1,48,6]{1,2,0:T(8,128)S(1)} %maximum_bitcast_fusion), channel_id=1, replica_groups=mesh['gx'=16,'gy'=8] {'gx'}, dimensions={0}, use_global_device_ids=true | all-gather | bytes 19584 | tf_op jit(solution)/shard_map/all_gather | solution.py:280
  50.3 0.2 copy.29
  50.5 0.1 pad_add_fusion.place
  50.6 9.6 %all-gather.3.cloned.1.call-done.x = bf16[768,1856]{1,0:T(8,128)(2,1)} async-done(((bf16[48,1856]{1,0:T(8,128)(2,1)}), bf16[768,1856]{1,0:T(8,128)(2,1)}) %all-gather.3.cloned.1.call-update) | async-done | bytes 2850832 | tf_op jit(solution)/shard_map/all_gather | solution.py:272
  60.2 1.8 copy-done.1
  62.0 8.1 %query_projection.1 = (bf16[4,112,896]{2,1,0:T(8,128)(2,1)S(1)}, bf16[4,112,896]{2,1,0:T(8,128)(2,1)S(1)}) custom-call(s32[2]{0:T(128)S(1)} %pad_add_fusion.place, bf16[768,1856]{1,0:T(8,128)(2,1)S(1)} %copy-done.1, f32[768,6]{1,0:T(8,128)S(1)} %bitcast.21, f32[1,1856]{1,0:T(1,128)S(1)} %broadcast_in_dim.65.gain, f32[1,1856]{1,0:T(1,128)S(1)} %broadcast_in_dim.66.bias, ...), custom_call_target="tpu_custom_call" | custom-call | tf_op jit(solution)/shard_map/query_projection/pallas_call | solution.py:299
  70.1 1.0 collective-permute-start
  71.1 1.9 collective-permute-done.received
  73.0 0.2 add_cores.1
  73.2 1.3 collective-permute-start.1
  74.5 2.4 %collective-permute-start.2 = (bf16[112,896]{1,0:T(8,128)(2,1)S(1)}, bf16[112,896]{1,0:T(8,128)(2,1)S(1)}, u32[]{:S(2)}, u32[]{:S(2)}) collective-permute-start(bf16[112,896]{1,0:T(8,128)(2,1)S(1)} %get-tuple-element.17), channel_id=1, source_target_pairs={{0,4},{1,5},{2,6},{3,7},{4,0},{5,1},{6,2},{7,3},{8,12},{9,13},{10,... | collective-permute-start | bytes 602120 | tf_op jit(solution)/shard_map/ppermute | solution.py:331
  76.9 1.1 collective-permute-start.3
  78.1 0.1 convert_element_type.47
  78.2 2.5 %collective-permute-done.1.b = bf16[112,896]{1,0:T(8,128)(2,1)S(1)} collective-permute-done((bf16[112,896]{1,0:T(8,128)(2,1)S(1)}, bf16[112,896]{1,0:T(8,128)(2,1)S(1)}, u32[]{:S(2)}, u32[]{:S(2)}) %collective-permute-start.1) | collective-permute-done | bytes 200736 | tf_op jit(solution)/shard_map/ppermute | solution.py:329
  80.7 5.3 %collective-permute-done.2.c = bf16[112,896]{1,0:T(8,128)(2,1)S(1)} collective-permute-done((bf16[112,896]{1,0:T(8,128)(2,1)S(1)}, bf16[112,896]{1,0:T(8,128)(2,1)S(1)}, u32[]{:S(2)}, u32[]{:S(2)}) %collective-permute-start.2) | collective-permute-done | bytes 200736 | tf_op jit(solution)/shard_map/ppermute | solution.py:331
  86.0 1.0 collect.1
  86.9 4.3 %all-to-all-start = ((bf16[16,6,896]{2,1,0:T(8,128)(2,1)}), bf16[16,6,896]{2,1,0:T(8,128)(2,1)S(1)}, u32[]{:S(2)}, u32[]{:S(2)}) async-start(bf16[16,6,896]{2,1,0:T(8,128)(2,1)} %get-tuple-element.19), calls=%async_computation | async-start | bytes 458752 | tf_op jit(solution)/shard_map/all_to_all | solution.py:342
  91.2 0.1 fusion.17
  91.3 0.1 tile.10
  91.5 7.1 %all-to-all-done.queries = bf16[16,6,896]{2,1,0:T(8,128)(2,1)S(1)} async-done(((bf16[16,6,896]{2,1,0:T(8,128)(2,1)}), bf16[16,6,896]{2,1,0:T(8,128)(2,1)S(1)}, u32[]{:S(2)}, u32[]{:S(2)}) %all-to-all-start) | async-done | bytes 172064 | tf_op jit(solution)/shard_map/all_to_all | solution.py:342
  98.6 10.9 %attention.1 = bf16[16,6,896]{2,1,0:T(8,128)(2,1)} custom-call(s32[3]{0:T(128)S(1)} %copy-done.4, bf16[16,6,896]{2,1,0:T(8,128)(2,1)S(1)} %all-to-all-done.queries, f32[16,512]{1,0:T(8,128)S(1)} %get-tuple-element.20.pairs, f32[8,128]{1,0:T(8,128)S(1)} %pad.18.cosine, f32[8,128]{1,0:T(8,128)S(1)} %select_maximum_fusion.sine, bf16[3,2048,512]{2,1,0:T(8,128)(2,1)} %keys.1, ...), custom_call_target="tpu_custom_call" | custom-call | tf_op jit(solution)/shard_map/attention/pallas_call | solution.py:354
  109.5 3.5 %all-to-all-start.1 = ((bf16[16,6,896]{2,1,0:T(8,128)(2,1)}), bf16[16,6,896]{2,1,0:T(8,128)(2,1)S(1)}, u32[]{:S(2)}, u32[]{:S(2)}) async-start(bf16[16,6,896]{2,1,0:T(8,128)(2,1)} %attention.1), calls=%async_computation.1 | async-start | bytes 458752 | tf_op jit(solution)/shard_map/all_to_all | solution.py:381
  113.1 7.2 %all-to-all-done.1.block = bf16[16,6,896]{2,1,0:T(8,128)(2,1)S(1)} async-done(((bf16[16,6,896]{2,1,0:T(8,128)(2,1)}), bf16[16,6,896]{2,1,0:T(8,128)(2,1)S(1)}, u32[]{:S(2)}, u32[]{:S(2)}) %all-to-all-start.1) | async-done | bytes 172064 | tf_op jit(solution)/shard_map/all_to_all | solution.py:381
  120.3 0.1 repack.1.b0
  120.4 3.5 %collective-permute-start.6 = (bf16[96,896]{1,0:T(8,128)(2,1)S(1)}, bf16[96,896]{1,0:T(8,128)(2,1)S(1)}, u32[]{:S(2)}, u32[]{:S(2)}) collective-permute-start(bf16[96,896]{1,0:T(8,128)(2,1)S(1)} %repack.1.b0), channel_id=1, source_target_pairs={{0,6},{1,7},{2,0},{3,1},{4,2},{5,3},{6,4},{7,5},{8,14},{9,15},{10,... | collective-permute-start | bytes 516104 | tf_op jit(solution)/shard_map/ppermute | solution.py:389
  124.0 1.5 collective-permute-start.5
  125.4 0.8 collective-permute-start.4
  126.2 0.2 fusion.12
  126.4 3.6 %collective-permute-start.7 = (bf16[96,896]{1,0:T(8,128)(2,1)S(1)}, bf16[96,896]{1,0:T(8,128)(2,1)S(1)}, u32[]{:S(2)}, u32[]{:S(2)}) collective-permute-start(bf16[96,896]{1,0:T(8,128)(2,1)S(1)} %repack.1.b0), channel_id=1, source_target_pairs={{0,1},{1,0},{2,3},{3,2},{4,5},{5,4},{6,7},{7,6},{8,9},{9,8},{10,11... | collective-permute-start | bytes 516104 | tf_op jit(solution)/shard_map/ppermute | solution.py:390
  130.0 2.9 %collective-permute-start.10 = (bf16[96,896]{1,0:T(8,128)(2,1)S(1)}, bf16[96,896]{1,0:T(8,128)(2,1)S(1)}, u32[]{:S(2)}, u32[]{:S(2)}) collective-permute-start(bf16[96,896]{1,0:T(8,128)(2,1)S(1)} %collective-permute-done.6.b3), channel_id=1, source_target_pairs={{0,1},{1,0},{2,3},{3,2},{4,5},{5,4},{6,7},{7,6},{8,9},{9,8},{10,11... | collective-permute-start | bytes 516104 | tf_op jit(solution)/shard_map/ppermute | solution.py:390
  132.9 1.7 collective-permute-start.9
  134.6 1.8 collective-permute-start.8
  136.4 5.8 %copy.32.weight = bf16[896,1856]{1,0:T(8,128)(2,1)} copy(bf16[896,1856]{0,1:T(8,128)(2,1)} %param.31) | data formatting | bytes 6651904 | tf_op args[14]
  142.3 8.7 %output_projection.1 = bf16[16,48,1856]{2,1,0:T(8,128)(2,1)S(1)} custom-call(s32[2]{0:T(128)S(1)} %pad_add_fusion.place, bf16[96,896]{1,0:T(8,128)(2,1)S(1)} %repack.1.b0, bf16[96,896]{1,0:T(8,128)(2,1)S(1)} %collective-permute-done.4.b1, bf16[96,896]{1,0:T(8,128)(2,1)S(1)} %collective-permute-done.5.b2, bf16[96,896]{1,0:T(8,128)(2,1)S(1)} %collective-permute-done.6.b3, ...), custom_call_target="tpu_custom_call" | custom-call | tf_op jit(solution)/shard_map/output_projection/pallas_call | solution.py:397
  151.0 39.9 %all_to_all.15.parts = bf16[16,48,1856]{2,1,0:T(8,128)(2,1)S(1)} all-to-all(bf16[16,48,1856]{2,1,0:T(8,128)(2,1)S(1)} %output_projection.1), channel_id=1, replica_groups=mesh['gx'=16,'gy'=8] {'gx'}, dimensions={0} | all-to-all | bytes 5701632 | tf_op jit(solution)/shard_map/all_to_all | solution.py:406
  190.9 1.1 total.1
  (39 shorter events, 0.5 us)
Async XLA Ops:
  6.5 22.5 %copy-start = (f32[4,1024]{1,0:T(4,128)S(1)}, f32[4,1024]{1,0:T(4,128)}, u32[]{:S(2)}) copy-start(f32[4,1024]{1,0:T(4,128)} %param.26) | copy-start | bytes 49156
  6.5 53.6 %copy-start.3 = (f32[4,896]{1,0:T(4,128)S(1)}, f32[4,896]{1,0:T(4,128)}, u32[]{:S(2)}) copy-start(f32[4,896]{1,0:T(4,128)} %extra.2) | copy-start | bytes 43012
  6.5 53.6 %all-gather.3.cloned.1.call-start = ((), (), s32[]{:S(2)}) async-start(), calls=%async_computation.3 | async-start | bytes 3133440 | tf_op jit(solution)/shard_map/all_gather | solution.py:272
  60.2 1.8 copy-start.1
  62.0 16.0 %copy-start.4 = (s32[3]{0:T(128)S(1)}, s32[3]{0:T(128)}, u32[]{:S(2)}) copy-start(s32[3]{0:T(128)} %lengths.1) | copy-start | bytes 40
  70.1 2.9 %collective-permute-start = (bf16[4,112,896]{2,1,0:T(8,128)(2,1)S(1)}, bf16[4,112,896]{2,1,0:T(8,128)(2,1)S(1)}, u32[]{:S(2)}, u32[]{:S(2)}) collective-permute-start(bf16[4,112,896]{2,1,0:T(8,128)(2,1)S(1)} %get-tuple-element.14), channel_id=1, source_target_pairs={{0,1},{1,0},{2,3},{3,2},{4,5},{5,4},{6,7},{7,6},{8,9},{9,8},{10,11... | collective-permute-start | bytes 2408456 | tf_op jit(solution)/shard_map/ppermute | solution.py:324
  73.2 7.5 %collective-permute-start.1 = (bf16[112,896]{1,0:T(8,128)(2,1)S(1)}, bf16[112,896]{1,0:T(8,128)(2,1)S(1)}, u32[]{:S(2)}, u32[]{:S(2)}) collective-permute-start(bf16[112,896]{1,0:T(8,128)(2,1)S(1)} %get-tuple-element.16), channel_id=1, source_target_pairs={{0,2},{1,3},{2,4},{3,5},{4,6},{5,7},{6,0},{7,1},{8,10},{9,11},{10,... | collective-permute-start | bytes 602120 | tf_op jit(solution)/shard_map/ppermute | solution.py:329
  74.5 11.5 %collective-permute-start.2 = (bf16[112,896]{1,0:T(8,128)(2,1)S(1)}, bf16[112,896]{1,0:T(8,128)(2,1)S(1)}, u32[]{:S(2)}, u32[]{:S(2)}) collective-permute-start(bf16[112,896]{1,0:T(8,128)(2,1)S(1)} %get-tuple-element.17), channel_id=1, source_target_pairs={{0,4},{1,5},{2,6},{3,7},{4,0},{5,1},{6,2},{7,3},{8,12},{9,13},{10,... | collective-permute-start | bytes 602120 | tf_op jit(solution)/shard_map/ppermute | solution.py:331
  76.9 9.0 %collective-permute-start.3 = (bf16[112,896]{1,0:T(8,128)(2,1)S(1)}, bf16[112,896]{1,0:T(8,128)(2,1)S(1)}, u32[]{:S(2)}, u32[]{:S(2)}) collective-permute-start(bf16[112,896]{1,0:T(8,128)(2,1)S(1)} %get-tuple-element.18), channel_id=1, source_target_pairs={{0,6},{1,7},{2,0},{3,1},{4,2},{5,3},{6,4},{7,5},{8,14},{9,15},{10,... | collective-permute-start | bytes 602120 | tf_op jit(solution)/shard_map/ppermute | solution.py:330
  86.9 11.7 %all-to-all-start = ((bf16[16,6,896]{2,1,0:T(8,128)(2,1)}), bf16[16,6,896]{2,1,0:T(8,128)(2,1)S(1)}, u32[]{:S(2)}, u32[]{:S(2)}) async-start(bf16[16,6,896]{2,1,0:T(8,128)(2,1)} %get-tuple-element.19), calls=%async_computation | async-start | bytes 458752 | tf_op jit(solution)/shard_map/all_to_all | solution.py:342
  98.6 14.4 %copy-start.6 = (s32[64]{0:T(128)S(1)}, s32[64]{0:T(128)}, u32[]{:S(2)}) copy-start(s32[64]{0:T(128)} %param.30) | copy-start | bytes 772
  98.6 37.8 %copy-start.5 = (f32[1856]{0:T(1024)S(1)}, f32[1856]{0:T(1024)}, u32[]{:S(2)}) copy-start(f32[1856]{0:T(1024)} %param.32) | copy-start | bytes 22276
  109.5 10.9 %all-to-all-start.1 = ((bf16[16,6,896]{2,1,0:T(8,128)(2,1)}), bf16[16,6,896]{2,1,0:T(8,128)(2,1)S(1)}, u32[]{:S(2)}, u32[]{:S(2)}) async-start(bf16[16,6,896]{2,1,0:T(8,128)(2,1)} %attention.1), calls=%async_computation.1 | async-start | bytes 458752 | tf_op jit(solution)/shard_map/all_to_all | solution.py:381
  113.1 29.2 %copy-start.2 = (f32[4,1856]{1,0:T(4,128)S(1)}, f32[4,1856]{1,0:T(4,128)}, u32[]{:S(2)}) copy-start(f32[4,1856]{1,0:T(4,128)} %extra.3) | copy-start | bytes 89092
  120.4 9.6 %collective-permute-start.6 = (bf16[96,896]{1,0:T(8,128)(2,1)S(1)}, bf16[96,896]{1,0:T(8,128)(2,1)S(1)}, u32[]{:S(2)}, u32[]{:S(2)}) collective-permute-start(bf16[96,896]{1,0:T(8,128)(2,1)S(1)} %repack.1.b0), channel_id=1, source_target_pairs={{0,6},{1,7},{2,0},{3,1},{4,2},{5,3},{6,4},{7,5},{8,14},{9,15},{10,... | collective-permute-start | bytes 516104 | tf_op jit(solution)/shard_map/ppermute | solution.py:389
  124.0 8.9 %collective-permute-start.5 = (bf16[96,896]{1,0:T(8,128)(2,1)S(1)}, bf16[96,896]{1,0:T(8,128)(2,1)S(1)}, u32[]{:S(2)}, u32[]{:S(2)}) collective-permute-start(bf16[96,896]{1,0:T(8,128)(2,1)S(1)} %repack.1.b0), channel_id=1, source_target_pairs={{0,4},{1,5},{2,6},{3,7},{4,0},{5,1},{6,2},{7,3},{8,12},{9,13},{10,... | collective-permute-start | bytes 516104 | tf_op jit(solution)/shard_map/ppermute | solution.py:389
  125.4 9.2 %collective-permute-start.4 = (bf16[96,896]{1,0:T(8,128)(2,1)S(1)}, bf16[96,896]{1,0:T(8,128)(2,1)S(1)}, u32[]{:S(2)}, u32[]{:S(2)}) collective-permute-start(bf16[96,896]{1,0:T(8,128)(2,1)S(1)} %repack.1.b0), channel_id=1, source_target_pairs={{0,2},{1,3},{2,4},{3,5},{4,6},{5,7},{6,0},{7,1},{8,10},{9,11},{10,... | collective-permute-start | bytes 516104 | tf_op jit(solution)/shard_map/ppermute | solution.py:389
  126.4 15.8 %collective-permute-start.7 = (bf16[96,896]{1,0:T(8,128)(2,1)S(1)}, bf16[96,896]{1,0:T(8,128)(2,1)S(1)}, u32[]{:S(2)}, u32[]{:S(2)}) collective-permute-start(bf16[96,896]{1,0:T(8,128)(2,1)S(1)} %repack.1.b0), channel_id=1, source_target_pairs={{0,1},{1,0},{2,3},{3,2},{4,5},{5,4},{6,7},{7,6},{8,9},{9,8},{10,11... | collective-permute-start | bytes 516104 | tf_op jit(solution)/shard_map/ppermute | solution.py:390
  130.0 12.3 %collective-permute-start.10 = (bf16[96,896]{1,0:T(8,128)(2,1)S(1)}, bf16[96,896]{1,0:T(8,128)(2,1)S(1)}, u32[]{:S(2)}, u32[]{:S(2)}) collective-permute-start(bf16[96,896]{1,0:T(8,128)(2,1)S(1)} %collective-permute-done.6.b3), channel_id=1, source_target_pairs={{0,1},{1,0},{2,3},{3,2},{4,5},{5,4},{6,7},{7,6},{8,9},{9,8},{10,11... | collective-permute-start | bytes 516104 | tf_op jit(solution)/shard_map/ppermute | solution.py:390
  132.9 9.4 %collective-permute-start.9 = (bf16[96,896]{1,0:T(8,128)(2,1)S(1)}, bf16[96,896]{1,0:T(8,128)(2,1)S(1)}, u32[]{:S(2)}, u32[]{:S(2)}) collective-permute-start(bf16[96,896]{1,0:T(8,128)(2,1)S(1)} %collective-permute-done.5.b2), channel_id=1, source_target_pairs={{0,1},{1,0},{2,3},{3,2},{4,5},{5,4},{6,7},{7,6},{8,9},{9,8},{10,11... | collective-permute-start | bytes 516104 | tf_op jit(solution)/shard_map/ppermute | solution.py:390
  134.6 7.7 %collective-permute-start.8 = (bf16[96,896]{1,0:T(8,128)(2,1)S(1)}, bf16[96,896]{1,0:T(8,128)(2,1)S(1)}, u32[]{:S(2)}, u32[]{:S(2)}) collective-permute-start(bf16[96,896]{1,0:T(8,128)(2,1)S(1)} %collective-permute-done.4.b1), channel_id=1, source_target_pairs={{0,1},{1,0},{2,3},{3,2},{4,5},{5,4},{6,7},{7,6},{8,9},{9,8},{10,11... | collective-permute-start | bytes 516104 | tf_op jit(solution)/shard_map/ppermute | solution.py:390
Sparse Core Ops, SparseCore 0:
  9.5 50.6 all-gather.2

commit v2 on v1

--- a/solution.py
+++ b/solution.py
@@ -23,6 +23,8 @@
 BF = jnp.bfloat16
 F32 = jnp.float32
 MIB = 1024 * 1024
+STEPS = (0, 1, 3, 2)
+NT = (((1,), (1,)), ((), ()))
 
 
 def lanes_of(columns):
@@ -38,34 +40,59 @@
     return pl.BlockSpec(shape, lambda *_: (0,) * len(shape))
 
 
+def normalize_kernel(place, parts, x, gain, bias, picked, plain, own, keep, send):
+    sums = jnp.sum(parts[...], axis=0)
+    rows = x.shape[0]
+    unit = lax.broadcasted_iota(jnp.int32, (rows, rows), 0) == lax.broadcasted_iota(jnp.int32, (rows, rows), 1)
+    sums = lax.dot_general(
+        unit.astype(F32), sums, NT, precision=lax.Precision.HIGHEST, preferred_element_type=F32
+    )
+    average = sums[:, 0:1] / D
+    variance = sums[:, 1:2] / D - average * average
+    normed = (x[...].astype(F32) - average) * lax.rsqrt(variance + epsilon) * gain[...] + bias[...]
+    rounded = normed.astype(BF)
+    outlier = jnp.dot(rounded, picked[...], preferred_element_type=F32)
+    regular = rounded.astype(F32) * plain[...]
+    features = x.shape[1]
+    own[:, 0:features] = regular.astype(BF)
+    own[:, features:] = outlier[:, 0:64].astype(BF)
+    half = rows // 2
+    first = place[1] == 0
+    for out, flag in ((keep, first), (send, jnp.logical_not(first))):
+        out[:, 0:features] = jnp.where(flag, regular[0:half], regular[half:]).astype(BF)
+        out[:, features:] = jnp.where(flag, outlier[0:half, 0:64], outlier[half:, 0:64]).astype(BF)
+
+
 def query_kernel(
-    place, x, stats, gain, bias, gain_out, bias_out, scale, extra, weight, pairs, keep, send, acc
+    place, a0, a1, a2, a3, b0, b1, b2, b3, scale, extra, weight, pairs, keep, send, acc
 ):
-    step = pl.program_id(0)
-    rows = x.shape[0]
-    average = stats[:, 0:1] / D
-    variance = stats[:, 1:2] / D - average * average
-    inverse = lax.rsqrt(variance + epsilon)
-    regular = ((x[...].astype(F32) - average) * inverse * gain[...] + bias[...]).astype(BF)
-    term = jnp.dot(regular, weight[...], preferred_element_type=F32) * scale[...]
-    for k in range(OUTL):
-        value = (stats[:, 2 + k : 3 + k] - average) * inverse * gain_out[:, k : k + 1]
-        value = (value + bias_out[:, k : k + 1]).astype(BF).astype(F32)
-        term = term + value * extra[k : k + 1, :]
-    put(acc, pl.ds(pl.multiple_of(step * rows, rows), rows), term)
-
-    @pl.when(step == pl.num_programs(0) - 1)
-    def _():
-        y = place[0]
-        c = place[1]
-        for out, core in ((keep, c), (send, 1 - c)):
-            for d in range(N_Y):
-                j = 2 * lax.rem(y + d, N_Y) + core
-                for k in range(6):
-                    for n, lanes in lanes_of(896):
-                        out[d, 16 * k : 16 * k + 16, lanes] = acc[n, pl.ds(6 * j + k, 16, stride=48), :].astype(BF)
-                out[d, 96:112, 0:512] = pairs[j].astype(BF)
-                out[d, 96:112, 512:896] = jnp.zeros((16, 384), BF)
+    y = place[0]
+    c = place[1]
+    z = place[2]
+    x = place[3]
+    features = weight.shape[0]
+    for d2, (near, far) in enumerate(((a0, b0), (a1, b1), (a2, b2), (a3, b3))):
+        rows = jnp.concatenate([near[0], far[...]], axis=0)
+        term = jnp.dot(rows[:, 0:features], weight[...], preferred_element_type=F32) * scale[...]
+        value = rows[:, features:].astype(F32)
+        for k in range(OUTL):
+            term = term + value[:, k : k + 1] * extra[k : k + 1, :]
+        for side in range(2):
+            half = c if side == 0 else 1 - c
+            for d1 in range(4):
+                along_x = lax.rem(x + 4 - jnp.where(half == 0, STEPS[d1], d2), 4)
+                along_z = lax.rem(z + 4 - jnp.where(half == 0, d2, STEPS[d1]), 4)
+                at = pl.multiple_of((along_z * 4 + along_x) * 48 + half * 24, 8)
+                row = side * 96 + d1 * 24
+                put(acc, pl.ds(at, 24), term[row : row + 24, :])
+    for out, core in ((keep, c), (send, 1 - c)):
+        for d in range(N_Y):
+            j = 2 * lax.rem(y + d, N_Y) + core
+            for k in range(6):
+                for n, lanes in lanes_of(896):
+                    out[d, 16 * k : 16 * k + 16, lanes] = acc[n, pl.ds(6 * j + k, 16, stride=48), :].astype(BF)
+            out[d, 96:112, 0:512] = pairs[j].astype(BF)
+            out[d, 96:112, 512:896] = jnp.zeros((16, 384), BF)
 
 
 def add_kernel(keep, received, o0, o1, o2, o3):
@@ -132,7 +159,6 @@
                     block[at : at + 8, :] = jnp.where(own, both, 0.0)
 
     rows = LOCAL_HEADS * 16
-    nt = (((1,), (1,)), ((), ()))
     row = lax.broadcasted_iota(jnp.int32, (rows, 128), 0)
     column = lax.broadcasted_iota(jnp.int32, (rows, 128), 1)
     token = (row // 8) % 2
@@ -143,7 +169,7 @@
         side = slice(256 * g, 256 * g + 256)
         query = block[...].astype(BF)
         grouped.append(query)
-        scores = lax.dot_general(query, fresh_key[:, side].astype(BF), nt, preferred_element_type=F32)
+        scores = lax.dot_general(query, fresh_key[:, side].astype(BF), NT, preferred_element_type=F32)
         scores = jnp.where(visible, scores, -jnp.inf)
         top = jnp.max(scores, axis=1, keepdims=True)
         prob = jnp.exp(scores - top)
@@ -162,7 +188,7 @@
             side = slice(256 * g, 256 * g + 256)
             key = keys[0, pl.ds(at, CHUNK), side]
             value = values[0, pl.ds(at, CHUNK), side]
-            scores = lax.dot_general(grouped[g], key, nt, preferred_element_type=F32)
+            scores = lax.dot_general(grouped[g], key, NT, preferred_element_type=F32)
             scores = jnp.where(active, scores, -jnp.inf)
             higher = jnp.maximum(top, jnp.max(scores, axis=1, keepdims=True))
             shrink = jnp.exp(top - higher)
@@ -214,7 +240,7 @@
         rows = slice(n * step, n * step + step)
         part = left[rows, :]
         picked = jnp.dot(part, chosen[...], preferred_element_type=F32)
-        term = jnp.dot(part * plain[...], weight[...], preferred_element_type=F32) * scale[...]
+        term = lax.dot_general(part * plain[...], weight[...], NT, preferred_element_type=F32) * scale[...]
         for k in range(OUTL):
             term = term + picked[:, k : k + 1] * extra[k : k + 1, :]
         put(acc, rows, term)
@@ -237,6 +263,19 @@
 
 def over_y(shift):
     return [(2 * y + c, 2 * ((y + shift) % N_Y) + c) for y in range(N_Y) for c in range(2)]
+
+
+def shift_plane(first, shift):
+    pairs = []
+    for z in range(4):
+        for x in range(4):
+            for j in range(2 * N_Y):
+                if (j % 2 == 0) == first:
+                    to = z * 4 + (x + shift) % 4
+                else:
+                    to = (z + shift) % 4 * 4 + x
+                pairs.append(((z * 4 + x) * 2 * N_Y + j, to * 2 * N_Y + j))
+    return pairs
 
 
 SIBLING = [(j, j ^ 1) for j in range(2 * N_Y)]
@@ -267,60 +306,60 @@
     out_columns = output_int.shape[1]
     me_x = lax.axis_index("gx")
     me_y = lax.axis_index("gy")
-    place = jnp.stack([me_y // 2, me_y % 2]).astype(jnp.int32)
-
-    gathered = lax.all_gather(activations, "gx", axis=0, tiled=True)
+    place = jnp.stack([me_y // 2, me_y % 2, me_x // 4, me_x % 4]).astype(jnp.int32)
+    smem = pl.BlockSpec(memory_space=pltpu.SMEM)
+    vmem = pl.BlockSpec(memory_space=pltpu.VMEM)
 
     widened = activations.astype(F32)
-    sums = lax.psum(
-        jnp.stack([jnp.sum(widened, axis=1), jnp.sum(widened * widened, axis=1)], axis=1), "gy"
+    sums = jnp.stack([jnp.sum(widened, axis=1), jnp.sum(widened * widened, axis=1)])
+    sums = lax.all_to_all(
+        jnp.broadcast_to(sums[None], (2 * N_Y, 2, block_rows)), "gy", split_axis=0, concat_axis=0, tiled=True
     )
     picked = jnp.arange(features, dtype=jnp.int32)[:, None] == input_outliers[None, :]
-    raw = jnp.dot(activations, picked.astype(BF), preferred_element_type=F32)
-    stats = lax.all_gather(jnp.concatenate([sums, raw], axis=1), "gx", axis=0, tiled=True)
-
-    is_outlier = jnp.any(picked, axis=1)
-    gain_regular = jnp.where(is_outlier, 0.0, norm_gain)
-    bias_regular = jnp.where(is_outlier, 0.0, norm_bias)
-    gain_out = jnp.sum(jnp.where(picked, norm_gain[:, None], 0.0), axis=0)
-    bias_out = jnp.sum(jnp.where(picked, norm_bias[:, None], 0.0), axis=0)
-
-    average = sums[:, 0:1] / D
-    inverse = lax.rsqrt(sums[:, 1:2] / D - average * average + epsilon)
-    own_regular = ((widened - average) * inverse * gain_regular + bias_regular).astype(BF)
-    own_outlier = ((raw - average) * inverse * gain_out + bias_out).astype(BF)
-    pairs = jnp.dot(own_regular, keyvalue_int, preferred_element_type=F32) * keyvalue_scale
-    pairs = pairs + jnp.dot(own_outlier.astype(F32), keyvalue_float, precision=lax.Precision.HIGHEST)
+    regular = jnp.where(jnp.any(picked, axis=1), 0.0, 1.0)[None]
+    padded = features + 64
+    own, kept, sent = pl.pallas_call(
+        normalize_kernel,
+        in_specs=[smem] + [vmem] * 6,
+        out_specs=[vmem] * 3,
+        out_shape=[
+            jax.ShapeDtypeStruct((block_rows, padded), BF),
+            jax.ShapeDtypeStruct((block_rows // 2, padded), BF),
+            jax.ShapeDtypeStruct((block_rows // 2, padded), BF),
+        ],
+        compiler_params=params(),
+        name="normalize",
+    )(
+        place, sums, activations, norm_gain[None], norm_bias[None],
+        jnp.pad(picked.astype(BF), ((0, 0), (0, 128 - OUTL))), regular,
+    )
+    plane = ("gx", "gy")
+    both = jnp.stack([kept, lax.ppermute(sent, "gy", SIBLING)])
+    both = jnp.concatenate(
+        [both] + [lax.ppermute(both, plane, shift_plane(True, d)) for d in (1, 3, 2)], axis=1
+    )
+    arrived = [both] + [lax.ppermute(both, plane, shift_plane(False, d)) for d in (1, 3, 2)]
+    others = [lax.ppermute(block[1], "gy", SIBLING) for block in arrived]
+    order = (0, 1, 3, 2)
+    arrived = [arrived[n] for n in order]
+    others = [others[n] for n in order]
+
+    pairs = jnp.dot(own[:, 0:features], keyvalue_int, preferred_element_type=F32) * keyvalue_scale
+    own_outlier = own[:, features : features + OUTL].astype(F32)
+    pairs = pairs + jnp.dot(own_outlier, keyvalue_float, precision=lax.Precision.HIGHEST)
     pairs = pairs.reshape(8, 6, 2, 512).transpose(0, 2, 1, 3).reshape(8, 12, 512)
     pairs = jnp.pad(pairs, ((0, 0), (0, 4), (0, 0)))
 
-    part_rows = tokens // 4
-    smem = pl.BlockSpec(memory_space=pltpu.SMEM)
     keep, send = pl.pallas_call(
         query_kernel,
-        grid=(4,),
-        in_specs=[
-            smem,
-            pl.BlockSpec((part_rows, features), lambda n: (n, 0)),
-            pl.BlockSpec((part_rows, 6), lambda n: (n, 0)),
-            whole((1, features)),
-            whole((1, features)),
-            whole((1, OUTL)),
-            whole((1, OUTL)),
-            whole((1, columns)),
-            whole((OUTL, columns)),
-            whole((features, columns)),
-            whole((8, 16, 512)),
-        ],
-        out_specs=[whole((N_Y, 112, columns))] * 2,
+        grid=(1,),
+        in_specs=[smem] + [whole((1, 96, padded))] * 4 + [vmem] * 8,
+        out_specs=[vmem] * 2,
         out_shape=[jax.ShapeDtypeStruct((N_Y, 112, columns), BF)] * 2,
         scratch_shapes=[pltpu.VMEM((7, tokens, 128), F32)],
         compiler_params=params(),
         name="query_projection",
-    )(
-        place, gathered, stats, gain_regular[None], bias_regular[None], gain_out[None], bias_out[None],
-        query_scale[None], query_float, query_int, pairs,
-    )
+    )(place, *arrived, *others, query_scale[None], query_float, query_int, pairs)
     received = lax.ppermute(send, "gy", SIBLING)
     piece = jax.ShapeDtypeStruct((112, columns), BF)
     mine, to1, to2, to3 = pl.pallas_call(
@@ -393,7 +432,6 @@
     chosen = jnp.arange(columns, dtype=jnp.int32)[:, None] == middle[None, :]
     plain = jnp.where(jnp.any(chosen, axis=1), 0.0, 1.0).astype(BF)[None]
     chosen = jnp.pad(chosen.astype(BF), ((0, 0), (0, 128 - OUTL)))
-    vmem = pl.BlockSpec(memory_space=pltpu.VMEM)
     partial = pl.pallas_call(
         output_kernel,
         in_specs=[smem] + [vmem] * 13,
@@ -402,7 +440,7 @@
         scratch_shapes=[pltpu.VMEM((tokens, columns), BF), pltpu.VMEM((15, tokens, 128), F32)],
         compiler_params=params(),
         name="output_projection",
-    )(place, *blocks, chosen, plain, output_scale[None], output_float, output_int)
+    )(place, *blocks, chosen, plain, output_scale[None], output_float, output_int.T)
     parts = lax.all_to_all(partial, "gx", split_axis=0, concat_axis=0, tiled=True)
     return pl.pallas_call(
         total_kernel,

time: 200 us -> 181 us (0.905)
  blocking collectives: 73.8 us -> 39.7 us
  starting transfers between devices: 29.3 us -> 50.7 us
  between operations: 13.6 us -> 0.3 us
  waiting for transfers between devices: 34.3 us -> 45.7 us
  matrix products: 4.44 us -> 1.06 us
    all_gather x1 -> x0, blocking collectives: 20.4 us -> none  [on_device(): lax.all_gather(jnp.concatenate([sums, raw], axis=1), 'gx', axis=0, tiled=...]
    ppermute x0 -> x11, starting transfers between devices: none -> 18.2 us  [the longest x4 8.32 us: on_device(): others = [lax.ppermute(block[1], 'gy', SIBLING) for block in arrived]]
    ppermute x0 -> x11, waiting for transfers between devices: none -> 17.3 us  [the longest x3 11.3 us: on_device(): lax.ppermute(both, plane, shift_plane(False, d))]
    psum x1 -> x0, blocking collectives: 13.5 us -> none  [on_device(): lax.psum(jnp.stack([jnp.sum(widened, axis=1), jnp.sum(widened * widened,...]
    all_gather x1 -> x0, waiting for transfers between devices: 9.57 us -> none  [on_device(): gathered = lax.all_gather(activations, 'gx', axis=0, tiled=True)]
    unnamed x15 -> x20, local copies, waits for them, and re-layouts: 7.66 us -> 0.96 us
    all_to_all x0 -> x1, starting transfers between devices: none -> 5.97 us  [on_device(): lax.all_to_all(jnp.broadcast_to(sums[None], (2 * N_Y, 2, block_rows)), 'g...]
    dot_general x3 -> x2, matrix products: 4.44 us -> 1.06 us  [the longest x1 0.78 us: on_device(): jnp.dot(own[:, 0:features], keyvalue_int, preferred_element_type=F32)]
  transfers between devices with their start and end apart: 14 -> 25, of which waited for: 6 -> 13; matrix products, arithmetic and copies ran while one was open for 8% -> 5% of each run, Pallas kernels for 0% -> 0%
where the time goes in v2:
time: 181 us; the launch traced here: 180 us
  starting transfers between devices  50.7 us (28%)
  waiting for transfers between devices  45.7 us (25%)
  blocking collectives  39.7 us (22%)
  Pallas kernels  31.3 us (17%)
  local copies, waits for them, and re-layouts  8.34 us (5%)
  other arithmetic  2.96 us (2%)
    all_to_all x1, blocking collectives, on_device(): lax.all_to_all(partial, 'gx', split_axis=0, concat_axis=0, tiled=True)  39.7 us
    ppermute x3, waiting for transfers between devices, on_device(): lax.ppermute(both, plane, shift_plane(False, d))  11.3 us
    pallas_call x1, Pallas kernels, on_device(): pl.pallas_call(attend_kernel, grid=(3,), in_specs=[smem, whole((16, 6, co...  10.6 us
    ppermute x4, starting transfers between devices, on_device(): blocks = blocks + [lax.ppermute(b, 'gy', SIBLING) for b in blocks]  9.74 us
    pallas_call x1, Pallas kernels, on_device(): pl.pallas_call(output_kernel, in_specs=[smem] + [vmem] * 13, out_specs=vm...  9.12 us
    ppermute x4, starting transfers between devices, on_device(): others = [lax.ppermute(block[1], 'gy', SIBLING) for block in arrived]  8.32 us
    pallas_call x1, Pallas kernels, on_device(): pl.pallas_call(query_kernel, grid=(1,), in_specs=[smem] + [whole((1, 96,...  8.16 us
    all_to_all x1, waiting for transfers between devices, on_device(): lax.all_to_all(attended, 'gx', split_axis=0, concat_axis=0, tiled=True)  7.28 us
  transfers between devices with their start and end apart: 25, of which 13 were waited for; matrix products, arithmetic and copies ran while one was open for 5% of the time, Pallas kernels for 0%

profile of v2, /device:TPU:1, one launch (start us, length us, event | category | flops | bytes accessed | tf_op | source)
XLA Modules:
  0.0 180.0 jit_solution(12375238705330951347)
XLA Ops:
  0.0 1.1 convert_reduce_fusion
  1.7 6.0 %all-to-all-start = ((f32[8,2,48]{2,1,0:T(2,128)}), f32[8,2,48]{2,1,0:T(2,128)S(1)}, u32[]{:S(2)}, u32[]{:S(2)}) async-start(f32[8,2,48]{2,1,0:T(2,128)} %broadcast_in_dim.44), calls=%async_computation | async-start | bytes 16384 | tf_op jit(solution)/shard_map/all_to_all | solution.py:315
  7.7 1.0 fusion.2
  10.4 1.9 %all-to-all-done.parts = f32[8,2,48]{2,1,0:T(2,128)S(1)} async-done(((f32[8,2,48]{2,1,0:T(2,128)}), f32[8,2,48]{2,1,0:T(2,128)S(1)}, u32[]{:S(2)}, u32[]{:S(2)}) %all-to-all-start) | async-done | bytes 3104 | tf_op jit(solution)/shard_map/all_to_all | solution.py:315
  12.3 0.9 copy-done.1
  13.2 1.2 normalize.1
  14.4 0.8 collective-permute-start
  15.2 0.9 collective-permute-done
  16.2 1.7 collective-permute-start.1
  17.9 2.2 %collective-permute-start.2 = (bf16[2,24,1920]{2,1,0:T(8,128)(2,1)S(1)}, bf16[2,24,1920]{2,1,0:T(8,128)(2,1)S(1)}, u32[]{:S(2)}, u32[]{:S(2)}) collective-permute-start(bf16[2,24,1920]{2,1,0:T(8,128)(2,1)S(1)} %pad_maximum_fusion.1), channel_id=1, source_target_pairs={{0,24},{1,97},{2,26},{3,99},{4,28},{5,101},{6,30},{7,103},{8,0},{9... | collective-permute-start | bytes 552968 | tf_op jit(solution)/shard_map/ppermute | solution.py:339
  20.1 1.2 collective-permute-start.3
  21.3 1.6 collective-permute-done.1
  22.9 3.4 %collective-permute-done.3 = bf16[2,24,1920]{2,1,0:T(8,128)(2,1)S(1)} collective-permute-done((bf16[2,24,1920]{2,1,0:T(8,128)(2,1)S(1)}, bf16[2,24,1920]{2,1,0:T(8,128)(2,1)S(1)}, u32[]{:S(2)}, u32[]{:S(2)}) %collective-permute-start.3) | collective-permute-done | bytes 184352 | tf_op jit(solution)/shard_map/ppermute | solution.py:339
  26.4 2.3 %collective-permute-start.6 = (bf16[2,96,1920]{2,1,0:T(8,128)(2,1)S(1)}, bf16[2,96,1920]{2,1,0:T(8,128)(2,1)S(1)}, u32[]{:S(2)}, u32[]{:S(2)}) collective-permute-start(bf16[2,96,1920]{2,1,0:T(8,128)(2,1)S(1)} %pad_maximum_fusion.a0), channel_id=1, source_target_pairs={{0,96},{1,25},{2,98},{3,27},{4,100},{5,29},{6,102},{7,31},{8,104},... | collective-permute-start | bytes 2211848 | tf_op jit(solution)/shard_map/ppermute | solution.py:341
  28.7 1.7 collective-permute-start.5
  30.4 0.8 slice_bitcast_fusion.3
  31.2 2.5 %collective-permute-start.7 = (bf16[96,1920]{1,0:T(8,128)(2,1)}, bf16[96,1920]{1,0:T(8,128)(2,1)S(1)}, u32[]{:S(2)}, u32[]{:S(2)}) collective-permute-start(bf16[96,1920]{1,0:T(8,128)(2,1)} %slice_bitcast_fusion.3), channel_id=1, source_target_pairs={{0,1},{1,0},{2,3},{3,2},{4,5},{5,4},{6,7},{7,6},{8,9},{9,8},{10,11... | collective-permute-start | bytes 1105928 | tf_op jit(solution)/shard_map/ppermute | solution.py:342
  33.7 11.3 %collective-permute-done.6.a3 = bf16[2,96,1920]{2,1,0:T(8,128)(2,1)S(1)} collective-permute-done((bf16[2,96,1920]{2,1,0:T(8,128)(2,1)S(1)}, bf16[2,96,1920]{2,1,0:T(8,128)(2,1)S(1)}, u32[]{:S(2)}, u32[]{:S(2)}) %collective-permute-start.6) | collective-permute-done | bytes 737312 | tf_op jit(solution)/shard_map/ppermute | solution.py:341
  45.0 0.8 slice_bitcast_fusion
  45.8 2.9 %collective-permute-start.10 = (bf16[96,1920]{1,0:T(8,128)(2,1)}, bf16[96,1920]{1,0:T(8,128)(2,1)}, u32[]{:S(2)}, u32[]{:S(2)}) collective-permute-start(bf16[96,1920]{1,0:T(8,128)(2,1)} %slice_bitcast_fusion), channel_id=1, source_target_pairs={{0,1},{1,0},{2,3},{3,2},{4,5},{5,4},{6,7},{7,6},{8,9},{9,8},{10,11... | collective-permute-start | bytes 1105928 | tf_op jit(solution)/shard_map/ppermute | solution.py:342
  49.5 2.9 %collective-permute-start.8 = (bf16[96,1920]{1,0:T(8,128)(2,1)}, bf16[96,1920]{1,0:T(8,128)(2,1)}, u32[]{:S(2)}, u32[]{:S(2)}) collective-permute-start(bf16[96,1920]{1,0:T(8,128)(2,1)} %slice_bitcast_fusion.2), channel_id=1, source_target_pairs={{0,1},{1,0},{2,3},{3,2},{4,5},{5,4},{6,7},{7,6},{8,9},{9,8},{10,11... | collective-permute-start | bytes 1105928 | tf_op jit(solution)/shard_map/ppermute | solution.py:342
  52.4 0.8 slice_bitcast_fusion.1
  53.2 0.8 convolution_multiply_fusion
  54.3 0.8 reshape.87
  55.1 1.0 copy.19
  56.3 8.2 %query_projection.1 = (bf16[4,112,896]{2,1,0:T(8,128)(2,1)S(1)}, bf16[4,112,896]{2,1,0:T(8,128)(2,1)}) custom-call(s32[4]{0:T(128)S(1)} %pad_add_fusion.place, bf16[2,96,1920]{2,1,0:T(8,128)(2,1)S(1)} %pad_maximum_fusion.a0, bf16[2,96,1920]{2,1,0:T(8,128)(2,1)S(1)} %collective-permute-done.4.a1, bf16[2,96,1920]{2,1,0:T(8,128)(2,1)S(1)} %collective-permute-done.5.a2, ...), custom_call_target="tpu_custom_call" | custom-call | tf_op jit(solution)/shard_map/query_projection/pallas_call | solution.py:353
  65.0 2.1 %collective-permute-done.11.received = bf16[4,112,896]{2,1,0:T(8,128)(2,1)S(1)} collective-permute-done((bf16[4,112,896]{2,1,0:T(8,128)(2,1)}, bf16[4,112,896]{2,1,0:T(8,128)(2,1)S(1)}, u32[]{:S(2)}, u32[]{:S(2)}) %collective-permute-start.11) | collective-permute-done | bytes 802848 | tf_op jit(solution)/shard_map/ppermute | solution.py:363
  67.7 1.8 collective-permute-start.13
  69.4 0.9 collective-permute-start.14
  70.5 4.9 %collective-permute-done.12.b = bf16[112,896]{1,0:T(8,128)(2,1)S(1)} collective-permute-done((bf16[112,896]{1,0:T(8,128)(2,1)S(1)}, bf16[112,896]{1,0:T(8,128)(2,1)S(1)}, u32[]{:S(2)}, u32[]{:S(2)}) %collective-permute-start.12) | collective-permute-done | bytes 200736 | tf_op jit(solution)/shard_map/ppermute | solution.py:368
  75.4 3.1 %collective-permute-done.13.c = bf16[112,896]{1,0:T(8,128)(2,1)S(1)} collective-permute-done((bf16[112,896]{1,0:T(8,128)(2,1)S(1)}, bf16[112,896]{1,0:T(8,128)(2,1)S(1)}, u32[]{:S(2)}, u32[]{:S(2)}) %collective-permute-start.13) | collective-permute-done | bytes 200736 | tf_op jit(solution)/shard_map/ppermute | solution.py:370
  78.5 0.9 collective-permute-done.14.d
  79.4 0.9 collect.1
  80.4 3.7 %all-to-all-start.1 = ((bf16[16,6,896]{2,1,0:T(8,128)(2,1)}), bf16[16,6,896]{2,1,0:T(8,128)(2,1)S(1)}, u32[]{:S(2)}, u32[]{:S(2)}) async-start(bf16[16,6,896]{2,1,0:T(8,128)(2,1)} %get-tuple-element.25), calls=%async_computation.1 | async-start | bytes 458752 | tf_op jit(solution)/shard_map/all_to_all | solution.py:381
  84.4 7.1 %all-to-all-done.1.queries = bf16[16,6,896]{2,1,0:T(8,128)(2,1)S(1)} async-done(((bf16[16,6,896]{2,1,0:T(8,128)(2,1)}), bf16[16,6,896]{2,1,0:T(8,128)(2,1)S(1)}, u32[]{:S(2)}, u32[]{:S(2)}) %all-to-all-start.1) | async-done | bytes 172064 | tf_op jit(solution)/shard_map/all_to_all | solution.py:381
  91.5 10.6 %attention.1 = bf16[16,6,896]{2,1,0:T(8,128)(2,1)} custom-call(s32[3]{0:T(128)S(1)} %copy-done.4, bf16[16,6,896]{2,1,0:T(8,128)(2,1)S(1)} %all-to-all-done.1.queries, f32[16,512]{1,0:T(8,128)S(1)} %get-tuple-element.26.pairs, f32[8,128]{1,0:T(8,128)S(1)} %pad.26.cosine, f32[8,128]{1,0:T(8,128)S(1)} %select_maximum_fusion.sine, bf16[3,2048,512]{2,1,0:T(8,128)(2,1)} %keys.1, ...), custom_call_target="tpu_custom_call" | custom-call | tf_op jit(solution)/shard_map/attention/pallas_call | solution.py:393
  102.1 4.5 %all-to-all-start.2 = ((bf16[16,6,896]{2,1,0:T(8,128)(2,1)}), bf16[16,6,896]{2,1,0:T(8,128)(2,1)S(1)}, u32[]{:S(2)}, u32[]{:S(2)}) async-start(bf16[16,6,896]{2,1,0:T(8,128)(2,1)} %attention.1), calls=%async_computation.2 | async-start | bytes 458752 | tf_op jit(solution)/shard_map/all_to_all | solution.py:420
  106.7 7.3 %all-to-all-done.2.block = bf16[16,6,896]{2,1,0:T(8,128)(2,1)S(1)} async-done(((bf16[16,6,896]{2,1,0:T(8,128)(2,1)}), bf16[16,6,896]{2,1,0:T(8,128)(2,1)S(1)}, u32[]{:S(2)}, u32[]{:S(2)}) %all-to-all-start.2) | async-done | bytes 172064 | tf_op jit(solution)/shard_map/all_to_all | solution.py:420
  114.1 1.8 %collective-permute-start.15 = (bf16[96,896]{1,0:T(8,128)(2,1)S(1)}, bf16[96,896]{1,0:T(8,128)(2,1)S(1)}, u32[]{:S(2)}, u32[]{:S(2)}) collective-permute-start(bf16[96,896]{1,0:T(8,128)(2,1)S(1)} %repack.1.b0), channel_id=1, source_target_pairs={{0,2},{1,3},{2,4},{3,5},{4,6},{5,7},{6,0},{7,1},{8,10},{9,11},{10,... | collective-permute-start | bytes 516104 | tf_op jit(solution)/shard_map/ppermute | solution.py:428
  115.9 3.2 %collective-permute-start.16 = (bf16[96,896]{1,0:T(8,128)(2,1)S(1)}, bf16[96,896]{1,0:T(8,128)(2,1)S(1)}, u32[]{:S(2)}, u32[]{:S(2)}) collective-permute-start(bf16[96,896]{1,0:T(8,128)(2,1)S(1)} %repack.1.b0), channel_id=1, source_target_pairs={{0,4},{1,5},{2,6},{3,7},{4,0},{5,1},{6,2},{7,3},{8,12},{9,13},{10,... | collective-permute-start | bytes 516104 | tf_op jit(solution)/shard_map/ppermute | solution.py:428
  119.3 4.0 %collective-permute-start.18 = (bf16[96,896]{1,0:T(8,128)(2,1)S(1)}, bf16[96,896]{1,0:T(8,128)(2,1)S(1)}, u32[]{:S(2)}, u32[]{:S(2)}) collective-permute-start(bf16[96,896]{1,0:T(8,128)(2,1)S(1)} %repack.1.b0), channel_id=1, source_target_pairs={{0,1},{1,0},{2,3},{3,2},{4,5},{5,4},{6,7},{7,6},{8,9},{9,8},{10,11... | collective-permute-start | bytes 516104 | tf_op jit(solution)/shard_map/ppermute | solution.py:429
  123.3 3.0 %collective-permute-start.19 = (bf16[96,896]{1,0:T(8,128)(2,1)S(1)}, bf16[96,896]{1,0:T(8,128)(2,1)S(1)}, u32[]{:S(2)}, u32[]{:S(2)}) collective-permute-start(bf16[96,896]{1,0:T(8,128)(2,1)S(1)} %collective-permute-done.15.b1), channel_id=1, source_target_pairs={{0,1},{1,0},{2,3},{3,2},{4,5},{5,4},{6,7},{7,6},{8,9},{9,8},{10,11... | collective-permute-start | bytes 516104 | tf_op jit(solution)/shard_map/ppermute | solution.py:429
  126.4 1.9 %collective-permute-start.20 = (bf16[96,896]{1,0:T(8,128)(2,1)S(1)}, bf16[96,896]{1,0:T(8,128)(2,1)S(1)}, u32[]{:S(2)}, u32[]{:S(2)}) collective-permute-start(bf16[96,896]{1,0:T(8,128)(2,1)S(1)} %collective-permute-done.16.b2), channel_id=1, source_target_pairs={{0,1},{1,0},{2,3},{3,2},{4,5},{5,4},{6,7},{7,6},{8,9},{9,8},{10,11... | collective-permute-start | bytes 516104 | tf_op jit(solution)/shard_map/ppermute | solution.py:429
  128.3 0.8 collective-permute-start.21
  129.3 0.8 collective-permute-done.21.s3
  130.1 9.1 %output_projection.1 = bf16[16,48,1856]{2,1,0:T(8,128)(2,1)S(1)} custom-call(s32[4]{0:T(128)S(1)} %pad_add_fusion.place, bf16[96,896]{1,0:T(8,128)(2,1)S(1)} %repack.1.b0, bf16[96,896]{1,0:T(8,128)(2,1)S(1)} %collective-permute-done.15.b1, bf16[96,896]{1,0:T(8,128)(2,1)S(1)} %collective-permute-done.16.b2, bf16[96,896]{1,0:T(8,128)(2,1)S(1)} %collective-permute-done.17.b3, ...), custom_call_target="tpu_custom_call" | custom-call | tf_op jit(solution)/shard_map/output_projection/pallas_call | solution.py:435
  139.3 39.7 %all_to_all.20.parts = bf16[16,48,1856]{2,1,0:T(8,128)(2,1)S(1)} all-to-all(bf16[16,48,1856]{2,1,0:T(8,128)(2,1)S(1)} %output_projection.1), channel_id=1, replica_groups=mesh['gx'=16,'gy'=8] {'gx'}, dimensions={0} | all-to-all | bytes 5701632 | tf_op jit(solution)/shard_map/all_to_all | solution.py:444
  178.9 1.1 total.1
  (68 shorter events, 5.6 us)
Async XLA Ops:
  0.0 54.0 %copy-start = (f32[4,1024]{1,0:T(4,128)S(1)}, f32[4,1024]{1,0:T(4,128)}, u32[]{:S(2)}) copy-start(f32[4,1024]{1,0:T(4,128)} %param.26) | copy-start | bytes 49156
  0.0 28.7 %copy-start.7 = (f32[896]{0:T(1024)S(1)}, f32[896]{0:T(1024)}, u32[]{:S(2)}) copy-start(f32[896]{0:T(1024)} %param.22) | copy-start | bytes 10756
  1.7 10.6 %all-to-all-start = ((f32[8,2,48]{2,1,0:T(2,128)}), f32[8,2,48]{2,1,0:T(2,128)S(1)}, u32[]{:S(2)}, u32[]{:S(2)}) async-start(f32[8,2,48]{2,1,0:T(2,128)} %broadcast_in_dim.44), calls=%async_computation | async-start | bytes 16384 | tf_op jit(solution)/shard_map/all_to_all | solution.py:315
  8.8 44.3 %copy-start.8 = (f32[1024]{0:T(1024)S(1)}, f32[1024]{0:T(1024)}, u32[]{:S(2)}) copy-start(f32[1024]{0:T(1024)} %param.24) | copy-start | bytes 12292
  12.3 0.9 copy-start.1
  13.2 39.9 %copy-start.5 = (bf16[1856,1024]{1,0:T(8,128)(2,1)S(1)}, bf16[1856,1024]{1,0:T(8,128)(2,1)}, u32[]{:S(2)}) copy-start(bf16[1856,1024]{1,0:T(8,128)(2,1)} %param.23) | copy-start | bytes 11403268
  14.4 1.7 collective-permute-start
  16.2 6.8 %collective-permute-start.1 = (bf16[2,24,1920]{2,1,0:T(8,128)(2,1)S(1)}, bf16[2,24,1920]{2,1,0:T(8,128)(2,1)S(1)}, u32[]{:S(2)}, u32[]{:S(2)}) collective-permute-start(bf16[2,24,1920]{2,1,0:T(8,128)(2,1)S(1)} %pad_maximum_fusion.1), channel_id=1, source_target_pairs={{0,8},{1,33},{2,10},{3,35},{4,12},{5,37},{6,14},{7,39},{8,16},{9,4... | collective-permute-start | bytes 552968 | tf_op jit(solution)/shard_map/ppermute | solution.py:339
  17.9 5.1 %collective-permute-start.2 = (bf16[2,24,1920]{2,1,0:T(8,128)(2,1)S(1)}, bf16[2,24,1920]{2,1,0:T(8,128)(2,1)S(1)}, u32[]{:S(2)}, u32[]{:S(2)}) collective-permute-start(bf16[2,24,1920]{2,1,0:T(8,128)(2,1)S(1)} %pad_maximum_fusion.1), channel_id=1, source_target_pairs={{0,24},{1,97},{2,26},{3,99},{4,28},{5,101},{6,30},{7,103},{8,0},{9... | collective-permute-start | bytes 552968 | tf_op jit(solution)/shard_map/ppermute | solution.py:339
  20.1 6.3 %collective-permute-start.3 = (bf16[2,24,1920]{2,1,0:T(8,128)(2,1)S(1)}, bf16[2,24,1920]{2,1,0:T(8,128)(2,1)S(1)}, u32[]{:S(2)}, u32[]{:S(2)}) collective-permute-start(bf16[2,24,1920]{2,1,0:T(8,128)(2,1)S(1)} %pad_maximum_fusion.1), channel_id=1, source_target_pairs={{0,16},{1,65},{2,18},{3,67},{4,20},{5,69},{6,22},{7,71},{8,24},{9,... | collective-permute-start | bytes 552968 | tf_op jit(solution)/shard_map/ppermute | solution.py:339
  26.4 18.6 %collective-permute-start.6 = (bf16[2,96,1920]{2,1,0:T(8,128)(2,1)S(1)}, bf16[2,96,1920]{2,1,0:T(8,128)(2,1)S(1)}, u32[]{:S(2)}, u32[]{:S(2)}) collective-permute-start(bf16[2,96,1920]{2,1,0:T(8,128)(2,1)S(1)} %pad_maximum_fusion.a0), channel_id=1, source_target_pairs={{0,96},{1,25},{2,98},{3,27},{4,100},{5,29},{6,102},{7,31},{8,104},... | collective-permute-start | bytes 2211848 | tf_op jit(solution)/shard_map/ppermute | solution.py:341
  28.7 20.0 %collective-permute-start.4 = (bf16[2,96,1920]{2,1,0:T(8,128)(2,1)S(1)}, bf16[2,96,1920]{2,1,0:T(8,128)(2,1)S(1)}, u32[]{:S(2)}, u32[]{:S(2)}) collective-permute-start(bf16[2,96,1920]{2,1,0:T(8,128)(2,1)S(1)} %pad_maximum_fusion.a0), channel_id=1, source_target_pairs={{0,32},{1,9},{2,34},{3,11},{4,36},{5,13},{6,38},{7,15},{8,40},{9,1... | collective-permute-start | bytes 2211848 | tf_op jit(solution)/shard_map/ppermute | solution.py:341
  28.7 23.7 %collective-permute-start.5 = (bf16[2,96,1920]{2,1,0:T(8,128)(2,1)S(1)}, bf16[2,96,1920]{2,1,0:T(8,128)(2,1)S(1)}, u32[]{:S(2)}, u32[]{:S(2)}) collective-permute-start(bf16[2,96,1920]{2,1,0:T(8,128)(2,1)S(1)} %pad_maximum_fusion.a0), channel_id=1, source_target_pairs={{0,64},{1,17},{2,66},{3,19},{4,68},{5,21},{6,70},{7,23},{8,72},{9,... | collective-permute-start | bytes 2211848 | tf_op jit(solution)/shard_map/ppermute | solution.py:341
  31.2 25.1 %collective-permute-start.7 = (bf16[96,1920]{1,0:T(8,128)(2,1)}, bf16[96,1920]{1,0:T(8,128)(2,1)S(1)}, u32[]{:S(2)}, u32[]{:S(2)}) collective-permute-start(bf16[96,1920]{1,0:T(8,128)(2,1)} %slice_bitcast_fusion.3), channel_id=1, source_target_pairs={{0,1},{1,0},{2,3},{3,2},{4,5},{5,4},{6,7},{7,6},{8,9},{9,8},{10,11... | collective-permute-start | bytes 1105928 | tf_op jit(solution)/shard_map/ppermute | solution.py:342
  45.8 10.5 %collective-permute-start.10 = (bf16[96,1920]{1,0:T(8,128)(2,1)}, bf16[96,1920]{1,0:T(8,128)(2,1)}, u32[]{:S(2)}, u32[]{:S(2)}) collective-permute-start(bf16[96,1920]{1,0:T(8,128)(2,1)} %slice_bitcast_fusion), channel_id=1, source_target_pairs={{0,1},{1,0},{2,3},{3,2},{4,5},{5,4},{6,7},{7,6},{8,9},{9,8},{10,11... | collective-permute-start | bytes 1105928 | tf_op jit(solution)/shard_map/ppermute | solution.py:342
  49.5 6.8 %collective-permute-start.8 = (bf16[96,1920]{1,0:T(8,128)(2,1)}, bf16[96,1920]{1,0:T(8,128)(2,1)}, u32[]{:S(2)}, u32[]{:S(2)}) collective-permute-start(bf16[96,1920]{1,0:T(8,128)(2,1)} %slice_bitcast_fusion.2), channel_id=1, source_target_pairs={{0,1},{1,0},{2,3},{3,2},{4,5},{5,4},{6,7},{7,6},{8,9},{9,8},{10,11... | collective-permute-start | bytes 1105928 | tf_op jit(solution)/shard_map/ppermute | solution.py:342
  53.1 3.1 %collective-permute-start.9 = (bf16[96,1920]{1,0:T(8,128)(2,1)}, bf16[96,1920]{1,0:T(8,128)(2,1)}, u32[]{:S(2)}, u32[]{:S(2)}) collective-permute-start(bf16[96,1920]{1,0:T(8,128)(2,1)} %slice_bitcast_fusion.1), channel_id=1, source_target_pairs={{0,1},{1,0},{2,3},{3,2},{4,5},{5,4},{6,7},{7,6},{8,9},{9,8},{10,11... | collective-permute-start | bytes 1105928 | tf_op jit(solution)/shard_map/ppermute | solution.py:342
  53.2 3.1 %copy-start.3 = (f32[4,896]{1,0:T(4,128)S(1)}, f32[4,896]{1,0:T(4,128)}, u32[]{:S(2)}) copy-start(f32[4,896]{1,0:T(4,128)} %extra.2) | copy-start | bytes 43012
  56.2 14.1 %copy-start.4 = (s32[3]{0:T(128)S(1)}, s32[3]{0:T(128)}, u32[]{:S(2)}) copy-start(s32[3]{0:T(128)} %lengths.1) | copy-start | bytes 40
  64.5 2.6 %collective-permute-start.11 = (bf16[4,112,896]{2,1,0:T(8,128)(2,1)}, bf16[4,112,896]{2,1,0:T(8,128)(2,1)S(1)}, u32[]{:S(2)}, u32[]{:S(2)}) collective-permute-start(bf16[4,112,896]{2,1,0:T(8,128)(2,1)} %get-tuple-element.20), channel_id=1, source_target_pairs={{0,1},{1,0},{2,3},{3,2},{4,5},{5,4},{6,7},{7,6},{8,9},{9,8},{10,11... | collective-permute-start | bytes 2408456 | tf_op jit(solution)/shard_map/ppermute | solution.py:363
  67.3 8.1 %collective-permute-start.12 = (bf16[112,896]{1,0:T(8,128)(2,1)S(1)}, bf16[112,896]{1,0:T(8,128)(2,1)S(1)}, u32[]{:S(2)}, u32[]{:S(2)}) collective-permute-start(bf16[112,896]{1,0:T(8,128)(2,1)S(1)} %get-tuple-element.22), channel_id=1, source_target_pairs={{0,2},{1,3},{2,4},{3,5},{4,6},{5,7},{6,0},{7,1},{8,10},{9,11},{10,... | collective-permute-start | bytes 602120 | tf_op jit(solution)/shard_map/ppermute | solution.py:368
  67.7 10.9 %collective-permute-start.13 = (bf16[112,896]{1,0:T(8,128)(2,1)S(1)}, bf16[112,896]{1,0:T(8,128)(2,1)S(1)}, u32[]{:S(2)}, u32[]{:S(2)}) collective-permute-start(bf16[112,896]{1,0:T(8,128)(2,1)S(1)} %get-tuple-element.23), channel_id=1, source_target_pairs={{0,4},{1,5},{2,6},{3,7},{4,0},{5,1},{6,2},{7,3},{8,12},{9,13},{10,... | collective-permute-start | bytes 602120 | tf_op jit(solution)/shard_map/ppermute | solution.py:370
  69.4 10.0 %collective-permute-start.14 = (bf16[112,896]{1,0:T(8,128)(2,1)S(1)}, bf16[112,896]{1,0:T(8,128)(2,1)S(1)}, u32[]{:S(2)}, u32[]{:S(2)}) collective-permute-start(bf16[112,896]{1,0:T(8,128)(2,1)S(1)} %get-tuple-element.24), channel_id=1, source_target_pairs={{0,6},{1,7},{2,0},{3,1},{4,2},{5,3},{6,4},{7,5},{8,14},{9,15},{10,... | collective-permute-start | bytes 602120 | tf_op jit(solution)/shard_map/ppermute | solution.py:369
  80.4 11.2 %all-to-all-start.1 = ((bf16[16,6,896]{2,1,0:T(8,128)(2,1)}), bf16[16,6,896]{2,1,0:T(8,128)(2,1)S(1)}, u32[]{:S(2)}, u32[]{:S(2)}) async-start(bf16[16,6,896]{2,1,0:T(8,128)(2,1)} %get-tuple-element.25), calls=%async_computation.1 | async-start | bytes 458752 | tf_op jit(solution)/shard_map/all_to_all | solution.py:381
  91.5 15.1 %copy-start.9 = (s32[64]{0:T(128)S(1)}, s32[64]{0:T(128)}, u32[]{:S(2)}) copy-start(s32[64]{0:T(128)} %param.30) | copy-start | bytes 772
  91.5 37.6 %copy-start.6 = (f32[1856]{0:T(1024)S(1)}, f32[1856]{0:T(1024)}, u32[]{:S(2)}) copy-start(f32[1856]{0:T(1024)} %param.32) | copy-start | bytes 22276
  91.5 38.6 %copy-start.2 = (f32[4,1856]{1,0:T(4,128)S(1)}, f32[4,1856]{1,0:T(4,128)}, u32[]{:S(2)}) copy-start(f32[4,1856]{1,0:T(4,128)} %extra.3) | copy-start | bytes 89092
  102.1 11.8 %all-to-all-start.2 = ((bf16[16,6,896]{2,1,0:T(8,128)(2,1)}), bf16[16,6,896]{2,1,0:T(8,128)(2,1)S(1)}, u32[]{:S(2)}, u32[]{:S(2)}) async-start(bf16[16,6,896]{2,1,0:T(8,128)(2,1)} %attention.1), calls=%async_computation.2 | async-start | bytes 458752 | tf_op jit(solution)/shard_map/all_to_all | solution.py:420
  114.1 9.3 %collective-permute-start.15 = (bf16[96,896]{1,0:T(8,128)(2,1)S(1)}, bf16[96,896]{1,0:T(8,128)(2,1)S(1)}, u32[]{:S(2)}, u32[]{:S(2)}) collective-permute-start(bf16[96,896]{1,0:T(8,128)(2,1)S(1)} %repack.1.b0), channel_id=1, source_target_pairs={{0,2},{1,3},{2,4},{3,5},{4,6},{5,7},{6,0},{7,1},{8,10},{9,11},{10,... | collective-permute-start | bytes 516104 | tf_op jit(solution)/shard_map/ppermute | solution.py:428
  115.9 10.5 %collective-permute-start.16 = (bf16[96,896]{1,0:T(8,128)(2,1)S(1)}, bf16[96,896]{1,0:T(8,128)(2,1)S(1)}, u32[]{:S(2)}, u32[]{:S(2)}) collective-permute-start(bf16[96,896]{1,0:T(8,128)(2,1)S(1)} %repack.1.b0), channel_id=1, source_target_pairs={{0,4},{1,5},{2,6},{3,7},{4,0},{5,1},{6,2},{7,3},{8,12},{9,13},{10,... | collective-permute-start | bytes 516104 | tf_op jit(solution)/shard_map/ppermute | solution.py:428
  119.1 9.1 %collective-permute-start.17 = (bf16[96,896]{1,0:T(8,128)(2,1)S(1)}, bf16[96,896]{1,0:T(8,128)(2,1)S(1)}, u32[]{:S(2)}, u32[]{:S(2)}) collective-permute-start(bf16[96,896]{1,0:T(8,128)(2,1)S(1)} %repack.1.b0), channel_id=1, source_target_pairs={{0,6},{1,7},{2,0},{3,1},{4,2},{5,3},{6,4},{7,5},{8,14},{9,15},{10,... | collective-permute-start | bytes 516104 | tf_op jit(solution)/shard_map/ppermute | solution.py:428
  119.3 9.9 %collective-permute-start.18 = (bf16[96,896]{1,0:T(8,128)(2,1)S(1)}, bf16[96,896]{1,0:T(8,128)(2,1)S(1)}, u32[]{:S(2)}, u32[]{:S(2)}) collective-permute-start(bf16[96,896]{1,0:T(8,128)(2,1)S(1)} %repack.1.b0), channel_id=1, source_target_pairs={{0,1},{1,0},{2,3},{3,2},{4,5},{5,4},{6,7},{7,6},{8,9},{9,8},{10,11... | collective-permute-start | bytes 516104 | tf_op jit(solution)/shard_map/ppermute | solution.py:429
  123.3 5.9 %collective-permute-start.19 = (bf16[96,896]{1,0:T(8,128)(2,1)S(1)}, bf16[96,896]{1,0:T(8,128)(2,1)S(1)}, u32[]{:S(2)}, u32[]{:S(2)}) collective-permute-start(bf16[96,896]{1,0:T(8,128)(2,1)S(1)} %collective-permute-done.15.b1), channel_id=1, source_target_pairs={{0,1},{1,0},{2,3},{3,2},{4,5},{5,4},{6,7},{7,6},{8,9},{9,8},{10,11... | collective-permute-start | bytes 516104 | tf_op jit(solution)/shard_map/ppermute | solution.py:429
  126.4 2.9 %collective-permute-start.20 = (bf16[96,896]{1,0:T(8,128)(2,1)S(1)}, bf16[96,896]{1,0:T(8,128)(2,1)S(1)}, u32[]{:S(2)}, u32[]{:S(2)}) collective-permute-start(bf16[96,896]{1,0:T(8,128)(2,1)S(1)} %collective-permute-done.16.b2), channel_id=1, source_target_pairs={{0,1},{1,0},{2,3},{3,2},{4,5},{5,4},{6,7},{7,6},{8,9},{9,8},{10,11... | collective-permute-start | bytes 516104 | tf_op jit(solution)/shard_map/ppermute | solution.py:429
  128.3 1.9 %collective-permute-start.21 = (bf16[96,896]{1,0:T(8,128)(2,1)S(1)}, bf16[96,896]{1,0:T(8,128)(2,1)S(1)}, u32[]{:S(2)}, u32[]{:S(2)}) collective-permute-start(bf16[96,896]{1,0:T(8,128)(2,1)S(1)} %collective-permute-done.17.b3), channel_id=1, source_target_pairs={{0,1},{1,0},{2,3},{3,2},{4,5},{5,4},{6,7},{7,6},{8,9},{9,8},{10,11... | collective-permute-start | bytes 516104 | tf_op jit(solution)/shard_map/ppermute | solution.py:429

commit v3 on v2

--- a/solution.py
+++ b/solution.py
@@ -61,6 +61,19 @@
     for out, flag in ((keep, first), (send, jnp.logical_not(first))):
         out[:, 0:features] = jnp.where(flag, regular[0:half], regular[half:]).astype(BF)
         out[:, features:] = jnp.where(flag, outlier[0:half, 0:64], outlier[half:, 0:64]).astype(BF)
+
+
+def pair_kernel(own, scale, extra, weight, out):
+    features = weight.shape[0]
+    term = jnp.dot(own[:, 0:features], weight[...], preferred_element_type=F32) * scale[...]
+    value = own[:, features:].astype(F32)
+    for k in range(OUTL):
+        term = term + value[:, k : k + 1] * extra[k : k + 1, :]
+    for j in range(2 * N_Y):
+        rows = slice(6 * j, 6 * j + 6)
+        out[j, 0:6, :] = term[rows, 0:512]
+        out[j, 6:12, :] = term[rows, 512:1024]
+        out[j, 12:16, :] = jnp.zeros((4, 512), F32)
 
 
 def query_kernel(
@@ -327,7 +340,7 @@
             jax.ShapeDtypeStruct((block_rows // 2, padded), BF),
             jax.ShapeDtypeStruct((block_rows // 2, padded), BF),
         ],
-        compiler_params=params(),
+        compiler_params=params(8),
         name="normalize",
     )(
         place, sums, activations, norm_gain[None], norm_bias[None],
@@ -338,17 +351,18 @@
     both = jnp.concatenate(
         [both] + [lax.ppermute(both, plane, shift_plane(True, d)) for d in (1, 3, 2)], axis=1
     )
+    pairs = pl.pallas_call(
+        pair_kernel,
+        out_shape=jax.ShapeDtypeStruct((2 * N_Y, 16, 512), F32),
+        compiler_params=params(16),
+        name="pair_projection",
+    )(own, keyvalue_scale[None], keyvalue_float, keyvalue_int)
+    both, pairs = lax.optimization_barrier((both, pairs))
     arrived = [both] + [lax.ppermute(both, plane, shift_plane(False, d)) for d in (1, 3, 2)]
     others = [lax.ppermute(block[1], "gy", SIBLING) for block in arrived]
     order = (0, 1, 3, 2)
     arrived = [arrived[n] for n in order]
     others = [others[n] for n in order]
-
-    pairs = jnp.dot(own[:, 0:features], keyvalue_int, preferred_element_type=F32) * keyvalue_scale
-    own_outlier = own[:, features : features + OUTL].astype(F32)
-    pairs = pairs + jnp.dot(own_outlier, keyvalue_float, precision=lax.Precision.HIGHEST)
-    pairs = pairs.reshape(8, 6, 2, 512).transpose(0, 2, 1, 3).reshape(8, 12, 512)
-    pairs = jnp.pad(pairs, ((0, 0), (0, 4), (0, 0)))
 
     keep, send = pl.pallas_call(
         query_kernel,
@@ -357,13 +371,13 @@
         out_specs=[vmem] * 2,
         out_shape=[jax.ShapeDtypeStruct((N_Y, 112, columns), BF)] * 2,
         scratch_shapes=[pltpu.VMEM((7, tokens, 128), F32)],
-        compiler_params=params(),
+        compiler_params=params(24),
         name="query_projection",
     )(place, *arrived, *others, query_scale[None], query_float, query_int, pairs)
     received = lax.ppermute(send, "gy", SIBLING)
     piece = jax.ShapeDtypeStruct((112, columns), BF)
     mine, to1, to2, to3 = pl.pallas_call(
-        add_kernel, out_shape=[piece] * 4, compiler_params=params(), name="add_cores"
+        add_kernel, out_shape=[piece] * 4, compiler_params=params(8), name="add_cores"
     )(keep, received)
     from1 = lax.ppermute(to1, "gy", over_y(1))
     from3 = lax.ppermute(to3, "gy", over_y(3))
@@ -375,7 +389,7 @@
             jax.ShapeDtypeStruct((16, 512), F32),
         ],
         scratch_shapes=[pltpu.VMEM((7, 112, 128), F32)],
-        compiler_params=params(),
+        compiler_params=params(8),
         name="collect",
     )(mine, from1, from2, from3)
     queries = lax.all_to_all(summed, "gx", split_axis=0, concat_axis=0, tiled=True)
@@ -413,7 +427,7 @@
             pltpu.VMEM((224, 256), F32),
             pltpu.VMEM((7, 96, 128), F32),
         ],
-        compiler_params=params(),
+        compiler_params=params(24),
         name="attention",
     )(lengths, queries, pair_sums, cosine, sine, key_cache, value_cache)
 
@@ -422,7 +436,7 @@
         repack_kernel,
         out_shape=jax.ShapeDtypeStruct((96, columns), BF),
         scratch_shapes=[pltpu.VMEM((7, 128, 128), F32)],
-        compiler_params=params(),
+        compiler_params=params(8),
         name="repack",
     )(back)
     blocks = [mine] + [lax.ppermute(mine, "gy", over_y(d)) for d in (1, 2, 3)]
@@ -438,14 +452,14 @@
         out_specs=vmem,
         out_shape=jax.ShapeDtypeStruct((16, block_rows, out_columns), BF),
         scratch_shapes=[pltpu.VMEM((tokens, columns), BF), pltpu.VMEM((15, tokens, 128), F32)],
-        compiler_params=params(),
+        compiler_params=params(28),
         name="output_projection",
     )(place, *blocks, chosen, plain, output_scale[None], output_float, output_int.T)
     parts = lax.all_to_all(partial, "gx", split_axis=0, concat_axis=0, tiled=True)
     return pl.pallas_call(
         total_kernel,
         out_shape=jax.ShapeDtypeStruct((block_rows, out_columns), BF),
-        compiler_params=params(),
+        compiler_params=params(16),
         name="total",
     )(parts)
 

time: 181 us -> 182 us (level)
  local copies, waits for them, and re-layouts: 8.34 us -> 18.8 us
  Pallas kernels: 31.3 us -> 23.7 us
  waiting for transfers between devices: 45.7 us -> 42.5 us
    unnamed x20 -> x40, local copies, waits for them, and re-layouts: 0.96 us -> 14 us
    pallas_call x1, Pallas kernels: 10.6 us -> 6.19 us  [on_device(): pl.pallas_call(attend_kernel, grid=(3,), in_specs=[smem, whole((16, 6, co...]
    squeeze x4, local copies, waits for them, and re-layouts: 3.11 us -> 0.11 us  [on_device(): others = [lax.ppermute(block[1], 'gy', SIBLING) for block in arrived]]
    ppermute x3, waiting for transfers between devices: 5.07 us -> 2.15 us  [on_device(): lax.ppermute(both, plane, shift_plane(True, d))]
    pallas_call x1, Pallas kernels: 8.16 us -> 5.48 us  [on_device(): pl.pallas_call(query_kernel, grid=(1,), in_specs=[smem] + [whole((1, 96,...]
    reshape x3 -> x0, local copies, waits for them, and re-layouts: 1.95 us -> none  [on_device(): pairs.reshape(8, 6, 2, 512).transpose(0, 2, 1, 3).reshape(8, 12, 512)]
  transfers between devices with their start and end apart: 25 -> 25, of which waited for: 13 -> 15; matrix products, arithmetic and copies ran while one was open for 5% -> 4% of each run, Pallas kernels for 0% -> 0%
where the time goes in v3:
time: 182 us; the launch traced here: 181 us
  starting transfers between devices  51.5 us (28%)
  waiting for transfers between devices  42.5 us (23%)
  blocking collectives  40 us (22%)
  Pallas kernels  23.7 us (13%)
  local copies, waits for them, and re-layouts  18.8 us (10%)
  other arithmetic  4.21 us (2%)
    all_to_all x1, blocking collectives, on_device(): lax.all_to_all(partial, 'gx', split_axis=0, concat_axis=0, tiled=True)  40 us
    unnamed x40, local copies, waits for them, and re-layouts  14 us
    ppermute x3, waiting for transfers between devices, on_device(): lax.ppermute(both, plane, shift_plane(False, d))  12.3 us
    ppermute x4, starting transfers between devices, on_device(): others = [lax.ppermute(block[1], 'gy', SIBLING) for block in arrived]  8.98 us
    ppermute x4, starting transfers between devices, on_device(): blocks = blocks + [lax.ppermute(b, 'gy', SIBLING) for b in blocks]  8.13 us
    pallas_call x1, Pallas kernels, on_device(): pl.pallas_call(output_kernel, in_specs=[smem] + [vmem] * 13, out_specs=vm...  7.82 us
    pallas_call x1, Pallas kernels, on_device(): pl.pallas_call(attend_kernel, grid=(3,), in_specs=[smem, whole((16, 6, co...  6.19 us
    all_to_all x1, waiting for transfers between devices, on_device(): lax.all_to_all(attended, 'gx', split_axis=0, concat_axis=0, tiled=True)  6.12 us
  transfers between devices with their start and end apart: 25, of which 15 were waited for; matrix products, arithmetic and copies ran while one was open for 4% of the time, Pallas kernels for 0%

profile of v3, /device:TPU:1, one launch (start us, length us, event | category | flops | bytes accessed | tf_op | source)
XLA Modules:
  0.0 181.1 jit_solution(16472317298207474175)
XLA Ops:
  0.0 1.1 convert_reduce_fusion
  1.7 6.0 %all-to-all-start = ((f32[8,2,48]{2,1,0:T(2,128)}), f32[8,2,48]{2,1,0:T(2,128)S(1)}, u32[]{:S(2)}, u32[]{:S(2)}) async-start(f32[8,2,48]{2,1,0:T(2,128)} %broadcast_in_dim.46), calls=%async_computation | async-start | bytes 16384 | tf_op jit(solution)/shard_map/all_to_all | solution.py:328
  7.7 1.0 fusion.1
  10.4 1.9 %all-to-all-done.parts = f32[8,2,48]{2,1,0:T(2,128)S(1)} async-done(((f32[8,2,48]{2,1,0:T(2,128)}), f32[8,2,48]{2,1,0:T(2,128)S(1)}, u32[]{:S(2)}, u32[]{:S(2)}) %all-to-all-start) | async-done | bytes 3104 | tf_op jit(solution)/shard_map/all_to_all | solution.py:328
  12.3 0.9 copy-done.6
  13.2 1.2 normalize.1
  14.4 0.8 collective-permute-start
  15.2 0.9 collective-permute-done
  16.1 1.7 collective-permute-start.1
  17.9 2.2 %collective-permute-start.2 = (bf16[2,24,1920]{2,1,0:T(8,128)(2,1)S(1)}, bf16[2,24,1920]{2,1,0:T(8,128)(2,1)S(1)}, u32[]{:S(2)}, u32[]{:S(2)}) collective-permute-start(bf16[2,24,1920]{2,1,0:T(8,128)(2,1)S(1)} %pad_maximum_fusion.1), channel_id=1, source_target_pairs={{0,24},{1,97},{2,26},{3,99},{4,28},{5,101},{6,30},{7,103},{8,0},{9... | collective-permute-start | bytes 552968 | tf_op jit(solution)/shard_map/ppermute | solution.py:352
  20.1 1.2 collective-permute-start.3
  21.3 2.1 %copy-done.2 = bf16[1856,1024]{1,0:T(8,128)(2,1)S(1)} copy-done((bf16[1856,1024]{1,0:T(8,128)(2,1)S(1)}, bf16[1856,1024]{1,0:T(8,128)(2,1)}, u32[]{:S(2)}) %copy-start.2) | copy-done | bytes 3801112
  23.4 0.8 pair_projection.1.pairs
  24.2 2.1 %collective-permute-done.3 = bf16[2,24,1920]{2,1,0:T(8,128)(2,1)S(1)} collective-permute-done((bf16[2,24,1920]{2,1,0:T(8,128)(2,1)S(1)}, bf16[2,24,1920]{2,1,0:T(8,128)(2,1)S(1)}, u32[]{:S(2)}, u32[]{:S(2)}) %collective-permute-start.3) | collective-permute-done | bytes 184352 | tf_op jit(solution)/shard_map/ppermute | solution.py:352
  26.4 2.3 %collective-permute-start.6 = (bf16[2,96,1920]{2,1,0:T(8,128)(2,1)S(1)}, bf16[2,96,1920]{2,1,0:T(8,128)(2,1)S(1)}, u32[]{:S(2)}, u32[]{:S(2)}) collective-permute-start(bf16[2,96,1920]{2,1,0:T(8,128)(2,1)S(1)} %pad_maximum_fusion.a0), channel_id=1, source_target_pairs={{0,96},{1,25},{2,98},{3,27},{4,100},{5,29},{6,102},{7,31},{8,104},... | collective-permute-start | bytes 2211848 | tf_op jit(solution)/shard_map/ppermute | solution.py:361
  28.7 1.7 collective-permute-start.5
  30.5 2.6 %collective-permute-start.7 = (bf16[96,1920]{1,0:T(8,128)(2,1)S(1)}, bf16[96,1920]{1,0:T(8,128)(2,1)S(1)}, u32[]{:S(2)}, u32[]{:S(2)}) collective-permute-start(bf16[96,1920]{1,0:T(8,128)(2,1)S(1)} %slice_bitcast_fusion.3), channel_id=1, source_target_pairs={{0,1},{1,0},{2,3},{3,2},{4,5},{5,4},{6,7},{7,6},{8,9},{9,8},{10,11... | collective-permute-start | bytes 1105928 | tf_op jit(solution)/shard_map/ppermute | solution.py:362
  33.0 12.0 %collective-permute-done.6.a3 = bf16[2,96,1920]{2,1,0:T(8,128)(2,1)S(1)} collective-permute-done((bf16[2,96,1920]{2,1,0:T(8,128)(2,1)S(1)}, bf16[2,96,1920]{2,1,0:T(8,128)(2,1)S(1)}, u32[]{:S(2)}, u32[]{:S(2)}) %collective-permute-start.6) | collective-permute-done | bytes 737312 | tf_op jit(solution)/shard_map/ppermute | solution.py:361
  45.0 3.0 %collective-permute-start.10 = (bf16[96,1920]{1,0:T(8,128)(2,1)S(1)}, bf16[96,1920]{1,0:T(8,128)(2,1)S(1)}, u32[]{:S(2)}, u32[]{:S(2)}) collective-permute-start(bf16[96,1920]{1,0:T(8,128)(2,1)S(1)} %slice_bitcast_fusion), channel_id=1, source_target_pairs={{0,1},{1,0},{2,3},{3,2},{4,5},{5,4},{6,7},{7,6},{8,9},{9,8},{10,11... | collective-permute-start | bytes 1105928 | tf_op jit(solution)/shard_map/ppermute | solution.py:362
  48.4 3.3 %collective-permute-start.8 = (bf16[96,1920]{1,0:T(8,128)(2,1)S(1)}, bf16[96,1920]{1,0:T(8,128)(2,1)S(1)}, u32[]{:S(2)}, u32[]{:S(2)}) collective-permute-start(bf16[96,1920]{1,0:T(8,128)(2,1)S(1)} %slice_bitcast_fusion.2), channel_id=1, source_target_pairs={{0,1},{1,0},{2,3},{3,2},{4,5},{5,4},{6,7},{7,6},{8,9},{9,8},{10,11... | collective-permute-start | bytes 1105928 | tf_op jit(solution)/shard_map/ppermute | solution.py:362
  51.9 1.1 collective-permute-done.8.b1
  53.6 5.5 %query_projection.1 = (bf16[4,112,896]{2,1,0:T(8,128)(2,1)S(1)}, bf16[4,112,896]{2,1,0:T(8,128)(2,1)S(1)}) custom-call(s32[4]{0:T(128)S(1)} %pad_add_fusion.place, bf16[2,96,1920]{2,1,0:T(8,128)(2,1)S(1)} %pad_maximum_fusion.a0, bf16[2,96,1920]{2,1,0:T(8,128)(2,1)S(1)} %collective-permute-done.4.a1, bf16[2,96,1920]{2,1,0:T(8,128)(2,1)S(1)} %collective-permute-done.5.a2, ...), custom_call_target="tpu_custom_call" | custom-call | tf_op jit(solution)/shard_map/query_projection/pallas_call | solution.py:367
  59.5 1.9 %collective-permute-done.11.received = bf16[4,112,896]{2,1,0:T(8,128)(2,1)S(1)} collective-permute-done((bf16[4,112,896]{2,1,0:T(8,128)(2,1)S(1)}, bf16[4,112,896]{2,1,0:T(8,128)(2,1)S(1)}, u32[]{:S(2)}, u32[]{:S(2)}) %collective-permute-start.11) | collective-permute-done | bytes 802848 | tf_op jit(solution)/shard_map/ppermute | solution.py:377
  62.0 1.8 collective-permute-start.13
  63.8 0.9 collective-permute-start.14
  64.8 4.9 %collective-permute-done.12.b = bf16[112,896]{1,0:T(8,128)(2,1)S(1)} collective-permute-done((bf16[112,896]{1,0:T(8,128)(2,1)S(1)}, bf16[112,896]{1,0:T(8,128)(2,1)S(1)}, u32[]{:S(2)}, u32[]{:S(2)}) %collective-permute-start.12) | collective-permute-done | bytes 200736 | tf_op jit(solution)/shard_map/ppermute | solution.py:382
  69.7 3.2 %collective-permute-done.13.c = bf16[112,896]{1,0:T(8,128)(2,1)S(1)} collective-permute-done((bf16[112,896]{1,0:T(8,128)(2,1)S(1)}, bf16[112,896]{1,0:T(8,128)(2,1)S(1)}, u32[]{:S(2)}, u32[]{:S(2)}) %collective-permute-start.13) | collective-permute-done | bytes 200736 | tf_op jit(solution)/shard_map/ppermute | solution.py:384
  72.9 0.9 collective-permute-done.14.d
  73.8 0.9 collect.1
  75.3 3.5 %all-to-all-start.1 = ((bf16[16,6,896]{2,1,0:T(8,128)(2,1)}), bf16[16,6,896]{2,1,0:T(8,128)(2,1)S(1)}, u32[]{:S(2)}, u32[]{:S(2)}) async-start(bf16[16,6,896]{2,1,0:T(8,128)(2,1)} %get-tuple-element.29), calls=%async_computation.1 | async-start | bytes 458752 | tf_op jit(solution)/shard_map/all_to_all | solution.py:395
  80.3 5.9 %all-to-all-done.1.queries = bf16[16,6,896]{2,1,0:T(8,128)(2,1)S(1)} async-done(((bf16[16,6,896]{2,1,0:T(8,128)(2,1)}), bf16[16,6,896]{2,1,0:T(8,128)(2,1)S(1)}, u32[]{:S(2)}, u32[]{:S(2)}) %all-to-all-start.1) | async-done | bytes 172064 | tf_op jit(solution)/shard_map/all_to_all | solution.py:395
  86.2 2.8 %copy-done = bf16[3,2048,512]{2,1,0:T(8,128)(2,1)S(1)} copy-done((bf16[3,2048,512]{2,1,0:T(8,128)(2,1)S(1)}, bf16[3,2048,512]{2,1,0:T(8,128)(2,1)}, u32[]{:S(2)}) %copy-start) | copy-done | bytes 6291480
  89.0 2.8 %copy-done.1 = bf16[3,2048,512]{2,1,0:T(8,128)(2,1)S(1)} copy-done((bf16[3,2048,512]{2,1,0:T(8,128)(2,1)S(1)}, bf16[3,2048,512]{2,1,0:T(8,128)(2,1)}, u32[]{:S(2)}) %copy-start.1) | copy-done | bytes 6291480
  91.8 0.8 copy-done.8
  94.5 6.2 %attention.1 = bf16[16,6,896]{2,1,0:T(8,128)(2,1)S(1)} custom-call(s32[3]{0:T(128)S(1)} %copy-done.18, bf16[16,6,896]{2,1,0:T(8,128)(2,1)S(1)} %all-to-all-done.1.queries, f32[16,512]{1,0:T(8,128)S(1)} %copy-done.8, f32[8,128]{1,0:T(8,128)S(1)} %copy-done.12, f32[8,128]{1,0:T(8,128)S(1)} %copy-done.11, bf16[3,2048,512]{2,1,0:T(8,128)(2,1)S(1)} %copy-done, ...), custom_call_target="tpu_custom_call" | custom-call | tf_op jit(solution)/shard_map/attention/pallas_call | solution.py:407
  101.4 6.0 %all-to-all-start.2 = ((bf16[16,6,896]{2,1,0:T(8,128)(2,1)}), bf16[16,6,896]{2,1,0:T(8,128)(2,1)S(1)}, u32[]{:S(2)}, u32[]{:S(2)}) async-start(bf16[16,6,896]{2,1,0:T(8,128)(2,1)} %copy-done.5), calls=%async_computation.2 | async-start | bytes 458752 | tf_op jit(solution)/shard_map/all_to_all | solution.py:434
  107.5 1.2 dynamic_slice.3
  108.7 6.1 %all-to-all-done.2.block = bf16[16,6,896]{2,1,0:T(8,128)(2,1)S(1)} async-done(((bf16[16,6,896]{2,1,0:T(8,128)(2,1)}), bf16[16,6,896]{2,1,0:T(8,128)(2,1)S(1)}, u32[]{:S(2)}, u32[]{:S(2)}) %all-to-all-start.2) | async-done | bytes 172064 | tf_op jit(solution)/shard_map/all_to_all | solution.py:434
  114.9 0.8 collective-permute-start.15
  115.7 4.7 %collective-permute-start.16 = (bf16[96,896]{1,0:T(8,128)(2,1)S(1)}, bf16[96,896]{1,0:T(8,128)(2,1)S(1)}, u32[]{:S(2)}, u32[]{:S(2)}) collective-permute-start(bf16[96,896]{1,0:T(8,128)(2,1)S(1)} %repack.1.b0), channel_id=1, source_target_pairs={{0,4},{1,5},{2,6},{3,7},{4,0},{5,1},{6,2},{7,3},{8,12},{9,13},{10,... | collective-permute-start | bytes 516104 | tf_op jit(solution)/shard_map/ppermute | solution.py:442
  120.4 0.9 fusion.2
  121.3 2.9 %collective-permute-start.18 = (bf16[96,896]{1,0:T(8,128)(2,1)S(1)}, bf16[96,896]{1,0:T(8,128)(2,1)S(1)}, u32[]{:S(2)}, u32[]{:S(2)}) collective-permute-start(bf16[96,896]{1,0:T(8,128)(2,1)S(1)} %repack.1.b0), channel_id=1, source_target_pairs={{0,1},{1,0},{2,3},{3,2},{4,5},{5,4},{6,7},{7,6},{8,9},{9,8},{10,11... | collective-permute-start | bytes 516104 | tf_op jit(solution)/shard_map/ppermute | solution.py:443
  124.2 3.4 %collective-permute-start.19 = (bf16[96,896]{1,0:T(8,128)(2,1)S(1)}, bf16[96,896]{1,0:T(8,128)(2,1)S(1)}, u32[]{:S(2)}, u32[]{:S(2)}) collective-permute-start(bf16[96,896]{1,0:T(8,128)(2,1)S(1)} %collective-permute-done.15.b1), channel_id=1, source_target_pairs={{0,1},{1,0},{2,3},{3,2},{4,5},{5,4},{6,7},{7,6},{8,9},{9,8},{10,11... | collective-permute-start | bytes 516104 | tf_op jit(solution)/shard_map/ppermute | solution.py:443
  127.6 1.8 %collective-permute-start.20 = (bf16[96,896]{1,0:T(8,128)(2,1)S(1)}, bf16[96,896]{1,0:T(8,128)(2,1)S(1)}, u32[]{:S(2)}, u32[]{:S(2)}) collective-permute-start(bf16[96,896]{1,0:T(8,128)(2,1)S(1)} %collective-permute-done.16.b2), channel_id=1, source_target_pairs={{0,1},{1,0},{2,3},{3,2},{4,5},{5,4},{6,7},{7,6},{8,9},{9,8},{10,11... | collective-permute-start | bytes 516104 | tf_op jit(solution)/shard_map/ppermute | solution.py:443
  130.9 0.8 copy-done.9
  132.2 7.8 %output_projection.1 = bf16[16,48,1856]{2,1,0:T(8,128)(2,1)S(1)} custom-call(s32[4]{0:T(128)S(1)} %copy-done.15, bf16[96,896]{1,0:T(8,128)(2,1)S(1)} %repack.1.b0, bf16[96,896]{1,0:T(8,128)(2,1)S(1)} %collective-permute-done.15.b1, bf16[96,896]{1,0:T(8,128)(2,1)S(1)} %collective-permute-done.16.b2, bf16[96,896]{1,0:T(8,128)(2,1)S(1)} %collective-permute-done.17.b3, ...), custom_call_target="tpu_custom_call" | custom-call | tf_op jit(solution)/shard_map/output_projection/pallas_call | solution.py:449
  140.0 40.0 %all_to_all.20.parts = bf16[16,48,1856]{2,1,0:T(8,128)(2,1)S(1)} all-to-all(bf16[16,48,1856]{2,1,0:T(8,128)(2,1)S(1)} %output_projection.1), channel_id=1, replica_groups=mesh['gx'=16,'gy'=8] {'gx'}, dimensions={0} | all-to-all | bytes 5701632 | tf_op jit(solution)/shard_map/all_to_all | solution.py:458
  180.1 1.1 total.1
  (83 shorter events, 11.5 us)
Async XLA Ops:
  0.0 21.3 %copy-start.16 = (f32[1024]{0:T(1024)S(1)}, f32[1024]{0:T(1024)}, u32[]{:S(2)}) copy-start(f32[1024]{0:T(1024)} %param.24) | copy-start | bytes 12292
  0.0 21.3 %copy-start.10 = (f32[4,1024]{1,0:T(4,128)S(1)}, f32[4,1024]{1,0:T(4,128)}, u32[]{:S(2)}) copy-start(f32[4,1024]{1,0:T(4,128)} %extra.3) | copy-start | bytes 49156
  1.7 10.6 %all-to-all-start = ((f32[8,2,48]{2,1,0:T(2,128)}), f32[8,2,48]{2,1,0:T(2,128)S(1)}, u32[]{:S(2)}, u32[]{:S(2)}) async-start(f32[8,2,48]{2,1,0:T(2,128)} %broadcast_in_dim.46), calls=%async_computation | async-start | bytes 16384 | tf_op jit(solution)/shard_map/all_to_all | solution.py:328
  9.0 44.6 %copy-start.14 = (s32[4]{0:T(128)}, s32[4]{0:T(128)S(1)}, u32[]{:S(2)}) copy-start(s32[4]{0:T(128)S(1)} %pad_add_fusion.place) | copy-start | bytes 52
  12.3 0.9 copy-start.6
  14.4 1.7 collective-permute-start
  16.1 8.0 %collective-permute-start.1 = (bf16[2,24,1920]{2,1,0:T(8,128)(2,1)S(1)}, bf16[2,24,1920]{2,1,0:T(8,128)(2,1)S(1)}, u32[]{:S(2)}, u32[]{:S(2)}) collective-permute-start(bf16[2,24,1920]{2,1,0:T(8,128)(2,1)S(1)} %pad_maximum_fusion.1), channel_id=1, source_target_pairs={{0,8},{1,33},{2,10},{3,35},{4,12},{5,37},{6,14},{7,39},{8,16},{9,4... | collective-permute-start | bytes 552968 | tf_op jit(solution)/shard_map/ppermute | solution.py:352
  17.9 6.3 %collective-permute-start.2 = (bf16[2,24,1920]{2,1,0:T(8,128)(2,1)S(1)}, bf16[2,24,1920]{2,1,0:T(8,128)(2,1)S(1)}, u32[]{:S(2)}, u32[]{:S(2)}) collective-permute-start(bf16[2,24,1920]{2,1,0:T(8,128)(2,1)S(1)} %pad_maximum_fusion.1), channel_id=1, source_target_pairs={{0,24},{1,97},{2,26},{3,99},{4,28},{5,101},{6,30},{7,103},{8,0},{9... | collective-permute-start | bytes 552968 | tf_op jit(solution)/shard_map/ppermute | solution.py:352
  20.1 6.3 %collective-permute-start.3 = (bf16[2,24,1920]{2,1,0:T(8,128)(2,1)S(1)}, bf16[2,24,1920]{2,1,0:T(8,128)(2,1)S(1)}, u32[]{:S(2)}, u32[]{:S(2)}) collective-permute-start(bf16[2,24,1920]{2,1,0:T(8,128)(2,1)S(1)} %pad_maximum_fusion.1), channel_id=1, source_target_pairs={{0,16},{1,65},{2,18},{3,67},{4,20},{5,69},{6,22},{7,71},{8,24},{9,... | collective-permute-start | bytes 552968 | tf_op jit(solution)/shard_map/ppermute | solution.py:352
  21.3 2.1 %copy-start.2 = (bf16[1856,1024]{1,0:T(8,128)(2,1)S(1)}, bf16[1856,1024]{1,0:T(8,128)(2,1)}, u32[]{:S(2)}) copy-start(bf16[1856,1024]{1,0:T(8,128)(2,1)} %weight.2) | copy-start | bytes 11403268
  26.4 27.2 %copy-start.4 = (bf16[1856,896]{1,0:T(8,128)(2,1)S(1)}, bf16[1856,896]{1,0:T(8,128)(2,1)}, u32[]{:S(2)}) copy-start(bf16[1856,896]{1,0:T(8,128)(2,1)} %weight.3) | copy-start | bytes 9977860
  26.4 25.5 %copy-start.19 = (f32[896]{0:T(1024)S(1)}, f32[896]{0:T(1024)}, u32[]{:S(2)}) copy-start(f32[896]{0:T(1024)} %param.22) | copy-start | bytes 10756
  26.4 27.2 %copy-start.13 = (f32[4,896]{1,0:T(4,128)S(1)}, f32[4,896]{1,0:T(4,128)}, u32[]{:S(2)}) copy-start(f32[4,896]{1,0:T(4,128)} %extra.4) | copy-start | bytes 43012
  26.4 18.6 %collective-permute-start.6 = (bf16[2,96,1920]{2,1,0:T(8,128)(2,1)S(1)}, bf16[2,96,1920]{2,1,0:T(8,128)(2,1)S(1)}, u32[]{:S(2)}, u32[]{:S(2)}) collective-permute-start(bf16[2,96,1920]{2,1,0:T(8,128)(2,1)S(1)} %pad_maximum_fusion.a0), channel_id=1, source_target_pairs={{0,96},{1,25},{2,98},{3,27},{4,100},{5,29},{6,102},{7,31},{8,104},... | collective-permute-start | bytes 2211848 | tf_op jit(solution)/shard_map/ppermute | solution.py:361
  28.7 19.7 %collective-permute-start.4 = (bf16[2,96,1920]{2,1,0:T(8,128)(2,1)S(1)}, bf16[2,96,1920]{2,1,0:T(8,128)(2,1)S(1)}, u32[]{:S(2)}, u32[]{:S(2)}) collective-permute-start(bf16[2,96,1920]{2,1,0:T(8,128)(2,1)S(1)} %pad_maximum_fusion.a0), channel_id=1, source_target_pairs={{0,32},{1,9},{2,34},{3,11},{4,36},{5,13},{6,38},{7,15},{8,40},{9,1... | collective-permute-start | bytes 2211848 | tf_op jit(solution)/shard_map/ppermute | solution.py:361
  28.7 23.0 %collective-permute-start.5 = (bf16[2,96,1920]{2,1,0:T(8,128)(2,1)S(1)}, bf16[2,96,1920]{2,1,0:T(8,128)(2,1)S(1)}, u32[]{:S(2)}, u32[]{:S(2)}) collective-permute-start(bf16[2,96,1920]{2,1,0:T(8,128)(2,1)S(1)} %pad_maximum_fusion.a0), channel_id=1, source_target_pairs={{0,64},{1,17},{2,66},{3,19},{4,68},{5,21},{6,70},{7,23},{8,72},{9,... | collective-permute-start | bytes 2211848 | tf_op jit(solution)/shard_map/ppermute | solution.py:361
  30.5 21.4 %collective-permute-start.7 = (bf16[96,1920]{1,0:T(8,128)(2,1)S(1)}, bf16[96,1920]{1,0:T(8,128)(2,1)S(1)}, u32[]{:S(2)}, u32[]{:S(2)}) collective-permute-start(bf16[96,1920]{1,0:T(8,128)(2,1)S(1)} %slice_bitcast_fusion.3), channel_id=1, source_target_pairs={{0,1},{1,0},{2,3},{3,2},{4,5},{5,4},{6,7},{7,6},{8,9},{9,8},{10,11... | collective-permute-start | bytes 1105928 | tf_op jit(solution)/shard_map/ppermute | solution.py:362
  45.0 6.9 %collective-permute-start.10 = (bf16[96,1920]{1,0:T(8,128)(2,1)S(1)}, bf16[96,1920]{1,0:T(8,128)(2,1)S(1)}, u32[]{:S(2)}, u32[]{:S(2)}) collective-permute-start(bf16[96,1920]{1,0:T(8,128)(2,1)S(1)} %slice_bitcast_fusion), channel_id=1, source_target_pairs={{0,1},{1,0},{2,3},{3,2},{4,5},{5,4},{6,7},{7,6},{8,9},{9,8},{10,11... | collective-permute-start | bytes 1105928 | tf_op jit(solution)/shard_map/ppermute | solution.py:362
  48.4 4.6 %collective-permute-start.8 = (bf16[96,1920]{1,0:T(8,128)(2,1)S(1)}, bf16[96,1920]{1,0:T(8,128)(2,1)S(1)}, u32[]{:S(2)}, u32[]{:S(2)}) collective-permute-start(bf16[96,1920]{1,0:T(8,128)(2,1)S(1)} %slice_bitcast_fusion.2), channel_id=1, source_target_pairs={{0,1},{1,0},{2,3},{3,2},{4,5},{5,4},{6,7},{7,6},{8,9},{9,8},{10,11... | collective-permute-start | bytes 1105928 | tf_op jit(solution)/shard_map/ppermute | solution.py:362
  51.8 1.8 collective-permute-start.9
  59.1 5.6 %copy-start.17 = (s32[3]{0:T(128)S(1)}, s32[3]{0:T(128)}, u32[]{:S(2)}) copy-start(s32[3]{0:T(128)} %lengths.1) | copy-start | bytes 40
  59.1 2.4 %collective-permute-start.11 = (bf16[4,112,896]{2,1,0:T(8,128)(2,1)S(1)}, bf16[4,112,896]{2,1,0:T(8,128)(2,1)S(1)}, u32[]{:S(2)}, u32[]{:S(2)}) collective-permute-start(bf16[4,112,896]{2,1,0:T(8,128)(2,1)S(1)} %get-tuple-element.24), channel_id=1, source_target_pairs={{0,1},{1,0},{2,3},{3,2},{4,5},{5,4},{6,7},{7,6},{8,9},{9,8},{10,11... | collective-permute-start | bytes 2408456 | tf_op jit(solution)/shard_map/ppermute | solution.py:377
  61.7 8.1 %collective-permute-start.12 = (bf16[112,896]{1,0:T(8,128)(2,1)S(1)}, bf16[112,896]{1,0:T(8,128)(2,1)S(1)}, u32[]{:S(2)}, u32[]{:S(2)}) collective-permute-start(bf16[112,896]{1,0:T(8,128)(2,1)S(1)} %get-tuple-element.26), channel_id=1, source_target_pairs={{0,2},{1,3},{2,4},{3,5},{4,6},{5,7},{6,0},{7,1},{8,10},{9,11},{10,... | collective-permute-start | bytes 602120 | tf_op jit(solution)/shard_map/ppermute | solution.py:382
  62.0 10.9 %collective-permute-start.13 = (bf16[112,896]{1,0:T(8,128)(2,1)S(1)}, bf16[112,896]{1,0:T(8,128)(2,1)S(1)}, u32[]{:S(2)}, u32[]{:S(2)}) collective-permute-start(bf16[112,896]{1,0:T(8,128)(2,1)S(1)} %get-tuple-element.27), channel_id=1, source_target_pairs={{0,4},{1,5},{2,6},{3,7},{4,0},{5,1},{6,2},{7,3},{8,12},{9,13},{10,... | collective-permute-start | bytes 602120 | tf_op jit(solution)/shard_map/ppermute | solution.py:384
  63.8 10.0 %collective-permute-start.14 = (bf16[112,896]{1,0:T(8,128)(2,1)S(1)}, bf16[112,896]{1,0:T(8,128)(2,1)S(1)}, u32[]{:S(2)}, u32[]{:S(2)}) collective-permute-start(bf16[112,896]{1,0:T(8,128)(2,1)S(1)} %get-tuple-element.28), channel_id=1, source_target_pairs={{0,6},{1,7},{2,0},{3,1},{4,2},{5,3},{6,4},{7,5},{8,14},{9,15},{10,... | collective-permute-start | bytes 602120 | tf_op jit(solution)/shard_map/ppermute | solution.py:383
  74.7 0.6 copy-start.7
  75.3 10.9 %all-to-all-start.1 = ((bf16[16,6,896]{2,1,0:T(8,128)(2,1)}), bf16[16,6,896]{2,1,0:T(8,128)(2,1)S(1)}, u32[]{:S(2)}, u32[]{:S(2)}) async-start(bf16[16,6,896]{2,1,0:T(8,128)(2,1)} %get-tuple-element.29), calls=%async_computation.1 | async-start | bytes 458752 | tf_op jit(solution)/shard_map/all_to_all | solution.py:395
  86.2 2.8 %copy-start = (bf16[3,2048,512]{2,1,0:T(8,128)(2,1)S(1)}, bf16[3,2048,512]{2,1,0:T(8,128)(2,1)}, u32[]{:S(2)}) copy-start(bf16[3,2048,512]{2,1,0:T(8,128)(2,1)} %keys.1) | copy-start | bytes 18874372
  89.0 2.8 %copy-start.1 = (bf16[3,2048,512]{2,1,0:T(8,128)(2,1)S(1)}, bf16[3,2048,512]{2,1,0:T(8,128)(2,1)}, u32[]{:S(2)}) copy-start(bf16[3,2048,512]{2,1,0:T(8,128)(2,1)} %values.1) | copy-start | bytes 18874372
  91.8 0.8 copy-start.8
  92.5 0.7 copy-start.11
  93.2 0.7 copy-start.12
  93.9 0.7 copy-start.18
  94.5 36.3 %copy-start.3 = (bf16[896,1856]{0,1:T(8,128)(2,1)S(1)}, bf16[896,1856]{0,1:T(8,128)(2,1)}, u32[]{:S(2)}) copy-start(bf16[896,1856]{0,1:T(8,128)(2,1)} %param.31) | copy-start | bytes 9977860
  100.7 0.7 copy-start.5
  101.4 13.4 %all-to-all-start.2 = ((bf16[16,6,896]{2,1,0:T(8,128)(2,1)}), bf16[16,6,896]{2,1,0:T(8,128)(2,1)S(1)}, u32[]{:S(2)}, u32[]{:S(2)}) async-start(bf16[16,6,896]{2,1,0:T(8,128)(2,1)} %copy-done.5), calls=%async_computation.2 | async-start | bytes 458752 | tf_op jit(solution)/shard_map/all_to_all | solution.py:434
  114.9 9.3 %collective-permute-start.15 = (bf16[96,896]{1,0:T(8,128)(2,1)S(1)}, bf16[96,896]{1,0:T(8,128)(2,1)S(1)}, u32[]{:S(2)}, u32[]{:S(2)}) collective-permute-start(bf16[96,896]{1,0:T(8,128)(2,1)S(1)} %repack.1.b0), channel_id=1, source_target_pairs={{0,2},{1,3},{2,4},{3,5},{4,6},{5,7},{6,0},{7,1},{8,10},{9,11},{10,... | collective-permute-start | bytes 516104 | tf_op jit(solution)/shard_map/ppermute | solution.py:442
  115.7 11.9 %collective-permute-start.16 = (bf16[96,896]{1,0:T(8,128)(2,1)S(1)}, bf16[96,896]{1,0:T(8,128)(2,1)S(1)}, u32[]{:S(2)}, u32[]{:S(2)}) collective-permute-start(bf16[96,896]{1,0:T(8,128)(2,1)S(1)} %repack.1.b0), channel_id=1, source_target_pairs={{0,4},{1,5},{2,6},{3,7},{4,0},{5,1},{6,2},{7,3},{8,12},{9,13},{10,... | collective-permute-start | bytes 516104 | tf_op jit(solution)/shard_map/ppermute | solution.py:442
  120.4 9.0 %collective-permute-start.17 = (bf16[96,896]{1,0:T(8,128)(2,1)S(1)}, bf16[96,896]{1,0:T(8,128)(2,1)S(1)}, u32[]{:S(2)}, u32[]{:S(2)}) collective-permute-start(bf16[96,896]{1,0:T(8,128)(2,1)S(1)} %repack.1.b0), channel_id=1, source_target_pairs={{0,6},{1,7},{2,0},{3,1},{4,2},{5,3},{6,4},{7,5},{8,14},{9,15},{10,... | collective-permute-start | bytes 516104 | tf_op jit(solution)/shard_map/ppermute | solution.py:442
  121.3 8.9 %collective-permute-start.18 = (bf16[96,896]{1,0:T(8,128)(2,1)S(1)}, bf16[96,896]{1,0:T(8,128)(2,1)S(1)}, u32[]{:S(2)}, u32[]{:S(2)}) collective-permute-start(bf16[96,896]{1,0:T(8,128)(2,1)S(1)} %repack.1.b0), channel_id=1, source_target_pairs={{0,1},{1,0},{2,3},{3,2},{4,5},{5,4},{6,7},{7,6},{8,9},{9,8},{10,11... | collective-permute-start | bytes 516104 | tf_op jit(solution)/shard_map/ppermute | solution.py:443
  124.2 6.0 %collective-permute-start.19 = (bf16[96,896]{1,0:T(8,128)(2,1)S(1)}, bf16[96,896]{1,0:T(8,128)(2,1)S(1)}, u32[]{:S(2)}, u32[]{:S(2)}) collective-permute-start(bf16[96,896]{1,0:T(8,128)(2,1)S(1)} %collective-permute-done.15.b1), channel_id=1, source_target_pairs={{0,1},{1,0},{2,3},{3,2},{4,5},{5,4},{6,7},{7,6},{8,9},{9,8},{10,11... | collective-permute-start | bytes 516104 | tf_op jit(solution)/shard_map/ppermute | solution.py:443
  127.6 2.9 %collective-permute-start.20 = (bf16[96,896]{1,0:T(8,128)(2,1)S(1)}, bf16[96,896]{1,0:T(8,128)(2,1)S(1)}, u32[]{:S(2)}, u32[]{:S(2)}) collective-permute-start(bf16[96,896]{1,0:T(8,128)(2,1)S(1)} %collective-permute-done.16.b2), channel_id=1, source_target_pairs={{0,1},{1,0},{2,3},{3,2},{4,5},{5,4},{6,7},{7,6},{8,9},{9,8},{10,11... | collective-permute-start | bytes 516104 | tf_op jit(solution)/shard_map/ppermute | solution.py:443
  129.4 1.4 collective-permute-start.21
  130.9 0.8 copy-start.9
  131.6 0.6 copy-start.15

commit v4 on v3

--- a/solution.py
+++ b/solution.py
@@ -132,105 +132,120 @@
 
 def attend_kernel(
     lengths, queries, pairs, cosine, sine, keys, values, out,
-    staged, rotated, fresh_key, fresh_value, block0, block1, result,
+    staged, rotated, fresh_key, fresh_value, blocks, mixture, result, key_buf, value_buf, sems,
 ):
-    r = pl.program_id(0)
-    length = lengths[r]
-
-    @pl.when(r == 0)
-    def _():
-        for i in range(16):
-            put(staged, slice(8 * i, 8 * i + 6), queries[i].astype(F32))
-        for k in range(6):
-            for col in range(7):
-                lanes = slice(128 * col, 128 * col + 128)
-                part = staged[col, pl.ds(k, 16, stride=8), :]
-                turned = rotate_lanes(part, cosine[k : k + 1, :], sine[k : k + 1, :])
-                rotated[16 * k : 16 * k + 16, lanes] = turned.astype(BF).astype(F32) * 0.125
-        fresh_key[...] = jnp.zeros_like(fresh_key)
-        fresh_value[...] = jnp.zeros_like(fresh_value)
-        rounded = pairs[...].astype(BF).astype(F32)
-        for col in range(4):
+    requests = keys.shape[0]
+    window = keys.shape[1]
+
+    def fetch(r, n, which):
+        source, target = ((keys, key_buf), (values, value_buf))[which]
+        rows = pl.ds(pl.multiple_of(n * CHUNK, CHUNK), CHUNK)
+        return pltpu.make_async_copy(source.at[r, rows], target.at[r, rows], sems.at[r, n, which])
+
+    for r in range(requests):
+        for n in range(window // CHUNK):
+
+            @pl.when(lengths[r] > n * CHUNK)
+            def _():
+                fetch(r, n, 0).start()
+                fetch(r, n, 1).start()
+
+    for i in range(16):
+        put(staged, slice(8 * i, 8 * i + 6), queries[i].astype(F32))
+    for k in range(6):
+        for col in range(7):
             lanes = slice(128 * col, 128 * col + 128)
-            fresh_key[0:6, lanes] = rotate_lanes(rounded[0:6, lanes], cosine[0:6, :], sine[0:6, :])
-        fresh_value[0:6, :] = rounded[6:12, :]
+            part = staged[col, pl.ds(k, 16, stride=8), :]
+            turned = rotate_lanes(part, cosine[k : k + 1, :], sine[k : k + 1, :])
+            rotated[16 * k : 16 * k + 16, lanes] = turned.astype(BF).astype(F32) * 0.125
+    fresh_key[...] = jnp.zeros_like(fresh_key)
+    fresh_value[...] = jnp.zeros_like(fresh_value)
+    rounded = pairs[...].astype(BF).astype(F32)
+    for col in range(4):
+        lanes = slice(128 * col, 128 * col + 128)
+        fresh_key[0:6, lanes] = rotate_lanes(rounded[0:6, lanes], cosine[0:6, :], sine[0:6, :])
+    fresh_value[0:6, :] = rounded[6:12, :]
 
     sub = lax.broadcasted_iota(jnp.int32, (8, 256), 0)
     lane = lax.broadcasted_iota(jnp.int32, (8, 256), 1)
     own = sub // 2 == lane // 64
     low = lax.broadcasted_iota(jnp.int32, (8, 128), 1) < 64
-    for g, block in enumerate((block0, block1)):
-        for t in range(NEW):
-            start = pl.multiple_of((NEW * r + t) * 16 + 8 * g, 8)
-            for col in range(7):
-                part = rotated[pl.ds(start, 8), 128 * col : 128 * col + 128]
-                other = pltpu.roll(part, 64, axis=1)
-                for half in range(2):
-                    both = jnp.where(low, part, other) if half == 0 else jnp.where(low, other, part)
-                    both = jnp.concatenate([both, both], axis=1)
-                    at = (2 * col + half) * 16 + t * 8
-                    block[at : at + 8, :] = jnp.where(own, both, 0.0)
-
     rows = LOCAL_HEADS * 16
     row = lax.broadcasted_iota(jnp.int32, (rows, 128), 0)
     column = lax.broadcasted_iota(jnp.int32, (rows, 128), 1)
-    token = (row // 8) % 2
-    visible = (column // 2 == r) & (column % 2 <= token)
-    state = []
-    grouped = []
-    for g, block in enumerate((block0, block1)):
-        side = slice(256 * g, 256 * g + 256)
-        query = block[...].astype(BF)
-        grouped.append(query)
-        scores = lax.dot_general(query, fresh_key[:, side].astype(BF), NT, preferred_element_type=F32)
-        scores = jnp.where(visible, scores, -jnp.inf)
-        top = jnp.max(scores, axis=1, keepdims=True)
-        prob = jnp.exp(scores - top)
-        total = jnp.sum(prob, axis=1, keepdims=True)
-        mixed = jnp.dot(prob.astype(BF), fresh_value[:, side].astype(BF), preferred_element_type=F32)
-        state.append((top, total, mixed))
-
+    causal = column % 2 <= (row // 8) % 2
     place = lax.broadcasted_iota(jnp.int32, (rows, CHUNK), 1)
 
-    def body(n, state):
-        at = pl.multiple_of(n * CHUNK, CHUNK)
-        active = place < length - at
-        new = []
+    starts = []
+    for r in range(requests):
+        state = []
         for g in range(2):
-            top, total, mixed = state[g]
+            for t in range(NEW):
+                start = (NEW * r + t) * 16 + 8 * g
+                for col in range(7):
+                    part = rotated[start : start + 8, 128 * col : 128 * col + 128]
+                    other = pltpu.roll(part, 64, axis=1)
+                    for half in range(2):
+                        both = jnp.where(low, part, other) if half == 0 else jnp.where(low, other, part)
+                        both = jnp.concatenate([both, both], axis=1)
+                        at = (2 * col + half) * 16 + t * 8
+                        blocks[2 * r + g, at : at + 8, :] = jnp.where(own, both, 0.0)
             side = slice(256 * g, 256 * g + 256)
-            key = keys[0, pl.ds(at, CHUNK), side]
-            value = values[0, pl.ds(at, CHUNK), side]
-            scores = lax.dot_general(grouped[g], key, NT, preferred_element_type=F32)
-            scores = jnp.where(active, scores, -jnp.inf)
-            higher = jnp.maximum(top, jnp.max(scores, axis=1, keepdims=True))
-            shrink = jnp.exp(top - higher)
-            prob = jnp.exp(scores - higher)
-            total = total * shrink + jnp.sum(prob, axis=1, keepdims=True)
-            mixed = mixed * shrink + jnp.dot(prob.astype(BF), value, preferred_element_type=F32)
-            new.append((higher, total, mixed))
-        return tuple(new)
-
-    state = lax.fori_loop(0, (length + CHUNK - 1) // CHUNK, body, tuple(state))
-    for g in range(2):
-        top, total, mixed = state[g]
-        block0[...] = mixed / total
-        for t in range(NEW):
-            start = pl.multiple_of((NEW * r + t) * 16 + 8 * g, 8)
-            for col in range(7):
-                folded = []
-                for half in range(2):
-                    at = (2 * col + half) * 16 + t * 8
-                    part = jnp.where(own, block0[at : at + 8, :], 0.0)
-                    part = part[:, 0:128] + part[:, 128:256]
-                    folded.append(part + pltpu.roll(part, 64, axis=1))
-                result[col, pl.ds(start, 8), :] = jnp.where(low, folded[0], folded[1])
-
-    @pl.when(r == pl.num_programs(0) - 1)
-    def _():
-        for i in range(16):
-            for n, lanes in lanes_of(896):
-                out[i, :, lanes] = result[n, pl.ds(i, 6, stride=16), :].astype(BF)
+            query = blocks[2 * r + g].astype(BF)
+            scores = lax.dot_general(query, fresh_key[:, side].astype(BF), NT, preferred_element_type=F32)
+            scores = jnp.where(causal & (column // 2 == r), scores, -jnp.inf)
+            top = jnp.max(scores, axis=1, keepdims=True)
+            prob = jnp.exp(scores - top)
+            total = jnp.sum(prob, axis=1, keepdims=True)
+            mixture[2 * r + g] = jnp.dot(
+                prob.astype(BF), fresh_value[:, side].astype(BF), preferred_element_type=F32
+            )
+            state.append((top, total))
+        starts.append(tuple(state))
+
+    for r in range(requests):
+        length = lengths[r]
+
+        def body(n, state):
+            at = pl.multiple_of(n * CHUNK, CHUNK)
+            active = place < length - at
+            fetch(r, n, 0).wait()
+            fetch(r, n, 1).wait()
+            new = []
+            for g in range(2):
+                top, total = state[g]
+                side = slice(256 * g, 256 * g + 256)
+                key = key_buf[r, pl.ds(at, CHUNK), side]
+                value = value_buf[r, pl.ds(at, CHUNK), side]
+                query = blocks[2 * r + g].astype(BF)
+                scores = lax.dot_general(query, key, NT, preferred_element_type=F32)
+                scores = jnp.where(active, scores, -jnp.inf)
+                higher = jnp.maximum(top, jnp.max(scores, axis=1, keepdims=True))
+                shrink = jnp.exp(top - higher)
+                prob = jnp.exp(scores - higher)
+                total = total * shrink + jnp.sum(prob, axis=1, keepdims=True)
+                mixture[2 * r + g] = mixture[2 * r + g] * shrink + jnp.dot(
+                    prob.astype(BF), value, preferred_element_type=F32
+                )
+                new.append((higher, total))
+            return tuple(new)
+
+        state = lax.fori_loop(0, (length + CHUNK - 1) // CHUNK, body, starts[r])
+        for g in range(2):
+            blocks[2 * r + g] = mixture[2 * r + g] / state[g][1]
+            for t in range(NEW):
+                start = (NEW * r + t) * 16 + 8 * g
+                for col in range(7):
+                    folded = []
+                    for half in range(2):
+                        at = (2 * col + half) * 16 + t * 8
+                        part = jnp.where(own, blocks[2 * r + g, at : at + 8, :], 0.0)
+                        part = part[:, 0:128] + part[:, 128:256]
+                        folded.append(part + pltpu.roll(part, 64, axis=1))
+                    result[col, start : start + 8, :] = jnp.where(low, folded[0], folded[1])
+    for i in range(16):
+        for n, lanes in lanes_of(896):
+            out[i, :, lanes] = result[n, pl.ds(i, 6, stride=16), :].astype(BF)
 
 
 def repack_kernel(block, out, staged):
@@ -403,31 +418,26 @@
     cosine = jnp.pad(cosine, ((0, 2), (0, 0)))
     sine = jnp.pad(sine, ((0, 2), (0, 0)))
 
-    window = key_cache.shape[1]
+    requests, window, cached = key_cache.shape
+    hbm = pl.BlockSpec(memory_space=pltpu.HBM)
     attended = pl.pallas_call(
         attend_kernel,
-        grid=(3,),
-        in_specs=[
-            smem,
-            whole((16, 6, columns)),
-            whole((16, 512)),
-            whole((8, 128)),
-            whole((8, 128)),
-            pl.BlockSpec((1, window, 512), lambda n: (n, 0, 0)),
-            pl.BlockSpec((1, window, 512), lambda n: (n, 0, 0)),
-        ],
-        out_specs=whole((16, 6, columns)),
+        in_specs=[smem, vmem, vmem, vmem, vmem, hbm, hbm],
+        out_specs=vmem,
         out_shape=jax.ShapeDtypeStruct((16, 6, columns), BF),
         scratch_shapes=[
             pltpu.VMEM((7, 128, 128), F32),
             pltpu.VMEM((96, columns), F32),
-            pltpu.VMEM((128, 512), F32),
-            pltpu.VMEM((128, 512), F32),
-            pltpu.VMEM((224, 256), F32),
-            pltpu.VMEM((224, 256), F32),
+            pltpu.VMEM((128, cached), F32),
+            pltpu.VMEM((128, cached), F32),
+            pltpu.VMEM((6, 224, 256), F32),
+            pltpu.VMEM((6, 224, 256), F32),
             pltpu.VMEM((7, 96, 128), F32),
+            pltpu.VMEM((requests, window, cached), BF),
+            pltpu.VMEM((requests, window, cached), BF),
+            pltpu.SemaphoreType.DMA((requests, window // CHUNK, 2)),
         ],
-        compiler_params=params(24),
+        compiler_params=params(57),
         name="attention",
     )(lengths, queries, pair_sums, cosine, sine, key_cache, value_cache)
 

time: 182 us -> 174 us (0.956)
  local copies, waits for them, and re-layouts: 18.8 us -> 10.6 us
  Pallas kernels: 23.7 us -> 27.2 us
  starting transfers between devices: 51.5 us -> 48.1 us
    unnamed x40 -> x28, local copies, waits for them, and re-layouts: 14 us -> 5.75 us
    pallas_call x1, Pallas kernels: 6.19 us -> 9.63 us  [on_device(): pl.pallas_call(attend_kernel, in_specs=[smem, vmem, vmem, vmem, vmem, hbm...]
    all_to_all x1, starting transfers between devices: 6.01 us -> 3.54 us  [on_device(): lax.all_to_all(attended, 'gx', split_axis=0, concat_axis=0, tiled=True)]
  transfers between devices with their start and end apart: 25 -> 25, of which waited for: 15 -> 14; matrix products, arithmetic and copies ran while one was open for 4% -> 4% of each run, Pallas kernels for 0% -> 0%
where the time goes in v4:
time: 174 us; the launch traced here: 173 us
  starting transfers between devices  48.1 us (28%)
  waiting for transfers between devices  42.6 us (24%)
  blocking collectives  40 us (23%)
  Pallas kernels  27.2 us (16%)
  local copies, waits for them, and re-layouts  10.6 us (6%)
  other arithmetic  4.21 us (2%)
    all_to_all x1, blocking collectives, on_device(): lax.all_to_all(partial, 'gx', split_axis=0, concat_axis=0, tiled=True)  40 us
    ppermute x3, waiting for transfers between devices, on_device(): lax.ppermute(both, plane, shift_plane(False, d))  12.3 us
    pallas_call x1, Pallas kernels, on_device(): pl.pallas_call(attend_kernel, in_specs=[smem, vmem, vmem, vmem, vmem, hbm...  9.63 us
    ppermute x4, starting transfers between devices, on_device(): others = [lax.ppermute(block[1], 'gy', SIBLING) for block in arrived]  8.98 us
    ppermute x4, starting transfers between devices, on_device(): blocks = blocks + [lax.ppermute(b, 'gy', SIBLING) for b in blocks]  8.35 us
    pallas_call x1, Pallas kernels, on_device(): pl.pallas_call(output_kernel, in_specs=[smem] + [vmem] * 13, out_specs=vm...  7.82 us
    all_to_all x1, waiting for transfers between devices, on_device(): lax.all_to_all(attended, 'gx', split_axis=0, concat_axis=0, tiled=True)  6.41 us
    all_to_all x1, starting transfers between devices, on_device(): lax.all_to_all(jnp.broadcast_to(sums[None], (2 * N_Y, 2, block_rows)), 'g...  5.97 us
  transfers between devices with their start and end apart: 25, of which 14 were waited for; matrix products, arithmetic and copies ran while one was open for 4% of the time, Pallas kernels for 0%

profile of v4, /device:TPU:1, one launch (start us, length us, event | category | flops | bytes accessed | tf_op | source)
XLA Modules:
  0.0 173.0 jit_solution(8241212097074222181)
XLA Ops:
  0.0 1.1 convert_reduce_fusion
  1.7 6.0 %all-to-all-start = ((f32[8,2,48]{2,1,0:T(2,128)}), f32[8,2,48]{2,1,0:T(2,128)S(1)}, u32[]{:S(2)}, u32[]{:S(2)}) async-start(f32[8,2,48]{2,1,0:T(2,128)} %broadcast_in_dim.46), calls=%async_computation | async-start | bytes 16384 | tf_op jit(solution)/shard_map/all_to_all | solution.py:343
  7.7 1.0 fusion.1
  9.0 0.7 broadcast_in_dim.47.gain
  9.7 0.7 broadcast_in_dim.48.bias
  10.4 1.9 %all-to-all-done.parts = f32[8,2,48]{2,1,0:T(2,128)S(1)} async-done(((f32[8,2,48]{2,1,0:T(2,128)}), f32[8,2,48]{2,1,0:T(2,128)S(1)}, u32[]{:S(2)}, u32[]{:S(2)}) %all-to-all-start) | async-done | bytes 3104 | tf_op jit(solution)/shard_map/all_to_all | solution.py:343
  12.3 0.9 copy-done.3
  13.2 1.2 normalize.1
  14.4 0.8 collective-permute-start
  15.2 0.9 collective-permute-done
  16.1 1.7 collective-permute-start.1
  17.9 2.2 %collective-permute-start.2 = (bf16[2,24,1920]{2,1,0:T(8,128)(2,1)S(1)}, bf16[2,24,1920]{2,1,0:T(8,128)(2,1)S(1)}, u32[]{:S(2)}, u32[]{:S(2)}) collective-permute-start(bf16[2,24,1920]{2,1,0:T(8,128)(2,1)S(1)} %pad_maximum_fusion.1), channel_id=1, source_target_pairs={{0,24},{1,97},{2,26},{3,99},{4,28},{5,101},{6,30},{7,103},{8,0},{9... | collective-permute-start | bytes 552968 | tf_op jit(solution)/shard_map/ppermute | solution.py:367
  20.1 1.2 collective-permute-start.3
  21.3 2.1 %copy-done = bf16[1856,1024]{1,0:T(8,128)(2,1)S(1)} copy-done((bf16[1856,1024]{1,0:T(8,128)(2,1)S(1)}, bf16[1856,1024]{1,0:T(8,128)(2,1)}, u32[]{:S(2)}) %copy-start) | copy-done | bytes 3801112
  23.4 0.8 pair_projection.1.pairs
  24.2 2.1 %collective-permute-done.3 = bf16[2,24,1920]{2,1,0:T(8,128)(2,1)S(1)} collective-permute-done((bf16[2,24,1920]{2,1,0:T(8,128)(2,1)S(1)}, bf16[2,24,1920]{2,1,0:T(8,128)(2,1)S(1)}, u32[]{:S(2)}, u32[]{:S(2)}) %collective-permute-start.3) | collective-permute-done | bytes 184352 | tf_op jit(solution)/shard_map/ppermute | solution.py:367
  26.4 2.3 %collective-permute-start.6 = (bf16[2,96,1920]{2,1,0:T(8,128)(2,1)S(1)}, bf16[2,96,1920]{2,1,0:T(8,128)(2,1)S(1)}, u32[]{:S(2)}, u32[]{:S(2)}) collective-permute-start(bf16[2,96,1920]{2,1,0:T(8,128)(2,1)S(1)} %pad_maximum_fusion.a0), channel_id=1, source_target_pairs={{0,96},{1,25},{2,98},{3,27},{4,100},{5,29},{6,102},{7,31},{8,104},... | collective-permute-start | bytes 2211848 | tf_op jit(solution)/shard_map/ppermute | solution.py:376
  28.7 1.7 collective-permute-start.5
  30.5 2.6 %collective-permute-start.7 = (bf16[96,1920]{1,0:T(8,128)(2,1)S(1)}, bf16[96,1920]{1,0:T(8,128)(2,1)S(1)}, u32[]{:S(2)}, u32[]{:S(2)}) collective-permute-start(bf16[96,1920]{1,0:T(8,128)(2,1)S(1)} %slice_bitcast_fusion.3), channel_id=1, source_target_pairs={{0,1},{1,0},{2,3},{3,2},{4,5},{5,4},{6,7},{7,6},{8,9},{9,8},{10,11... | collective-permute-start | bytes 1105928 | tf_op jit(solution)/shard_map/ppermute | solution.py:377
  33.0 12.0 %collective-permute-done.6.a3 = bf16[2,96,1920]{2,1,0:T(8,128)(2,1)S(1)} collective-permute-done((bf16[2,96,1920]{2,1,0:T(8,128)(2,1)S(1)}, bf16[2,96,1920]{2,1,0:T(8,128)(2,1)S(1)}, u32[]{:S(2)}, u32[]{:S(2)}) %collective-permute-start.6) | collective-permute-done | bytes 737312 | tf_op jit(solution)/shard_map/ppermute | solution.py:376
  45.0 3.0 %collective-permute-start.10 = (bf16[96,1920]{1,0:T(8,128)(2,1)S(1)}, bf16[96,1920]{1,0:T(8,128)(2,1)S(1)}, u32[]{:S(2)}, u32[]{:S(2)}) collective-permute-start(bf16[96,1920]{1,0:T(8,128)(2,1)S(1)} %slice_bitcast_fusion), channel_id=1, source_target_pairs={{0,1},{1,0},{2,3},{3,2},{4,5},{5,4},{6,7},{7,6},{8,9},{9,8},{10,11... | collective-permute-start | bytes 1105928 | tf_op jit(solution)/shard_map/ppermute | solution.py:377
  48.4 3.3 %collective-permute-start.8 = (bf16[96,1920]{1,0:T(8,128)(2,1)S(1)}, bf16[96,1920]{1,0:T(8,128)(2,1)S(1)}, u32[]{:S(2)}, u32[]{:S(2)}) collective-permute-start(bf16[96,1920]{1,0:T(8,128)(2,1)S(1)} %slice_bitcast_fusion.2), channel_id=1, source_target_pairs={{0,1},{1,0},{2,3},{3,2},{4,5},{5,4},{6,7},{7,6},{8,9},{9,8},{10,11... | collective-permute-start | bytes 1105928 | tf_op jit(solution)/shard_map/ppermute | solution.py:377
  51.9 1.1 collective-permute-done.8.b1
  53.6 5.5 %query_projection.1 = (bf16[4,112,896]{2,1,0:T(8,128)(2,1)S(1)}, bf16[4,112,896]{2,1,0:T(8,128)(2,1)S(1)}) custom-call(s32[4]{0:T(128)S(1)} %pad_add_fusion.place, bf16[2,96,1920]{2,1,0:T(8,128)(2,1)S(1)} %pad_maximum_fusion.a0, bf16[2,96,1920]{2,1,0:T(8,128)(2,1)S(1)} %collective-permute-done.4.a1, bf16[2,96,1920]{2,1,0:T(8,128)(2,1)S(1)} %collective-permute-done.5.a2, ...), custom_call_target="tpu_custom_call" | custom-call | tf_op jit(solution)/shard_map/query_projection/pallas_call | solution.py:382
  59.5 1.9 %collective-permute-done.11.received = bf16[4,112,896]{2,1,0:T(8,128)(2,1)S(1)} collective-permute-done((bf16[4,112,896]{2,1,0:T(8,128)(2,1)S(1)}, bf16[4,112,896]{2,1,0:T(8,128)(2,1)S(1)}, u32[]{:S(2)}, u32[]{:S(2)}) %collective-permute-start.11) | collective-permute-done | bytes 802848 | tf_op jit(solution)/shard_map/ppermute | solution.py:392
  62.0 1.8 %collective-permute-start.13 = (bf16[112,896]{1,0:T(8,128)(2,1)S(1)}, bf16[112,896]{1,0:T(8,128)(2,1)S(1)}, u32[]{:S(2)}, u32[]{:S(2)}) collective-permute-start(bf16[112,896]{1,0:T(8,128)(2,1)S(1)} %get-tuple-element.27), channel_id=1, source_target_pairs={{0,4},{1,5},{2,6},{3,7},{4,0},{5,1},{6,2},{7,3},{8,12},{9,13},{10,... | collective-permute-start | bytes 602120 | tf_op jit(solution)/shard_map/ppermute | solution.py:399
  63.8 0.9 collective-permute-start.14
  64.8 4.9 %collective-permute-done.12.b = bf16[112,896]{1,0:T(8,128)(2,1)S(1)} collective-permute-done((bf16[112,896]{1,0:T(8,128)(2,1)S(1)}, bf16[112,896]{1,0:T(8,128)(2,1)S(1)}, u32[]{:S(2)}, u32[]{:S(2)}) %collective-permute-start.12) | collective-permute-done | bytes 200736 | tf_op jit(solution)/shard_map/ppermute | solution.py:397
  69.7 3.2 %collective-permute-done.13.c = bf16[112,896]{1,0:T(8,128)(2,1)S(1)} collective-permute-done((bf16[112,896]{1,0:T(8,128)(2,1)S(1)}, bf16[112,896]{1,0:T(8,128)(2,1)S(1)}, u32[]{:S(2)}, u32[]{:S(2)}) %collective-permute-start.13) | collective-permute-done | bytes 200736 | tf_op jit(solution)/shard_map/ppermute | solution.py:399
  72.9 0.9 collective-permute-done.14.d
  73.8 0.9 collect.1
  75.3 3.5 %all-to-all-start.1 = ((bf16[16,6,896]{2,1,0:T(8,128)(2,1)}), bf16[16,6,896]{2,1,0:T(8,128)(2,1)S(1)}, u32[]{:S(2)}, u32[]{:S(2)}) async-start(bf16[16,6,896]{2,1,0:T(8,128)(2,1)} %get-tuple-element.29), calls=%async_computation.1 | async-start | bytes 458752 | tf_op jit(solution)/shard_map/all_to_all | solution.py:410
  80.4 5.9 %all-to-all-done.1.queries = bf16[16,6,896]{2,1,0:T(8,128)(2,1)S(1)} async-done(((bf16[16,6,896]{2,1,0:T(8,128)(2,1)}), bf16[16,6,896]{2,1,0:T(8,128)(2,1)S(1)}, u32[]{:S(2)}, u32[]{:S(2)}) %all-to-all-start.1) | async-done | bytes 172064 | tf_op jit(solution)/shard_map/all_to_all | solution.py:410
  86.2 0.7 copy-done.11
  86.9 9.6 %attention.1 = bf16[16,6,896]{2,1,0:T(8,128)(2,1)} custom-call(s32[3]{0:T(128)} %lengths.1, bf16[16,6,896]{2,1,0:T(8,128)(2,1)} %copy-done.11, f32[16,512]{1,0:T(8,128)} %copy-done.4, f32[8,128]{1,0:T(8,128)} %pad.21.cosine, f32[8,128]{1,0:T(8,128)} %select_maximum_fusion.sine, bf16[3,2048,512]{2,1,0:T(8,128)(2,1)} %keys.1, bf16[3,2048,512]{2,1,0:T(8,128)(2,1)} %values.1), custom_call_target="tpu_custom_call" | custom-call | tf_op jit(solution)/shard_map/attention/pallas_call | solution.py:423
  96.5 3.5 %all-to-all-start.2 = ((bf16[16,6,896]{2,1,0:T(8,128)(2,1)}), bf16[16,6,896]{2,1,0:T(8,128)(2,1)S(1)}, u32[]{:S(2)}, u32[]{:S(2)}) async-start(bf16[16,6,896]{2,1,0:T(8,128)(2,1)} %attention.1), calls=%async_computation.2 | async-start | bytes 458752 | tf_op jit(solution)/shard_map/all_to_all | solution.py:444
  100.1 1.2 dynamic_slice.3
  101.3 6.4 %all-to-all-done.2.block = bf16[16,6,896]{2,1,0:T(8,128)(2,1)S(1)} async-done(((bf16[16,6,896]{2,1,0:T(8,128)(2,1)}), bf16[16,6,896]{2,1,0:T(8,128)(2,1)S(1)}, u32[]{:S(2)}, u32[]{:S(2)}) %all-to-all-start.2) | async-done | bytes 172064 | tf_op jit(solution)/shard_map/all_to_all | solution.py:444
  107.9 4.3 %collective-permute-start.16 = (bf16[96,896]{1,0:T(8,128)(2,1)S(1)}, bf16[96,896]{1,0:T(8,128)(2,1)S(1)}, u32[]{:S(2)}, u32[]{:S(2)}) collective-permute-start(bf16[96,896]{1,0:T(8,128)(2,1)S(1)} %repack.1.b0), channel_id=1, source_target_pairs={{0,4},{1,5},{2,6},{3,7},{4,0},{5,1},{6,2},{7,3},{8,12},{9,13},{10,... | collective-permute-start | bytes 516104 | tf_op jit(solution)/shard_map/ppermute | solution.py:452
  112.2 0.9 fusion.2
  113.1 3.9 %collective-permute-start.18 = (bf16[96,896]{1,0:T(8,128)(2,1)S(1)}, bf16[96,896]{1,0:T(8,128)(2,1)S(1)}, u32[]{:S(2)}, u32[]{:S(2)}) collective-permute-start(bf16[96,896]{1,0:T(8,128)(2,1)S(1)} %repack.1.b0), channel_id=1, source_target_pairs={{0,1},{1,0},{2,3},{3,2},{4,5},{5,4},{6,7},{7,6},{8,9},{9,8},{10,11... | collective-permute-start | bytes 516104 | tf_op jit(solution)/shard_map/ppermute | solution.py:453
  117.0 2.4 %collective-permute-start.19 = (bf16[96,896]{1,0:T(8,128)(2,1)S(1)}, bf16[96,896]{1,0:T(8,128)(2,1)S(1)}, u32[]{:S(2)}, u32[]{:S(2)}) collective-permute-start(bf16[96,896]{1,0:T(8,128)(2,1)S(1)} %collective-permute-done.15.b1), channel_id=1, source_target_pairs={{0,1},{1,0},{2,3},{3,2},{4,5},{5,4},{6,7},{7,6},{8,9},{9,8},{10,11... | collective-permute-start | bytes 516104 | tf_op jit(solution)/shard_map/ppermute | solution.py:453
  119.4 1.9 %collective-permute-start.20 = (bf16[96,896]{1,0:T(8,128)(2,1)S(1)}, bf16[96,896]{1,0:T(8,128)(2,1)S(1)}, u32[]{:S(2)}, u32[]{:S(2)}) collective-permute-start(bf16[96,896]{1,0:T(8,128)(2,1)S(1)} %collective-permute-done.16.b2), channel_id=1, source_target_pairs={{0,1},{1,0},{2,3},{3,2},{4,5},{5,4},{6,7},{7,6},{8,9},{9,8},{10,11... | collective-permute-start | bytes 516104 | tf_op jit(solution)/shard_map/ppermute | solution.py:453
  121.4 0.7 broadcast_in_dim.55.scale
  122.6 0.8 copy-done.5
  124.1 7.8 %output_projection.1 = bf16[16,48,1856]{2,1,0:T(8,128)(2,1)S(1)} custom-call(s32[4]{0:T(128)S(1)} %copy-done.9, bf16[96,896]{1,0:T(8,128)(2,1)S(1)} %repack.1.b0, bf16[96,896]{1,0:T(8,128)(2,1)S(1)} %collective-permute-done.15.b1, bf16[96,896]{1,0:T(8,128)(2,1)S(1)} %collective-permute-done.16.b2, bf16[96,896]{1,0:T(8,128)(2,1)S(1)} %collective-permute-done.17.b3, ...), custom_call_target="tpu_custom_call" | custom-call | tf_op jit(solution)/shard_map/output_projection/pallas_call | solution.py:459
  131.9 40.0 %all_to_all.20.parts = bf16[16,48,1856]{2,1,0:T(8,128)(2,1)S(1)} all-to-all(bf16[16,48,1856]{2,1,0:T(8,128)(2,1)S(1)} %output_projection.1), channel_id=1, replica_groups=mesh['gx'=16,'gy'=8] {'gx'}, dimensions={0} | all-to-all | bytes 5701632 | tf_op jit(solution)/shard_map/all_to_all | solution.py:468
  171.9 1.1 total.1
  (71 shorter events, 6.9 us)
Async XLA Ops:
  0.0 21.3 %copy-start.10 = (f32[1024]{0:T(1024)S(1)}, f32[1024]{0:T(1024)}, u32[]{:S(2)}) copy-start(f32[1024]{0:T(1024)} %param.24) | copy-start | bytes 12292
  0.0 21.3 %copy-start.6 = (f32[4,1024]{1,0:T(4,128)S(1)}, f32[4,1024]{1,0:T(4,128)}, u32[]{:S(2)}) copy-start(f32[4,1024]{1,0:T(4,128)} %extra.3) | copy-start | bytes 49156
  1.7 10.6 %all-to-all-start = ((f32[8,2,48]{2,1,0:T(2,128)}), f32[8,2,48]{2,1,0:T(2,128)S(1)}, u32[]{:S(2)}, u32[]{:S(2)}) async-start(f32[8,2,48]{2,1,0:T(2,128)} %broadcast_in_dim.46), calls=%async_computation | async-start | bytes 16384 | tf_op jit(solution)/shard_map/all_to_all | solution.py:343
  9.0 44.6 %copy-start.8 = (s32[4]{0:T(128)}, s32[4]{0:T(128)S(1)}, u32[]{:S(2)}) copy-start(s32[4]{0:T(128)S(1)} %pad_add_fusion.place) | copy-start | bytes 52
  12.3 0.9 copy-start.3
  14.4 1.7 collective-permute-start
  16.1 8.0 %collective-permute-start.1 = (bf16[2,24,1920]{2,1,0:T(8,128)(2,1)S(1)}, bf16[2,24,1920]{2,1,0:T(8,128)(2,1)S(1)}, u32[]{:S(2)}, u32[]{:S(2)}) collective-permute-start(bf16[2,24,1920]{2,1,0:T(8,128)(2,1)S(1)} %pad_maximum_fusion.1), channel_id=1, source_target_pairs={{0,8},{1,33},{2,10},{3,35},{4,12},{5,37},{6,14},{7,39},{8,16},{9,4... | collective-permute-start | bytes 552968 | tf_op jit(solution)/shard_map/ppermute | solution.py:367
  17.9 6.3 %collective-permute-start.2 = (bf16[2,24,1920]{2,1,0:T(8,128)(2,1)S(1)}, bf16[2,24,1920]{2,1,0:T(8,128)(2,1)S(1)}, u32[]{:S(2)}, u32[]{:S(2)}) collective-permute-start(bf16[2,24,1920]{2,1,0:T(8,128)(2,1)S(1)} %pad_maximum_fusion.1), channel_id=1, source_target_pairs={{0,24},{1,97},{2,26},{3,99},{4,28},{5,101},{6,30},{7,103},{8,0},{9... | collective-permute-start | bytes 552968 | tf_op jit(solution)/shard_map/ppermute | solution.py:367
  20.1 6.3 %collective-permute-start.3 = (bf16[2,24,1920]{2,1,0:T(8,128)(2,1)S(1)}, bf16[2,24,1920]{2,1,0:T(8,128)(2,1)S(1)}, u32[]{:S(2)}, u32[]{:S(2)}) collective-permute-start(bf16[2,24,1920]{2,1,0:T(8,128)(2,1)S(1)} %pad_maximum_fusion.1), channel_id=1, source_target_pairs={{0,16},{1,65},{2,18},{3,67},{4,20},{5,69},{6,22},{7,71},{8,24},{9,... | collective-permute-start | bytes 552968 | tf_op jit(solution)/shard_map/ppermute | solution.py:367
  21.3 2.1 %copy-start = (bf16[1856,1024]{1,0:T(8,128)(2,1)S(1)}, bf16[1856,1024]{1,0:T(8,128)(2,1)}, u32[]{:S(2)}) copy-start(bf16[1856,1024]{1,0:T(8,128)(2,1)} %weight.2) | copy-start | bytes 11403268
  26.4 27.2 %copy-start.2 = (bf16[1856,896]{1,0:T(8,128)(2,1)S(1)}, bf16[1856,896]{1,0:T(8,128)(2,1)}, u32[]{:S(2)}) copy-start(bf16[1856,896]{1,0:T(8,128)(2,1)} %weight.3) | copy-start | bytes 9977860
  26.4 25.5 %copy-start.12 = (f32[896]{0:T(1024)S(1)}, f32[896]{0:T(1024)}, u32[]{:S(2)}) copy-start(f32[896]{0:T(1024)} %param.22) | copy-start | bytes 10756
  26.4 27.2 %copy-start.7 = (f32[4,896]{1,0:T(4,128)S(1)}, f32[4,896]{1,0:T(4,128)}, u32[]{:S(2)}) copy-start(f32[4,896]{1,0:T(4,128)} %extra.4) | copy-start | bytes 43012
  26.4 18.6 %collective-permute-start.6 = (bf16[2,96,1920]{2,1,0:T(8,128)(2,1)S(1)}, bf16[2,96,1920]{2,1,0:T(8,128)(2,1)S(1)}, u32[]{:S(2)}, u32[]{:S(2)}) collective-permute-start(bf16[2,96,1920]{2,1,0:T(8,128)(2,1)S(1)} %pad_maximum_fusion.a0), channel_id=1, source_target_pairs={{0,96},{1,25},{2,98},{3,27},{4,100},{5,29},{6,102},{7,31},{8,104},... | collective-permute-start | bytes 2211848 | tf_op jit(solution)/shard_map/ppermute | solution.py:376
  28.7 19.7 %collective-permute-start.4 = (bf16[2,96,1920]{2,1,0:T(8,128)(2,1)S(1)}, bf16[2,96,1920]{2,1,0:T(8,128)(2,1)S(1)}, u32[]{:S(2)}, u32[]{:S(2)}) collective-permute-start(bf16[2,96,1920]{2,1,0:T(8,128)(2,1)S(1)} %pad_maximum_fusion.a0), channel_id=1, source_target_pairs={{0,32},{1,9},{2,34},{3,11},{4,36},{5,13},{6,38},{7,15},{8,40},{9,1... | collective-permute-start | bytes 2211848 | tf_op jit(solution)/shard_map/ppermute | solution.py:376
  28.7 23.0 %collective-permute-start.5 = (bf16[2,96,1920]{2,1,0:T(8,128)(2,1)S(1)}, bf16[2,96,1920]{2,1,0:T(8,128)(2,1)S(1)}, u32[]{:S(2)}, u32[]{:S(2)}) collective-permute-start(bf16[2,96,1920]{2,1,0:T(8,128)(2,1)S(1)} %pad_maximum_fusion.a0), channel_id=1, source_target_pairs={{0,64},{1,17},{2,66},{3,19},{4,68},{5,21},{6,70},{7,23},{8,72},{9,... | collective-permute-start | bytes 2211848 | tf_op jit(solution)/shard_map/ppermute | solution.py:376
  30.5 21.4 %collective-permute-start.7 = (bf16[96,1920]{1,0:T(8,128)(2,1)S(1)}, bf16[96,1920]{1,0:T(8,128)(2,1)S(1)}, u32[]{:S(2)}, u32[]{:S(2)}) collective-permute-start(bf16[96,1920]{1,0:T(8,128)(2,1)S(1)} %slice_bitcast_fusion.3), channel_id=1, source_target_pairs={{0,1},{1,0},{2,3},{3,2},{4,5},{5,4},{6,7},{7,6},{8,9},{9,8},{10,11... | collective-permute-start | bytes 1105928 | tf_op jit(solution)/shard_map/ppermute | solution.py:377
  45.0 6.9 %collective-permute-start.10 = (bf16[96,1920]{1,0:T(8,128)(2,1)S(1)}, bf16[96,1920]{1,0:T(8,128)(2,1)S(1)}, u32[]{:S(2)}, u32[]{:S(2)}) collective-permute-start(bf16[96,1920]{1,0:T(8,128)(2,1)S(1)} %slice_bitcast_fusion), channel_id=1, source_target_pairs={{0,1},{1,0},{2,3},{3,2},{4,5},{5,4},{6,7},{7,6},{8,9},{9,8},{10,11... | collective-permute-start | bytes 1105928 | tf_op jit(solution)/shard_map/ppermute | solution.py:377
  48.4 4.6 %collective-permute-start.8 = (bf16[96,1920]{1,0:T(8,128)(2,1)S(1)}, bf16[96,1920]{1,0:T(8,128)(2,1)S(1)}, u32[]{:S(2)}, u32[]{:S(2)}) collective-permute-start(bf16[96,1920]{1,0:T(8,128)(2,1)S(1)} %slice_bitcast_fusion.2), channel_id=1, source_target_pairs={{0,1},{1,0},{2,3},{3,2},{4,5},{5,4},{6,7},{7,6},{8,9},{9,8},{10,11... | collective-permute-start | bytes 1105928 | tf_op jit(solution)/shard_map/ppermute | solution.py:377
  51.8 1.8 %collective-permute-start.9 = (bf16[96,1920]{1,0:T(8,128)(2,1)S(1)}, bf16[96,1920]{1,0:T(8,128)(2,1)S(1)}, u32[]{:S(2)}, u32[]{:S(2)}) collective-permute-start(bf16[96,1920]{1,0:T(8,128)(2,1)S(1)} %slice_bitcast_fusion.1), channel_id=1, source_target_pairs={{0,1},{1,0},{2,3},{3,2},{4,5},{5,4},{6,7},{7,6},{8,9},{9,8},{10,11... | collective-permute-start | bytes 1105928 | tf_op jit(solution)/shard_map/ppermute | solution.py:377
  59.1 5.6 %copy-start.13 = (s32[3]{0:T(128)S(1)}, s32[3]{0:T(128)}, u32[]{:S(2)}) copy-start(s32[3]{0:T(128)} %lengths.1) | copy-start | bytes 40
  59.1 2.4 %collective-permute-start.11 = (bf16[4,112,896]{2,1,0:T(8,128)(2,1)S(1)}, bf16[4,112,896]{2,1,0:T(8,128)(2,1)S(1)}, u32[]{:S(2)}, u32[]{:S(2)}) collective-permute-start(bf16[4,112,896]{2,1,0:T(8,128)(2,1)S(1)} %get-tuple-element.24), channel_id=1, source_target_pairs={{0,1},{1,0},{2,3},{3,2},{4,5},{5,4},{6,7},{7,6},{8,9},{9,8},{10,11... | collective-permute-start | bytes 2408456 | tf_op jit(solution)/shard_map/ppermute | solution.py:392
  61.7 8.1 %collective-permute-start.12 = (bf16[112,896]{1,0:T(8,128)(2,1)S(1)}, bf16[112,896]{1,0:T(8,128)(2,1)S(1)}, u32[]{:S(2)}, u32[]{:S(2)}) collective-permute-start(bf16[112,896]{1,0:T(8,128)(2,1)S(1)} %get-tuple-element.26), channel_id=1, source_target_pairs={{0,2},{1,3},{2,4},{3,5},{4,6},{5,7},{6,0},{7,1},{8,10},{9,11},{10,... | collective-permute-start | bytes 602120 | tf_op jit(solution)/shard_map/ppermute | solution.py:397
  62.0 10.9 %collective-permute-start.13 = (bf16[112,896]{1,0:T(8,128)(2,1)S(1)}, bf16[112,896]{1,0:T(8,128)(2,1)S(1)}, u32[]{:S(2)}, u32[]{:S(2)}) collective-permute-start(bf16[112,896]{1,0:T(8,128)(2,1)S(1)} %get-tuple-element.27), channel_id=1, source_target_pairs={{0,4},{1,5},{2,6},{3,7},{4,0},{5,1},{6,2},{7,3},{8,12},{9,13},{10,... | collective-permute-start | bytes 602120 | tf_op jit(solution)/shard_map/ppermute | solution.py:399
  63.8 10.0 %collective-permute-start.14 = (bf16[112,896]{1,0:T(8,128)(2,1)S(1)}, bf16[112,896]{1,0:T(8,128)(2,1)S(1)}, u32[]{:S(2)}, u32[]{:S(2)}) collective-permute-start(bf16[112,896]{1,0:T(8,128)(2,1)S(1)} %get-tuple-element.28), channel_id=1, source_target_pairs={{0,6},{1,7},{2,0},{3,1},{4,2},{5,3},{6,4},{7,5},{8,14},{9,15},{10,... | collective-permute-start | bytes 602120 | tf_op jit(solution)/shard_map/ppermute | solution.py:398
  74.7 0.6 copy-start.4
  75.3 10.9 %all-to-all-start.1 = ((bf16[16,6,896]{2,1,0:T(8,128)(2,1)}), bf16[16,6,896]{2,1,0:T(8,128)(2,1)S(1)}, u32[]{:S(2)}, u32[]{:S(2)}) async-start(bf16[16,6,896]{2,1,0:T(8,128)(2,1)} %get-tuple-element.29), calls=%async_computation.1 | async-start | bytes 458752 | tf_op jit(solution)/shard_map/all_to_all | solution.py:410
  86.2 0.7 copy-start.11
  86.9 35.7 %copy-start.1 = (bf16[896,1856]{0,1:T(8,128)(2,1)S(1)}, bf16[896,1856]{0,1:T(8,128)(2,1)}, u32[]{:S(2)}) copy-start(bf16[896,1856]{0,1:T(8,128)(2,1)} %param.31) | copy-start | bytes 9977860
  96.5 11.2 %all-to-all-start.2 = ((bf16[16,6,896]{2,1,0:T(8,128)(2,1)}), bf16[16,6,896]{2,1,0:T(8,128)(2,1)S(1)}, u32[]{:S(2)}, u32[]{:S(2)}) async-start(bf16[16,6,896]{2,1,0:T(8,128)(2,1)} %attention.1), calls=%async_computation.2 | async-start | bytes 458752 | tf_op jit(solution)/shard_map/all_to_all | solution.py:444
  107.8 9.1 %collective-permute-start.15 = (bf16[96,896]{1,0:T(8,128)(2,1)S(1)}, bf16[96,896]{1,0:T(8,128)(2,1)S(1)}, u32[]{:S(2)}, u32[]{:S(2)}) collective-permute-start(bf16[96,896]{1,0:T(8,128)(2,1)S(1)} %repack.1.b0), channel_id=1, source_target_pairs={{0,2},{1,3},{2,4},{3,5},{4,6},{5,7},{6,0},{7,1},{8,10},{9,11},{10,... | collective-permute-start | bytes 516104 | tf_op jit(solution)/shard_map/ppermute | solution.py:452
  107.9 11.4 %collective-permute-start.16 = (bf16[96,896]{1,0:T(8,128)(2,1)S(1)}, bf16[96,896]{1,0:T(8,128)(2,1)S(1)}, u32[]{:S(2)}, u32[]{:S(2)}) collective-permute-start(bf16[96,896]{1,0:T(8,128)(2,1)S(1)} %repack.1.b0), channel_id=1, source_target_pairs={{0,4},{1,5},{2,6},{3,7},{4,0},{5,1},{6,2},{7,3},{8,12},{9,13},{10,... | collective-permute-start | bytes 516104 | tf_op jit(solution)/shard_map/ppermute | solution.py:452
  112.2 9.0 %collective-permute-start.17 = (bf16[96,896]{1,0:T(8,128)(2,1)S(1)}, bf16[96,896]{1,0:T(8,128)(2,1)S(1)}, u32[]{:S(2)}, u32[]{:S(2)}) collective-permute-start(bf16[96,896]{1,0:T(8,128)(2,1)S(1)} %repack.1.b0), channel_id=1, source_target_pairs={{0,6},{1,7},{2,0},{3,1},{4,2},{5,3},{6,4},{7,5},{8,14},{9,15},{10,... | collective-permute-start | bytes 516104 | tf_op jit(solution)/shard_map/ppermute | solution.py:452
  113.1 9.1 %collective-permute-start.18 = (bf16[96,896]{1,0:T(8,128)(2,1)S(1)}, bf16[96,896]{1,0:T(8,128)(2,1)S(1)}, u32[]{:S(2)}, u32[]{:S(2)}) collective-permute-start(bf16[96,896]{1,0:T(8,128)(2,1)S(1)} %repack.1.b0), channel_id=1, source_target_pairs={{0,1},{1,0},{2,3},{3,2},{4,5},{5,4},{6,7},{7,6},{8,9},{9,8},{10,11... | collective-permute-start | bytes 516104 | tf_op jit(solution)/shard_map/ppermute | solution.py:453
  117.0 5.3 %collective-permute-start.19 = (bf16[96,896]{1,0:T(8,128)(2,1)S(1)}, bf16[96,896]{1,0:T(8,128)(2,1)S(1)}, u32[]{:S(2)}, u32[]{:S(2)}) collective-permute-start(bf16[96,896]{1,0:T(8,128)(2,1)S(1)} %collective-permute-done.15.b1), channel_id=1, source_target_pairs={{0,1},{1,0},{2,3},{3,2},{4,5},{5,4},{6,7},{7,6},{8,9},{9,8},{10,11... | collective-permute-start | bytes 516104 | tf_op jit(solution)/shard_map/ppermute | solution.py:453
  119.4 2.9 %collective-permute-start.20 = (bf16[96,896]{1,0:T(8,128)(2,1)S(1)}, bf16[96,896]{1,0:T(8,128)(2,1)S(1)}, u32[]{:S(2)}, u32[]{:S(2)}) collective-permute-start(bf16[96,896]{1,0:T(8,128)(2,1)S(1)} %collective-permute-done.16.b2), channel_id=1, source_target_pairs={{0,1},{1,0},{2,3},{3,2},{4,5},{5,4},{6,7},{7,6},{8,9},{9,8},{10,11... | collective-permute-start | bytes 516104 | tf_op jit(solution)/shard_map/ppermute | solution.py:453
  121.2 1.4 collective-permute-start.21
  122.6 0.8 copy-start.5
  123.4 0.7 copy-start.9

commit v5 on v4

--- a/solution.py
+++ b/solution.py
@@ -40,35 +40,74 @@
     return pl.BlockSpec(shape, lambda *_: (0,) * len(shape))
 
 
-def normalize_kernel(place, parts, x, gain, bias, picked, plain, own, keep, send):
-    sums = jnp.sum(parts[...], axis=0)
-    rows = x.shape[0]
-    unit = lax.broadcasted_iota(jnp.int32, (rows, rows), 0) == lax.broadcasted_iota(jnp.int32, (rows, rows), 1)
-    sums = lax.dot_general(
-        unit.astype(F32), sums, NT, precision=lax.Precision.HIGHEST, preferred_element_type=F32
-    )
-    average = sums[:, 0:1] / D
-    variance = sums[:, 1:2] / D - average * average
-    normed = (x[...].astype(F32) - average) * lax.rsqrt(variance + epsilon) * gain[...] + bias[...]
-    rounded = normed.astype(BF)
-    outlier = jnp.dot(rounded, picked[...], preferred_element_type=F32)
-    regular = rounded.astype(F32) * plain[...]
-    features = x.shape[1]
-    own[:, 0:features] = regular.astype(BF)
+def prepare_kernel(place, x, picked, own, keep, send):
+    outlier = jnp.dot(x[...], picked[...], preferred_element_type=F32)
+    values = x[...].astype(F32)
+    rows, features = x.shape
+    own[:, 0:features] = x[...]
     own[:, features:] = outlier[:, 0:64].astype(BF)
     half = rows // 2
     first = place[1] == 0
     for out, flag in ((keep, first), (send, jnp.logical_not(first))):
-        out[:, 0:features] = jnp.where(flag, regular[0:half], regular[half:]).astype(BF)
+        out[:, 0:features] = jnp.where(flag, values[0:half], values[half:]).astype(BF)
         out[:, features:] = jnp.where(flag, outlier[0:half, 0:64], outlier[half:, 0:64]).astype(BF)
 
 
-def pair_kernel(own, scale, extra, weight, out):
+def diagonal(size):
+    return lax.broadcasted_iota(jnp.int32, (size, size), 0) == lax.broadcasted_iota(
+        jnp.int32, (size, size), 1
+    )
+
+
+def sums_kernel(both, out):
+    features = both.shape[2] - 64
+    rows = both.shape[1]
+    first = jnp.zeros((rows, 1), F32)
+    second = jnp.zeros((rows, 1), F32)
+    for part in range(2):
+        values = both[part, :, 0:features].astype(F32)
+        first = first + jnp.sum(values, axis=1, keepdims=True)
+        second = second + jnp.sum(values * values, axis=1, keepdims=True)
+    unit = diagonal(rows)
+    first = jnp.sum(jnp.where(unit, first, 0.0), axis=0, keepdims=True)
+    second = jnp.sum(jnp.where(unit, second, 0.0), axis=0, keepdims=True)
+    for n in range(16):
+        out[n, 0:1, :] = first
+        out[n, 1:2, :] = second
+
+
+def moments(sums):
+    unit = diagonal(sums.shape[1])
+    average = jnp.sum(jnp.where(unit, sums[0:1, :], 0.0), axis=1, keepdims=True) / D
+    squares = jnp.sum(jnp.where(unit, sums[1:2, :], 0.0), axis=1, keepdims=True) / D
+    return average, lax.rsqrt(squares - average * average + epsilon)
+
+
+def normalize(rows, average, inverse, gain, bias, gain_out, bias_out, features):
+    regular = ((rows[:, 0:features].astype(F32) - average) * inverse * gain + bias).astype(BF)
+    outlier = (rows[:, features : features + OUTL].astype(F32) - average) * inverse * gain_out + bias_out
+    return regular, outlier.astype(BF).astype(F32)
+
+
+def pair_kernel(place, own, mine, other, gain, bias, gain_out, bias_out, scale, extra, weight, out):
+    c = place[1]
+    z = place[2]
+    x = place[3]
     features = weight.shape[0]
-    term = jnp.dot(own[:, 0:features], weight[...], preferred_element_type=F32) * scale[...]
-    value = own[:, features:].astype(F32)
+    half = own.shape[0] // 2
+    first = c == 0
+    mine_at = mine[jnp.where(first, z, x)]
+    other_at = other[jnp.where(first, x, z)]
+    average0, inverse0 = moments(jnp.where(first, mine_at, other_at))
+    average1, inverse1 = moments(jnp.where(first, other_at, mine_at))
+    average = jnp.concatenate([average0[0:half], average1[0:half]], axis=0)
+    inverse = jnp.concatenate([inverse0[0:half], inverse1[0:half]], axis=0)
+    regular, outlier = normalize(
+        own[...], average, inverse, gain[...], bias[...], gain_out[...], bias_out[...], features
+    )
+    term = jnp.dot(regular, weight[...], preferred_element_type=F32) * scale[...]
     for k in range(OUTL):
-        term = term + value[:, k : k + 1] * extra[k : k + 1, :]
+        term = term + outlier[:, k : k + 1] * extra[k : k + 1, :]
     for j in range(2 * N_Y):
         rows = slice(6 * j, 6 * j + 6)
         out[j, 0:6, :] = term[rows, 0:512]
@@ -77,7 +116,8 @@
 
 
 def query_kernel(
-    place, a0, a1, a2, a3, b0, b1, b2, b3, scale, extra, weight, pairs, keep, send, acc
+    place, a0, a1, a2, a3, b0, b1, b2, b3, mine, other, gain, bias, gain_out, bias_out,
+    scale, extra, weight, pairs, keep, send, acc,
 ):
     y = place[0]
     c = place[1]
@@ -85,9 +125,19 @@
     x = place[3]
     features = weight.shape[0]
     for d2, (near, far) in enumerate(((a0, b0), (a1, b1), (a2, b2), (a3, b3))):
-        rows = jnp.concatenate([near[0], far[...]], axis=0)
-        term = jnp.dot(rows[:, 0:features], weight[...], preferred_element_type=F32) * scale[...]
-        value = rows[:, features:].astype(F32)
+        regulars = []
+        outliers = []
+        for side, rows in enumerate((near[0], far[...])):
+            sums = (mine, other)[side][lax.rem(jnp.where((c == 0) == (side == 0), z, x) + 4 - d2, 4)]
+            average, inverse = moments(sums)
+            regular, outlier = normalize(
+                rows, average, inverse, gain[...], bias[...], gain_out[...], bias_out[...], features
+            )
+            regulars.append(regular)
+            outliers.append(outlier)
+        rows = jnp.concatenate(regulars, axis=0)
+        value = jnp.concatenate(outliers, axis=0)
+        term = jnp.dot(rows, weight[...], preferred_element_type=F32) * scale[...]
         for k in range(OUTL):
             term = term + value[:, k : k + 1] * extra[k : k + 1, :]
         for side in range(2):
@@ -304,6 +354,19 @@
                     to = (z + shift) % 4 * 4 + x
                 pairs.append(((z * 4 + x) * 2 * N_Y + j, to * 2 * N_Y + j))
     return pairs
+
+
+def sheets():
+    groups = []
+    for first in (True, False):
+        for fixed in range(4):
+            group = []
+            for moving in range(4):
+                z, x = (moving, fixed) if first else (fixed, moving)
+                for y in range(N_Y):
+                    group.append((z * 4 + x) * 2 * N_Y + 2 * y + (0 if first else 1))
+            groups.append(group)
+    return groups
 
 
 SIBLING = [(j, j ^ 1) for j in range(2 * N_Y)]
@@ -338,17 +401,16 @@
     smem = pl.BlockSpec(memory_space=pltpu.SMEM)
     vmem = pl.BlockSpec(memory_space=pltpu.VMEM)
 
-    widened = activations.astype(F32)
-    sums = jnp.stack([jnp.sum(widened, axis=1), jnp.sum(widened * widened, axis=1)])
-    sums = lax.all_to_all(
-        jnp.broadcast_to(sums[None], (2 * N_Y, 2, block_rows)), "gy", split_axis=0, concat_axis=0, tiled=True
-    )
     picked = jnp.arange(features, dtype=jnp.int32)[:, None] == input_outliers[None, :]
-    regular = jnp.where(jnp.any(picked, axis=1), 0.0, 1.0)[None]
+    is_outlier = jnp.any(picked, axis=1)
+    gain = jnp.where(is_outlier, 0.0, norm_gain)[None]
+    bias = jnp.where(is_outlier, 0.0, norm_bias)[None]
+    gain_out = jnp.sum(jnp.where(picked, norm_gain[:, None], 0.0), axis=0)[None]
+    bias_out = jnp.sum(jnp.where(picked, norm_bias[:, None], 0.0), axis=0)[None]
     padded = features + 64
     own, kept, sent = pl.pallas_call(
-        normalize_kernel,
-        in_specs=[smem] + [vmem] * 6,
+        prepare_kernel,
+        in_specs=[smem] + [vmem] * 2,
         out_specs=[vmem] * 3,
         out_shape=[
             jax.ShapeDtypeStruct((block_rows, padded), BF),
@@ -356,24 +418,37 @@
             jax.ShapeDtypeStruct((block_rows // 2, padded), BF),
         ],
         compiler_params=params(8),
-        name="normalize",
-    )(
-        place, sums, activations, norm_gain[None], norm_bias[None],
-        jnp.pad(picked.astype(BF), ((0, 0), (0, 128 - OUTL))), regular,
-    )
+        name="prepare",
+    )(place, activations, jnp.pad(picked.astype(BF), ((0, 0), (0, 128 - OUTL))))
     plane = ("gx", "gy")
     both = jnp.stack([kept, lax.ppermute(sent, "gy", SIBLING)])
     both = jnp.concatenate(
         [both] + [lax.ppermute(both, plane, shift_plane(True, d)) for d in (1, 3, 2)], axis=1
     )
+    arrived = [both] + [lax.ppermute(both, plane, shift_plane(False, d)) for d in (1, 3, 2)]
+    sums = pl.pallas_call(
+        sums_kernel,
+        out_shape=jax.ShapeDtypeStruct((16, 2, 96), F32),
+        compiler_params=params(8),
+        name="row_sums",
+    )(both)
+    sums = lax.all_to_all(
+        sums, plane, split_axis=0, concat_axis=0, tiled=True, axis_index_groups=sheets()
+    )
+    mine = jnp.sum(sums.reshape(4, N_Y, 2, 96), axis=1)
+    other = lax.ppermute(mine, "gy", SIBLING)
+    *arrived, mine, other = lax.optimization_barrier((*arrived, mine, other))
     pairs = pl.pallas_call(
         pair_kernel,
+        in_specs=[smem] + [vmem] * 10,
+        out_specs=vmem,
         out_shape=jax.ShapeDtypeStruct((2 * N_Y, 16, 512), F32),
         compiler_params=params(16),
         name="pair_projection",
-    )(own, keyvalue_scale[None], keyvalue_float, keyvalue_int)
-    both, pairs = lax.optimization_barrier((both, pairs))
-    arrived = [both] + [lax.ppermute(both, plane, shift_plane(False, d)) for d in (1, 3, 2)]
+    )(
+        place, own, mine, other, gain, bias, gain_out, bias_out,
+        keyvalue_scale[None], keyvalue_float, keyvalue_int,
+    )
     others = [lax.ppermute(block[1], "gy", SIBLING) for block in arrived]
     order = (0, 1, 3, 2)
     arrived = [arrived[n] for n in order]
@@ -382,13 +457,16 @@
     keep, send = pl.pallas_call(
         query_kernel,
         grid=(1,),
-        in_specs=[smem] + [whole((1, 96, padded))] * 4 + [vmem] * 8,
+        in_specs=[smem] + [whole((1, 96, padded))] * 4 + [vmem] * 14,
         out_specs=[vmem] * 2,
         out_shape=[jax.ShapeDtypeStruct((N_Y, 112, columns), BF)] * 2,
         scratch_shapes=[pltpu.VMEM((7, tokens, 128), F32)],
         compiler_params=params(24),
         name="query_projection",
-    )(place, *arrived, *others, query_scale[None], query_float, query_int, pairs)
+    )(
+        place, *arrived, *others, mine, other, gain, bias, gain_out, bias_out,
+        query_scale[None], query_float, query_int, pairs,
+    )
     received = lax.ppermute(send, "gy", SIBLING)
     piece = jax.ShapeDtypeStruct((112, columns), BF)
     mine, to1, to2, to3 = pl.pallas_call(

time: 174 us -> 167 us (0.960)
  blocking collectives: 40 us -> 58.4 us
  waiting for transfers between devices: 42.6 us -> 29.1 us
  starting transfers between devices: 48.1 us -> 43.2 us
  local copies, waits for them, and re-layouts: 10.6 us -> 6.91 us
  Pallas kernels: 27.2 us -> 25.2 us
    all_to_all x0 -> x1, blocking collectives: none -> 18.6 us  [on_device(): lax.all_to_all(sums, plane, split_axis=0, concat_axis=0, tiled=True, axis...]
    ppermute x3, waiting for transfers between devices: 12.3 us -> 0.01 us  [on_device(): lax.ppermute(both, plane, shift_plane(False, d))]
    ppermute x4, starting transfers between devices: 8.98 us -> 1.34 us  [on_device(): others = [lax.ppermute(block[1], 'gy', SIBLING) for block in arrived]]
    all_to_all x1 -> x0, starting transfers between devices: 5.97 us -> none  [on_device(): lax.all_to_all(jnp.broadcast_to(sums[None], (2 * N_Y, 2, block_rows)), 'g...]
    pallas_call x1, Pallas kernels: 9.63 us -> 6.21 us  [on_device(): pl.pallas_call(attend_kernel, in_specs=[smem, vmem, vmem, vmem, vmem, hbm...]
    ppermute x3, waiting for transfers between devices: 2.15 us -> 5.07 us  [on_device(): lax.ppermute(both, plane, shift_plane(True, d))]
    ppermute x1, waiting for transfers between devices: 4.89 us -> 2.41 us  [on_device(): from1 = lax.ppermute(to1, 'gy', over_y(1))]
    ppermute x1, waiting for transfers between devices: 3.15 us -> 5.42 us  [on_device(): from2 = lax.ppermute(to2, 'gy', over_y(2))]
  transfers between devices with their start and end apart: 25 -> 25, of which waited for: 14 -> 10; matrix products, arithmetic and copies ran while one was open for 4% -> 3% of each run, Pallas kernels for 0% -> 1%
where the time goes in v5:
time: 167 us
  blocking collectives  58.4 us (35%)
  starting transfers between devices  43.2 us (26%)
  waiting for transfers between devices  29.1 us (17%)
  Pallas kernels  25.2 us (15%)
  local copies, waits for them, and re-layouts  6.91 us (4%)
  other arithmetic  3.68 us (2%)
    all_to_all x1, blocking collectives, on_device(): lax.all_to_all(partial, 'gx', split_axis=0, concat_axis=0, tiled=True)  39.8 us
    all_to_all x1, blocking collectives, on_device(): lax.all_to_all(sums, plane, split_axis=0, concat_axis=0, tiled=True, axis...  18.6 us
    ppermute x4, starting transfers between devices, on_device(): blocks = blocks + [lax.ppermute(b, 'gy', SIBLING) for b in blocks]  9.98 us
    pallas_call x1, Pallas kernels, on_device(): pl.pallas_call(output_kernel, in_specs=[smem] + [vmem] * 13, out_specs=vm...  7.82 us
    pallas_call x1, Pallas kernels, on_device(): pl.pallas_call(query_kernel, grid=(1,), in_specs=[smem] + [whole((1, 96,...  6.23 us
    pallas_call x1, Pallas kernels, on_device(): pl.pallas_call(attend_kernel, in_specs=[smem, vmem, vmem, vmem, vmem, hbm...  6.21 us
    all_to_all x1, waiting for transfers between devices, on_device(): lax.all_to_all(attended, 'gx', split_axis=0, concat_axis=0, tiled=True)  6.12 us
    all_to_all x1, waiting for transfers between devices, on_device(): lax.all_to_all(summed, 'gx', split_axis=0, concat_axis=0, tiled=True)  5.9 us
  transfers between devices with their start and end apart: 25, of which 10 were waited for; matrix products, arithmetic and copies ran while one was open for 3% of the time, Pallas kernels for 1%

profile of v5, /device:TPU:1, one launch (start us, length us, event | category | flops | bytes accessed | tf_op | source)
XLA Modules:
  0.0 166.7 jit_solution(10002367111424652822)
XLA Ops:
  0.0 1.0 fusion
  1.2 0.9 copy-done.3
  2.2 0.8 prepare.1
  3.0 1.5 collective-permute-start
  4.5 0.9 collective-permute-done
  5.5 1.8 %collective-permute-start.1 = (bf16[2,24,1920]{2,1,0:T(8,128)(2,1)S(1)}, bf16[2,24,1920]{2,1,0:T(8,128)(2,1)S(1)}, u32[]{:S(2)}, u32[]{:S(2)}) collective-permute-start(bf16[2,24,1920]{2,1,0:T(8,128)(2,1)S(1)} %pad_maximum_fusion.1), channel_id=1, source_target_pairs={{0,8},{1,33},{2,10},{3,35},{4,12},{5,37},{6,14},{7,39},{8,16},{9,4... | collective-permute-start | bytes 552968 | tf_op jit(solution)/shard_map/ppermute | solution.py:426
  7.2 2.2 %collective-permute-start.2 = (bf16[2,24,1920]{2,1,0:T(8,128)(2,1)S(1)}, bf16[2,24,1920]{2,1,0:T(8,128)(2,1)S(1)}, u32[]{:S(2)}, u32[]{:S(2)}) collective-permute-start(bf16[2,24,1920]{2,1,0:T(8,128)(2,1)S(1)} %pad_maximum_fusion.1), channel_id=1, source_target_pairs={{0,24},{1,97},{2,26},{3,99},{4,28},{5,101},{6,30},{7,103},{8,0},{9... | collective-permute-start | bytes 552968 | tf_op jit(solution)/shard_map/ppermute | solution.py:426
  9.4 1.2 collective-permute-start.3
  10.7 1.6 collective-permute-done.1
  12.3 3.4 %collective-permute-done.3 = bf16[2,24,1920]{2,1,0:T(8,128)(2,1)S(1)} collective-permute-done((bf16[2,24,1920]{2,1,0:T(8,128)(2,1)S(1)}, bf16[2,24,1920]{2,1,0:T(8,128)(2,1)S(1)}, u32[]{:S(2)}, u32[]{:S(2)}) %collective-permute-start.3) | collective-permute-done | bytes 184352 | tf_op jit(solution)/shard_map/ppermute | solution.py:426
  15.8 1.0 collective-permute-start.4
  16.8 1.8 %collective-permute-start.5 = (bf16[2,96,1920]{2,1,0:T(8,128)(2,1)S(1)}, bf16[2,96,1920]{2,1,0:T(8,128)(2,1)S(1)}, u32[]{:S(2)}, u32[]{:S(2)}) collective-permute-start(bf16[2,96,1920]{2,1,0:T(8,128)(2,1)S(1)} %pad_maximum_fusion.both.a0), channel_id=1, source_target_pairs={{0,96},{1,25},{2,98},{3,27},{4,100},{5,29},{6,102},{7,31},{8,104},... | collective-permute-start | bytes 2211848 | tf_op jit(solution)/shard_map/ppermute | solution.py:428
  18.6 1.2 collective-permute-start.6
  20.1 18.6 %all_to_all.20 = f32[16,2,96]{2,1,0:T(2,128)S(1)} all-to-all(f32[16,2,96]{2,1,0:T(2,128)S(1)} %row_sums.1), channel_id=1, replica_groups={{0,2,4,6,32,34,36,38,64,66,68,70,96,98,100,102},{8,10,12,14,40,42,44,46..., dimensions={0} | all-to-all | bytes 24576 | tf_op jit(solution)/shard_map/all_to_all | solution.py:435
  38.7 0.8 collective-permute-start.7
  39.5 0.8 collective-permute-done.7.other
  42.5 1.5 pair_projection.1.pairs
  44.4 6.2 %query_projection.1 = (bf16[4,112,896]{2,1,0:T(8,128)(2,1)S(1)}, bf16[4,112,896]{2,1,0:T(8,128)(2,1)S(1)}) custom-call(s32[4]{0:T(128)S(1)} %pad_add_fusion.place, bf16[2,96,1920]{2,1,0:T(8,128)(2,1)S(1)} %pad_maximum_fusion.both.a0, bf16[2,96,1920]{2,1,0:T(8,128)(2,1)S(1)} %collective-permute-done.4.a1, bf16[2,96,1920]{2,1,0:T(8,128)(2,1)S(1)} %collective-permute-done.6.a2, ...), custom_call_target="tpu_custom_call" | custom-call | tf_op jit(solution)/shard_map/query_projection/pallas_call | solution.py:457
  50.6 0.6 collective-permute-start.12
  51.2 2.0 %collective-permute-done.12.received = bf16[4,112,896]{2,1,0:T(8,128)(2,1)S(1)} collective-permute-done((bf16[4,112,896]{2,1,0:T(8,128)(2,1)S(1)}, bf16[4,112,896]{2,1,0:T(8,128)(2,1)S(1)}, u32[]{:S(2)}, u32[]{:S(2)}) %collective-permute-start.12) | collective-permute-done | bytes 802848 | tf_op jit(solution)/shard_map/ppermute | solution.py:470
  53.4 1.4 collective-permute-start.13
  54.8 2.6 %collective-permute-start.14 = (bf16[112,896]{1,0:T(8,128)(2,1)S(1)}, bf16[112,896]{1,0:T(8,128)(2,1)S(1)}, u32[]{:S(2)}, u32[]{:S(2)}) collective-permute-start(bf16[112,896]{1,0:T(8,128)(2,1)S(1)} %get-tuple-element.35), channel_id=1, source_target_pairs={{0,4},{1,5},{2,6},{3,7},{4,0},{5,1},{6,2},{7,3},{8,12},{9,13},{10,... | collective-permute-start | bytes 602120 | tf_op jit(solution)/shard_map/ppermute | solution.py:477
  57.4 1.1 collective-permute-start.15
  58.6 2.4 %collective-permute-done.13.b = bf16[112,896]{1,0:T(8,128)(2,1)S(1)} collective-permute-done((bf16[112,896]{1,0:T(8,128)(2,1)S(1)}, bf16[112,896]{1,0:T(8,128)(2,1)S(1)}, u32[]{:S(2)}, u32[]{:S(2)}) %collective-permute-start.13) | collective-permute-done | bytes 200736 | tf_op jit(solution)/shard_map/ppermute | solution.py:475
  61.0 5.4 %collective-permute-done.14.c = bf16[112,896]{1,0:T(8,128)(2,1)S(1)} collective-permute-done((bf16[112,896]{1,0:T(8,128)(2,1)S(1)}, bf16[112,896]{1,0:T(8,128)(2,1)S(1)}, u32[]{:S(2)}, u32[]{:S(2)}) %collective-permute-start.14) | collective-permute-done | bytes 200736 | tf_op jit(solution)/shard_map/ppermute | solution.py:477
  66.5 0.9 collect.1
  67.4 0.6 copy-done.4
  68.0 4.3 %all-to-all-start.1 = ((bf16[16,6,896]{2,1,0:T(8,128)(2,1)}), bf16[16,6,896]{2,1,0:T(8,128)(2,1)S(1)}, u32[]{:S(2)}, u32[]{:S(2)}) async-start(bf16[16,6,896]{2,1,0:T(8,128)(2,1)} %get-tuple-element.37), calls=%async_computation.1 | async-start | bytes 458752 | tf_op jit(solution)/shard_map/all_to_all | solution.py:488
  73.2 0.7 select_maximum_fusion.sine
  73.8 5.9 %all-to-all-done.1.queries = bf16[16,6,896]{2,1,0:T(8,128)(2,1)S(1)} async-done(((bf16[16,6,896]{2,1,0:T(8,128)(2,1)}), bf16[16,6,896]{2,1,0:T(8,128)(2,1)S(1)}, u32[]{:S(2)}, u32[]{:S(2)}) %all-to-all-start.1) | async-done | bytes 172064 | tf_op jit(solution)/shard_map/all_to_all | solution.py:488
  79.7 0.7 copy-done.11
  80.4 6.2 %attention.1 = bf16[16,6,896]{2,1,0:T(8,128)(2,1)} custom-call(s32[3]{0:T(128)} %lengths.1, bf16[16,6,896]{2,1,0:T(8,128)(2,1)} %copy-done.11, f32[16,512]{1,0:T(8,128)} %copy-done.4, f32[8,128]{1,0:T(8,128)} %pad.21.cosine, f32[8,128]{1,0:T(8,128)} %select_maximum_fusion.sine, bf16[3,2048,512]{2,1,0:T(8,128)(2,1)} %keys.1, bf16[3,2048,512]{2,1,0:T(8,128)(2,1)} %values.1), custom_call_target="tpu_custom_call" | custom-call | tf_op jit(solution)/shard_map/attention/pallas_call | solution.py:501
  86.6 4.8 %all-to-all-start.2 = ((bf16[16,6,896]{2,1,0:T(8,128)(2,1)}), bf16[16,6,896]{2,1,0:T(8,128)(2,1)S(1)}, u32[]{:S(2)}, u32[]{:S(2)}) async-start(bf16[16,6,896]{2,1,0:T(8,128)(2,1)} %attention.1), calls=%async_computation.2 | async-start | bytes 458752 | tf_op jit(solution)/shard_map/all_to_all | solution.py:522
  91.4 1.2 dynamic_slice.3
  92.7 6.1 %all-to-all-done.2.block = bf16[16,6,896]{2,1,0:T(8,128)(2,1)S(1)} async-done(((bf16[16,6,896]{2,1,0:T(8,128)(2,1)}), bf16[16,6,896]{2,1,0:T(8,128)(2,1)S(1)}, u32[]{:S(2)}, u32[]{:S(2)}) %all-to-all-start.2) | async-done | bytes 172064 | tf_op jit(solution)/shard_map/all_to_all | solution.py:522
  98.9 1.9 %collective-permute-start.16 = (bf16[96,896]{1,0:T(8,128)(2,1)S(1)}, bf16[96,896]{1,0:T(8,128)(2,1)S(1)}, u32[]{:S(2)}, u32[]{:S(2)}) collective-permute-start(bf16[96,896]{1,0:T(8,128)(2,1)S(1)} %repack.1.b0), channel_id=1, source_target_pairs={{0,2},{1,3},{2,4},{3,5},{4,6},{5,7},{6,0},{7,1},{8,10},{9,11},{10,... | collective-permute-start | bytes 516104 | tf_op jit(solution)/shard_map/ppermute | solution.py:530
  100.7 2.7 %collective-permute-start.17 = (bf16[96,896]{1,0:T(8,128)(2,1)S(1)}, bf16[96,896]{1,0:T(8,128)(2,1)S(1)}, u32[]{:S(2)}, u32[]{:S(2)}) collective-permute-start(bf16[96,896]{1,0:T(8,128)(2,1)S(1)} %repack.1.b0), channel_id=1, source_target_pairs={{0,4},{1,5},{2,6},{3,7},{4,0},{5,1},{6,2},{7,3},{8,12},{9,13},{10,... | collective-permute-start | bytes 516104 | tf_op jit(solution)/shard_map/ppermute | solution.py:530
  103.5 1.1 collective-permute-start.18
  104.5 0.9 fusion.1
  105.4 5.5 %collective-permute-start.19 = (bf16[96,896]{1,0:T(8,128)(2,1)S(1)}, bf16[96,896]{1,0:T(8,128)(2,1)S(1)}, u32[]{:S(2)}, u32[]{:S(2)}) collective-permute-start(bf16[96,896]{1,0:T(8,128)(2,1)S(1)} %repack.1.b0), channel_id=1, source_target_pairs={{0,1},{1,0},{2,3},{3,2},{4,5},{5,4},{6,7},{7,6},{8,9},{9,8},{10,11... | collective-permute-start | bytes 516104 | tf_op jit(solution)/shard_map/ppermute | solution.py:531
  111.0 1.0 collective-permute-start.20
  111.9 3.3 %collective-permute-start.21 = (bf16[96,896]{1,0:T(8,128)(2,1)S(1)}, bf16[96,896]{1,0:T(8,128)(2,1)S(1)}, u32[]{:S(2)}, u32[]{:S(2)}) collective-permute-start(bf16[96,896]{1,0:T(8,128)(2,1)S(1)} %collective-permute-done.17.b2), channel_id=1, source_target_pairs={{0,1},{1,0},{2,3},{3,2},{4,5},{5,4},{6,7},{7,6},{8,9},{9,8},{10,11... | collective-permute-start | bytes 516104 | tf_op jit(solution)/shard_map/ppermute | solution.py:531
  115.4 0.7 broadcast_in_dim.74.scale
  116.6 0.8 copy-done.5
  117.4 0.7 copy-done.9
  118.1 7.8 %output_projection.1 = bf16[16,48,1856]{2,1,0:T(8,128)(2,1)S(1)} custom-call(s32[4]{0:T(128)S(1)} %copy-done.9, bf16[96,896]{1,0:T(8,128)(2,1)S(1)} %repack.1.b0, bf16[96,896]{1,0:T(8,128)(2,1)S(1)} %collective-permute-done.16.b1, bf16[96,896]{1,0:T(8,128)(2,1)S(1)} %collective-permute-done.17.b2, bf16[96,896]{1,0:T(8,128)(2,1)S(1)} %collective-permute-done.18.b3, ...), custom_call_target="tpu_custom_call" | custom-call | tf_op jit(solution)/shard_map/output_projection/pallas_call | solution.py:537
  125.9 39.8 %all_to_all.21.parts = bf16[16,48,1856]{2,1,0:T(8,128)(2,1)S(1)} all-to-all(bf16[16,48,1856]{2,1,0:T(8,128)(2,1)S(1)} %output_projection.1), channel_id=1, replica_groups=mesh['gx'=16,'gy'=8] {'gx'}, dimensions={0} | all-to-all | bytes 5701632 | tf_op jit(solution)/shard_map/all_to_all | solution.py:546
  165.7 1.1 total.1
  (77 shorter events, 5.0 us)
Async XLA Ops:
  1.2 0.9 copy-start.3
  2.2 41.8 %copy-start.8 = (s32[4]{0:T(128)}, s32[4]{0:T(128)S(1)}, u32[]{:S(2)}) copy-start(s32[4]{0:T(128)S(1)} %pad_add_fusion.place) | copy-start | bytes 52
  3.0 2.4 %collective-permute-start = (bf16[24,1920]{1,0:T(8,128)(2,1)S(1)}, bf16[24,1920]{1,0:T(8,128)(2,1)S(1)}, u32[]{:S(2)}, u32[]{:S(2)}) collective-permute-start(bf16[24,1920]{1,0:T(8,128)(2,1)S(1)} %get-tuple-element.23), channel_id=1, source_target_pairs={{0,1},{1,0},{2,3},{3,2},{4,5},{5,4},{6,7},{7,6},{8,9},{9,8},{10,11... | collective-permute-start | bytes 276488 | tf_op jit(solution)/shard_map/ppermute | solution.py:424
  5.5 6.8 %collective-permute-start.1 = (bf16[2,24,1920]{2,1,0:T(8,128)(2,1)S(1)}, bf16[2,24,1920]{2,1,0:T(8,128)(2,1)S(1)}, u32[]{:S(2)}, u32[]{:S(2)}) collective-permute-start(bf16[2,24,1920]{2,1,0:T(8,128)(2,1)S(1)} %pad_maximum_fusion.1), channel_id=1, source_target_pairs={{0,8},{1,33},{2,10},{3,35},{4,12},{5,37},{6,14},{7,39},{8,16},{9,4... | collective-permute-start | bytes 552968 | tf_op jit(solution)/shard_map/ppermute | solution.py:426
  7.2 5.1 %collective-permute-start.2 = (bf16[2,24,1920]{2,1,0:T(8,128)(2,1)S(1)}, bf16[2,24,1920]{2,1,0:T(8,128)(2,1)S(1)}, u32[]{:S(2)}, u32[]{:S(2)}) collective-permute-start(bf16[2,24,1920]{2,1,0:T(8,128)(2,1)S(1)} %pad_maximum_fusion.1), channel_id=1, source_target_pairs={{0,24},{1,97},{2,26},{3,99},{4,28},{5,101},{6,30},{7,103},{8,0},{9... | collective-permute-start | bytes 552968 | tf_op jit(solution)/shard_map/ppermute | solution.py:426
  9.4 6.3 %collective-permute-start.3 = (bf16[2,24,1920]{2,1,0:T(8,128)(2,1)S(1)}, bf16[2,24,1920]{2,1,0:T(8,128)(2,1)S(1)}, u32[]{:S(2)}, u32[]{:S(2)}) collective-permute-start(bf16[2,24,1920]{2,1,0:T(8,128)(2,1)S(1)} %pad_maximum_fusion.1), channel_id=1, source_target_pairs={{0,16},{1,65},{2,18},{3,67},{4,20},{5,69},{6,22},{7,71},{8,24},{9,... | collective-permute-start | bytes 552968 | tf_op jit(solution)/shard_map/ppermute | solution.py:426
  15.8 24.5 %collective-permute-start.4 = (bf16[2,96,1920]{2,1,0:T(8,128)(2,1)S(1)}, bf16[2,96,1920]{2,1,0:T(8,128)(2,1)S(1)}, u32[]{:S(2)}, u32[]{:S(2)}) collective-permute-start(bf16[2,96,1920]{2,1,0:T(8,128)(2,1)S(1)} %pad_maximum_fusion.both.a0), channel_id=1, source_target_pairs={{0,32},{1,9},{2,34},{3,11},{4,36},{5,13},{6,38},{7,15},{8,40},{9,1... | collective-permute-start | bytes 2211848 | tf_op jit(solution)/shard_map/ppermute | solution.py:428
  16.8 23.5 %collective-permute-start.5 = (bf16[2,96,1920]{2,1,0:T(8,128)(2,1)S(1)}, bf16[2,96,1920]{2,1,0:T(8,128)(2,1)S(1)}, u32[]{:S(2)}, u32[]{:S(2)}) collective-permute-start(bf16[2,96,1920]{2,1,0:T(8,128)(2,1)S(1)} %pad_maximum_fusion.both.a0), channel_id=1, source_target_pairs={{0,96},{1,25},{2,98},{3,27},{4,100},{5,29},{6,102},{7,31},{8,104},... | collective-permute-start | bytes 2211848 | tf_op jit(solution)/shard_map/ppermute | solution.py:428
  18.6 23.2 %copy-start.12 = (f32[1856]{0:T(1024)S(1)}, f32[1856]{0:T(1024)}, u32[]{:S(2)}) copy-start(f32[1856]{0:T(1024)} %param.19) | copy-start | bytes 22276
  18.6 23.2 %copy-start.13 = (f32[1856]{0:T(1024)S(1)}, f32[1856]{0:T(1024)}, u32[]{:S(2)}) copy-start(f32[1856]{0:T(1024)} %param.18) | copy-start | bytes 22276
  18.6 21.7 %collective-permute-start.6 = (bf16[2,96,1920]{2,1,0:T(8,128)(2,1)S(1)}, bf16[2,96,1920]{2,1,0:T(8,128)(2,1)S(1)}, u32[]{:S(2)}, u32[]{:S(2)}) collective-permute-start(bf16[2,96,1920]{2,1,0:T(8,128)(2,1)S(1)} %pad_maximum_fusion.both.a0), channel_id=1, source_target_pairs={{0,64},{1,17},{2,66},{3,19},{4,68},{5,21},{6,70},{7,23},{8,72},{9,... | collective-permute-start | bytes 2211848 | tf_op jit(solution)/shard_map/ppermute | solution.py:428
  19.8 22.6 %copy-start = (bf16[1856,1024]{1,0:T(8,128)(2,1)S(1)}, bf16[1856,1024]{1,0:T(8,128)(2,1)}, u32[]{:S(2)}) copy-start(bf16[1856,1024]{1,0:T(8,128)(2,1)} %weight.2) | copy-start | bytes 11403268
  38.7 3.1 %copy-start.14 = (f32[896]{0:T(1024)S(1)}, f32[896]{0:T(1024)}, u32[]{:S(2)}) copy-start(f32[896]{0:T(1024)} %param.22) | copy-start | bytes 10756
  38.7 3.2 %copy-start.15 = (s32[4]{0:T(128)S(1)}, s32[4]{0:T(128)}, u32[]{:S(2)}) copy-start(s32[4]{0:T(128)} %param.20) | copy-start | bytes 52
  38.7 3.7 %copy-start.6 = (f32[4,1024]{1,0:T(4,128)S(1)}, f32[4,1024]{1,0:T(4,128)}, u32[]{:S(2)}) copy-start(f32[4,1024]{1,0:T(4,128)} %extra.3) | copy-start | bytes 49156
  38.7 3.7 %copy-start.10 = (f32[1024]{0:T(1024)S(1)}, f32[1024]{0:T(1024)}, u32[]{:S(2)}) copy-start(f32[1024]{0:T(1024)} %param.24) | copy-start | bytes 12292
  38.7 1.6 collective-permute-start.7
  40.3 3.6 %collective-permute-start.10 = (bf16[96,1920]{1,0:T(8,128)(2,1)S(1)}, bf16[96,1920]{1,0:T(8,128)(2,1)S(1)}, u32[]{:S(2)}, u32[]{:S(2)}) collective-permute-start(bf16[96,1920]{1,0:T(8,128)(2,1)S(1)} %slice_bitcast_fusion.1), channel_id=1, source_target_pairs={{0,1},{1,0},{2,3},{3,2},{4,5},{5,4},{6,7},{7,6},{8,9},{9,8},{10,11... | collective-permute-start | bytes 1105928 | tf_op jit(solution)/shard_map/ppermute | solution.py:452
  40.8 3.2 %collective-permute-start.11 = (bf16[96,1920]{1,0:T(8,128)(2,1)S(1)}, bf16[96,1920]{1,0:T(8,128)(2,1)S(1)}, u32[]{:S(2)}, u32[]{:S(2)}) collective-permute-start(bf16[96,1920]{1,0:T(8,128)(2,1)S(1)} %slice_bitcast_fusion), channel_id=1, source_target_pairs={{0,1},{1,0},{2,3},{3,2},{4,5},{5,4},{6,7},{7,6},{8,9},{9,8},{10,11... | collective-permute-start | bytes 1105928 | tf_op jit(solution)/shard_map/ppermute | solution.py:452
  41.1 2.9 %collective-permute-start.8 = (bf16[96,1920]{1,0:T(8,128)(2,1)S(1)}, bf16[96,1920]{1,0:T(8,128)(2,1)S(1)}, u32[]{:S(2)}, u32[]{:S(2)}) collective-permute-start(bf16[96,1920]{1,0:T(8,128)(2,1)S(1)} %slice_bitcast_fusion.3), channel_id=1, source_target_pairs={{0,1},{1,0},{2,3},{3,2},{4,5},{5,4},{6,7},{7,6},{8,9},{9,8},{10,11... | collective-permute-start | bytes 1105928 | tf_op jit(solution)/shard_map/ppermute | solution.py:452
  41.5 2.5 %collective-permute-start.9 = (bf16[96,1920]{1,0:T(8,128)(2,1)S(1)}, bf16[96,1920]{1,0:T(8,128)(2,1)S(1)}, u32[]{:S(2)}, u32[]{:S(2)}) collective-permute-start(bf16[96,1920]{1,0:T(8,128)(2,1)S(1)} %slice_bitcast_fusion.2), channel_id=1, source_target_pairs={{0,1},{1,0},{2,3},{3,2},{4,5},{5,4},{6,7},{7,6},{8,9},{9,8},{10,11... | collective-permute-start | bytes 1105928 | tf_op jit(solution)/shard_map/ppermute | solution.py:452
  42.4 1.9 %copy-start.2 = (bf16[1856,896]{1,0:T(8,128)(2,1)S(1)}, bf16[1856,896]{1,0:T(8,128)(2,1)}, u32[]{:S(2)}) copy-start(bf16[1856,896]{1,0:T(8,128)(2,1)} %weight.3) | copy-start | bytes 9977860
  42.4 1.9 %copy-start.7 = (f32[4,896]{1,0:T(4,128)S(1)}, f32[4,896]{1,0:T(4,128)}, u32[]{:S(2)}) copy-start(f32[4,896]{1,0:T(4,128)} %extra.4) | copy-start | bytes 43012
  50.6 7.8 %copy-start.16 = (s32[3]{0:T(128)S(1)}, s32[3]{0:T(128)}, u32[]{:S(2)}) copy-start(s32[3]{0:T(128)} %lengths.1) | copy-start | bytes 40
  50.6 2.6 %collective-permute-start.12 = (bf16[4,112,896]{2,1,0:T(8,128)(2,1)S(1)}, bf16[4,112,896]{2,1,0:T(8,128)(2,1)S(1)}, u32[]{:S(2)}, u32[]{:S(2)}) collective-permute-start(bf16[4,112,896]{2,1,0:T(8,128)(2,1)S(1)} %get-tuple-element.32), channel_id=1, source_target_pairs={{0,1},{1,0},{2,3},{3,2},{4,5},{5,4},{6,7},{7,6},{8,9},{9,8},{10,11... | collective-permute-start | bytes 2408456 | tf_op jit(solution)/shard_map/ppermute | solution.py:470
  53.4 7.6 %collective-permute-start.13 = (bf16[112,896]{1,0:T(8,128)(2,1)S(1)}, bf16[112,896]{1,0:T(8,128)(2,1)S(1)}, u32[]{:S(2)}, u32[]{:S(2)}) collective-permute-start(bf16[112,896]{1,0:T(8,128)(2,1)S(1)} %get-tuple-element.34), channel_id=1, source_target_pairs={{0,2},{1,3},{2,4},{3,5},{4,6},{5,7},{6,0},{7,1},{8,10},{9,11},{10,... | collective-permute-start | bytes 602120 | tf_op jit(solution)/shard_map/ppermute | solution.py:475
  54.8 11.7 %collective-permute-start.14 = (bf16[112,896]{1,0:T(8,128)(2,1)S(1)}, bf16[112,896]{1,0:T(8,128)(2,1)S(1)}, u32[]{:S(2)}, u32[]{:S(2)}) collective-permute-start(bf16[112,896]{1,0:T(8,128)(2,1)S(1)} %get-tuple-element.35), channel_id=1, source_target_pairs={{0,4},{1,5},{2,6},{3,7},{4,0},{5,1},{6,2},{7,3},{8,12},{9,13},{10,... | collective-permute-start | bytes 602120 | tf_op jit(solution)/shard_map/ppermute | solution.py:477
  57.4 9.1 %collective-permute-start.15 = (bf16[112,896]{1,0:T(8,128)(2,1)S(1)}, bf16[112,896]{1,0:T(8,128)(2,1)S(1)}, u32[]{:S(2)}, u32[]{:S(2)}) collective-permute-start(bf16[112,896]{1,0:T(8,128)(2,1)S(1)} %get-tuple-element.36), channel_id=1, source_target_pairs={{0,6},{1,7},{2,0},{3,1},{4,2},{5,3},{6,4},{7,5},{8,14},{9,15},{10,... | collective-permute-start | bytes 602120 | tf_op jit(solution)/shard_map/ppermute | solution.py:476
  67.4 0.6 copy-start.4
  68.0 11.7 %all-to-all-start.1 = ((bf16[16,6,896]{2,1,0:T(8,128)(2,1)}), bf16[16,6,896]{2,1,0:T(8,128)(2,1)S(1)}, u32[]{:S(2)}, u32[]{:S(2)}) async-start(bf16[16,6,896]{2,1,0:T(8,128)(2,1)} %get-tuple-element.37), calls=%async_computation.1 | async-start | bytes 458752 | tf_op jit(solution)/shard_map/all_to_all | solution.py:488
  79.7 0.7 copy-start.11
  80.4 36.2 %copy-start.1 = (bf16[896,1856]{0,1:T(8,128)(2,1)S(1)}, bf16[896,1856]{0,1:T(8,128)(2,1)}, u32[]{:S(2)}) copy-start(bf16[896,1856]{0,1:T(8,128)(2,1)} %param.31) | copy-start | bytes 9977860
  86.6 12.1 %all-to-all-start.2 = ((bf16[16,6,896]{2,1,0:T(8,128)(2,1)}), bf16[16,6,896]{2,1,0:T(8,128)(2,1)S(1)}, u32[]{:S(2)}, u32[]{:S(2)}) async-start(bf16[16,6,896]{2,1,0:T(8,128)(2,1)} %attention.1), calls=%async_computation.2 | async-start | bytes 458752 | tf_op jit(solution)/shard_map/all_to_all | solution.py:522
  98.9 12.1 %collective-permute-start.16 = (bf16[96,896]{1,0:T(8,128)(2,1)S(1)}, bf16[96,896]{1,0:T(8,128)(2,1)S(1)}, u32[]{:S(2)}, u32[]{:S(2)}) collective-permute-start(bf16[96,896]{1,0:T(8,128)(2,1)S(1)} %repack.1.b0), channel_id=1, source_target_pairs={{0,2},{1,3},{2,4},{3,5},{4,6},{5,7},{6,0},{7,1},{8,10},{9,11},{10,... | collective-permute-start | bytes 516104 | tf_op jit(solution)/shard_map/ppermute | solution.py:530
  100.7 11.2 %collective-permute-start.17 = (bf16[96,896]{1,0:T(8,128)(2,1)S(1)}, bf16[96,896]{1,0:T(8,128)(2,1)S(1)}, u32[]{:S(2)}, u32[]{:S(2)}) collective-permute-start(bf16[96,896]{1,0:T(8,128)(2,1)S(1)} %repack.1.b0), channel_id=1, source_target_pairs={{0,4},{1,5},{2,6},{3,7},{4,0},{5,1},{6,2},{7,3},{8,12},{9,13},{10,... | collective-permute-start | bytes 516104 | tf_op jit(solution)/shard_map/ppermute | solution.py:530
  103.5 11.8 %collective-permute-start.18 = (bf16[96,896]{1,0:T(8,128)(2,1)S(1)}, bf16[96,896]{1,0:T(8,128)(2,1)S(1)}, u32[]{:S(2)}, u32[]{:S(2)}) collective-permute-start(bf16[96,896]{1,0:T(8,128)(2,1)S(1)} %repack.1.b0), channel_id=1, source_target_pairs={{0,6},{1,7},{2,0},{3,1},{4,2},{5,3},{6,4},{7,5},{8,14},{9,15},{10,... | collective-permute-start | bytes 516104 | tf_op jit(solution)/shard_map/ppermute | solution.py:530
  105.4 10.8 %collective-permute-start.19 = (bf16[96,896]{1,0:T(8,128)(2,1)S(1)}, bf16[96,896]{1,0:T(8,128)(2,1)S(1)}, u32[]{:S(2)}, u32[]{:S(2)}) collective-permute-start(bf16[96,896]{1,0:T(8,128)(2,1)S(1)} %repack.1.b0), channel_id=1, source_target_pairs={{0,1},{1,0},{2,3},{3,2},{4,5},{5,4},{6,7},{7,6},{8,9},{9,8},{10,11... | collective-permute-start | bytes 516104 | tf_op jit(solution)/shard_map/ppermute | solution.py:531
  111.0 5.3 %collective-permute-start.20 = (bf16[96,896]{1,0:T(8,128)(2,1)S(1)}, bf16[96,896]{1,0:T(8,128)(2,1)S(1)}, u32[]{:S(2)}, u32[]{:S(2)}) collective-permute-start(bf16[96,896]{1,0:T(8,128)(2,1)S(1)} %collective-permute-done.16.b1), channel_id=1, source_target_pairs={{0,1},{1,0},{2,3},{3,2},{4,5},{5,4},{6,7},{7,6},{8,9},{9,8},{10,11... | collective-permute-start | bytes 516104 | tf_op jit(solution)/shard_map/ppermute | solution.py:531
  111.9 4.3 %collective-permute-start.21 = (bf16[96,896]{1,0:T(8,128)(2,1)S(1)}, bf16[96,896]{1,0:T(8,128)(2,1)S(1)}, u32[]{:S(2)}, u32[]{:S(2)}) collective-permute-start(bf16[96,896]{1,0:T(8,128)(2,1)S(1)} %collective-permute-done.17.b2), channel_id=1, source_target_pairs={{0,1},{1,0},{2,3},{3,2},{4,5},{5,4},{6,7},{7,6},{8,9},{9,8},{10,11... | collective-permute-start | bytes 516104 | tf_op jit(solution)/shard_map/ppermute | solution.py:531
  115.2 1.4 collective-permute-start.22
  116.6 0.8 copy-start.5
  117.4 0.7 copy-start.9

commit v6 on v5

--- a/solution.py
+++ b/solution.py
@@ -40,14 +40,26 @@
     return pl.BlockSpec(shape, lambda *_: (0,) * len(shape))
 
 
-def prepare_kernel(place, x, picked, own, keep, send):
-    outlier = jnp.dot(x[...], picked[...], preferred_element_type=F32)
+def here():
+    i = lax.axis_index("gx")
+    j = lax.axis_index("gy")
+    return lax.div(j, 2), lax.rem(j, 2), lax.div(i, 4), lax.rem(i, 4)
+
+
+def prepare_kernel(positions, x, own, keep, send):
+    rows, features = x.shape
+    place = lax.broadcasted_iota(jnp.int32, (features, 128), 0)
+    column = lax.broadcasted_iota(jnp.int32, (features, 128), 1)
+    picked = (place == positions[0]) & (column == 0)
+    for k in range(1, OUTL):
+        picked = picked | ((place == positions[k]) & (column == k))
+    picked = picked.astype(F32).astype(BF)
+    outlier = jnp.dot(x[...], picked, preferred_element_type=F32)
     values = x[...].astype(F32)
-    rows, features = x.shape
     own[:, 0:features] = x[...]
     own[:, features:] = outlier[:, 0:64].astype(BF)
     half = rows // 2
-    first = place[1] == 0
+    first = here()[1] == 0
     for out, flag in ((keep, first), (send, jnp.logical_not(first))):
         out[:, 0:features] = jnp.where(flag, values[0:half], values[half:]).astype(BF)
         out[:, features:] = jnp.where(flag, outlier[0:half, 0:64], outlier[half:, 0:64]).astype(BF)
@@ -89,10 +101,8 @@
     return regular, outlier.astype(BF).astype(F32)
 
 
-def pair_kernel(place, own, mine, other, gain, bias, gain_out, bias_out, scale, extra, weight, out):
-    c = place[1]
-    z = place[2]
-    x = place[3]
+def pair_kernel(own, mine, other, gain, bias, gain_out, bias_out, scale, extra, weight, out):
+    _, c, z, x = here()
     features = weight.shape[0]
     half = own.shape[0] // 2
     first = c == 0
@@ -116,13 +126,10 @@
 
 
 def query_kernel(
-    place, a0, a1, a2, a3, b0, b1, b2, b3, mine, other, gain, bias, gain_out, bias_out,
+    a0, a1, a2, a3, b0, b1, b2, b3, mine, other, gain, bias, gain_out, bias_out,
     scale, extra, weight, pairs, keep, send, acc,
 ):
-    y = place[0]
-    c = place[1]
-    z = place[2]
-    x = place[3]
+    y, c, z, x = here()
     features = weight.shape[0]
     for d2, (near, far) in enumerate(((a0, b0), (a1, b1), (a2, b2), (a3, b3))):
         regulars = []
@@ -306,9 +313,8 @@
             out[16 * k : 16 * k + 16, lanes] = staged[n, pl.ds(k, 16, stride=8), :].astype(BF)
 
 
-def output_kernel(place, b0, b1, b2, b3, s0, s1, s2, s3, chosen, plain, scale, extra, weight, out, left, acc):
-    y = place[0]
-    c = place[1]
+def output_kernel(b0, b1, b2, b3, s0, s1, s2, s3, chosen, plain, scale, extra, weight, out, left, acc):
+    y, c, _, _ = here()
     for blocks, core in (((b0, b1, b2, b3), c), ((s0, s1, s2, s3), 1 - c)):
         for d, block in enumerate(blocks):
             j = 2 * lax.rem(y + N_Y - d, N_Y) + core
@@ -396,8 +402,6 @@
     columns = query_int.shape[1]
     out_columns = output_int.shape[1]
     me_x = lax.axis_index("gx")
-    me_y = lax.axis_index("gy")
-    place = jnp.stack([me_y // 2, me_y % 2, me_x // 4, me_x % 4]).astype(jnp.int32)
     smem = pl.BlockSpec(memory_space=pltpu.SMEM)
     vmem = pl.BlockSpec(memory_space=pltpu.VMEM)
 
@@ -410,7 +414,7 @@
     padded = features + 64
     own, kept, sent = pl.pallas_call(
         prepare_kernel,
-        in_specs=[smem] + [vmem] * 2,
+        in_specs=[smem, vmem],
         out_specs=[vmem] * 3,
         out_shape=[
             jax.ShapeDtypeStruct((block_rows, padded), BF),
@@ -419,7 +423,7 @@
         ],
         compiler_params=params(8),
         name="prepare",
-    )(place, activations, jnp.pad(picked.astype(BF), ((0, 0), (0, 128 - OUTL))))
+    )(input_outliers, activations)
     plane = ("gx", "gy")
     both = jnp.stack([kept, lax.ppermute(sent, "gy", SIBLING)])
     both = jnp.concatenate(
@@ -440,13 +444,13 @@
     *arrived, mine, other = lax.optimization_barrier((*arrived, mine, other))
     pairs = pl.pallas_call(
         pair_kernel,
-        in_specs=[smem] + [vmem] * 10,
+        in_specs=[vmem] * 10,
         out_specs=vmem,
         out_shape=jax.ShapeDtypeStruct((2 * N_Y, 16, 512), F32),
         compiler_params=params(16),
         name="pair_projection",
     )(
-        place, own, mine, other, gain, bias, gain_out, bias_out,
+        own, mine, other, gain, bias, gain_out, bias_out,
         keyvalue_scale[None], keyvalue_float, keyvalue_int,
     )
     others = [lax.ppermute(block[1], "gy", SIBLING) for block in arrived]
@@ -457,14 +461,14 @@
     keep, send = pl.pallas_call(
         query_kernel,
         grid=(1,),
-        in_specs=[smem] + [whole((1, 96, padded))] * 4 + [vmem] * 14,
+        in_specs=[whole((1, 96, padded))] * 4 + [vmem] * 14,
         out_specs=[vmem] * 2,
         out_shape=[jax.ShapeDtypeStruct((N_Y, 112, columns), BF)] * 2,
         scratch_shapes=[pltpu.VMEM((7, tokens, 128), F32)],
         compiler_params=params(24),
         name="query_projection",
     )(
-        place, *arrived, *others, mine, other, gain, bias, gain_out, bias_out,
+        *arrived, *others, mine, other, gain, bias, gain_out, bias_out,
         query_scale[None], query_float, query_int, pairs,
     )
     received = lax.ppermute(send, "gy", SIBLING)
@@ -536,13 +540,13 @@
     chosen = jnp.pad(chosen.astype(BF), ((0, 0), (0, 128 - OUTL)))
     partial = pl.pallas_call(
         output_kernel,
-        in_specs=[smem] + [vmem] * 13,
+        in_specs=[vmem] * 13,
         out_specs=vmem,
         out_shape=jax.ShapeDtypeStruct((16, block_rows, out_columns), BF),
         scratch_shapes=[pltpu.VMEM((tokens, columns), BF), pltpu.VMEM((15, tokens, 128), F32)],
         compiler_params=params(28),
         name="output_projection",
-    )(place, *blocks, chosen, plain, output_scale[None], output_float, output_int.T)
+    )(*blocks, chosen, plain, output_scale[None], output_float, output_int.T)
     parts = lax.all_to_all(partial, "gx", split_axis=0, concat_axis=0, tiled=True)
     return pl.pallas_call(
         total_kernel,

time: 167 us -> 165 us (0.988)
    unnamed x34 -> x32, local copies, waits for them, and re-layouts: 4.05 us -> 4.12 us
  transfers between devices with their start and end apart: 25 -> 25, of which waited for: 10 -> 11; matrix products, arithmetic and copies ran while one was open for 3% -> 3% of each run, Pallas kernels for 1% -> 1%
where the time goes in v6:
time: 165 us; the launch traced here: 164 us
  blocking collectives  58.3 us (35%)
  starting transfers between devices  42.6 us (26%)
  waiting for transfers between devices  29.4 us (18%)
  Pallas kernels  24.5 us (15%)
  local copies, waits for them, and re-layouts  6.97 us (4%)
  other arithmetic  2.2 us (1%)
    all_to_all x1, blocking collectives, on_device(): lax.all_to_all(partial, 'gx', split_axis=0, concat_axis=0, tiled=True)  39.7 us
    all_to_all x1, blocking collectives, on_device(): lax.all_to_all(sums, plane, split_axis=0, concat_axis=0, tiled=True, axis...  18.6 us
    ppermute x4, starting transfers between devices, on_device(): blocks = blocks + [lax.ppermute(b, 'gy', SIBLING) for b in blocks]  9.4 us
    pallas_call x1, Pallas kernels, on_device(): pl.pallas_call(output_kernel, in_specs=[vmem] * 13, out_specs=vmem, out_s...  7.29 us
    pallas_call x1, Pallas kernels, on_device(): pl.pallas_call(attend_kernel, in_specs=[smem, vmem, vmem, vmem, vmem, hbm...  6.22 us
    all_to_all x1, waiting for transfers between devices, on_device(): lax.all_to_all(attended, 'gx', split_axis=0, concat_axis=0, tiled=True)  6.12 us
    all_to_all x1, waiting for transfers between devices, on_device(): lax.all_to_all(summed, 'gx', split_axis=0, concat_axis=0, tiled=True)  5.9 us
    pallas_call x1, Pallas kernels, on_device(): pl.pallas_call(query_kernel, grid=(1,), in_specs=[whole((1, 96, padded))]...  5.64 us
  transfers between devices with their start and end apart: 25, of which 11 were waited for; matrix products, arithmetic and copies ran while one was open for 3% of the time, Pallas kernels for 1%

profile of v6, /device:TPU:1, one launch (start us, length us, event | category | flops | bytes accessed | tf_op | source)
XLA Modules:
  0.0 164.3 jit_solution(11850260272371274093)
XLA Ops:
  0.0 0.9 copy-done.3
  0.9 0.7 copy-done.8
  1.6 1.8 %prepare.1 = (bf16[48,1920]{1,0:T(8,128)(2,1)S(1)}, bf16[24,1920]{1,0:T(8,128)(2,1)S(1)}, bf16[24,1920]{1,0:T(8,128)(2,1)S(1)}) custom-call(s32[4]{0:T(128)S(1)} %copy-done.8, bf16[48,1856]{1,0:T(8,128)(2,1)S(1)} %copy-done.3), custom_call_target="tpu_custom_call" | custom-call | tf_op jit(solution)/shard_map/prepare/pallas_call | solution.py:415
  3.4 1.5 collective-permute-start
  4.9 0.9 collective-permute-done
  5.9 1.8 %collective-permute-start.1 = (bf16[2,24,1920]{2,1,0:T(8,128)(2,1)S(1)}, bf16[2,24,1920]{2,1,0:T(8,128)(2,1)S(1)}, u32[]{:S(2)}, u32[]{:S(2)}) collective-permute-start(bf16[2,24,1920]{2,1,0:T(8,128)(2,1)S(1)} %pad_maximum_fusion.1), channel_id=1, source_target_pairs={{0,8},{1,33},{2,10},{3,35},{4,12},{5,37},{6,14},{7,39},{8,16},{9,4... | collective-permute-start | bytes 552968 | tf_op jit(solution)/shard_map/ppermute | solution.py:430
  7.7 2.2 %collective-permute-start.2 = (bf16[2,24,1920]{2,1,0:T(8,128)(2,1)S(1)}, bf16[2,24,1920]{2,1,0:T(8,128)(2,1)S(1)}, u32[]{:S(2)}, u32[]{:S(2)}) collective-permute-start(bf16[2,24,1920]{2,1,0:T(8,128)(2,1)S(1)} %pad_maximum_fusion.1), channel_id=1, source_target_pairs={{0,24},{1,97},{2,26},{3,99},{4,28},{5,101},{6,30},{7,103},{8,0},{9... | collective-permute-start | bytes 552968 | tf_op jit(solution)/shard_map/ppermute | solution.py:430
  9.9 1.2 collective-permute-start.3
  11.1 1.6 collective-permute-done.1
  12.7 3.4 %collective-permute-done.3 = bf16[2,24,1920]{2,1,0:T(8,128)(2,1)S(1)} collective-permute-done((bf16[2,24,1920]{2,1,0:T(8,128)(2,1)S(1)}, bf16[2,24,1920]{2,1,0:T(8,128)(2,1)S(1)}, u32[]{:S(2)}, u32[]{:S(2)}) %collective-permute-start.3) | collective-permute-done | bytes 184352 | tf_op jit(solution)/shard_map/ppermute | solution.py:430
  16.2 1.0 collective-permute-start.4
  17.2 1.8 %collective-permute-start.5 = (bf16[2,96,1920]{2,1,0:T(8,128)(2,1)S(1)}, bf16[2,96,1920]{2,1,0:T(8,128)(2,1)S(1)}, u32[]{:S(2)}, u32[]{:S(2)}) collective-permute-start(bf16[2,96,1920]{2,1,0:T(8,128)(2,1)S(1)} %pad_maximum_fusion.both.a0), channel_id=1, source_target_pairs={{0,96},{1,25},{2,98},{3,27},{4,100},{5,29},{6,102},{7,31},{8,104},... | collective-permute-start | bytes 2211848 | tf_op jit(solution)/shard_map/ppermute | solution.py:432
  19.0 1.2 collective-permute-start.6
  20.5 18.6 %all_to_all.20 = f32[16,2,96]{2,1,0:T(2,128)S(1)} all-to-all(f32[16,2,96]{2,1,0:T(2,128)S(1)} %row_sums.1), channel_id=1, replica_groups={{0,2,4,6,32,34,36,38,64,66,68,70,96,98,100,102},{8,10,12,14,40,42,44,46..., dimensions={0} | all-to-all | bytes 24576 | tf_op jit(solution)/shard_map/all_to_all | solution.py:439
  39.1 0.8 collective-permute-start.7
  39.9 0.8 collective-permute-done.7.other
  42.6 1.0 pair_projection.1.pairs
  44.5 5.6 %query_projection.1 = (bf16[4,112,896]{2,1,0:T(8,128)(2,1)S(1)}, bf16[4,112,896]{2,1,0:T(8,128)(2,1)S(1)}) custom-call(bf16[2,96,1920]{2,1,0:T(8,128)(2,1)S(1)} %pad_maximum_fusion.both.a0, bf16[2,96,1920]{2,1,0:T(8,128)(2,1)S(1)} %collective-permute-done.4.a1, bf16[2,96,1920]{2,1,0:T(8,128)(2,1)S(1)} %collective-permute-done.6.a2, ...), custom_call_target="tpu_custom_call" | custom-call | tf_op jit(solution)/shard_map/query_projection/pallas_call | solution.py:461
  50.2 0.6 collective-permute-start.12
  50.8 2.0 %collective-permute-done.12.received = bf16[4,112,896]{2,1,0:T(8,128)(2,1)S(1)} collective-permute-done((bf16[4,112,896]{2,1,0:T(8,128)(2,1)S(1)}, bf16[4,112,896]{2,1,0:T(8,128)(2,1)S(1)}, u32[]{:S(2)}, u32[]{:S(2)}) %collective-permute-start.12) | collective-permute-done | bytes 802848 | tf_op jit(solution)/shard_map/ppermute | solution.py:474
  53.0 1.4 collective-permute-start.13
  54.3 2.6 %collective-permute-start.14 = (bf16[112,896]{1,0:T(8,128)(2,1)S(1)}, bf16[112,896]{1,0:T(8,128)(2,1)S(1)}, u32[]{:S(2)}, u32[]{:S(2)}) collective-permute-start(bf16[112,896]{1,0:T(8,128)(2,1)S(1)} %get-tuple-element.35), channel_id=1, source_target_pairs={{0,4},{1,5},{2,6},{3,7},{4,0},{5,1},{6,2},{7,3},{8,12},{9,13},{10,... | collective-permute-start | bytes 602120 | tf_op jit(solution)/shard_map/ppermute | solution.py:481
  57.0 1.1 collective-permute-start.15
  58.2 2.4 %collective-permute-done.13.b = bf16[112,896]{1,0:T(8,128)(2,1)S(1)} collective-permute-done((bf16[112,896]{1,0:T(8,128)(2,1)S(1)}, bf16[112,896]{1,0:T(8,128)(2,1)S(1)}, u32[]{:S(2)}, u32[]{:S(2)}) %collective-permute-start.13) | collective-permute-done | bytes 200736 | tf_op jit(solution)/shard_map/ppermute | solution.py:479
  60.6 5.4 %collective-permute-done.14.c = bf16[112,896]{1,0:T(8,128)(2,1)S(1)} collective-permute-done((bf16[112,896]{1,0:T(8,128)(2,1)S(1)}, bf16[112,896]{1,0:T(8,128)(2,1)S(1)}, u32[]{:S(2)}, u32[]{:S(2)}) %collective-permute-start.14) | collective-permute-done | bytes 200736 | tf_op jit(solution)/shard_map/ppermute | solution.py:481
  66.0 0.9 collect.1
  67.0 0.6 copy-done.4
  67.6 4.3 %all-to-all-start.1 = ((bf16[16,6,896]{2,1,0:T(8,128)(2,1)}), bf16[16,6,896]{2,1,0:T(8,128)(2,1)S(1)}, u32[]{:S(2)}, u32[]{:S(2)}) async-start(bf16[16,6,896]{2,1,0:T(8,128)(2,1)} %get-tuple-element.37), calls=%async_computation.1 | async-start | bytes 458752 | tf_op jit(solution)/shard_map/all_to_all | solution.py:492
  72.1 0.6 pad.13.cosine
  72.7 0.7 select_maximum_fusion.sine
  73.4 5.9 %all-to-all-done.1.queries = bf16[16,6,896]{2,1,0:T(8,128)(2,1)S(1)} async-done(((bf16[16,6,896]{2,1,0:T(8,128)(2,1)}), bf16[16,6,896]{2,1,0:T(8,128)(2,1)S(1)}, u32[]{:S(2)}, u32[]{:S(2)}) %all-to-all-start.1) | async-done | bytes 172064 | tf_op jit(solution)/shard_map/all_to_all | solution.py:492
  79.3 0.7 copy-done.11
  80.0 6.2 %attention.1 = bf16[16,6,896]{2,1,0:T(8,128)(2,1)} custom-call(s32[3]{0:T(128)} %lengths.1, bf16[16,6,896]{2,1,0:T(8,128)(2,1)} %copy-done.11, f32[16,512]{1,0:T(8,128)} %copy-done.4, f32[8,128]{1,0:T(8,128)} %pad.13.cosine, f32[8,128]{1,0:T(8,128)} %select_maximum_fusion.sine, bf16[3,2048,512]{2,1,0:T(8,128)(2,1)} %keys.1, bf16[3,2048,512]{2,1,0:T(8,128)(2,1)} %values.1), custom_call_target="tpu_custom_call" | custom-call | tf_op jit(solution)/shard_map/attention/pallas_call | solution.py:505
  86.2 5.5 %all-to-all-start.2 = ((bf16[16,6,896]{2,1,0:T(8,128)(2,1)}), bf16[16,6,896]{2,1,0:T(8,128)(2,1)S(1)}, u32[]{:S(2)}, u32[]{:S(2)}) async-start(bf16[16,6,896]{2,1,0:T(8,128)(2,1)} %attention.1), calls=%async_computation.2 | async-start | bytes 458752 | tf_op jit(solution)/shard_map/all_to_all | solution.py:526
  91.7 1.2 dynamic_slice.3
  93.0 6.1 %all-to-all-done.2.block = bf16[16,6,896]{2,1,0:T(8,128)(2,1)S(1)} async-done(((bf16[16,6,896]{2,1,0:T(8,128)(2,1)}), bf16[16,6,896]{2,1,0:T(8,128)(2,1)S(1)}, u32[]{:S(2)}, u32[]{:S(2)}) %all-to-all-start.2) | async-done | bytes 172064 | tf_op jit(solution)/shard_map/all_to_all | solution.py:526
  99.2 1.0 collective-permute-start.16
  100.2 3.0 %collective-permute-start.17 = (bf16[96,896]{1,0:T(8,128)(2,1)S(1)}, bf16[96,896]{1,0:T(8,128)(2,1)S(1)}, u32[]{:S(2)}, u32[]{:S(2)}) collective-permute-start(bf16[96,896]{1,0:T(8,128)(2,1)S(1)} %repack.1.b0), channel_id=1, source_target_pairs={{0,4},{1,5},{2,6},{3,7},{4,0},{5,1},{6,2},{7,3},{8,12},{9,13},{10,... | collective-permute-start | bytes 516104 | tf_op jit(solution)/shard_map/ppermute | solution.py:534
  103.2 1.0 collective-permute-start.18
  104.2 0.9 fusion.1
  105.0 4.7 %collective-permute-start.19 = (bf16[96,896]{1,0:T(8,128)(2,1)S(1)}, bf16[96,896]{1,0:T(8,128)(2,1)S(1)}, u32[]{:S(2)}, u32[]{:S(2)}) collective-permute-start(bf16[96,896]{1,0:T(8,128)(2,1)S(1)} %repack.1.b0), channel_id=1, source_target_pairs={{0,1},{1,0},{2,3},{3,2},{4,5},{5,4},{6,7},{7,6},{8,9},{9,8},{10,11... | collective-permute-start | bytes 516104 | tf_op jit(solution)/shard_map/ppermute | solution.py:535
  109.8 3.8 %collective-permute-start.20 = (bf16[96,896]{1,0:T(8,128)(2,1)S(1)}, bf16[96,896]{1,0:T(8,128)(2,1)S(1)}, u32[]{:S(2)}, u32[]{:S(2)}) collective-permute-start(bf16[96,896]{1,0:T(8,128)(2,1)S(1)} %collective-permute-done.16.b1), channel_id=1, source_target_pairs={{0,1},{1,0},{2,3},{3,2},{4,5},{5,4},{6,7},{7,6},{8,9},{9,8},{10,11... | collective-permute-start | bytes 516104 | tf_op jit(solution)/shard_map/ppermute | solution.py:535
  113.6 0.9 collective-permute-start.22
  114.5 0.7 broadcast_in_dim.74.scale
  115.5 0.8 copy-done.5
  116.2 7.3 %output_projection.1 = bf16[16,48,1856]{2,1,0:T(8,128)(2,1)S(1)} custom-call(bf16[96,896]{1,0:T(8,128)(2,1)S(1)} %repack.1.b0, bf16[96,896]{1,0:T(8,128)(2,1)S(1)} %collective-permute-done.16.b1, bf16[96,896]{1,0:T(8,128)(2,1)S(1)} %collective-permute-done.17.b2, bf16[96,896]{1,0:T(8,128)(2,1)S(1)} %collective-permute-done.18.b3, ...), custom_call_target="tpu_custom_call" | custom-call | tf_op jit(solution)/shard_map/output_projection/pallas_call | solution.py:541
  123.5 39.7 %all_to_all.21.parts = bf16[16,48,1856]{2,1,0:T(8,128)(2,1)S(1)} all-to-all(bf16[16,48,1856]{2,1,0:T(8,128)(2,1)S(1)} %output_projection.1), channel_id=1, replica_groups=mesh['gx'=16,'gy'=8] {'gx'}, dimensions={0} | all-to-all | bytes 5701632 | tf_op jit(solution)/shard_map/all_to_all | solution.py:550
  163.2 1.1 total.1
  (73 shorter events, 4.1 us)
Async XLA Ops:
  0.0 0.9 copy-start.3
  0.9 0.7 copy-start.8
  3.4 2.4 %collective-permute-start = (bf16[24,1920]{1,0:T(8,128)(2,1)S(1)}, bf16[24,1920]{1,0:T(8,128)(2,1)S(1)}, u32[]{:S(2)}, u32[]{:S(2)}) collective-permute-start(bf16[24,1920]{1,0:T(8,128)(2,1)S(1)} %get-tuple-element.23), channel_id=1, source_target_pairs={{0,1},{1,0},{2,3},{3,2},{4,5},{5,4},{6,7},{7,6},{8,9},{9,8},{10,11... | collective-permute-start | bytes 276488 | tf_op jit(solution)/shard_map/ppermute | solution.py:428
  5.9 6.8 %collective-permute-start.1 = (bf16[2,24,1920]{2,1,0:T(8,128)(2,1)S(1)}, bf16[2,24,1920]{2,1,0:T(8,128)(2,1)S(1)}, u32[]{:S(2)}, u32[]{:S(2)}) collective-permute-start(bf16[2,24,1920]{2,1,0:T(8,128)(2,1)S(1)} %pad_maximum_fusion.1), channel_id=1, source_target_pairs={{0,8},{1,33},{2,10},{3,35},{4,12},{5,37},{6,14},{7,39},{8,16},{9,4... | collective-permute-start | bytes 552968 | tf_op jit(solution)/shard_map/ppermute | solution.py:430
  7.7 5.1 %collective-permute-start.2 = (bf16[2,24,1920]{2,1,0:T(8,128)(2,1)S(1)}, bf16[2,24,1920]{2,1,0:T(8,128)(2,1)S(1)}, u32[]{:S(2)}, u32[]{:S(2)}) collective-permute-start(bf16[2,24,1920]{2,1,0:T(8,128)(2,1)S(1)} %pad_maximum_fusion.1), channel_id=1, source_target_pairs={{0,24},{1,97},{2,26},{3,99},{4,28},{5,101},{6,30},{7,103},{8,0},{9... | collective-permute-start | bytes 552968 | tf_op jit(solution)/shard_map/ppermute | solution.py:430
  9.9 6.3 %collective-permute-start.3 = (bf16[2,24,1920]{2,1,0:T(8,128)(2,1)S(1)}, bf16[2,24,1920]{2,1,0:T(8,128)(2,1)S(1)}, u32[]{:S(2)}, u32[]{:S(2)}) collective-permute-start(bf16[2,24,1920]{2,1,0:T(8,128)(2,1)S(1)} %pad_maximum_fusion.1), channel_id=1, source_target_pairs={{0,16},{1,65},{2,18},{3,67},{4,20},{5,69},{6,22},{7,71},{8,24},{9,... | collective-permute-start | bytes 552968 | tf_op jit(solution)/shard_map/ppermute | solution.py:430
  16.2 24.5 %collective-permute-start.4 = (bf16[2,96,1920]{2,1,0:T(8,128)(2,1)S(1)}, bf16[2,96,1920]{2,1,0:T(8,128)(2,1)S(1)}, u32[]{:S(2)}, u32[]{:S(2)}) collective-permute-start(bf16[2,96,1920]{2,1,0:T(8,128)(2,1)S(1)} %pad_maximum_fusion.both.a0), channel_id=1, source_target_pairs={{0,32},{1,9},{2,34},{3,11},{4,36},{5,13},{6,38},{7,15},{8,40},{9,1... | collective-permute-start | bytes 2211848 | tf_op jit(solution)/shard_map/ppermute | solution.py:432
  17.2 23.5 %collective-permute-start.5 = (bf16[2,96,1920]{2,1,0:T(8,128)(2,1)S(1)}, bf16[2,96,1920]{2,1,0:T(8,128)(2,1)S(1)}, u32[]{:S(2)}, u32[]{:S(2)}) collective-permute-start(bf16[2,96,1920]{2,1,0:T(8,128)(2,1)S(1)} %pad_maximum_fusion.both.a0), channel_id=1, source_target_pairs={{0,96},{1,25},{2,98},{3,27},{4,100},{5,29},{6,102},{7,31},{8,104},... | collective-permute-start | bytes 2211848 | tf_op jit(solution)/shard_map/ppermute | solution.py:432
  19.0 23.2 %copy-start.9 = (s32[4]{0:T(128)S(1)}, s32[4]{0:T(128)}, u32[]{:S(2)}) copy-start(s32[4]{0:T(128)} %positions.1) | copy-start | bytes 52
  19.0 23.3 %copy-start.12 = (f32[1856]{0:T(1024)S(1)}, f32[1856]{0:T(1024)}, u32[]{:S(2)}) copy-start(f32[1856]{0:T(1024)} %param.19) | copy-start | bytes 22276
  19.0 23.3 %copy-start.13 = (f32[1856]{0:T(1024)S(1)}, f32[1856]{0:T(1024)}, u32[]{:S(2)}) copy-start(f32[1856]{0:T(1024)} %param.18) | copy-start | bytes 22276
  19.0 21.7 %collective-permute-start.6 = (bf16[2,96,1920]{2,1,0:T(8,128)(2,1)S(1)}, bf16[2,96,1920]{2,1,0:T(8,128)(2,1)S(1)}, u32[]{:S(2)}, u32[]{:S(2)}) collective-permute-start(bf16[2,96,1920]{2,1,0:T(8,128)(2,1)S(1)} %pad_maximum_fusion.both.a0), channel_id=1, source_target_pairs={{0,64},{1,17},{2,66},{3,19},{4,68},{5,21},{6,70},{7,23},{8,72},{9,... | collective-permute-start | bytes 2211848 | tf_op jit(solution)/shard_map/ppermute | solution.py:432
  20.2 22.4 %copy-start = (bf16[1856,1024]{1,0:T(8,128)(2,1)S(1)}, bf16[1856,1024]{1,0:T(8,128)(2,1)}, u32[]{:S(2)}) copy-start(bf16[1856,1024]{1,0:T(8,128)(2,1)} %weight.2) | copy-start | bytes 11403268
  39.1 3.3 %copy-start.14 = (f32[896]{0:T(1024)S(1)}, f32[896]{0:T(1024)}, u32[]{:S(2)}) copy-start(f32[896]{0:T(1024)} %param.22) | copy-start | bytes 10756
  39.1 3.5 %copy-start.6 = (f32[4,1024]{1,0:T(4,128)S(1)}, f32[4,1024]{1,0:T(4,128)}, u32[]{:S(2)}) copy-start(f32[4,1024]{1,0:T(4,128)} %extra.3) | copy-start | bytes 49156
  39.1 3.5 %copy-start.10 = (f32[1024]{0:T(1024)S(1)}, f32[1024]{0:T(1024)}, u32[]{:S(2)}) copy-start(f32[1024]{0:T(1024)} %param.24) | copy-start | bytes 12292
  39.1 1.6 collective-permute-start.7
  40.8 2.8 %collective-permute-start.10 = (bf16[96,1920]{1,0:T(8,128)(2,1)S(1)}, bf16[96,1920]{1,0:T(8,128)(2,1)S(1)}, u32[]{:S(2)}, u32[]{:S(2)}) collective-permute-start(bf16[96,1920]{1,0:T(8,128)(2,1)S(1)} %slice_bitcast_fusion.1), channel_id=1, source_target_pairs={{0,1},{1,0},{2,3},{3,2},{4,5},{5,4},{6,7},{7,6},{8,9},{9,8},{10,11... | collective-permute-start | bytes 1105928 | tf_op jit(solution)/shard_map/ppermute | solution.py:456
  41.2 2.4 %collective-permute-start.11 = (bf16[96,1920]{1,0:T(8,128)(2,1)S(1)}, bf16[96,1920]{1,0:T(8,128)(2,1)S(1)}, u32[]{:S(2)}, u32[]{:S(2)}) collective-permute-start(bf16[96,1920]{1,0:T(8,128)(2,1)S(1)} %slice_bitcast_fusion), channel_id=1, source_target_pairs={{0,1},{1,0},{2,3},{3,2},{4,5},{5,4},{6,7},{7,6},{8,9},{9,8},{10,11... | collective-permute-start | bytes 1105928 | tf_op jit(solution)/shard_map/ppermute | solution.py:456
  41.5 2.1 %collective-permute-start.8 = (bf16[96,1920]{1,0:T(8,128)(2,1)S(1)}, bf16[96,1920]{1,0:T(8,128)(2,1)S(1)}, u32[]{:S(2)}, u32[]{:S(2)}) collective-permute-start(bf16[96,1920]{1,0:T(8,128)(2,1)S(1)} %slice_bitcast_fusion.3), channel_id=1, source_target_pairs={{0,1},{1,0},{2,3},{3,2},{4,5},{5,4},{6,7},{7,6},{8,9},{9,8},{10,11... | collective-permute-start | bytes 1105928 | tf_op jit(solution)/shard_map/ppermute | solution.py:456
  41.9 2.2 %collective-permute-start.9 = (bf16[96,1920]{1,0:T(8,128)(2,1)S(1)}, bf16[96,1920]{1,0:T(8,128)(2,1)S(1)}, u32[]{:S(2)}, u32[]{:S(2)}) collective-permute-start(bf16[96,1920]{1,0:T(8,128)(2,1)S(1)} %slice_bitcast_fusion.2), channel_id=1, source_target_pairs={{0,1},{1,0},{2,3},{3,2},{4,5},{5,4},{6,7},{7,6},{8,9},{9,8},{10,11... | collective-permute-start | bytes 1105928 | tf_op jit(solution)/shard_map/ppermute | solution.py:456
  42.6 1.9 %copy-start.1 = (bf16[1856,896]{1,0:T(8,128)(2,1)S(1)}, bf16[1856,896]{1,0:T(8,128)(2,1)}, u32[]{:S(2)}) copy-start(bf16[1856,896]{1,0:T(8,128)(2,1)} %weight.3) | copy-start | bytes 9977860
  42.6 1.9 %copy-start.7 = (f32[4,896]{1,0:T(4,128)S(1)}, f32[4,896]{1,0:T(4,128)}, u32[]{:S(2)}) copy-start(f32[4,896]{1,0:T(4,128)} %extra.4) | copy-start | bytes 43012
  50.2 7.8 %copy-start.15 = (s32[3]{0:T(128)S(1)}, s32[3]{0:T(128)}, u32[]{:S(2)}) copy-start(s32[3]{0:T(128)} %lengths.1) | copy-start | bytes 40
  50.2 2.6 %collective-permute-start.12 = (bf16[4,112,896]{2,1,0:T(8,128)(2,1)S(1)}, bf16[4,112,896]{2,1,0:T(8,128)(2,1)S(1)}, u32[]{:S(2)}, u32[]{:S(2)}) collective-permute-start(bf16[4,112,896]{2,1,0:T(8,128)(2,1)S(1)} %get-tuple-element.32), channel_id=1, source_target_pairs={{0,1},{1,0},{2,3},{3,2},{4,5},{5,4},{6,7},{7,6},{8,9},{9,8},{10,11... | collective-permute-start | bytes 2408456 | tf_op jit(solution)/shard_map/ppermute | solution.py:474
  53.0 7.6 %collective-permute-start.13 = (bf16[112,896]{1,0:T(8,128)(2,1)S(1)}, bf16[112,896]{1,0:T(8,128)(2,1)S(1)}, u32[]{:S(2)}, u32[]{:S(2)}) collective-permute-start(bf16[112,896]{1,0:T(8,128)(2,1)S(1)} %get-tuple-element.34), channel_id=1, source_target_pairs={{0,2},{1,3},{2,4},{3,5},{4,6},{5,7},{6,0},{7,1},{8,10},{9,11},{10,... | collective-permute-start | bytes 602120 | tf_op jit(solution)/shard_map/ppermute | solution.py:479
  54.3 11.7 %collective-permute-start.14 = (bf16[112,896]{1,0:T(8,128)(2,1)S(1)}, bf16[112,896]{1,0:T(8,128)(2,1)S(1)}, u32[]{:S(2)}, u32[]{:S(2)}) collective-permute-start(bf16[112,896]{1,0:T(8,128)(2,1)S(1)} %get-tuple-element.35), channel_id=1, source_target_pairs={{0,4},{1,5},{2,6},{3,7},{4,0},{5,1},{6,2},{7,3},{8,12},{9,13},{10,... | collective-permute-start | bytes 602120 | tf_op jit(solution)/shard_map/ppermute | solution.py:481
  57.0 9.1 %collective-permute-start.15 = (bf16[112,896]{1,0:T(8,128)(2,1)S(1)}, bf16[112,896]{1,0:T(8,128)(2,1)S(1)}, u32[]{:S(2)}, u32[]{:S(2)}) collective-permute-start(bf16[112,896]{1,0:T(8,128)(2,1)S(1)} %get-tuple-element.36), channel_id=1, source_target_pairs={{0,6},{1,7},{2,0},{3,1},{4,2},{5,3},{6,4},{7,5},{8,14},{9,15},{10,... | collective-permute-start | bytes 602120 | tf_op jit(solution)/shard_map/ppermute | solution.py:480
  67.0 0.6 copy-start.4
  67.6 11.7 %all-to-all-start.1 = ((bf16[16,6,896]{2,1,0:T(8,128)(2,1)}), bf16[16,6,896]{2,1,0:T(8,128)(2,1)S(1)}, u32[]{:S(2)}, u32[]{:S(2)}) async-start(bf16[16,6,896]{2,1,0:T(8,128)(2,1)} %get-tuple-element.37), calls=%async_computation.1 | async-start | bytes 458752 | tf_op jit(solution)/shard_map/all_to_all | solution.py:492
  79.3 0.7 copy-start.11
  80.0 35.5 %copy-start.2 = (bf16[896,1856]{0,1:T(8,128)(2,1)S(1)}, bf16[896,1856]{0,1:T(8,128)(2,1)}, u32[]{:S(2)}) copy-start(bf16[896,1856]{0,1:T(8,128)(2,1)} %param.31) | copy-start | bytes 9977860
  86.2 12.9 %all-to-all-start.2 = ((bf16[16,6,896]{2,1,0:T(8,128)(2,1)}), bf16[16,6,896]{2,1,0:T(8,128)(2,1)S(1)}, u32[]{:S(2)}, u32[]{:S(2)}) async-start(bf16[16,6,896]{2,1,0:T(8,128)(2,1)} %attention.1), calls=%async_computation.2 | async-start | bytes 458752 | tf_op jit(solution)/shard_map/all_to_all | solution.py:526
  99.2 10.6 %collective-permute-start.16 = (bf16[96,896]{1,0:T(8,128)(2,1)S(1)}, bf16[96,896]{1,0:T(8,128)(2,1)S(1)}, u32[]{:S(2)}, u32[]{:S(2)}) collective-permute-start(bf16[96,896]{1,0:T(8,128)(2,1)S(1)} %repack.1.b0), channel_id=1, source_target_pairs={{0,2},{1,3},{2,4},{3,5},{4,6},{5,7},{6,0},{7,1},{8,10},{9,11},{10,... | collective-permute-start | bytes 516104 | tf_op jit(solution)/shard_map/ppermute | solution.py:534
  100.2 13.4 %collective-permute-start.17 = (bf16[96,896]{1,0:T(8,128)(2,1)S(1)}, bf16[96,896]{1,0:T(8,128)(2,1)S(1)}, u32[]{:S(2)}, u32[]{:S(2)}) collective-permute-start(bf16[96,896]{1,0:T(8,128)(2,1)S(1)} %repack.1.b0), channel_id=1, source_target_pairs={{0,4},{1,5},{2,6},{3,7},{4,0},{5,1},{6,2},{7,3},{8,12},{9,13},{10,... | collective-permute-start | bytes 516104 | tf_op jit(solution)/shard_map/ppermute | solution.py:534
  103.2 10.4 %collective-permute-start.18 = (bf16[96,896]{1,0:T(8,128)(2,1)S(1)}, bf16[96,896]{1,0:T(8,128)(2,1)S(1)}, u32[]{:S(2)}, u32[]{:S(2)}) collective-permute-start(bf16[96,896]{1,0:T(8,128)(2,1)S(1)} %repack.1.b0), channel_id=1, source_target_pairs={{0,6},{1,7},{2,0},{3,1},{4,2},{5,3},{6,4},{7,5},{8,14},{9,15},{10,... | collective-permute-start | bytes 516104 | tf_op jit(solution)/shard_map/ppermute | solution.py:534
  105.0 10.2 %collective-permute-start.19 = (bf16[96,896]{1,0:T(8,128)(2,1)S(1)}, bf16[96,896]{1,0:T(8,128)(2,1)S(1)}, u32[]{:S(2)}, u32[]{:S(2)}) collective-permute-start(bf16[96,896]{1,0:T(8,128)(2,1)S(1)} %repack.1.b0), channel_id=1, source_target_pairs={{0,1},{1,0},{2,3},{3,2},{4,5},{5,4},{6,7},{7,6},{8,9},{9,8},{10,11... | collective-permute-start | bytes 516104 | tf_op jit(solution)/shard_map/ppermute | solution.py:535
  109.8 5.5 %collective-permute-start.20 = (bf16[96,896]{1,0:T(8,128)(2,1)S(1)}, bf16[96,896]{1,0:T(8,128)(2,1)S(1)}, u32[]{:S(2)}, u32[]{:S(2)}) collective-permute-start(bf16[96,896]{1,0:T(8,128)(2,1)S(1)} %collective-permute-done.16.b1), channel_id=1, source_target_pairs={{0,1},{1,0},{2,3},{3,2},{4,5},{5,4},{6,7},{7,6},{8,9},{9,8},{10,11... | collective-permute-start | bytes 516104 | tf_op jit(solution)/shard_map/ppermute | solution.py:535
  113.6 1.7 %collective-permute-start.21 = (bf16[96,896]{1,0:T(8,128)(2,1)S(1)}, bf16[96,896]{1,0:T(8,128)(2,1)S(1)}, u32[]{:S(2)}, u32[]{:S(2)}) collective-permute-start(bf16[96,896]{1,0:T(8,128)(2,1)S(1)} %collective-permute-done.17.b2), channel_id=1, source_target_pairs={{0,1},{1,0},{2,3},{3,2},{4,5},{5,4},{6,7},{7,6},{8,9},{9,8},{10,11... | collective-permute-start | bytes 516104 | tf_op jit(solution)/shard_map/ppermute | solution.py:535
  113.6 1.9 %collective-permute-start.22 = (bf16[96,896]{1,0:T(8,128)(2,1)S(1)}, bf16[96,896]{1,0:T(8,128)(2,1)S(1)}, u32[]{:S(2)}, u32[]{:S(2)}) collective-permute-start(bf16[96,896]{1,0:T(8,128)(2,1)S(1)} %collective-permute-done.18.b3), channel_id=1, source_target_pairs={{0,1},{1,0},{2,3},{3,2},{4,5},{5,4},{6,7},{7,6},{8,9},{9,8},{10,11... | collective-permute-start | bytes 516104 | tf_op jit(solution)/shard_map/ppermute | solution.py:535
  115.5 0.8 copy-start.5

commit v7 on v6

--- a/solution.py
+++ b/solution.py
@@ -313,32 +313,55 @@
             out[16 * k : 16 * k + 16, lanes] = staged[n, pl.ds(k, 16, stride=8), :].astype(BF)
 
 
-def output_kernel(b0, b1, b2, b3, s0, s1, s2, s3, chosen, plain, scale, extra, weight, out, left, acc):
-    y, c, _, _ = here()
+def output_kernel(
+    sending, b0, b1, b2, b3, s0, s1, s2, s3, chosen, plain, scale, extra, weight, out, left, acc
+):
+    y, c, z, x = here()
+    half = 1 - c if sending else c
     for blocks, core in (((b0, b1, b2, b3), c), ((s0, s1, s2, s3), 1 - c)):
         for d, block in enumerate(blocks):
             j = 2 * lax.rem(y + N_Y - d, N_Y) + core
             left[pl.ds(pl.multiple_of(96 * j, 96), 96), :] = block[...]
     step = 192
-    for n in range(768 // step):
-        rows = slice(n * step, n * step + step)
-        part = left[rows, :]
+    for n in range(384 // step):
+        part = left[pl.ds(pl.multiple_of(half * 384 + n * step, step), step), :]
         picked = jnp.dot(part, chosen[...], preferred_element_type=F32)
         term = lax.dot_general(part * plain[...], weight[...], NT, preferred_element_type=F32) * scale[...]
         for k in range(OUTL):
             term = term + picked[:, k : k + 1] * extra[k : k + 1, :]
-        put(acc, rows, term)
-    for i in range(16):
+        put(acc, slice(n * step, n * step + step), term)
+    for d in range(4):
+        owners = []
+        for f in range(4):
+            along_x = lax.rem(x + jnp.where(half == 0, f, d), 4)
+            along_z = lax.rem(z + jnp.where(half == 0, d, f), 4)
+            owners.append(along_z * 4 + along_x)
         for n, lanes in lanes_of(out.shape[2]):
-            got = acc[n, pl.ds(i, 48, stride=16), :].astype(BF)
-            out[i, :, lanes] = got[:, 0 : lanes.stop - lanes.start]
-
-
-def total_kernel(parts, out):
-    total = parts[0].astype(F32)
-    for i in range(1, 16):
-        total = total + parts[i].astype(F32)
-    out[...] = total.astype(BF)
+            got = [acc[n, pl.ds(i, 24, stride=16), :] for i in owners]
+            got = jnp.concatenate(got, axis=0).astype(BF)
+            out[d, :, lanes] = got[:, 0 : lanes.stop - lanes.start]
+
+
+def first_sum_kernel(mine, other, r1, r3, r2, o0, o1, o2, o3):
+    for part, start in enumerate((mine, other)):
+        total = start[0].astype(F32) + r1[part].astype(F32)
+        total = total + (r3[part].astype(F32) + r2[part].astype(F32))
+        for f, out in enumerate((o0, o1, o2, o3)):
+            out[part] = total[24 * f : 24 * f + 24, :].astype(BF)
+
+
+def last_sum_kernel(own, r1, r3, r2, keep, send):
+    for part, out in enumerate((keep, send)):
+        total = own[part].astype(F32) + r1[part].astype(F32)
+        out[...] = (total + (r3[part].astype(F32) + r2[part].astype(F32))).astype(BF)
+
+
+def join_kernel(mine, other, out):
+    first = here()[1] == 0
+    a = mine[...].astype(F32)
+    b = other[...].astype(F32)
+    joined = jnp.concatenate([jnp.where(first, a, b), jnp.where(first, b, a)], axis=0)
+    out[...] = joined.astype(BF)
 
 
 def params(mib=48):
@@ -538,22 +561,49 @@
     chosen = jnp.arange(columns, dtype=jnp.int32)[:, None] == middle[None, :]
     plain = jnp.where(jnp.any(chosen, axis=1), 0.0, 1.0).astype(BF)[None]
     chosen = jnp.pad(chosen.astype(BF), ((0, 0), (0, 128 - OUTL)))
-    partial = pl.pallas_call(
-        output_kernel,
-        in_specs=[vmem] * 13,
-        out_specs=vmem,
-        out_shape=jax.ShapeDtypeStruct((16, block_rows, out_columns), BF),
-        scratch_shapes=[pltpu.VMEM((tokens, columns), BF), pltpu.VMEM((15, tokens, 128), F32)],
-        compiler_params=params(28),
-        name="output_projection",
-    )(*blocks, chosen, plain, output_scale[None], output_float, output_int.T)
-    parts = lax.all_to_all(partial, "gx", split_axis=0, concat_axis=0, tiled=True)
+    half_rows = block_rows // 2
+
+    def project(sending):
+        return pl.pallas_call(
+            functools.partial(output_kernel, sending),
+            in_specs=[vmem] * 13,
+            out_specs=vmem,
+            out_shape=jax.ShapeDtypeStruct((4, 4 * half_rows, out_columns), BF),
+            scratch_shapes=[
+                pltpu.VMEM((tokens, columns), BF),
+                pltpu.VMEM((15, tokens // 2, 128), F32),
+            ],
+            compiler_params=params(24),
+            name="output_sent" if sending else "output_kept",
+        )(*blocks, chosen, plain, output_scale[None], output_float, output_int.T)
+
+    other = lax.ppermute(project(True), "gy", SIBLING)
+    kept = project(False)
+    steps = (1, 3, 2)
+    got = [
+        lax.ppermute(jnp.stack([kept[d], other[d]]), plane, shift_plane(False, d)) for d in steps
+    ]
+    quarter = jax.ShapeDtypeStruct((2, half_rows, out_columns), BF)
+    sums = pl.pallas_call(
+        first_sum_kernel,
+        grid=(1,),
+        in_specs=[whole((1, 4 * half_rows, out_columns))] * 2 + [vmem] * 3,
+        out_specs=[vmem] * 4,
+        out_shape=[quarter] * 4,
+        compiler_params=params(16),
+        name="first_sum",
+    )(kept, other, *got)
+    got = [lax.ppermute(sums[f], plane, shift_plane(True, f)) for f in steps]
+    half = jax.ShapeDtypeStruct((half_rows, out_columns), BF)
+    keep, send = pl.pallas_call(
+        last_sum_kernel, out_shape=[half] * 2, compiler_params=params(8), name="last_sum"
+    )(sums[0], *got)
     return pl.pallas_call(
-        total_kernel,
+        join_kernel,
         out_shape=jax.ShapeDtypeStruct((block_rows, out_columns), BF),
-        compiler_params=params(16),
-        name="total",
-    )(parts)
+        compiler_params=params(8),
+        name="join",
+    )(keep, lax.ppermute(send, "gy", SIBLING))
 
 
 def solution(mesh):

time: 165 us -> 159 us (0.964)
  blocking collectives: 58.3 us -> 18.6 us
  waiting for transfers between devices: 29.4 us -> 53.2 us
  Pallas kernels: 24.5 us -> 29.4 us
  starting transfers between devices: 42.6 us -> 47 us
    all_to_all x1 -> x0, blocking collectives: 39.7 us -> none  [on_device(): lax.all_to_all(partial, 'gx', split_axis=0, concat_axis=0, tiled=True)]
    ppermute x0 -> x8, waiting for transfers between devices: none -> 23.8 us  [the longest x3 17 us: on_device(): lax.ppermute(jnp.stack([kept[d], other[d]]), plane, shift_plane(False, d))]
    ppermute x0 -> x8, starting transfers between devices: none -> 8.88 us  [the longest x3 2.9 us: on_device(): lax.ppermute(jnp.stack([kept[d], other[d]]), plane, shift_plane(False, d))]
    pallas_call x1, Pallas kernels: 6.22 us -> 9.64 us  [on_device(): pl.pallas_call(attend_kernel, in_specs=[smem, vmem, vmem, vmem, vmem, hbm...]
    all_to_all x1, starting transfers between devices: 5.52 us -> 3.54 us  [on_device(): lax.all_to_all(attended, 'gx', split_axis=0, concat_axis=0, tiled=True)]
    ppermute x4, starting transfers between devices: 9.4 us -> 7.59 us  [on_device(): blocks = blocks + [lax.ppermute(b, 'gy', SIBLING) for b in blocks]]
    pallas_call x2 -> x5, Pallas kernels: 8.34 us -> 9.82 us  [the longest x2 8.64 us: project(): pl.pallas_call(functools.partial(output_kernel, sending), in_specs=[vmem]...]
  transfers between devices with their start and end apart: 25 -> 33, of which waited for: 11 -> 18; matrix products, arithmetic and copies ran while one was open for 3% -> 3% of each run, Pallas kernels for 1% -> 4%
where the time goes in v7:
time: 159 us; the launch traced here: 158 us
  waiting for transfers between devices  53.2 us (33%)
  starting transfers between devices  47 us (30%)
  Pallas kernels  29.4 us (18%)
  blocking collectives  18.6 us (12%)
  local copies, waits for them, and re-layouts  7.16 us (5%)
  other arithmetic  2.46 us (2%)
    all_to_all x1, blocking collectives, on_device(): lax.all_to_all(sums, plane, split_axis=0, concat_axis=0, tiled=True, axis...  18.6 us
    ppermute x3, waiting for transfers between devices, on_device(): lax.ppermute(jnp.stack([kept[d], other[d]]), plane, shift_plane(False, d))  17 us
    pallas_call x1, Pallas kernels, on_device(): pl.pallas_call(attend_kernel, in_specs=[smem, vmem, vmem, vmem, vmem, hbm...  9.64 us
    pallas_call x2, Pallas kernels, project(): pl.pallas_call(functools.partial(output_kernel, sending), in_specs=[vmem]...  8.64 us
    ppermute x4, starting transfers between devices, on_device(): blocks = blocks + [lax.ppermute(b, 'gy', SIBLING) for b in blocks]  7.59 us
    all_to_all x1, waiting for transfers between devices, on_device(): lax.all_to_all(attended, 'gx', split_axis=0, concat_axis=0, tiled=True)  6.08 us
    all_to_all x1, waiting for transfers between devices, on_device(): lax.all_to_all(summed, 'gx', split_axis=0, concat_axis=0, tiled=True)  5.9 us
    ppermute x3, waiting for transfers between devices, on_device(): got = [lax.ppermute(sums[f], plane, shift_plane(True, f)) for f in steps]  5.89 us
  transfers between devices with their start and end apart: 33, of which 18 were waited for; matrix products, arithmetic and copies ran while one was open for 3% of the time, Pallas kernels for 4%

profile of v7, /device:TPU:1, one launch (start us, length us, event | category | flops | bytes accessed | tf_op | source)
XLA Modules:
  0.0 158.2 jit_solution(1428932491381392228)
XLA Ops:
  0.0 0.9 copy-done.3
  1.6 1.8 %prepare.1 = (bf16[48,1920]{1,0:T(8,128)(2,1)S(1)}, bf16[24,1920]{1,0:T(8,128)(2,1)S(1)}, bf16[24,1920]{1,0:T(8,128)(2,1)S(1)}) custom-call(s32[4]{0:T(128)S(1)} %copy-done.8, bf16[48,1856]{1,0:T(8,128)(2,1)S(1)} %copy-done.3), custom_call_target="tpu_custom_call" | custom-call | tf_op jit(solution)/shard_map/prepare/pallas_call | solution.py:438
  3.4 1.5 collective-permute-start
  4.9 0.9 collective-permute-done
  5.9 1.8 %collective-permute-start.1 = (bf16[2,24,1920]{2,1,0:T(8,128)(2,1)S(1)}, bf16[2,24,1920]{2,1,0:T(8,128)(2,1)S(1)}, u32[]{:S(2)}, u32[]{:S(2)}) collective-permute-start(bf16[2,24,1920]{2,1,0:T(8,128)(2,1)S(1)} %pad_maximum_fusion.4), channel_id=1, source_target_pairs={{0,8},{1,33},{2,10},{3,35},{4,12},{5,37},{6,14},{7,39},{8,16},{9,4... | collective-permute-start | bytes 552968 | tf_op jit(solution)/shard_map/ppermute | solution.py:453
  7.7 2.2 %collective-permute-start.2 = (bf16[2,24,1920]{2,1,0:T(8,128)(2,1)S(1)}, bf16[2,24,1920]{2,1,0:T(8,128)(2,1)S(1)}, u32[]{:S(2)}, u32[]{:S(2)}) collective-permute-start(bf16[2,24,1920]{2,1,0:T(8,128)(2,1)S(1)} %pad_maximum_fusion.4), channel_id=1, source_target_pairs={{0,24},{1,97},{2,26},{3,99},{4,28},{5,101},{6,30},{7,103},{8,0},{9... | collective-permute-start | bytes 552968 | tf_op jit(solution)/shard_map/ppermute | solution.py:453
  9.9 1.2 collective-permute-start.3
  11.1 1.6 %collective-permute-done.1 = bf16[2,24,1920]{2,1,0:T(8,128)(2,1)S(1)} collective-permute-done((bf16[2,24,1920]{2,1,0:T(8,128)(2,1)S(1)}, bf16[2,24,1920]{2,1,0:T(8,128)(2,1)S(1)}, u32[]{:S(2)}, u32[]{:S(2)}) %collective-permute-start.1) | collective-permute-done | bytes 184352 | tf_op jit(solution)/shard_map/ppermute | solution.py:453
  12.7 3.4 %collective-permute-done.3 = bf16[2,24,1920]{2,1,0:T(8,128)(2,1)S(1)} collective-permute-done((bf16[2,24,1920]{2,1,0:T(8,128)(2,1)S(1)}, bf16[2,24,1920]{2,1,0:T(8,128)(2,1)S(1)}, u32[]{:S(2)}, u32[]{:S(2)}) %collective-permute-start.3) | collective-permute-done | bytes 184352 | tf_op jit(solution)/shard_map/ppermute | solution.py:453
  16.2 1.0 collective-permute-start.4
  17.2 1.8 %collective-permute-start.5 = (bf16[2,96,1920]{2,1,0:T(8,128)(2,1)S(1)}, bf16[2,96,1920]{2,1,0:T(8,128)(2,1)S(1)}, u32[]{:S(2)}, u32[]{:S(2)}) collective-permute-start(bf16[2,96,1920]{2,1,0:T(8,128)(2,1)S(1)} %pad_maximum_fusion.both.a0), channel_id=1, source_target_pairs={{0,96},{1,25},{2,98},{3,27},{4,100},{5,29},{6,102},{7,31},{8,104},... | collective-permute-start | bytes 2211848 | tf_op jit(solution)/shard_map/ppermute | solution.py:455
  19.0 1.2 collective-permute-start.6
  20.5 18.6 %all_to_all.15 = f32[16,2,96]{2,1,0:T(2,128)S(1)} all-to-all(f32[16,2,96]{2,1,0:T(2,128)S(1)} %row_sums.1), channel_id=1, replica_groups={{0,2,4,6,32,34,36,38,64,66,68,70,96,98,100,102},{8,10,12,14,40,42,44,46..., dimensions={0} | all-to-all | bytes 24576 | tf_op jit(solution)/shard_map/all_to_all | solution.py:462
  39.9 0.8 collective-permute-done.7.other
  42.6 1.0 pair_projection.1.pairs
  44.5 5.6 %query_projection.1 = (bf16[4,112,896]{2,1,0:T(8,128)(2,1)S(1)}, bf16[4,112,896]{2,1,0:T(8,128)(2,1)S(1)}) custom-call(bf16[2,96,1920]{2,1,0:T(8,128)(2,1)S(1)} %pad_maximum_fusion.both.a0, bf16[2,96,1920]{2,1,0:T(8,128)(2,1)S(1)} %collective-permute-done.4.a1, bf16[2,96,1920]{2,1,0:T(8,128)(2,1)S(1)} %collective-permute-done.6.a2, ...), custom_call_target="tpu_custom_call" | custom-call | tf_op jit(solution)/shard_map/query_projection/pallas_call | solution.py:484
  50.8 2.0 %collective-permute-done.12.received = bf16[4,112,896]{2,1,0:T(8,128)(2,1)S(1)} collective-permute-done((bf16[4,112,896]{2,1,0:T(8,128)(2,1)S(1)}, bf16[4,112,896]{2,1,0:T(8,128)(2,1)S(1)}, u32[]{:S(2)}, u32[]{:S(2)}) %collective-permute-start.12) | collective-permute-done | bytes 802848 | tf_op jit(solution)/shard_map/ppermute | solution.py:497
  53.0 1.4 collective-permute-start.13
  54.3 2.6 %collective-permute-start.14 = (bf16[112,896]{1,0:T(8,128)(2,1)S(1)}, bf16[112,896]{1,0:T(8,128)(2,1)S(1)}, u32[]{:S(2)}, u32[]{:S(2)}) collective-permute-start(bf16[112,896]{1,0:T(8,128)(2,1)S(1)} %get-tuple-element.41), channel_id=1, source_target_pairs={{0,4},{1,5},{2,6},{3,7},{4,0},{5,1},{6,2},{7,3},{8,12},{9,13},{10,... | collective-permute-start | bytes 602120 | tf_op jit(solution)/shard_map/ppermute | solution.py:504
  57.0 1.1 collective-permute-start.15
  58.2 2.4 %collective-permute-done.13.b = bf16[112,896]{1,0:T(8,128)(2,1)S(1)} collective-permute-done((bf16[112,896]{1,0:T(8,128)(2,1)S(1)}, bf16[112,896]{1,0:T(8,128)(2,1)S(1)}, u32[]{:S(2)}, u32[]{:S(2)}) %collective-permute-start.13) | collective-permute-done | bytes 200736 | tf_op jit(solution)/shard_map/ppermute | solution.py:502
  60.6 5.4 %collective-permute-done.14.c = bf16[112,896]{1,0:T(8,128)(2,1)S(1)} collective-permute-done((bf16[112,896]{1,0:T(8,128)(2,1)S(1)}, bf16[112,896]{1,0:T(8,128)(2,1)S(1)}, u32[]{:S(2)}, u32[]{:S(2)}) %collective-permute-start.14) | collective-permute-done | bytes 200736 | tf_op jit(solution)/shard_map/ppermute | solution.py:504
  66.0 1.0 collect.1
  67.6 4.3 %all-to-all-start.1 = ((bf16[16,6,896]{2,1,0:T(8,128)(2,1)}), bf16[16,6,896]{2,1,0:T(8,128)(2,1)S(1)}, u32[]{:S(2)}, u32[]{:S(2)}) async-start(bf16[16,6,896]{2,1,0:T(8,128)(2,1)} %get-tuple-element.43), calls=%async_computation.1 | async-start | bytes 458752 | tf_op jit(solution)/shard_map/all_to_all | solution.py:515
  73.4 5.9 %all-to-all-done.1.queries = bf16[16,6,896]{2,1,0:T(8,128)(2,1)S(1)} async-done(((bf16[16,6,896]{2,1,0:T(8,128)(2,1)}), bf16[16,6,896]{2,1,0:T(8,128)(2,1)S(1)}, u32[]{:S(2)}, u32[]{:S(2)}) %all-to-all-start.1) | async-done | bytes 172064 | tf_op jit(solution)/shard_map/all_to_all | solution.py:515
  80.0 9.6 %attention.1 = bf16[16,6,896]{2,1,0:T(8,128)(2,1)} custom-call(s32[3]{0:T(128)} %lengths.1, bf16[16,6,896]{2,1,0:T(8,128)(2,1)} %copy-done.11, f32[16,512]{1,0:T(8,128)} %copy-done.5, f32[8,128]{1,0:T(8,128)} %pad.13.cosine, f32[8,128]{1,0:T(8,128)} %select_maximum_fusion.sine, bf16[3,2048,512]{2,1,0:T(8,128)(2,1)} %keys.1, bf16[3,2048,512]{2,1,0:T(8,128)(2,1)} %values.1), custom_call_target="tpu_custom_call" | custom-call | tf_op jit(solution)/shard_map/attention/pallas_call | solution.py:528
  89.7 3.5 %all-to-all-start.2 = ((bf16[16,6,896]{2,1,0:T(8,128)(2,1)}), bf16[16,6,896]{2,1,0:T(8,128)(2,1)S(1)}, u32[]{:S(2)}, u32[]{:S(2)}) async-start(bf16[16,6,896]{2,1,0:T(8,128)(2,1)} %attention.1), calls=%async_computation.2 | async-start | bytes 458752 | tf_op jit(solution)/shard_map/all_to_all | solution.py:549
  93.2 1.2 dynamic_slice.3
  94.5 6.1 %all-to-all-done.2.block = bf16[16,6,896]{2,1,0:T(8,128)(2,1)S(1)} async-done(((bf16[16,6,896]{2,1,0:T(8,128)(2,1)}), bf16[16,6,896]{2,1,0:T(8,128)(2,1)S(1)}, u32[]{:S(2)}, u32[]{:S(2)}) %all-to-all-start.2) | async-done | bytes 172064 | tf_op jit(solution)/shard_map/all_to_all | solution.py:549
  100.7 2.5 %collective-permute-start.17 = (bf16[96,896]{1,0:T(8,128)(2,1)S(1)}, bf16[96,896]{1,0:T(8,128)(2,1)S(1)}, u32[]{:S(2)}, u32[]{:S(2)}) collective-permute-start(bf16[96,896]{1,0:T(8,128)(2,1)S(1)} %repack.1.b0), channel_id=1, source_target_pairs={{0,4},{1,5},{2,6},{3,7},{4,0},{5,1},{6,2},{7,3},{8,12},{9,13},{10,... | collective-permute-start | bytes 516104 | tf_op jit(solution)/shard_map/ppermute | solution.py:557
  103.2 1.7 %collective-permute-start.18 = (bf16[96,896]{1,0:T(8,128)(2,1)S(1)}, bf16[96,896]{1,0:T(8,128)(2,1)S(1)}, u32[]{:S(2)}, u32[]{:S(2)}) collective-permute-start(bf16[96,896]{1,0:T(8,128)(2,1)S(1)} %repack.1.b0), channel_id=1, source_target_pairs={{0,6},{1,7},{2,0},{3,1},{4,2},{5,3},{6,4},{7,5},{8,14},{9,15},{10,... | collective-permute-start | bytes 516104 | tf_op jit(solution)/shard_map/ppermute | solution.py:557
  104.9 0.9 fusion.1
  105.8 4.4 %collective-permute-start.19 = (bf16[96,896]{1,0:T(8,128)(2,1)S(1)}, bf16[96,896]{1,0:T(8,128)(2,1)S(1)}, u32[]{:S(2)}, u32[]{:S(2)}) collective-permute-start(bf16[96,896]{1,0:T(8,128)(2,1)S(1)} %repack.1.b0), channel_id=1, source_target_pairs={{0,1},{1,0},{2,3},{3,2},{4,5},{5,4},{6,7},{7,6},{8,9},{9,8},{10,11... | collective-permute-start | bytes 516104 | tf_op jit(solution)/shard_map/ppermute | solution.py:558
  110.1 2.4 %collective-permute-start.20 = (bf16[96,896]{1,0:T(8,128)(2,1)S(1)}, bf16[96,896]{1,0:T(8,128)(2,1)S(1)}, u32[]{:S(2)}, u32[]{:S(2)}) collective-permute-start(bf16[96,896]{1,0:T(8,128)(2,1)S(1)} %collective-permute-done.16.b1), channel_id=1, source_target_pairs={{0,1},{1,0},{2,3},{3,2},{4,5},{5,4},{6,7},{7,6},{8,9},{9,8},{10,11... | collective-permute-start | bytes 516104 | tf_op jit(solution)/shard_map/ppermute | solution.py:558
  112.5 0.8 collective-permute-start.22
  115.2 4.3 %output_sent.1 = bf16[4,96,1856]{2,1,0:T(8,128)(2,1)S(1)} custom-call(bf16[96,896]{1,0:T(8,128)(2,1)S(1)} %repack.1.b0, bf16[96,896]{1,0:T(8,128)(2,1)S(1)} %collective-permute-done.16.b1, bf16[96,896]{1,0:T(8,128)(2,1)S(1)} %collective-permute-done.17.b2, bf16[96,896]{1,0:T(8,128)(2,1)S(1)} %collective-permute-done.18.b3, ...), custom_call_target="tpu_custom_call" | custom-call | tf_op jit(solution)/shard_map/output_sent/pallas_call | solution.py:567
  119.9 4.3 %output_kept.1.mine = bf16[4,96,1856]{2,1,0:T(8,128)(2,1)S(1)} custom-call(bf16[96,896]{1,0:T(8,128)(2,1)S(1)} %repack.1.b0, bf16[96,896]{1,0:T(8,128)(2,1)S(1)} %collective-permute-done.16.b1, bf16[96,896]{1,0:T(8,128)(2,1)S(1)} %collective-permute-done.17.b2, bf16[96,896]{1,0:T(8,128)(2,1)S(1)} %collective-permute-done.18.b3, ...), custom_call_target="tpu_custom_call" | custom-call | tf_op jit(solution)/shard_map/output_kept/pallas_call | solution.py:567
  124.5 0.8 collective-permute-start.26
  125.4 2.0 %collective-permute-start.25 = (bf16[2,96,1856]{2,1,0:T(8,128)(2,1)S(1)}, bf16[2,96,1856]{2,1,0:T(8,128)(2,1)S(1)}, u32[]{:S(2)}, u32[]{:S(2)}) collective-permute-start(bf16[2,96,1856]{2,1,0:T(8,128)(2,1)S(1)} %pad_maximum_fusion.2), channel_id=1, source_target_pairs={{0,96},{1,25},{2,98},{3,27},{4,100},{5,29},{6,102},{7,31},{8,104},... | collective-permute-start | bytes 2138120 | tf_op jit(solution)/shard_map/ppermute | solution.py:584
  127.6 9.2 %collective-permute-done.26.r2 = bf16[2,96,1856]{2,1,0:T(8,128)(2,1)S(1)} collective-permute-done((bf16[2,96,1856]{2,1,0:T(8,128)(2,1)S(1)}, bf16[2,96,1856]{2,1,0:T(8,128)(2,1)S(1)}, u32[]{:S(2)}, u32[]{:S(2)}) %collective-permute-start.26) | collective-permute-done | bytes 712736 | tf_op jit(solution)/shard_map/ppermute | solution.py:584
  136.8 6.1 %collective-permute-done.25.r3 = bf16[2,96,1856]{2,1,0:T(8,128)(2,1)S(1)} collective-permute-done((bf16[2,96,1856]{2,1,0:T(8,128)(2,1)S(1)}, bf16[2,96,1856]{2,1,0:T(8,128)(2,1)S(1)}, u32[]{:S(2)}, u32[]{:S(2)}) %collective-permute-start.25) | collective-permute-done | bytes 712736 | tf_op jit(solution)/shard_map/ppermute | solution.py:584
  142.8 1.8 %collective-permute-done.24.r1 = bf16[2,96,1856]{2,1,0:T(8,128)(2,1)S(1)} collective-permute-done((bf16[2,96,1856]{2,1,0:T(8,128)(2,1)S(1)}, bf16[2,96,1856]{2,1,0:T(8,128)(2,1)S(1)}, u32[]{:S(2)}, u32[]{:S(2)}) %collective-permute-start.24) | collective-permute-done | bytes 712736 | tf_op jit(solution)/shard_map/ppermute | solution.py:584
  145.1 2.7 %collective-permute-start.28 = (bf16[2,24,1856]{2,1,0:T(8,128)(2,1)S(1)}, bf16[2,24,1856]{2,1,0:T(8,128)(2,1)S(1)}, u32[]{:S(2)}, u32[]{:S(2)}) collective-permute-start(bf16[2,24,1856]{2,1,0:T(8,128)(2,1)S(1)} %get-tuple-element.47), channel_id=1, source_target_pairs={{0,24},{1,97},{2,26},{3,99},{4,28},{5,101},{6,30},{7,103},{8,0},{9... | collective-permute-start | bytes 534536 | tf_op jit(solution)/shard_map/ppermute | solution.py:596
  147.8 3.2 %collective-permute-done.27.r1 = bf16[2,24,1856]{2,1,0:T(8,128)(2,1)S(1)} collective-permute-done((bf16[2,24,1856]{2,1,0:T(8,128)(2,1)S(1)}, bf16[2,24,1856]{2,1,0:T(8,128)(2,1)S(1)}, u32[]{:S(2)}, u32[]{:S(2)}) %collective-permute-start.27) | collective-permute-done | bytes 178208 | tf_op jit(solution)/shard_map/ppermute | solution.py:596
  151.0 1.2 collective-permute-done.28.r3
  152.2 1.4 collective-permute-done.29.r2
  153.7 2.8 %collective-permute-start.30 = (bf16[24,1856]{1,0:T(8,128)(2,1)S(1)}, bf16[24,1856]{1,0:T(8,128)(2,1)S(1)}, u32[]{:S(2)}, u32[]{:S(2)}) collective-permute-start(bf16[24,1856]{1,0:T(8,128)(2,1)S(1)} %get-tuple-element.50), channel_id=1, source_target_pairs={{0,1},{1,0},{2,3},{3,2},{4,5},{5,4},{6,7},{7,6},{8,9},{9,8},{10,11... | collective-permute-start | bytes 267272 | tf_op jit(solution)/shard_map/ppermute | solution.py:606
  156.5 0.9 collective-permute-done.30.other
  (96 shorter events, 12.5 us)
Async XLA Ops:
  0.0 0.9 copy-start.3
  0.9 0.7 copy-start.8
  3.4 2.4 %collective-permute-start = (bf16[24,1920]{1,0:T(8,128)(2,1)S(1)}, bf16[24,1920]{1,0:T(8,128)(2,1)S(1)}, u32[]{:S(2)}, u32[]{:S(2)}) collective-permute-start(bf16[24,1920]{1,0:T(8,128)(2,1)S(1)} %get-tuple-element.29), channel_id=1, source_target_pairs={{0,1},{1,0},{2,3},{3,2},{4,5},{5,4},{6,7},{7,6},{8,9},{9,8},{10,11... | collective-permute-start | bytes 276488 | tf_op jit(solution)/shard_map/ppermute | solution.py:451
  5.9 6.8 %collective-permute-start.1 = (bf16[2,24,1920]{2,1,0:T(8,128)(2,1)S(1)}, bf16[2,24,1920]{2,1,0:T(8,128)(2,1)S(1)}, u32[]{:S(2)}, u32[]{:S(2)}) collective-permute-start(bf16[2,24,1920]{2,1,0:T(8,128)(2,1)S(1)} %pad_maximum_fusion.4), channel_id=1, source_target_pairs={{0,8},{1,33},{2,10},{3,35},{4,12},{5,37},{6,14},{7,39},{8,16},{9,4... | collective-permute-start | bytes 552968 | tf_op jit(solution)/shard_map/ppermute | solution.py:453
  7.7 5.1 %collective-permute-start.2 = (bf16[2,24,1920]{2,1,0:T(8,128)(2,1)S(1)}, bf16[2,24,1920]{2,1,0:T(8,128)(2,1)S(1)}, u32[]{:S(2)}, u32[]{:S(2)}) collective-permute-start(bf16[2,24,1920]{2,1,0:T(8,128)(2,1)S(1)} %pad_maximum_fusion.4), channel_id=1, source_target_pairs={{0,24},{1,97},{2,26},{3,99},{4,28},{5,101},{6,30},{7,103},{8,0},{9... | collective-permute-start | bytes 552968 | tf_op jit(solution)/shard_map/ppermute | solution.py:453
  9.9 6.3 %collective-permute-start.3 = (bf16[2,24,1920]{2,1,0:T(8,128)(2,1)S(1)}, bf16[2,24,1920]{2,1,0:T(8,128)(2,1)S(1)}, u32[]{:S(2)}, u32[]{:S(2)}) collective-permute-start(bf16[2,24,1920]{2,1,0:T(8,128)(2,1)S(1)} %pad_maximum_fusion.4), channel_id=1, source_target_pairs={{0,16},{1,65},{2,18},{3,67},{4,20},{5,69},{6,22},{7,71},{8,24},{9,... | collective-permute-start | bytes 552968 | tf_op jit(solution)/shard_map/ppermute | solution.py:453
  16.2 24.5 %collective-permute-start.4 = (bf16[2,96,1920]{2,1,0:T(8,128)(2,1)S(1)}, bf16[2,96,1920]{2,1,0:T(8,128)(2,1)S(1)}, u32[]{:S(2)}, u32[]{:S(2)}) collective-permute-start(bf16[2,96,1920]{2,1,0:T(8,128)(2,1)S(1)} %pad_maximum_fusion.both.a0), channel_id=1, source_target_pairs={{0,32},{1,9},{2,34},{3,11},{4,36},{5,13},{6,38},{7,15},{8,40},{9,1... | collective-permute-start | bytes 2211848 | tf_op jit(solution)/shard_map/ppermute | solution.py:455
  17.2 23.5 %collective-permute-start.5 = (bf16[2,96,1920]{2,1,0:T(8,128)(2,1)S(1)}, bf16[2,96,1920]{2,1,0:T(8,128)(2,1)S(1)}, u32[]{:S(2)}, u32[]{:S(2)}) collective-permute-start(bf16[2,96,1920]{2,1,0:T(8,128)(2,1)S(1)} %pad_maximum_fusion.both.a0), channel_id=1, source_target_pairs={{0,96},{1,25},{2,98},{3,27},{4,100},{5,29},{6,102},{7,31},{8,104},... | collective-permute-start | bytes 2211848 | tf_op jit(solution)/shard_map/ppermute | solution.py:455
  19.0 23.2 %copy-start.9 = (s32[4]{0:T(128)S(1)}, s32[4]{0:T(128)}, u32[]{:S(2)}) copy-start(s32[4]{0:T(128)} %positions.1) | copy-start | bytes 52
  19.0 23.3 %copy-start.12 = (f32[1856]{0:T(1024)S(1)}, f32[1856]{0:T(1024)}, u32[]{:S(2)}) copy-start(f32[1856]{0:T(1024)} %param.19) | copy-start | bytes 22276
  19.0 23.3 %copy-start.13 = (f32[1856]{0:T(1024)S(1)}, f32[1856]{0:T(1024)}, u32[]{:S(2)}) copy-start(f32[1856]{0:T(1024)} %param.18) | copy-start | bytes 22276
  19.0 21.7 %collective-permute-start.6 = (bf16[2,96,1920]{2,1,0:T(8,128)(2,1)S(1)}, bf16[2,96,1920]{2,1,0:T(8,128)(2,1)S(1)}, u32[]{:S(2)}, u32[]{:S(2)}) collective-permute-start(bf16[2,96,1920]{2,1,0:T(8,128)(2,1)S(1)} %pad_maximum_fusion.both.a0), channel_id=1, source_target_pairs={{0,64},{1,17},{2,66},{3,19},{4,68},{5,21},{6,70},{7,23},{8,72},{9,... | collective-permute-start | bytes 2211848 | tf_op jit(solution)/shard_map/ppermute | solution.py:455
  20.2 22.4 %copy-start.1 = (bf16[1856,1024]{1,0:T(8,128)(2,1)S(1)}, bf16[1856,1024]{1,0:T(8,128)(2,1)}, u32[]{:S(2)}) copy-start(bf16[1856,1024]{1,0:T(8,128)(2,1)} %weight.2) | copy-start | bytes 11403268
  39.1 3.3 %copy-start.14 = (f32[896]{0:T(1024)S(1)}, f32[896]{0:T(1024)}, u32[]{:S(2)}) copy-start(f32[896]{0:T(1024)} %param.22) | copy-start | bytes 10756
  39.1 3.5 %copy-start.6 = (f32[4,1024]{1,0:T(4,128)S(1)}, f32[4,1024]{1,0:T(4,128)}, u32[]{:S(2)}) copy-start(f32[4,1024]{1,0:T(4,128)} %extra.4) | copy-start | bytes 49156
  39.1 3.5 %copy-start.10 = (f32[1024]{0:T(1024)S(1)}, f32[1024]{0:T(1024)}, u32[]{:S(2)}) copy-start(f32[1024]{0:T(1024)} %param.24) | copy-start | bytes 12292
  39.1 1.6 collective-permute-start.7
  40.8 2.8 %collective-permute-start.10 = (bf16[96,1920]{1,0:T(8,128)(2,1)S(1)}, bf16[96,1920]{1,0:T(8,128)(2,1)S(1)}, u32[]{:S(2)}, u32[]{:S(2)}) collective-permute-start(bf16[96,1920]{1,0:T(8,128)(2,1)S(1)} %slice_bitcast_fusion.1), channel_id=1, source_target_pairs={{0,1},{1,0},{2,3},{3,2},{4,5},{5,4},{6,7},{7,6},{8,9},{9,8},{10,11... | collective-permute-start | bytes 1105928 | tf_op jit(solution)/shard_map/ppermute | solution.py:479
  41.2 2.4 %collective-permute-start.11 = (bf16[96,1920]{1,0:T(8,128)(2,1)S(1)}, bf16[96,1920]{1,0:T(8,128)(2,1)S(1)}, u32[]{:S(2)}, u32[]{:S(2)}) collective-permute-start(bf16[96,1920]{1,0:T(8,128)(2,1)S(1)} %slice_bitcast_fusion), channel_id=1, source_target_pairs={{0,1},{1,0},{2,3},{3,2},{4,5},{5,4},{6,7},{7,6},{8,9},{9,8},{10,11... | collective-permute-start | bytes 1105928 | tf_op jit(solution)/shard_map/ppermute | solution.py:479
  41.5 2.1 %collective-permute-start.8 = (bf16[96,1920]{1,0:T(8,128)(2,1)S(1)}, bf16[96,1920]{1,0:T(8,128)(2,1)S(1)}, u32[]{:S(2)}, u32[]{:S(2)}) collective-permute-start(bf16[96,1920]{1,0:T(8,128)(2,1)S(1)} %slice_bitcast_fusion.3), channel_id=1, source_target_pairs={{0,1},{1,0},{2,3},{3,2},{4,5},{5,4},{6,7},{7,6},{8,9},{9,8},{10,11... | collective-permute-start | bytes 1105928 | tf_op jit(solution)/shard_map/ppermute | solution.py:479
  41.9 2.2 %collective-permute-start.9 = (bf16[96,1920]{1,0:T(8,128)(2,1)S(1)}, bf16[96,1920]{1,0:T(8,128)(2,1)S(1)}, u32[]{:S(2)}, u32[]{:S(2)}) collective-permute-start(bf16[96,1920]{1,0:T(8,128)(2,1)S(1)} %slice_bitcast_fusion.2), channel_id=1, source_target_pairs={{0,1},{1,0},{2,3},{3,2},{4,5},{5,4},{6,7},{7,6},{8,9},{9,8},{10,11... | collective-permute-start | bytes 1105928 | tf_op jit(solution)/shard_map/ppermute | solution.py:479
  42.6 1.9 %copy-start.2 = (bf16[1856,896]{1,0:T(8,128)(2,1)S(1)}, bf16[1856,896]{1,0:T(8,128)(2,1)}, u32[]{:S(2)}) copy-start(bf16[1856,896]{1,0:T(8,128)(2,1)} %weight.3) | copy-start | bytes 9977860
  42.6 1.9 %copy-start.7 = (f32[4,896]{1,0:T(4,128)S(1)}, f32[4,896]{1,0:T(4,128)}, u32[]{:S(2)}) copy-start(f32[4,896]{1,0:T(4,128)} %extra.5) | copy-start | bytes 43012
  50.2 7.8 %copy-start.15 = (s32[3]{0:T(128)S(1)}, s32[3]{0:T(128)}, u32[]{:S(2)}) copy-start(s32[3]{0:T(128)} %lengths.1) | copy-start | bytes 40
  50.2 2.6 %collective-permute-start.12 = (bf16[4,112,896]{2,1,0:T(8,128)(2,1)S(1)}, bf16[4,112,896]{2,1,0:T(8,128)(2,1)S(1)}, u32[]{:S(2)}, u32[]{:S(2)}) collective-permute-start(bf16[4,112,896]{2,1,0:T(8,128)(2,1)S(1)} %get-tuple-element.38), channel_id=1, source_target_pairs={{0,1},{1,0},{2,3},{3,2},{4,5},{5,4},{6,7},{7,6},{8,9},{9,8},{10,11... | collective-permute-start | bytes 2408456 | tf_op jit(solution)/shard_map/ppermute | solution.py:497
  53.0 7.6 %collective-permute-start.13 = (bf16[112,896]{1,0:T(8,128)(2,1)S(1)}, bf16[112,896]{1,0:T(8,128)(2,1)S(1)}, u32[]{:S(2)}, u32[]{:S(2)}) collective-permute-start(bf16[112,896]{1,0:T(8,128)(2,1)S(1)} %get-tuple-element.40), channel_id=1, source_target_pairs={{0,2},{1,3},{2,4},{3,5},{4,6},{5,7},{6,0},{7,1},{8,10},{9,11},{10,... | collective-permute-start | bytes 602120 | tf_op jit(solution)/shard_map/ppermute | solution.py:502
  54.3 11.7 %collective-permute-start.14 = (bf16[112,896]{1,0:T(8,128)(2,1)S(1)}, bf16[112,896]{1,0:T(8,128)(2,1)S(1)}, u32[]{:S(2)}, u32[]{:S(2)}) collective-permute-start(bf16[112,896]{1,0:T(8,128)(2,1)S(1)} %get-tuple-element.41), channel_id=1, source_target_pairs={{0,4},{1,5},{2,6},{3,7},{4,0},{5,1},{6,2},{7,3},{8,12},{9,13},{10,... | collective-permute-start | bytes 602120 | tf_op jit(solution)/shard_map/ppermute | solution.py:504
  57.0 9.1 %collective-permute-start.15 = (bf16[112,896]{1,0:T(8,128)(2,1)S(1)}, bf16[112,896]{1,0:T(8,128)(2,1)S(1)}, u32[]{:S(2)}, u32[]{:S(2)}) collective-permute-start(bf16[112,896]{1,0:T(8,128)(2,1)S(1)} %get-tuple-element.42), channel_id=1, source_target_pairs={{0,6},{1,7},{2,0},{3,1},{4,2},{5,3},{6,4},{7,5},{8,14},{9,15},{10,... | collective-permute-start | bytes 602120 | tf_op jit(solution)/shard_map/ppermute | solution.py:503
  67.6 11.7 %all-to-all-start.1 = ((bf16[16,6,896]{2,1,0:T(8,128)(2,1)}), bf16[16,6,896]{2,1,0:T(8,128)(2,1)S(1)}, u32[]{:S(2)}, u32[]{:S(2)}) async-start(bf16[16,6,896]{2,1,0:T(8,128)(2,1)} %get-tuple-element.43), calls=%async_computation.1 | async-start | bytes 458752 | tf_op jit(solution)/shard_map/all_to_all | solution.py:515
  79.3 0.7 copy-start.11
  80.0 34.4 %copy-start = (bf16[896,1856]{0,1:T(8,128)(2,1)S(1)}, bf16[896,1856]{0,1:T(8,128)(2,1)}, u32[]{:S(2)}) copy-start(bf16[896,1856]{0,1:T(8,128)(2,1)} %param.31) | copy-start | bytes 9977860
  89.7 10.9 %all-to-all-start.2 = ((bf16[16,6,896]{2,1,0:T(8,128)(2,1)}), bf16[16,6,896]{2,1,0:T(8,128)(2,1)S(1)}, u32[]{:S(2)}, u32[]{:S(2)}) async-start(bf16[16,6,896]{2,1,0:T(8,128)(2,1)} %attention.1), calls=%async_computation.2 | async-start | bytes 458752 | tf_op jit(solution)/shard_map/all_to_all | solution.py:549
  100.6 9.5 %collective-permute-start.16 = (bf16[96,896]{1,0:T(8,128)(2,1)S(1)}, bf16[96,896]{1,0:T(8,128)(2,1)S(1)}, u32[]{:S(2)}, u32[]{:S(2)}) collective-permute-start(bf16[96,896]{1,0:T(8,128)(2,1)S(1)} %repack.1.b0), channel_id=1, source_target_pairs={{0,2},{1,3},{2,4},{3,5},{4,6},{5,7},{6,0},{7,1},{8,10},{9,11},{10,... | collective-permute-start | bytes 516104 | tf_op jit(solution)/shard_map/ppermute | solution.py:557
  100.7 11.8 %collective-permute-start.17 = (bf16[96,896]{1,0:T(8,128)(2,1)S(1)}, bf16[96,896]{1,0:T(8,128)(2,1)S(1)}, u32[]{:S(2)}, u32[]{:S(2)}) collective-permute-start(bf16[96,896]{1,0:T(8,128)(2,1)S(1)} %repack.1.b0), channel_id=1, source_target_pairs={{0,4},{1,5},{2,6},{3,7},{4,0},{5,1},{6,2},{7,3},{8,12},{9,13},{10,... | collective-permute-start | bytes 516104 | tf_op jit(solution)/shard_map/ppermute | solution.py:557
  103.2 9.3 %collective-permute-start.18 = (bf16[96,896]{1,0:T(8,128)(2,1)S(1)}, bf16[96,896]{1,0:T(8,128)(2,1)S(1)}, u32[]{:S(2)}, u32[]{:S(2)}) collective-permute-start(bf16[96,896]{1,0:T(8,128)(2,1)S(1)} %repack.1.b0), channel_id=1, source_target_pairs={{0,6},{1,7},{2,0},{3,1},{4,2},{5,3},{6,4},{7,5},{8,14},{9,15},{10,... | collective-permute-start | bytes 516104 | tf_op jit(solution)/shard_map/ppermute | solution.py:557
  105.8 8.4 %collective-permute-start.19 = (bf16[96,896]{1,0:T(8,128)(2,1)S(1)}, bf16[96,896]{1,0:T(8,128)(2,1)S(1)}, u32[]{:S(2)}, u32[]{:S(2)}) collective-permute-start(bf16[96,896]{1,0:T(8,128)(2,1)S(1)} %repack.1.b0), channel_id=1, source_target_pairs={{0,1},{1,0},{2,3},{3,2},{4,5},{5,4},{6,7},{7,6},{8,9},{9,8},{10,11... | collective-permute-start | bytes 516104 | tf_op jit(solution)/shard_map/ppermute | solution.py:558
  110.1 4.0 %collective-permute-start.20 = (bf16[96,896]{1,0:T(8,128)(2,1)S(1)}, bf16[96,896]{1,0:T(8,128)(2,1)S(1)}, u32[]{:S(2)}, u32[]{:S(2)}) collective-permute-start(bf16[96,896]{1,0:T(8,128)(2,1)S(1)} %collective-permute-done.16.b1), channel_id=1, source_target_pairs={{0,1},{1,0},{2,3},{3,2},{4,5},{5,4},{6,7},{7,6},{8,9},{9,8},{10,11... | collective-permute-start | bytes 516104 | tf_op jit(solution)/shard_map/ppermute | solution.py:558
  112.5 1.7 %collective-permute-start.21 = (bf16[96,896]{1,0:T(8,128)(2,1)S(1)}, bf16[96,896]{1,0:T(8,128)(2,1)S(1)}, u32[]{:S(2)}, u32[]{:S(2)}) collective-permute-start(bf16[96,896]{1,0:T(8,128)(2,1)S(1)} %collective-permute-done.17.b2), channel_id=1, source_target_pairs={{0,1},{1,0},{2,3},{3,2},{4,5},{5,4},{6,7},{7,6},{8,9},{9,8},{10,11... | collective-permute-start | bytes 516104 | tf_op jit(solution)/shard_map/ppermute | solution.py:558
  112.5 1.9 %collective-permute-start.22 = (bf16[96,896]{1,0:T(8,128)(2,1)S(1)}, bf16[96,896]{1,0:T(8,128)(2,1)S(1)}, u32[]{:S(2)}, u32[]{:S(2)}) collective-permute-start(bf16[96,896]{1,0:T(8,128)(2,1)S(1)} %collective-permute-done.18.b3), channel_id=1, source_target_pairs={{0,1},{1,0},{2,3},{3,2},{4,5},{5,4},{6,7},{7,6},{8,9},{9,8},{10,11... | collective-permute-start | bytes 516104 | tf_op jit(solution)/shard_map/ppermute | solution.py:558
  114.4 0.8 copy-start.4
  119.5 4.9 %collective-permute-start.23 = (bf16[4,96,1856]{2,1,0:T(8,128)(2,1)S(1)}, bf16[4,96,1856]{2,1,0:T(8,128)(2,1)S(1)}, u32[]{:S(2)}, u32[]{:S(2)}) collective-permute-start(bf16[4,96,1856]{2,1,0:T(8,128)(2,1)S(1)} %output_sent.1), channel_id=1, source_target_pairs={{0,1},{1,0},{2,3},{3,2},{4,5},{5,4},{6,7},{7,6},{8,9},{9,8},{10,11... | collective-permute-start | bytes 4276232 | tf_op jit(solution)/shard_map/ppermute | solution.py:580
  124.5 12.2 %collective-permute-start.26 = (bf16[2,96,1856]{2,1,0:T(8,128)(2,1)S(1)}, bf16[2,96,1856]{2,1,0:T(8,128)(2,1)S(1)}, u32[]{:S(2)}, u32[]{:S(2)}) collective-permute-start(bf16[2,96,1856]{2,1,0:T(8,128)(2,1)S(1)} %pad_maximum_fusion.3), channel_id=1, source_target_pairs={{0,64},{1,17},{2,66},{3,19},{4,68},{5,21},{6,70},{7,23},{8,72},{9,... | collective-permute-start | bytes 2138120 | tf_op jit(solution)/shard_map/ppermute | solution.py:584
  125.4 17.4 %collective-permute-start.25 = (bf16[2,96,1856]{2,1,0:T(8,128)(2,1)S(1)}, bf16[2,96,1856]{2,1,0:T(8,128)(2,1)S(1)}, u32[]{:S(2)}, u32[]{:S(2)}) collective-permute-start(bf16[2,96,1856]{2,1,0:T(8,128)(2,1)S(1)} %pad_maximum_fusion.2), channel_id=1, source_target_pairs={{0,96},{1,25},{2,98},{3,27},{4,100},{5,29},{6,102},{7,31},{8,104},... | collective-permute-start | bytes 2138120 | tf_op jit(solution)/shard_map/ppermute | solution.py:584
  127.5 17.1 %collective-permute-start.24 = (bf16[2,96,1856]{2,1,0:T(8,128)(2,1)S(1)}, bf16[2,96,1856]{2,1,0:T(8,128)(2,1)S(1)}, u32[]{:S(2)}, u32[]{:S(2)}) collective-permute-start(bf16[2,96,1856]{2,1,0:T(8,128)(2,1)S(1)} %pad_maximum_fusion.1), channel_id=1, source_target_pairs={{0,32},{1,9},{2,34},{3,11},{4,36},{5,13},{6,38},{7,15},{8,40},{9,1... | collective-permute-start | bytes 2138120 | tf_op jit(solution)/shard_map/ppermute | solution.py:584
  145.0 6.0 %collective-permute-start.27 = (bf16[2,24,1856]{2,1,0:T(8,128)(2,1)S(1)}, bf16[2,24,1856]{2,1,0:T(8,128)(2,1)S(1)}, u32[]{:S(2)}, u32[]{:S(2)}) collective-permute-start(bf16[2,24,1856]{2,1,0:T(8,128)(2,1)S(1)} %get-tuple-element.46), channel_id=1, source_target_pairs={{0,8},{1,33},{2,10},{3,35},{4,12},{5,37},{6,14},{7,39},{8,16},{9,4... | collective-permute-start | bytes 534536 | tf_op jit(solution)/shard_map/ppermute | solution.py:596
  145.1 7.1 %collective-permute-start.28 = (bf16[2,24,1856]{2,1,0:T(8,128)(2,1)S(1)}, bf16[2,24,1856]{2,1,0:T(8,128)(2,1)S(1)}, u32[]{:S(2)}, u32[]{:S(2)}) collective-permute-start(bf16[2,24,1856]{2,1,0:T(8,128)(2,1)S(1)} %get-tuple-element.47), channel_id=1, source_target_pairs={{0,24},{1,97},{2,26},{3,99},{4,28},{5,101},{6,30},{7,103},{8,0},{9... | collective-permute-start | bytes 534536 | tf_op jit(solution)/shard_map/ppermute | solution.py:596
  147.8 5.9 %collective-permute-start.29 = (bf16[2,24,1856]{2,1,0:T(8,128)(2,1)S(1)}, bf16[2,24,1856]{2,1,0:T(8,128)(2,1)S(1)}, u32[]{:S(2)}, u32[]{:S(2)}) collective-permute-start(bf16[2,24,1856]{2,1,0:T(8,128)(2,1)S(1)} %get-tuple-element.48), channel_id=1, source_target_pairs={{0,16},{1,65},{2,18},{3,67},{4,20},{5,69},{6,22},{7,71},{8,24},{9,... | collective-permute-start | bytes 534536 | tf_op jit(solution)/shard_map/ppermute | solution.py:596
  153.7 3.7 %collective-permute-start.30 = (bf16[24,1856]{1,0:T(8,128)(2,1)S(1)}, bf16[24,1856]{1,0:T(8,128)(2,1)S(1)}, u32[]{:S(2)}, u32[]{:S(2)}) collective-permute-start(bf16[24,1856]{1,0:T(8,128)(2,1)S(1)} %get-tuple-element.50), channel_id=1, source_target_pairs={{0,1},{1,0},{2,3},{3,2},{4,5},{5,4},{6,7},{7,6},{8,9},{9,8},{10,11... | collective-permute-start | bytes 267272 | tf_op jit(solution)/shard_map/ppermute | solution.py:606
  (1 other events, 0.6 us)

commit v8 on v7

--- a/solution.py
+++ b/solution.py
@@ -314,7 +314,7 @@
 
 
 def output_kernel(
-    sending, b0, b1, b2, b3, s0, s1, s2, s3, chosen, plain, scale, extra, weight, out, left, acc
+    sending, b0, b1, b2, b3, s0, s1, s2, s3, chosen, plain, factors, weight, out, left, acc
 ):
     y, c, z, x = here()
     half = 1 - c if sending else c
@@ -326,9 +326,10 @@
     for n in range(384 // step):
         part = left[pl.ds(pl.multiple_of(half * 384 + n * step, step), step), :]
         picked = jnp.dot(part, chosen[...], preferred_element_type=F32)
-        term = lax.dot_general(part * plain[...], weight[...], NT, preferred_element_type=F32) * scale[...]
+        term = lax.dot_general(part * plain[...], weight[...], NT, preferred_element_type=F32)
+        term = term * factors[0:1, :]
         for k in range(OUTL):
-            term = term + picked[:, k : k + 1] * extra[k : k + 1, :]
+            term = term + picked[:, k : k + 1] * factors[k + 1 : k + 2, :]
         put(acc, slice(n * step, n * step + step), term)
     for d in range(4):
         owners = []
@@ -512,6 +513,12 @@
         compiler_params=params(8),
         name="collect",
     )(mine, from1, from2, from3)
+    middle = lax.dynamic_slice(middle_outliers, (me_x * OUTL,), (OUTL,))
+    chosen = jnp.arange(columns, dtype=jnp.int32)[:, None] == middle[None, :]
+    plain = jnp.where(jnp.any(chosen, axis=1), 0.0, 1.0).astype(BF)[None]
+    chosen = jnp.pad(chosen.astype(BF), ((0, 0), (0, 128 - OUTL)))
+    factors = jnp.concatenate([output_scale[None], output_float])
+    summed, chosen, plain, factors = lax.optimization_barrier((summed, chosen, plain, factors))
     queries = lax.all_to_all(summed, "gx", split_axis=0, concat_axis=0, tiled=True)
 
     positions = (lengths[:, None] + jnp.arange(NEW, dtype=jnp.int32)[None, :]).reshape(6, 1)
@@ -542,7 +549,7 @@
             pltpu.VMEM((requests, window, cached), BF),
             pltpu.SemaphoreType.DMA((requests, window // CHUNK, 2)),
         ],
-        compiler_params=params(57),
+        compiler_params=params(55),
         name="attention",
     )(lengths, queries, pair_sums, cosine, sine, key_cache, value_cache)
 
@@ -557,16 +564,12 @@
     blocks = [mine] + [lax.ppermute(mine, "gy", over_y(d)) for d in (1, 2, 3)]
     blocks = blocks + [lax.ppermute(b, "gy", SIBLING) for b in blocks]
 
-    middle = lax.dynamic_slice(middle_outliers, (me_x * OUTL,), (OUTL,))
-    chosen = jnp.arange(columns, dtype=jnp.int32)[:, None] == middle[None, :]
-    plain = jnp.where(jnp.any(chosen, axis=1), 0.0, 1.0).astype(BF)[None]
-    chosen = jnp.pad(chosen.astype(BF), ((0, 0), (0, 128 - OUTL)))
     half_rows = block_rows // 2
 
     def project(sending):
         return pl.pallas_call(
             functools.partial(output_kernel, sending),
-            in_specs=[vmem] * 13,
+            in_specs=[vmem] * 12,
             out_specs=vmem,
             out_shape=jax.ShapeDtypeStruct((4, 4 * half_rows, out_columns), BF),
             scratch_shapes=[
@@ -575,7 +578,7 @@
             ],
             compiler_params=params(24),
             name="output_sent" if sending else "output_kept",
-        )(*blocks, chosen, plain, output_scale[None], output_float, output_int.T)
+        )(*blocks, chosen, plain, factors, output_int.T)
 
     other = lax.ppermute(project(True), "gy", SIBLING)
     kept = project(False)

time: 159 us -> 169 us (1.063)
  blocking collectives: 18.6 us -> 34.3 us
  local copies, waits for them, and re-layouts: 7.16 us -> 12.8 us
  waiting for transfers between devices: 53.2 us -> 48 us
  starting transfers between devices: 47 us -> 42.8 us
    all_to_all x0 -> x1, blocking collectives: none -> 15.7 us  [on_device(): lax.all_to_all(attended, 'gx', split_axis=0, concat_axis=0, tiled=True)]
    all_to_all x1 -> x0, waiting for transfers between devices: 6.08 us -> none  [on_device(): lax.all_to_all(attended, 'gx', split_axis=0, concat_axis=0, tiled=True)]
    unnamed x32 -> x38, local copies, waits for them, and re-layouts: 4.14 us -> 7.95 us
    all_to_all x1 -> x0, starting transfers between devices: 3.54 us -> none  [on_device(): lax.all_to_all(attended, 'gx', split_axis=0, concat_axis=0, tiled=True)]
    pallas_call x1, Pallas kernels: 9.64 us -> 6.23 us  [on_device(): pl.pallas_call(attend_kernel, in_specs=[smem, vmem, vmem, vmem, vmem, hbm...]
    squeeze x4, local copies, waits for them, and re-layouts: 0.11 us -> 3.11 us  [on_device(): others = [lax.ppermute(block[1], 'gy', SIBLING) for block in arrived]]
    pallas_call x1, Pallas kernels: 5.64 us -> 7.69 us  [on_device(): pl.pallas_call(query_kernel, grid=(1,), in_specs=[whole((1, 96, padded))]...]
  transfers between devices with their start and end apart: 33 -> 32, of which waited for: 18 -> 19; matrix products, arithmetic and copies ran while one was open for 3% -> 4% of each run, Pallas kernels for 4% -> 3%
where the time goes in v8:
time: 169 us
  waiting for transfers between devices  48 us (28%)
  starting transfers between devices  42.8 us (25%)
  blocking collectives  34.3 us (20%)
  Pallas kernels  28 us (17%)
  local copies, waits for them, and re-layouts  12.8 us (8%)
  other arithmetic  2.56 us (2%)
    all_to_all x1, blocking collectives, on_device(): lax.all_to_all(sums, plane, split_axis=0, concat_axis=0, tiled=True, axis...  18.6 us
    ppermute x3, waiting for transfers between devices, on_device(): lax.ppermute(jnp.stack([kept[d], other[d]]), plane, shift_plane(False, d))  16.8 us
    all_to_all x1, blocking collectives, on_device(): lax.all_to_all(attended, 'gx', split_axis=0, concat_axis=0, tiled=True)  15.7 us
    ppermute x4, starting transfers between devices, on_device(): blocks = blocks + [lax.ppermute(b, 'gy', SIBLING) for b in blocks]  8.72 us
    pallas_call x2, Pallas kernels, project(): pl.pallas_call(functools.partial(output_kernel, sending), in_specs=[vmem]...  8.6 us
    unnamed x38, local copies, waits for them, and re-layouts  7.95 us
    pallas_call x1, Pallas kernels, on_device(): pl.pallas_call(query_kernel, grid=(1,), in_specs=[whole((1, 96, padded))]...  7.69 us
    pallas_call x1, Pallas kernels, on_device(): pl.pallas_call(attend_kernel, in_specs=[smem, vmem, vmem, vmem, vmem, hbm...  6.23 us
  transfers between devices with their start and end apart: 32, of which 19 were waited for; matrix products, arithmetic and copies ran while one was open for 4% of the time, Pallas kernels for 3%

profile of v8, /device:TPU:1, one launch (start us, length us, event | category | flops | bytes accessed | tf_op | source)
XLA Modules:
  0.0 168.8 jit_solution(4495452442852327560)
XLA Ops:
  0.0 0.9 copy-done.5
  1.6 1.8 %prepare.1 = (bf16[48,1920]{1,0:T(8,128)(2,1)S(1)}, bf16[24,1920]{1,0:T(8,128)(2,1)S(1)}, bf16[24,1920]{1,0:T(8,128)(2,1)S(1)}) custom-call(s32[4]{0:T(128)S(1)} %copy-done.9, bf16[48,1856]{1,0:T(8,128)(2,1)S(1)} %copy-done.5), custom_call_target="tpu_custom_call" | custom-call | tf_op jit(solution)/shard_map/prepare/pallas_call | solution.py:439
  3.4 1.5 collective-permute-start
  4.9 0.9 collective-permute-done
  5.9 1.8 %collective-permute-start.1 = (bf16[2,24,1920]{2,1,0:T(8,128)(2,1)S(1)}, bf16[2,24,1920]{2,1,0:T(8,128)(2,1)S(1)}, u32[]{:S(2)}, u32[]{:S(2)}) collective-permute-start(bf16[2,24,1920]{2,1,0:T(8,128)(2,1)S(1)} %pad_maximum_fusion.4), channel_id=1, source_target_pairs={{0,8},{1,33},{2,10},{3,35},{4,12},{5,37},{6,14},{7,39},{8,16},{9,4... | collective-permute-start | bytes 552968 | tf_op jit(solution)/shard_map/ppermute | solution.py:454
  7.7 2.2 %collective-permute-start.2 = (bf16[2,24,1920]{2,1,0:T(8,128)(2,1)S(1)}, bf16[2,24,1920]{2,1,0:T(8,128)(2,1)S(1)}, u32[]{:S(2)}, u32[]{:S(2)}) collective-permute-start(bf16[2,24,1920]{2,1,0:T(8,128)(2,1)S(1)} %pad_maximum_fusion.4), channel_id=1, source_target_pairs={{0,24},{1,97},{2,26},{3,99},{4,28},{5,101},{6,30},{7,103},{8,0},{9... | collective-permute-start | bytes 552968 | tf_op jit(solution)/shard_map/ppermute | solution.py:454
  9.9 1.2 collective-permute-start.3
  11.1 1.6 collective-permute-done.1
  12.7 3.4 %collective-permute-done.3 = bf16[2,24,1920]{2,1,0:T(8,128)(2,1)S(1)} collective-permute-done((bf16[2,24,1920]{2,1,0:T(8,128)(2,1)S(1)}, bf16[2,24,1920]{2,1,0:T(8,128)(2,1)S(1)}, u32[]{:S(2)}, u32[]{:S(2)}) %collective-permute-start.3) | collective-permute-done | bytes 184352 | tf_op jit(solution)/shard_map/ppermute | solution.py:454
  16.2 1.0 collective-permute-start.4
  17.2 1.8 %collective-permute-start.5 = (bf16[2,96,1920]{2,1,0:T(8,128)(2,1)S(1)}, bf16[2,96,1920]{2,1,0:T(8,128)(2,1)S(1)}, u32[]{:S(2)}, u32[]{:S(2)}) collective-permute-start(bf16[2,96,1920]{2,1,0:T(8,128)(2,1)S(1)} %pad_maximum_fusion.both.a0), channel_id=1, source_target_pairs={{0,96},{1,25},{2,98},{3,27},{4,100},{5,29},{6,102},{7,31},{8,104},... | collective-permute-start | bytes 2211848 | tf_op jit(solution)/shard_map/ppermute | solution.py:456
  19.0 1.2 collective-permute-start.6
  20.5 18.6 %all_to_all.15 = f32[16,2,96]{2,1,0:T(2,128)S(1)} all-to-all(f32[16,2,96]{2,1,0:T(2,128)S(1)} %row_sums.1), channel_id=1, replica_groups={{0,2,4,6,32,34,36,38,64,66,68,70,96,98,100,102},{8,10,12,14,40,42,44,46..., dimensions={0} | all-to-all | bytes 24576 | tf_op jit(solution)/shard_map/all_to_all | solution.py:463
  45.8 0.9 select_reduce_fusion
  46.8 2.1 %copy-done.1 = bf16[1856,1024]{1,0:T(8,128)(2,1)S(1)} copy-done((bf16[1856,1024]{1,0:T(8,128)(2,1)S(1)}, bf16[1856,1024]{1,0:T(8,128)(2,1)}, u32[]{:S(2)}) %copy-start.1) | copy-done | bytes 3801112
  48.9 1.0 pair_projection.1.pairs
  49.9 0.9 copy-done.2
  50.8 7.7 %query_projection.1 = (bf16[4,112,896]{2,1,0:T(8,128)(2,1)S(1)}, bf16[4,112,896]{2,1,0:T(8,128)(2,1)}) custom-call(bf16[2,96,1920]{2,1,0:T(8,128)(2,1)S(1)} %pad_maximum_fusion.both.a0, bf16[2,96,1920]{2,1,0:T(8,128)(2,1)S(1)} %collective-permute-done.4.a1, bf16[2,96,1920]{2,1,0:T(8,128)(2,1)S(1)} %collective-permute-done.6.a2, ...), custom_call_target="tpu_custom_call" | custom-call | tf_op jit(solution)/shard_map/query_projection/pallas_call | solution.py:485
  58.5 0.9 copy-done.3
  60.3 1.7 collective-permute-done.12.received
  61.9 1.1 copy-done.4
  63.2 1.4 collective-permute-start.13
  64.6 2.6 %collective-permute-start.14 = (bf16[112,896]{1,0:T(8,128)(2,1)S(1)}, bf16[112,896]{1,0:T(8,128)(2,1)S(1)}, u32[]{:S(2)}, u32[]{:S(2)}) collective-permute-start(bf16[112,896]{1,0:T(8,128)(2,1)S(1)} %get-tuple-element.45), channel_id=1, source_target_pairs={{0,4},{1,5},{2,6},{3,7},{4,0},{5,1},{6,2},{7,3},{8,12},{9,13},{10,... | collective-permute-start | bytes 602120 | tf_op jit(solution)/shard_map/ppermute | solution.py:505
  67.2 1.1 collective-permute-start.15
  68.3 2.6 %collective-permute-done.13.b = bf16[112,896]{1,0:T(8,128)(2,1)S(1)} collective-permute-done((bf16[112,896]{1,0:T(8,128)(2,1)S(1)}, bf16[112,896]{1,0:T(8,128)(2,1)S(1)}, u32[]{:S(2)}, u32[]{:S(2)}) %collective-permute-start.13) | collective-permute-done | bytes 200736 | tf_op jit(solution)/shard_map/ppermute | solution.py:503
  70.9 5.4 %collective-permute-done.14.c = bf16[112,896]{1,0:T(8,128)(2,1)S(1)} collective-permute-done((bf16[112,896]{1,0:T(8,128)(2,1)S(1)}, bf16[112,896]{1,0:T(8,128)(2,1)S(1)}, u32[]{:S(2)}, u32[]{:S(2)}) %collective-permute-start.14) | collective-permute-done | bytes 200736 | tf_op jit(solution)/shard_map/ppermute | solution.py:505
  76.3 0.9 collect.1
  77.9 4.3 %all-to-all-start.1 = ((bf16[16,6,896]{2,1,0:T(8,128)(2,1)}), bf16[16,6,896]{2,1,0:T(8,128)(2,1)S(1)}, u32[]{:S(2)}, u32[]{:S(2)}) async-start(bf16[16,6,896]{2,1,0:T(8,128)(2,1)} %get-tuple-element.48), calls=%async_computation.1 | async-start | bytes 458752 | tf_op jit(solution)/shard_map/all_to_all | solution.py:522
  83.7 5.9 %all-to-all-done.1.queries = bf16[16,6,896]{2,1,0:T(8,128)(2,1)S(1)} async-done(((bf16[16,6,896]{2,1,0:T(8,128)(2,1)}), bf16[16,6,896]{2,1,0:T(8,128)(2,1)S(1)}, u32[]{:S(2)}, u32[]{:S(2)}) %all-to-all-start.1) | async-done | bytes 172064 | tf_op jit(solution)/shard_map/all_to_all | solution.py:522
  90.2 6.2 %attention.1 = bf16[16,6,896]{2,1,0:T(8,128)(2,1)} custom-call(s32[3]{0:T(128)} %lengths.1, bf16[16,6,896]{2,1,0:T(8,128)(2,1)} %copy-done.12, f32[16,512]{1,0:T(8,128)} %copy-done.6, f32[8,128]{1,0:T(8,128)} %pad.16.cosine, f32[8,128]{1,0:T(8,128)} %select_maximum_fusion.sine, bf16[3,2048,512]{2,1,0:T(8,128)(2,1)} %keys.1, bf16[3,2048,512]{2,1,0:T(8,128)(2,1)} %values.1), custom_call_target="tpu_custom_call" | custom-call | tf_op jit(solution)/shard_map/attention/pallas_call | solution.py:535
  96.5 15.7 %all_to_all.16.block = bf16[16,6,896]{2,1,0:T(8,128)(2,1)S(1)} all-to-all(bf16[16,6,896]{2,1,0:T(8,128)(2,1)} %attention.1), channel_id=1, replica_groups=mesh['gx'=16,'gy'=8] {'gx'}, dimensions={0} | all-to-all | bytes 344064 | tf_op jit(solution)/shard_map/all_to_all | solution.py:556
  112.4 1.5 collective-permute-start.17
  113.8 1.2 collective-permute-start.18
  115.0 4.9 %collective-permute-start.19 = (bf16[96,896]{1,0:T(8,128)(2,1)S(1)}, bf16[96,896]{1,0:T(8,128)(2,1)S(1)}, u32[]{:S(2)}, u32[]{:S(2)}) collective-permute-start(bf16[96,896]{1,0:T(8,128)(2,1)S(1)} %repack.1.b0), channel_id=1, source_target_pairs={{0,1},{1,0},{2,3},{3,2},{4,5},{5,4},{6,7},{7,6},{8,9},{9,8},{10,11... | collective-permute-start | bytes 516104 | tf_op jit(solution)/shard_map/ppermute | solution.py:565
  120.8 3.2 %collective-permute-start.20 = (bf16[96,896]{1,0:T(8,128)(2,1)S(1)}, bf16[96,896]{1,0:T(8,128)(2,1)S(1)}, u32[]{:S(2)}, u32[]{:S(2)}) collective-permute-start(bf16[96,896]{1,0:T(8,128)(2,1)S(1)} %collective-permute-done.16.b1), channel_id=1, source_target_pairs={{0,1},{1,0},{2,3},{3,2},{4,5},{5,4},{6,7},{7,6},{8,9},{9,8},{10,11... | collective-permute-start | bytes 516104 | tf_op jit(solution)/shard_map/ppermute | solution.py:565
  125.8 4.3 %output_sent.1 = bf16[4,96,1856]{2,1,0:T(8,128)(2,1)S(1)} custom-call(bf16[96,896]{1,0:T(8,128)(2,1)S(1)} %repack.1.b0, bf16[96,896]{1,0:T(8,128)(2,1)S(1)} %collective-permute-done.16.b1, bf16[96,896]{1,0:T(8,128)(2,1)S(1)} %collective-permute-done.17.b2, bf16[96,896]{1,0:T(8,128)(2,1)S(1)} %collective-permute-done.18.b3, ...), custom_call_target="tpu_custom_call" | custom-call | tf_op jit(solution)/shard_map/output_sent/pallas_call | solution.py:570
  130.5 4.3 %output_kept.1.mine = bf16[4,96,1856]{2,1,0:T(8,128)(2,1)S(1)} custom-call(bf16[96,896]{1,0:T(8,128)(2,1)S(1)} %repack.1.b0, bf16[96,896]{1,0:T(8,128)(2,1)S(1)} %collective-permute-done.16.b1, bf16[96,896]{1,0:T(8,128)(2,1)S(1)} %collective-permute-done.17.b2, bf16[96,896]{1,0:T(8,128)(2,1)S(1)} %collective-permute-done.18.b3, ...), custom_call_target="tpu_custom_call" | custom-call | tf_op jit(solution)/shard_map/output_kept/pallas_call | solution.py:570
  135.1 1.0 collective-permute-start.26
  136.2 2.0 %collective-permute-start.25 = (bf16[2,96,1856]{2,1,0:T(8,128)(2,1)S(1)}, bf16[2,96,1856]{2,1,0:T(8,128)(2,1)S(1)}, u32[]{:S(2)}, u32[]{:S(2)}) collective-permute-start(bf16[2,96,1856]{2,1,0:T(8,128)(2,1)S(1)} %pad_maximum_fusion.2), channel_id=1, source_target_pairs={{0,96},{1,25},{2,98},{3,27},{4,100},{5,29},{6,102},{7,31},{8,104},... | collective-permute-start | bytes 2138120 | tf_op jit(solution)/shard_map/ppermute | solution.py:587
  138.4 8.9 %collective-permute-done.26.r2 = bf16[2,96,1856]{2,1,0:T(8,128)(2,1)S(1)} collective-permute-done((bf16[2,96,1856]{2,1,0:T(8,128)(2,1)S(1)}, bf16[2,96,1856]{2,1,0:T(8,128)(2,1)S(1)}, u32[]{:S(2)}, u32[]{:S(2)}) %collective-permute-start.26) | collective-permute-done | bytes 712736 | tf_op jit(solution)/shard_map/ppermute | solution.py:587
  147.3 6.0 %collective-permute-done.25.r3 = bf16[2,96,1856]{2,1,0:T(8,128)(2,1)S(1)} collective-permute-done((bf16[2,96,1856]{2,1,0:T(8,128)(2,1)S(1)}, bf16[2,96,1856]{2,1,0:T(8,128)(2,1)S(1)}, u32[]{:S(2)}, u32[]{:S(2)}) %collective-permute-start.25) | collective-permute-done | bytes 712736 | tf_op jit(solution)/shard_map/ppermute | solution.py:587
  153.3 1.8 %collective-permute-done.24.r1 = bf16[2,96,1856]{2,1,0:T(8,128)(2,1)S(1)} collective-permute-done((bf16[2,96,1856]{2,1,0:T(8,128)(2,1)S(1)}, bf16[2,96,1856]{2,1,0:T(8,128)(2,1)S(1)}, u32[]{:S(2)}, u32[]{:S(2)}) %collective-permute-start.24) | collective-permute-done | bytes 712736 | tf_op jit(solution)/shard_map/ppermute | solution.py:587
  155.6 2.7 %collective-permute-start.28 = (bf16[2,24,1856]{2,1,0:T(8,128)(2,1)S(1)}, bf16[2,24,1856]{2,1,0:T(8,128)(2,1)S(1)}, u32[]{:S(2)}, u32[]{:S(2)}) collective-permute-start(bf16[2,24,1856]{2,1,0:T(8,128)(2,1)S(1)} %get-tuple-element.55), channel_id=1, source_target_pairs={{0,24},{1,97},{2,26},{3,99},{4,28},{5,101},{6,30},{7,103},{8,0},{9... | collective-permute-start | bytes 534536 | tf_op jit(solution)/shard_map/ppermute | solution.py:599
  158.3 3.2 %collective-permute-done.27.r1 = bf16[2,24,1856]{2,1,0:T(8,128)(2,1)S(1)} collective-permute-done((bf16[2,24,1856]{2,1,0:T(8,128)(2,1)S(1)}, bf16[2,24,1856]{2,1,0:T(8,128)(2,1)S(1)}, u32[]{:S(2)}, u32[]{:S(2)}) %collective-permute-start.27) | collective-permute-done | bytes 178208 | tf_op jit(solution)/shard_map/ppermute | solution.py:599
  161.5 1.2 collective-permute-done.28.r3
  162.7 1.4 collective-permute-done.29.r2
  164.3 2.8 %collective-permute-start.30 = (bf16[24,1856]{1,0:T(8,128)(2,1)S(1)}, bf16[24,1856]{1,0:T(8,128)(2,1)S(1)}, u32[]{:S(2)}, u32[]{:S(2)}) collective-permute-start(bf16[24,1856]{1,0:T(8,128)(2,1)S(1)} %get-tuple-element.58), channel_id=1, source_target_pairs={{0,1},{1,0},{2,3},{3,2},{4,5},{5,4},{6,7},{7,6},{8,9},{9,8},{10,11... | collective-permute-start | bytes 267272 | tf_op jit(solution)/shard_map/ppermute | solution.py:609
  167.1 0.9 collective-permute-done.30.other
  (102 shorter events, 16.4 us)
Async XLA Ops:
  0.0 0.9 copy-start.5
  3.4 2.4 %collective-permute-start = (bf16[24,1920]{1,0:T(8,128)(2,1)S(1)}, bf16[24,1920]{1,0:T(8,128)(2,1)S(1)}, u32[]{:S(2)}, u32[]{:S(2)}) collective-permute-start(bf16[24,1920]{1,0:T(8,128)(2,1)S(1)} %get-tuple-element.33), channel_id=1, source_target_pairs={{0,1},{1,0},{2,3},{3,2},{4,5},{5,4},{6,7},{7,6},{8,9},{9,8},{10,11... | collective-permute-start | bytes 276488 | tf_op jit(solution)/shard_map/ppermute | solution.py:452
  5.9 6.8 %collective-permute-start.1 = (bf16[2,24,1920]{2,1,0:T(8,128)(2,1)S(1)}, bf16[2,24,1920]{2,1,0:T(8,128)(2,1)S(1)}, u32[]{:S(2)}, u32[]{:S(2)}) collective-permute-start(bf16[2,24,1920]{2,1,0:T(8,128)(2,1)S(1)} %pad_maximum_fusion.4), channel_id=1, source_target_pairs={{0,8},{1,33},{2,10},{3,35},{4,12},{5,37},{6,14},{7,39},{8,16},{9,4... | collective-permute-start | bytes 552968 | tf_op jit(solution)/shard_map/ppermute | solution.py:454
  7.7 5.1 %collective-permute-start.2 = (bf16[2,24,1920]{2,1,0:T(8,128)(2,1)S(1)}, bf16[2,24,1920]{2,1,0:T(8,128)(2,1)S(1)}, u32[]{:S(2)}, u32[]{:S(2)}) collective-permute-start(bf16[2,24,1920]{2,1,0:T(8,128)(2,1)S(1)} %pad_maximum_fusion.4), channel_id=1, source_target_pairs={{0,24},{1,97},{2,26},{3,99},{4,28},{5,101},{6,30},{7,103},{8,0},{9... | collective-permute-start | bytes 552968 | tf_op jit(solution)/shard_map/ppermute | solution.py:454
  9.9 6.3 %collective-permute-start.3 = (bf16[2,24,1920]{2,1,0:T(8,128)(2,1)S(1)}, bf16[2,24,1920]{2,1,0:T(8,128)(2,1)S(1)}, u32[]{:S(2)}, u32[]{:S(2)}) collective-permute-start(bf16[2,24,1920]{2,1,0:T(8,128)(2,1)S(1)} %pad_maximum_fusion.4), channel_id=1, source_target_pairs={{0,16},{1,65},{2,18},{3,67},{4,20},{5,69},{6,22},{7,71},{8,24},{9,... | collective-permute-start | bytes 552968 | tf_op jit(solution)/shard_map/ppermute | solution.py:454
  16.2 24.5 %collective-permute-start.4 = (bf16[2,96,1920]{2,1,0:T(8,128)(2,1)S(1)}, bf16[2,96,1920]{2,1,0:T(8,128)(2,1)S(1)}, u32[]{:S(2)}, u32[]{:S(2)}) collective-permute-start(bf16[2,96,1920]{2,1,0:T(8,128)(2,1)S(1)} %pad_maximum_fusion.both.a0), channel_id=1, source_target_pairs={{0,32},{1,9},{2,34},{3,11},{4,36},{5,13},{6,38},{7,15},{8,40},{9,1... | collective-permute-start | bytes 2211848 | tf_op jit(solution)/shard_map/ppermute | solution.py:456
  17.2 23.5 %collective-permute-start.5 = (bf16[2,96,1920]{2,1,0:T(8,128)(2,1)S(1)}, bf16[2,96,1920]{2,1,0:T(8,128)(2,1)S(1)}, u32[]{:S(2)}, u32[]{:S(2)}) collective-permute-start(bf16[2,96,1920]{2,1,0:T(8,128)(2,1)S(1)} %pad_maximum_fusion.both.a0), channel_id=1, source_target_pairs={{0,96},{1,25},{2,98},{3,27},{4,100},{5,29},{6,102},{7,31},{8,104},... | collective-permute-start | bytes 2211848 | tf_op jit(solution)/shard_map/ppermute | solution.py:456
  19.0 21.8 %collective-permute-start.6 = (bf16[2,96,1920]{2,1,0:T(8,128)(2,1)S(1)}, bf16[2,96,1920]{2,1,0:T(8,128)(2,1)S(1)}, u32[]{:S(2)}, u32[]{:S(2)}) collective-permute-start(bf16[2,96,1920]{2,1,0:T(8,128)(2,1)S(1)} %pad_maximum_fusion.both.a0), channel_id=1, source_target_pairs={{0,64},{1,17},{2,66},{3,19},{4,68},{5,21},{6,70},{7,23},{8,72},{9,... | collective-permute-start | bytes 2211848 | tf_op jit(solution)/shard_map/ppermute | solution.py:456
  39.1 5.8 %copy-start.10 = (s32[4]{0:T(128)S(1)}, s32[4]{0:T(128)}, u32[]{:S(2)}) copy-start(s32[4]{0:T(128)} %positions.1) | copy-start | bytes 52
  39.1 5.9 %copy-start.13 = (f32[1856]{0:T(1024)S(1)}, f32[1856]{0:T(1024)}, u32[]{:S(2)}) copy-start(f32[1856]{0:T(1024)} %param.19) | copy-start | bytes 22276
  39.1 5.9 %copy-start.14 = (f32[1856]{0:T(1024)S(1)}, f32[1856]{0:T(1024)}, u32[]{:S(2)}) copy-start(f32[1856]{0:T(1024)} %param.18) | copy-start | bytes 22276
  39.1 5.9 %copy-start.17 = (f32[896]{0:T(1024)S(1)}, f32[896]{0:T(1024)}, u32[]{:S(2)}) copy-start(f32[896]{0:T(1024)} %param.22) | copy-start | bytes 10756
  39.2 7.6 %copy-start.7 = (f32[4,1024]{1,0:T(4,128)S(1)}, f32[4,1024]{1,0:T(4,128)}, u32[]{:S(2)}) copy-start(f32[4,1024]{1,0:T(4,128)} %extra.2) | copy-start | bytes 49156
  39.2 7.6 %copy-start.11 = (f32[1024]{0:T(1024)S(1)}, f32[1024]{0:T(1024)}, u32[]{:S(2)}) copy-start(f32[1024]{0:T(1024)} %param.24) | copy-start | bytes 12292
  39.2 1.6 collective-permute-start.7
  41.5 8.3 %collective-permute-start.10 = (bf16[96,1920]{1,0:T(8,128)(2,1)}, bf16[96,1920]{1,0:T(8,128)(2,1)S(1)}, u32[]{:S(2)}, u32[]{:S(2)}) collective-permute-start(bf16[96,1920]{1,0:T(8,128)(2,1)} %slice_bitcast_fusion.1), channel_id=1, source_target_pairs={{0,1},{1,0},{2,3},{3,2},{4,5},{5,4},{6,7},{7,6},{8,9},{9,8},{10,11... | collective-permute-start | bytes 1105928 | tf_op jit(solution)/shard_map/ppermute | solution.py:480
  42.7 7.2 %collective-permute-start.11 = (bf16[96,1920]{1,0:T(8,128)(2,1)}, bf16[96,1920]{1,0:T(8,128)(2,1)}, u32[]{:S(2)}, u32[]{:S(2)}) collective-permute-start(bf16[96,1920]{1,0:T(8,128)(2,1)} %slice_bitcast_fusion), channel_id=1, source_target_pairs={{0,1},{1,0},{2,3},{3,2},{4,5},{5,4},{6,7},{7,6},{8,9},{9,8},{10,11... | collective-permute-start | bytes 1105928 | tf_op jit(solution)/shard_map/ppermute | solution.py:480
  43.6 6.3 %collective-permute-start.8 = (bf16[96,1920]{1,0:T(8,128)(2,1)}, bf16[96,1920]{1,0:T(8,128)(2,1)}, u32[]{:S(2)}, u32[]{:S(2)}) collective-permute-start(bf16[96,1920]{1,0:T(8,128)(2,1)} %slice_bitcast_fusion.3), channel_id=1, source_target_pairs={{0,1},{1,0},{2,3},{3,2},{4,5},{5,4},{6,7},{7,6},{8,9},{9,8},{10,11... | collective-permute-start | bytes 1105928 | tf_op jit(solution)/shard_map/ppermute | solution.py:480
  44.7 5.2 %collective-permute-start.9 = (bf16[96,1920]{1,0:T(8,128)(2,1)}, bf16[96,1920]{1,0:T(8,128)(2,1)}, u32[]{:S(2)}, u32[]{:S(2)}) collective-permute-start(bf16[96,1920]{1,0:T(8,128)(2,1)} %slice_bitcast_fusion.2), channel_id=1, source_target_pairs={{0,1},{1,0},{2,3},{3,2},{4,5},{5,4},{6,7},{7,6},{8,9},{9,8},{10,11... | collective-permute-start | bytes 1105928 | tf_op jit(solution)/shard_map/ppermute | solution.py:480
  46.8 2.1 %copy-start.1 = (bf16[1856,1024]{1,0:T(8,128)(2,1)S(1)}, bf16[1856,1024]{1,0:T(8,128)(2,1)}, u32[]{:S(2)}) copy-start(bf16[1856,1024]{1,0:T(8,128)(2,1)} %weight.2) | copy-start | bytes 11403268
  48.9 1.9 %copy-start.2 = (bf16[1856,896]{1,0:T(8,128)(2,1)S(1)}, bf16[1856,896]{1,0:T(8,128)(2,1)}, u32[]{:S(2)}) copy-start(bf16[1856,896]{1,0:T(8,128)(2,1)} %weight.3) | copy-start | bytes 9977860
  48.9 1.9 %copy-start.8 = (f32[4,896]{1,0:T(4,128)S(1)}, f32[4,896]{1,0:T(4,128)}, u32[]{:S(2)}) copy-start(f32[4,896]{1,0:T(4,128)} %extra.3) | copy-start | bytes 43012
  49.8 10.1 %copy-start.16 = (f32[1856]{0:T(1024)S(1)}, f32[1856]{0:T(1024)}, u32[]{:S(2)}) copy-start(f32[1856]{0:T(1024)} %param.32) | copy-start | bytes 22276
  49.8 10.2 %copy-start.18 = (s32[3]{0:T(128)S(1)}, s32[3]{0:T(128)}, u32[]{:S(2)}) copy-start(s32[3]{0:T(128)} %lengths.1) | copy-start | bytes 40
  58.5 0.9 copy-start.3
  59.4 8.9 %copy-start.15 = (f32[4,1856]{1,0:T(4,128)S(1)}, f32[4,1856]{1,0:T(4,128)}, u32[]{:S(2)}) copy-start(f32[4,1856]{1,0:T(4,128)} %param.33) | copy-start | bytes 89092
  59.4 2.5 %collective-permute-start.12 = (bf16[4,112,896]{2,1,0:T(8,128)(2,1)}, bf16[4,112,896]{2,1,0:T(8,128)(2,1)S(1)}, u32[]{:S(2)}, u32[]{:S(2)}) collective-permute-start(bf16[4,112,896]{2,1,0:T(8,128)(2,1)} %get-tuple-element.42), channel_id=1, source_target_pairs={{0,1},{1,0},{2,3},{3,2},{4,5},{5,4},{6,7},{7,6},{8,9},{9,8},{10,11... | collective-permute-start | bytes 2408456 | tf_op jit(solution)/shard_map/ppermute | solution.py:498
  61.9 1.1 copy-start.4
  63.2 7.7 %collective-permute-start.13 = (bf16[112,896]{1,0:T(8,128)(2,1)S(1)}, bf16[112,896]{1,0:T(8,128)(2,1)S(1)}, u32[]{:S(2)}, u32[]{:S(2)}) collective-permute-start(bf16[112,896]{1,0:T(8,128)(2,1)S(1)} %get-tuple-element.44), channel_id=1, source_target_pairs={{0,2},{1,3},{2,4},{3,5},{4,6},{5,7},{6,0},{7,1},{8,10},{9,11},{10,... | collective-permute-start | bytes 602120 | tf_op jit(solution)/shard_map/ppermute | solution.py:503
  64.6 11.7 %collective-permute-start.14 = (bf16[112,896]{1,0:T(8,128)(2,1)S(1)}, bf16[112,896]{1,0:T(8,128)(2,1)S(1)}, u32[]{:S(2)}, u32[]{:S(2)}) collective-permute-start(bf16[112,896]{1,0:T(8,128)(2,1)S(1)} %get-tuple-element.45), channel_id=1, source_target_pairs={{0,4},{1,5},{2,6},{3,7},{4,0},{5,1},{6,2},{7,3},{8,12},{9,13},{10,... | collective-permute-start | bytes 602120 | tf_op jit(solution)/shard_map/ppermute | solution.py:505
  67.2 9.1 %collective-permute-start.15 = (bf16[112,896]{1,0:T(8,128)(2,1)S(1)}, bf16[112,896]{1,0:T(8,128)(2,1)S(1)}, u32[]{:S(2)}, u32[]{:S(2)}) collective-permute-start(bf16[112,896]{1,0:T(8,128)(2,1)S(1)} %get-tuple-element.46), channel_id=1, source_target_pairs={{0,6},{1,7},{2,0},{3,1},{4,2},{5,3},{6,4},{7,5},{8,14},{9,15},{10,... | collective-permute-start | bytes 602120 | tf_op jit(solution)/shard_map/ppermute | solution.py:504
  77.9 11.7 %all-to-all-start.1 = ((bf16[16,6,896]{2,1,0:T(8,128)(2,1)}), bf16[16,6,896]{2,1,0:T(8,128)(2,1)S(1)}, u32[]{:S(2)}, u32[]{:S(2)}) async-start(bf16[16,6,896]{2,1,0:T(8,128)(2,1)} %get-tuple-element.48), calls=%async_computation.1 | async-start | bytes 458752 | tf_op jit(solution)/shard_map/all_to_all | solution.py:522
  90.2 35.5 %copy-start = (bf16[896,1856]{0,1:T(8,128)(2,1)S(1)}, bf16[896,1856]{0,1:T(8,128)(2,1)}, u32[]{:S(2)}) copy-start(bf16[896,1856]{0,1:T(8,128)(2,1)} %param.31) | copy-start | bytes 9977860
  112.3 8.6 %collective-permute-start.16 = (bf16[96,896]{1,0:T(8,128)(2,1)S(1)}, bf16[96,896]{1,0:T(8,128)(2,1)S(1)}, u32[]{:S(2)}, u32[]{:S(2)}) collective-permute-start(bf16[96,896]{1,0:T(8,128)(2,1)S(1)} %repack.1.b0), channel_id=1, source_target_pairs={{0,2},{1,3},{2,4},{3,5},{4,6},{5,7},{6,0},{7,1},{8,10},{9,11},{10,... | collective-permute-start | bytes 516104 | tf_op jit(solution)/shard_map/ppermute | solution.py:564
  112.4 11.7 %collective-permute-start.17 = (bf16[96,896]{1,0:T(8,128)(2,1)S(1)}, bf16[96,896]{1,0:T(8,128)(2,1)S(1)}, u32[]{:S(2)}, u32[]{:S(2)}) collective-permute-start(bf16[96,896]{1,0:T(8,128)(2,1)S(1)} %repack.1.b0), channel_id=1, source_target_pairs={{0,4},{1,5},{2,6},{3,7},{4,0},{5,1},{6,2},{7,3},{8,12},{9,13},{10,... | collective-permute-start | bytes 516104 | tf_op jit(solution)/shard_map/ppermute | solution.py:564
  113.8 10.2 %collective-permute-start.18 = (bf16[96,896]{1,0:T(8,128)(2,1)S(1)}, bf16[96,896]{1,0:T(8,128)(2,1)S(1)}, u32[]{:S(2)}, u32[]{:S(2)}) collective-permute-start(bf16[96,896]{1,0:T(8,128)(2,1)S(1)} %repack.1.b0), channel_id=1, source_target_pairs={{0,6},{1,7},{2,0},{3,1},{4,2},{5,3},{6,4},{7,5},{8,14},{9,15},{10,... | collective-permute-start | bytes 516104 | tf_op jit(solution)/shard_map/ppermute | solution.py:564
  115.0 9.6 %collective-permute-start.19 = (bf16[96,896]{1,0:T(8,128)(2,1)S(1)}, bf16[96,896]{1,0:T(8,128)(2,1)S(1)}, u32[]{:S(2)}, u32[]{:S(2)}) collective-permute-start(bf16[96,896]{1,0:T(8,128)(2,1)S(1)} %repack.1.b0), channel_id=1, source_target_pairs={{0,1},{1,0},{2,3},{3,2},{4,5},{5,4},{6,7},{7,6},{8,9},{9,8},{10,11... | collective-permute-start | bytes 516104 | tf_op jit(solution)/shard_map/ppermute | solution.py:565
  120.8 4.2 %collective-permute-start.20 = (bf16[96,896]{1,0:T(8,128)(2,1)S(1)}, bf16[96,896]{1,0:T(8,128)(2,1)S(1)}, u32[]{:S(2)}, u32[]{:S(2)}) collective-permute-start(bf16[96,896]{1,0:T(8,128)(2,1)S(1)} %collective-permute-done.16.b1), channel_id=1, source_target_pairs={{0,1},{1,0},{2,3},{3,2},{4,5},{5,4},{6,7},{7,6},{8,9},{9,8},{10,11... | collective-permute-start | bytes 516104 | tf_op jit(solution)/shard_map/ppermute | solution.py:565
  124.0 1.4 collective-permute-start.21
  124.1 1.7 %collective-permute-start.22 = (bf16[96,896]{1,0:T(8,128)(2,1)S(1)}, bf16[96,896]{1,0:T(8,128)(2,1)S(1)}, u32[]{:S(2)}, u32[]{:S(2)}) collective-permute-start(bf16[96,896]{1,0:T(8,128)(2,1)S(1)} %collective-permute-done.18.b3), channel_id=1, source_target_pairs={{0,1},{1,0},{2,3},{3,2},{4,5},{5,4},{6,7},{7,6},{8,9},{9,8},{10,11... | collective-permute-start | bytes 516104 | tf_op jit(solution)/shard_map/ppermute | solution.py:565
  130.1 4.8 %collective-permute-start.23 = (bf16[4,96,1856]{2,1,0:T(8,128)(2,1)S(1)}, bf16[4,96,1856]{2,1,0:T(8,128)(2,1)S(1)}, u32[]{:S(2)}, u32[]{:S(2)}) collective-permute-start(bf16[4,96,1856]{2,1,0:T(8,128)(2,1)S(1)} %output_sent.1), channel_id=1, source_target_pairs={{0,1},{1,0},{2,3},{3,2},{4,5},{5,4},{6,7},{7,6},{8,9},{9,8},{10,11... | collective-permute-start | bytes 4276232 | tf_op jit(solution)/shard_map/ppermute | solution.py:583
  135.1 12.2 %collective-permute-start.26 = (bf16[2,96,1856]{2,1,0:T(8,128)(2,1)S(1)}, bf16[2,96,1856]{2,1,0:T(8,128)(2,1)S(1)}, u32[]{:S(2)}, u32[]{:S(2)}) collective-permute-start(bf16[2,96,1856]{2,1,0:T(8,128)(2,1)S(1)} %pad_maximum_fusion.3), channel_id=1, source_target_pairs={{0,64},{1,17},{2,66},{3,19},{4,68},{5,21},{6,70},{7,23},{8,72},{9,... | collective-permute-start | bytes 2138120 | tf_op jit(solution)/shard_map/ppermute | solution.py:587
  136.2 17.1 %collective-permute-start.25 = (bf16[2,96,1856]{2,1,0:T(8,128)(2,1)S(1)}, bf16[2,96,1856]{2,1,0:T(8,128)(2,1)S(1)}, u32[]{:S(2)}, u32[]{:S(2)}) collective-permute-start(bf16[2,96,1856]{2,1,0:T(8,128)(2,1)S(1)} %pad_maximum_fusion.2), channel_id=1, source_target_pairs={{0,96},{1,25},{2,98},{3,27},{4,100},{5,29},{6,102},{7,31},{8,104},... | collective-permute-start | bytes 2138120 | tf_op jit(solution)/shard_map/ppermute | solution.py:587
  138.3 16.9 %collective-permute-start.24 = (bf16[2,96,1856]{2,1,0:T(8,128)(2,1)S(1)}, bf16[2,96,1856]{2,1,0:T(8,128)(2,1)S(1)}, u32[]{:S(2)}, u32[]{:S(2)}) collective-permute-start(bf16[2,96,1856]{2,1,0:T(8,128)(2,1)S(1)} %pad_maximum_fusion.1), channel_id=1, source_target_pairs={{0,32},{1,9},{2,34},{3,11},{4,36},{5,13},{6,38},{7,15},{8,40},{9,1... | collective-permute-start | bytes 2138120 | tf_op jit(solution)/shard_map/ppermute | solution.py:587
  155.5 6.0 %collective-permute-start.27 = (bf16[2,24,1856]{2,1,0:T(8,128)(2,1)S(1)}, bf16[2,24,1856]{2,1,0:T(8,128)(2,1)S(1)}, u32[]{:S(2)}, u32[]{:S(2)}) collective-permute-start(bf16[2,24,1856]{2,1,0:T(8,128)(2,1)S(1)} %get-tuple-element.54), channel_id=1, source_target_pairs={{0,8},{1,33},{2,10},{3,35},{4,12},{5,37},{6,14},{7,39},{8,16},{9,4... | collective-permute-start | bytes 534536 | tf_op jit(solution)/shard_map/ppermute | solution.py:599
  155.6 7.1 %collective-permute-start.28 = (bf16[2,24,1856]{2,1,0:T(8,128)(2,1)S(1)}, bf16[2,24,1856]{2,1,0:T(8,128)(2,1)S(1)}, u32[]{:S(2)}, u32[]{:S(2)}) collective-permute-start(bf16[2,24,1856]{2,1,0:T(8,128)(2,1)S(1)} %get-tuple-element.55), channel_id=1, source_target_pairs={{0,24},{1,97},{2,26},{3,99},{4,28},{5,101},{6,30},{7,103},{8,0},{9... | collective-permute-start | bytes 534536 | tf_op jit(solution)/shard_map/ppermute | solution.py:599
  158.3 5.9 %collective-permute-start.29 = (bf16[2,24,1856]{2,1,0:T(8,128)(2,1)S(1)}, bf16[2,24,1856]{2,1,0:T(8,128)(2,1)S(1)}, u32[]{:S(2)}, u32[]{:S(2)}) collective-permute-start(bf16[2,24,1856]{2,1,0:T(8,128)(2,1)S(1)} %get-tuple-element.56), channel_id=1, source_target_pairs={{0,16},{1,65},{2,18},{3,67},{4,20},{5,69},{6,22},{7,71},{8,24},{9,... | collective-permute-start | bytes 534536 | tf_op jit(solution)/shard_map/ppermute | solution.py:599
  164.3 3.8 %collective-permute-start.30 = (bf16[24,1856]{1,0:T(8,128)(2,1)S(1)}, bf16[24,1856]{1,0:T(8,128)(2,1)S(1)}, u32[]{:S(2)}, u32[]{:S(2)}) collective-permute-start(bf16[24,1856]{1,0:T(8,128)(2,1)S(1)} %get-tuple-element.58), channel_id=1, source_target_pairs={{0,1},{1,0},{2,3},{3,2},{4,5},{5,4},{6,7},{7,6},{8,9},{9,8},{10,11... | collective-permute-start | bytes 267272 | tf_op jit(solution)/shard_map/ppermute | solution.py:609
  (3 other events, 2.0 us)

commit v9 on v8

--- a/solution.py
+++ b/solution.py
@@ -513,12 +513,6 @@
         compiler_params=params(8),
         name="collect",
     )(mine, from1, from2, from3)
-    middle = lax.dynamic_slice(middle_outliers, (me_x * OUTL,), (OUTL,))
-    chosen = jnp.arange(columns, dtype=jnp.int32)[:, None] == middle[None, :]
-    plain = jnp.where(jnp.any(chosen, axis=1), 0.0, 1.0).astype(BF)[None]
-    chosen = jnp.pad(chosen.astype(BF), ((0, 0), (0, 128 - OUTL)))
-    factors = jnp.concatenate([output_scale[None], output_float])
-    summed, chosen, plain, factors = lax.optimization_barrier((summed, chosen, plain, factors))
     queries = lax.all_to_all(summed, "gx", split_axis=0, concat_axis=0, tiled=True)
 
     positions = (lengths[:, None] + jnp.arange(NEW, dtype=jnp.int32)[None, :]).reshape(6, 1)
@@ -549,11 +543,17 @@
             pltpu.VMEM((requests, window, cached), BF),
             pltpu.SemaphoreType.DMA((requests, window // CHUNK, 2)),
         ],
-        compiler_params=params(55),
+        compiler_params=params(57),
         name="attention",
     )(lengths, queries, pair_sums, cosine, sine, key_cache, value_cache)
 
     back = lax.all_to_all(attended, "gx", split_axis=0, concat_axis=0, tiled=True)
+    middle = lax.dynamic_slice(middle_outliers, (me_x * OUTL,), (OUTL,))
+    chosen = jnp.arange(columns, dtype=jnp.int32)[:, None] == middle[None, :]
+    plain = jnp.where(jnp.any(chosen, axis=1), 0.0, 1.0).astype(BF)[None]
+    chosen = jnp.pad(chosen.astype(BF), ((0, 0), (0, 128 - OUTL)))
+    factors = jnp.concatenate([output_scale[None], output_float])
+    back, chosen, plain, factors = lax.optimization_barrier((back, chosen, plain, factors))
     mine = pl.pallas_call(
         repack_kernel,
         out_shape=jax.ShapeDtypeStruct((96, columns), BF),

time: 169 us -> 163 us (0.964)
  blocking collectives: 34.3 us -> 18.6 us
  starting transfers between devices: 42.8 us -> 52.4 us
  local copies, waits for them, and re-layouts: 12.8 us -> 6.65 us
  waiting for transfers between devices: 48 us -> 50.9 us
  other arithmetic: 2.56 us -> 5.11 us
    all_to_all x1 -> x0, blocking collectives: 15.7 us -> none  [on_device(): lax.all_to_all(attended, 'gx', split_axis=0, concat_axis=0, tiled=True)]
    all_to_all x0 -> x1, waiting for transfers between devices: none -> 5.14 us  [on_device(): lax.all_to_all(attended, 'gx', split_axis=0, concat_axis=0, tiled=True)]
    all_to_all x0 -> x1, starting transfers between devices: none -> 4.19 us  [on_device(): lax.all_to_all(attended, 'gx', split_axis=0, concat_axis=0, tiled=True)]
    ppermute x3, starting transfers between devices: 2.74 us -> 6.49 us  [on_device(): blocks = [mine] + [lax.ppermute(mine, 'gy', over_y(d)) for d in (1, 2, 3)]]
    unnamed x38 -> x40, local copies, waits for them, and re-layouts: 7.95 us -> 4.9 us
    squeeze x4, local copies, waits for them, and re-layouts: 3.11 us -> 0.11 us  [on_device(): others = [lax.ppermute(block[1], 'gy', SIBLING) for block in arrived]]
    pallas_call x1, Pallas kernels: 6.23 us -> 8.26 us  [on_device(): pl.pallas_call(attend_kernel, in_specs=[smem, vmem, vmem, vmem, vmem, hbm...]
    pallas_call x1, Pallas kernels: 7.69 us -> 5.68 us  [on_device(): pl.pallas_call(query_kernel, grid=(1,), in_specs=[whole((1, 96, padded))]...]
  transfers between devices with their start and end apart: 32 -> 33, of which waited for: 19 -> 20; matrix products, arithmetic and copies ran while one was open for 4% -> 4% of each run, Pallas kernels for 3% -> 3%
where the time goes in v9:
time: 163 us
  starting transfers between devices  52.4 us (32%)
  waiting for transfers between devices  50.9 us (31%)
  Pallas kernels  29 us (18%)
  blocking collectives  18.6 us (11%)
  local copies, waits for them, and re-layouts  6.65 us (4%)
  other arithmetic  5.11 us (3%)
    all_to_all x1, blocking collectives, on_device(): lax.all_to_all(sums, plane, split_axis=0, concat_axis=0, tiled=True, axis...  18.6 us
    ppermute x3, waiting for transfers between devices, on_device(): lax.ppermute(jnp.stack([kept[d], other[d]]), plane, shift_plane(False, d))  17 us
    ppermute x4, starting transfers between devices, on_device(): blocks = blocks + [lax.ppermute(b, 'gy', SIBLING) for b in blocks]  10.1 us
    pallas_call x2, Pallas kernels, project(): pl.pallas_call(functools.partial(output_kernel, sending), in_specs=[vmem]...  8.59 us
    pallas_call x1, Pallas kernels, on_device(): pl.pallas_call(attend_kernel, in_specs=[smem, vmem, vmem, vmem, vmem, hbm...  8.26 us
    ppermute x3, starting transfers between devices, on_device(): blocks = [mine] + [lax.ppermute(mine, 'gy', over_y(d)) for d in (1, 2, 3)]  6.49 us
    all_to_all x1, waiting for transfers between devices, on_device(): lax.all_to_all(summed, 'gx', split_axis=0, concat_axis=0, tiled=True)  5.9 us
    ppermute x3, waiting for transfers between devices, on_device(): got = [lax.ppermute(sums[f], plane, shift_plane(True, f)) for f in steps]  5.89 us
  transfers between devices with their start and end apart: 33, of which 20 were waited for; matrix products, arithmetic and copies ran while one was open for 4% of the time, Pallas kernels for 3%

profile of v9, /device:TPU:1, one launch (start us, length us, event | category | flops | bytes accessed | tf_op | source)
XLA Modules:
  0.0 163.1 jit_solution(6221798277357164042)
XLA Ops:
  0.0 0.9 copy-done.4
  1.6 1.8 %prepare.1 = (bf16[48,1920]{1,0:T(8,128)(2,1)S(1)}, bf16[24,1920]{1,0:T(8,128)(2,1)S(1)}, bf16[24,1920]{1,0:T(8,128)(2,1)S(1)}) custom-call(s32[4]{0:T(128)S(1)} %copy-done.9, bf16[48,1856]{1,0:T(8,128)(2,1)S(1)} %copy-done.4), custom_call_target="tpu_custom_call" | custom-call | tf_op jit(solution)/shard_map/prepare/pallas_call | solution.py:439
  3.4 1.5 collective-permute-start
  4.9 0.9 collective-permute-done
  5.9 1.8 %collective-permute-start.1 = (bf16[2,24,1920]{2,1,0:T(8,128)(2,1)S(1)}, bf16[2,24,1920]{2,1,0:T(8,128)(2,1)S(1)}, u32[]{:S(2)}, u32[]{:S(2)}) collective-permute-start(bf16[2,24,1920]{2,1,0:T(8,128)(2,1)S(1)} %pad_maximum_fusion.4), channel_id=1, source_target_pairs={{0,8},{1,33},{2,10},{3,35},{4,12},{5,37},{6,14},{7,39},{8,16},{9,4... | collective-permute-start | bytes 552968 | tf_op jit(solution)/shard_map/ppermute | solution.py:454
  7.7 2.2 %collective-permute-start.2 = (bf16[2,24,1920]{2,1,0:T(8,128)(2,1)S(1)}, bf16[2,24,1920]{2,1,0:T(8,128)(2,1)S(1)}, u32[]{:S(2)}, u32[]{:S(2)}) collective-permute-start(bf16[2,24,1920]{2,1,0:T(8,128)(2,1)S(1)} %pad_maximum_fusion.4), channel_id=1, source_target_pairs={{0,24},{1,97},{2,26},{3,99},{4,28},{5,101},{6,30},{7,103},{8,0},{9... | collective-permute-start | bytes 552968 | tf_op jit(solution)/shard_map/ppermute | solution.py:454
  9.9 1.2 collective-permute-start.3
  11.1 1.6 collective-permute-done.1
  12.7 3.4 %collective-permute-done.3 = bf16[2,24,1920]{2,1,0:T(8,128)(2,1)S(1)} collective-permute-done((bf16[2,24,1920]{2,1,0:T(8,128)(2,1)S(1)}, bf16[2,24,1920]{2,1,0:T(8,128)(2,1)S(1)}, u32[]{:S(2)}, u32[]{:S(2)}) %collective-permute-start.3) | collective-permute-done | bytes 184352 | tf_op jit(solution)/shard_map/ppermute | solution.py:454
  16.2 1.0 collective-permute-start.4
  17.2 1.8 %collective-permute-start.5 = (bf16[2,96,1920]{2,1,0:T(8,128)(2,1)S(1)}, bf16[2,96,1920]{2,1,0:T(8,128)(2,1)S(1)}, u32[]{:S(2)}, u32[]{:S(2)}) collective-permute-start(bf16[2,96,1920]{2,1,0:T(8,128)(2,1)S(1)} %pad_maximum_fusion.both.a0), channel_id=1, source_target_pairs={{0,96},{1,25},{2,98},{3,27},{4,100},{5,29},{6,102},{7,31},{8,104},... | collective-permute-start | bytes 2211848 | tf_op jit(solution)/shard_map/ppermute | solution.py:456
  19.0 1.2 collective-permute-start.6
  20.5 18.6 %all_to_all.15 = f32[16,2,96]{2,1,0:T(2,128)S(1)} all-to-all(f32[16,2,96]{2,1,0:T(2,128)S(1)} %row_sums.1), channel_id=1, replica_groups={{0,2,4,6,32,34,36,38,64,66,68,70,96,98,100,102},{8,10,12,14,40,42,44,46..., dimensions={0} | all-to-all | bytes 24576 | tf_op jit(solution)/shard_map/all_to_all | solution.py:463
  42.6 1.0 pair_projection.1.pairs
  44.5 5.7 %query_projection.1 = (bf16[4,112,896]{2,1,0:T(8,128)(2,1)S(1)}, bf16[4,112,896]{2,1,0:T(8,128)(2,1)S(1)}) custom-call(bf16[2,96,1920]{2,1,0:T(8,128)(2,1)S(1)} %pad_maximum_fusion.both.a0, bf16[2,96,1920]{2,1,0:T(8,128)(2,1)S(1)} %collective-permute-done.4.a1, bf16[2,96,1920]{2,1,0:T(8,128)(2,1)S(1)} %collective-permute-done.6.a2, ...), custom_call_target="tpu_custom_call" | custom-call | tf_op jit(solution)/shard_map/query_projection/pallas_call | solution.py:485
  51.1 1.3 fusion.1
  53.0 1.4 collective-permute-start.13
  54.4 2.6 %collective-permute-start.14 = (bf16[112,896]{1,0:T(8,128)(2,1)S(1)}, bf16[112,896]{1,0:T(8,128)(2,1)S(1)}, u32[]{:S(2)}, u32[]{:S(2)}) collective-permute-start(bf16[112,896]{1,0:T(8,128)(2,1)S(1)} %get-tuple-element.45), channel_id=1, source_target_pairs={{0,4},{1,5},{2,6},{3,7},{4,0},{5,1},{6,2},{7,3},{8,12},{9,13},{10,... | collective-permute-start | bytes 602120 | tf_op jit(solution)/shard_map/ppermute | solution.py:505
  57.0 1.1 collective-permute-start.15
  58.7 1.9 %collective-permute-done.13.b = bf16[112,896]{1,0:T(8,128)(2,1)S(1)} collective-permute-done((bf16[112,896]{1,0:T(8,128)(2,1)S(1)}, bf16[112,896]{1,0:T(8,128)(2,1)S(1)}, u32[]{:S(2)}, u32[]{:S(2)}) %collective-permute-start.13) | collective-permute-done | bytes 200736 | tf_op jit(solution)/shard_map/ppermute | solution.py:503
  60.6 5.4 %collective-permute-done.14.c = bf16[112,896]{1,0:T(8,128)(2,1)S(1)} collective-permute-done((bf16[112,896]{1,0:T(8,128)(2,1)S(1)}, bf16[112,896]{1,0:T(8,128)(2,1)S(1)}, u32[]{:S(2)}, u32[]{:S(2)}) %collective-permute-start.14) | collective-permute-done | bytes 200736 | tf_op jit(solution)/shard_map/ppermute | solution.py:505
  66.0 0.9 collect.1
  67.6 4.4 %all-to-all-start.1 = ((bf16[16,6,896]{2,1,0:T(8,128)(2,1)}), bf16[16,6,896]{2,1,0:T(8,128)(2,1)S(1)}, u32[]{:S(2)}, u32[]{:S(2)}) async-start(bf16[16,6,896]{2,1,0:T(8,128)(2,1)} %get-tuple-element.47), calls=%async_computation.1 | async-start | bytes 458752 | tf_op jit(solution)/shard_map/all_to_all | solution.py:516
  73.5 5.9 %all-to-all-done.1.queries = bf16[16,6,896]{2,1,0:T(8,128)(2,1)S(1)} async-done(((bf16[16,6,896]{2,1,0:T(8,128)(2,1)}), bf16[16,6,896]{2,1,0:T(8,128)(2,1)S(1)}, u32[]{:S(2)}, u32[]{:S(2)}) %all-to-all-start.1) | async-done | bytes 172064 | tf_op jit(solution)/shard_map/all_to_all | solution.py:516
  80.0 8.3 %attention.1 = bf16[16,6,896]{2,1,0:T(8,128)(2,1)} custom-call(s32[3]{0:T(128)} %lengths.1, bf16[16,6,896]{2,1,0:T(8,128)(2,1)} %copy-done.12, f32[16,512]{1,0:T(8,128)} %copy-done.5, f32[8,128]{1,0:T(8,128)} %pad.14.cosine, f32[8,128]{1,0:T(8,128)} %select_maximum_fusion.sine, bf16[3,2048,512]{2,1,0:T(8,128)(2,1)} %keys.1, bf16[3,2048,512]{2,1,0:T(8,128)(2,1)} %values.1), custom_call_target="tpu_custom_call" | custom-call | tf_op jit(solution)/shard_map/attention/pallas_call | solution.py:529
  88.3 4.2 %all-to-all-start.2 = ((bf16[16,6,896]{2,1,0:T(8,128)(2,1)}), bf16[16,6,896]{2,1,0:T(8,128)(2,1)}, u32[]{:S(2)}, u32[]{:S(2)}) async-start(bf16[16,6,896]{2,1,0:T(8,128)(2,1)} %attention.1), calls=%async_computation.2 | async-start | bytes 458752 | tf_op jit(solution)/shard_map/all_to_all | solution.py:550
  93.8 1.0 pad_convert_fusion.chosen
  94.7 5.1 %all-to-all-done.2.block = bf16[16,6,896]{2,1,0:T(8,128)(2,1)} async-done(((bf16[16,6,896]{2,1,0:T(8,128)(2,1)}), bf16[16,6,896]{2,1,0:T(8,128)(2,1)}, u32[]{:S(2)}, u32[]{:S(2)}) %all-to-all-start.2) | async-done | bytes 172064 | tf_op jit(solution)/shard_map/all_to_all | solution.py:550
  99.9 1.0 repack.1.b0
  100.9 2.3 %collective-permute-start.16 = (bf16[96,896]{1,0:T(8,128)(2,1)S(1)}, bf16[96,896]{1,0:T(8,128)(2,1)S(1)}, u32[]{:S(2)}, u32[]{:S(2)}) collective-permute-start(bf16[96,896]{1,0:T(8,128)(2,1)S(1)} %repack.1.b0), channel_id=1, source_target_pairs={{0,2},{1,3},{2,4},{3,5},{4,6},{5,7},{6,0},{7,1},{8,10},{9,11},{10,... | collective-permute-start | bytes 516104 | tf_op jit(solution)/shard_map/ppermute | solution.py:564
  103.3 2.2 %collective-permute-start.17 = (bf16[96,896]{1,0:T(8,128)(2,1)S(1)}, bf16[96,896]{1,0:T(8,128)(2,1)S(1)}, u32[]{:S(2)}, u32[]{:S(2)}) collective-permute-start(bf16[96,896]{1,0:T(8,128)(2,1)S(1)} %repack.1.b0), channel_id=1, source_target_pairs={{0,4},{1,5},{2,6},{3,7},{4,0},{5,1},{6,2},{7,3},{8,12},{9,13},{10,... | collective-permute-start | bytes 516104 | tf_op jit(solution)/shard_map/ppermute | solution.py:564
  105.5 2.0 %collective-permute-start.18 = (bf16[96,896]{1,0:T(8,128)(2,1)S(1)}, bf16[96,896]{1,0:T(8,128)(2,1)S(1)}, u32[]{:S(2)}, u32[]{:S(2)}) collective-permute-start(bf16[96,896]{1,0:T(8,128)(2,1)S(1)} %repack.1.b0), channel_id=1, source_target_pairs={{0,6},{1,7},{2,0},{3,1},{4,2},{5,3},{6,4},{7,5},{8,14},{9,15},{10,... | collective-permute-start | bytes 516104 | tf_op jit(solution)/shard_map/ppermute | solution.py:564
  107.4 4.0 %collective-permute-start.19 = (bf16[96,896]{1,0:T(8,128)(2,1)S(1)}, bf16[96,896]{1,0:T(8,128)(2,1)S(1)}, u32[]{:S(2)}, u32[]{:S(2)}) collective-permute-start(bf16[96,896]{1,0:T(8,128)(2,1)S(1)} %repack.1.b0), channel_id=1, source_target_pairs={{0,1},{1,0},{2,3},{3,2},{4,5},{5,4},{6,7},{7,6},{8,9},{9,8},{10,11... | collective-permute-start | bytes 516104 | tf_op jit(solution)/shard_map/ppermute | solution.py:565
  111.4 5.2 %collective-permute-start.20 = (bf16[96,896]{1,0:T(8,128)(2,1)S(1)}, bf16[96,896]{1,0:T(8,128)(2,1)S(1)}, u32[]{:S(2)}, u32[]{:S(2)}) collective-permute-start(bf16[96,896]{1,0:T(8,128)(2,1)S(1)} %collective-permute-done.16.b1), channel_id=1, source_target_pairs={{0,1},{1,0},{2,3},{3,2},{4,5},{5,4},{6,7},{7,6},{8,9},{9,8},{10,11... | collective-permute-start | bytes 516104 | tf_op jit(solution)/shard_map/ppermute | solution.py:565
  116.6 0.9 collective-permute-start.22
  118.6 0.8 copy-done.3
  120.1 4.3 %output_sent.1 = bf16[4,96,1856]{2,1,0:T(8,128)(2,1)S(1)} custom-call(bf16[96,896]{1,0:T(8,128)(2,1)S(1)} %repack.1.b0, bf16[96,896]{1,0:T(8,128)(2,1)S(1)} %collective-permute-done.16.b1, bf16[96,896]{1,0:T(8,128)(2,1)S(1)} %collective-permute-done.17.b2, bf16[96,896]{1,0:T(8,128)(2,1)S(1)} %collective-permute-done.18.b3, ...), custom_call_target="tpu_custom_call" | custom-call | tf_op jit(solution)/shard_map/output_sent/pallas_call | solution.py:570
  124.8 4.3 %output_kept.1.mine = bf16[4,96,1856]{2,1,0:T(8,128)(2,1)S(1)} custom-call(bf16[96,896]{1,0:T(8,128)(2,1)S(1)} %repack.1.b0, bf16[96,896]{1,0:T(8,128)(2,1)S(1)} %collective-permute-done.16.b1, bf16[96,896]{1,0:T(8,128)(2,1)S(1)} %collective-permute-done.17.b2, bf16[96,896]{1,0:T(8,128)(2,1)S(1)} %collective-permute-done.18.b3, ...), custom_call_target="tpu_custom_call" | custom-call | tf_op jit(solution)/shard_map/output_kept/pallas_call | solution.py:570
  130.3 2.1 %collective-permute-start.25 = (bf16[2,96,1856]{2,1,0:T(8,128)(2,1)S(1)}, bf16[2,96,1856]{2,1,0:T(8,128)(2,1)S(1)}, u32[]{:S(2)}, u32[]{:S(2)}) collective-permute-start(bf16[2,96,1856]{2,1,0:T(8,128)(2,1)S(1)} %pad_maximum_fusion.2), channel_id=1, source_target_pairs={{0,96},{1,25},{2,98},{3,27},{4,100},{5,29},{6,102},{7,31},{8,104},... | collective-permute-start | bytes 2138120 | tf_op jit(solution)/shard_map/ppermute | solution.py:587
  132.5 9.1 %collective-permute-done.26.r2 = bf16[2,96,1856]{2,1,0:T(8,128)(2,1)S(1)} collective-permute-done((bf16[2,96,1856]{2,1,0:T(8,128)(2,1)S(1)}, bf16[2,96,1856]{2,1,0:T(8,128)(2,1)S(1)}, u32[]{:S(2)}, u32[]{:S(2)}) %collective-permute-start.26) | collective-permute-done | bytes 712736 | tf_op jit(solution)/shard_map/ppermute | solution.py:587
  141.6 6.0 %collective-permute-done.25.r3 = bf16[2,96,1856]{2,1,0:T(8,128)(2,1)S(1)} collective-permute-done((bf16[2,96,1856]{2,1,0:T(8,128)(2,1)S(1)}, bf16[2,96,1856]{2,1,0:T(8,128)(2,1)S(1)}, u32[]{:S(2)}, u32[]{:S(2)}) %collective-permute-start.25) | collective-permute-done | bytes 712736 | tf_op jit(solution)/shard_map/ppermute | solution.py:587
  147.7 1.8 %collective-permute-done.24.r1 = bf16[2,96,1856]{2,1,0:T(8,128)(2,1)S(1)} collective-permute-done((bf16[2,96,1856]{2,1,0:T(8,128)(2,1)S(1)}, bf16[2,96,1856]{2,1,0:T(8,128)(2,1)S(1)}, u32[]{:S(2)}, u32[]{:S(2)}) %collective-permute-start.24) | collective-permute-done | bytes 712736 | tf_op jit(solution)/shard_map/ppermute | solution.py:587
  149.9 2.7 %collective-permute-start.28 = (bf16[2,24,1856]{2,1,0:T(8,128)(2,1)S(1)}, bf16[2,24,1856]{2,1,0:T(8,128)(2,1)S(1)}, u32[]{:S(2)}, u32[]{:S(2)}) collective-permute-start(bf16[2,24,1856]{2,1,0:T(8,128)(2,1)S(1)} %get-tuple-element.55), channel_id=1, source_target_pairs={{0,24},{1,97},{2,26},{3,99},{4,28},{5,101},{6,30},{7,103},{8,0},{9... | collective-permute-start | bytes 534536 | tf_op jit(solution)/shard_map/ppermute | solution.py:599
  152.6 3.2 %collective-permute-done.27.r1 = bf16[2,24,1856]{2,1,0:T(8,128)(2,1)S(1)} collective-permute-done((bf16[2,24,1856]{2,1,0:T(8,128)(2,1)S(1)}, bf16[2,24,1856]{2,1,0:T(8,128)(2,1)S(1)}, u32[]{:S(2)}, u32[]{:S(2)}) %collective-permute-start.27) | collective-permute-done | bytes 178208 | tf_op jit(solution)/shard_map/ppermute | solution.py:599
  155.8 1.2 collective-permute-done.28.r3
  157.1 1.4 collective-permute-done.29.r2
  158.6 2.8 %collective-permute-start.30 = (bf16[24,1856]{1,0:T(8,128)(2,1)S(1)}, bf16[24,1856]{1,0:T(8,128)(2,1)S(1)}, u32[]{:S(2)}, u32[]{:S(2)}) collective-permute-start(bf16[24,1856]{1,0:T(8,128)(2,1)S(1)} %get-tuple-element.58), channel_id=1, source_target_pairs={{0,1},{1,0},{2,3},{3,2},{4,5},{5,4},{6,7},{7,6},{8,9},{9,8},{10,11... | collective-permute-start | bytes 267272 | tf_op jit(solution)/shard_map/ppermute | solution.py:609
  161.4 0.9 collective-permute-done.30.other
  (105 shorter events, 16.2 us)
Async XLA Ops:
  0.0 0.9 copy-start.4
  3.4 2.4 %collective-permute-start = (bf16[24,1920]{1,0:T(8,128)(2,1)S(1)}, bf16[24,1920]{1,0:T(8,128)(2,1)S(1)}, u32[]{:S(2)}, u32[]{:S(2)}) collective-permute-start(bf16[24,1920]{1,0:T(8,128)(2,1)S(1)} %get-tuple-element.33), channel_id=1, source_target_pairs={{0,1},{1,0},{2,3},{3,2},{4,5},{5,4},{6,7},{7,6},{8,9},{9,8},{10,11... | collective-permute-start | bytes 276488 | tf_op jit(solution)/shard_map/ppermute | solution.py:452
  5.9 6.8 %collective-permute-start.1 = (bf16[2,24,1920]{2,1,0:T(8,128)(2,1)S(1)}, bf16[2,24,1920]{2,1,0:T(8,128)(2,1)S(1)}, u32[]{:S(2)}, u32[]{:S(2)}) collective-permute-start(bf16[2,24,1920]{2,1,0:T(8,128)(2,1)S(1)} %pad_maximum_fusion.4), channel_id=1, source_target_pairs={{0,8},{1,33},{2,10},{3,35},{4,12},{5,37},{6,14},{7,39},{8,16},{9,4... | collective-permute-start | bytes 552968 | tf_op jit(solution)/shard_map/ppermute | solution.py:454
  7.7 5.1 %collective-permute-start.2 = (bf16[2,24,1920]{2,1,0:T(8,128)(2,1)S(1)}, bf16[2,24,1920]{2,1,0:T(8,128)(2,1)S(1)}, u32[]{:S(2)}, u32[]{:S(2)}) collective-permute-start(bf16[2,24,1920]{2,1,0:T(8,128)(2,1)S(1)} %pad_maximum_fusion.4), channel_id=1, source_target_pairs={{0,24},{1,97},{2,26},{3,99},{4,28},{5,101},{6,30},{7,103},{8,0},{9... | collective-permute-start | bytes 552968 | tf_op jit(solution)/shard_map/ppermute | solution.py:454
  9.9 6.3 %collective-permute-start.3 = (bf16[2,24,1920]{2,1,0:T(8,128)(2,1)S(1)}, bf16[2,24,1920]{2,1,0:T(8,128)(2,1)S(1)}, u32[]{:S(2)}, u32[]{:S(2)}) collective-permute-start(bf16[2,24,1920]{2,1,0:T(8,128)(2,1)S(1)} %pad_maximum_fusion.4), channel_id=1, source_target_pairs={{0,16},{1,65},{2,18},{3,67},{4,20},{5,69},{6,22},{7,71},{8,24},{9,... | collective-permute-start | bytes 552968 | tf_op jit(solution)/shard_map/ppermute | solution.py:454
  16.2 24.5 %collective-permute-start.4 = (bf16[2,96,1920]{2,1,0:T(8,128)(2,1)S(1)}, bf16[2,96,1920]{2,1,0:T(8,128)(2,1)S(1)}, u32[]{:S(2)}, u32[]{:S(2)}) collective-permute-start(bf16[2,96,1920]{2,1,0:T(8,128)(2,1)S(1)} %pad_maximum_fusion.both.a0), channel_id=1, source_target_pairs={{0,32},{1,9},{2,34},{3,11},{4,36},{5,13},{6,38},{7,15},{8,40},{9,1... | collective-permute-start | bytes 2211848 | tf_op jit(solution)/shard_map/ppermute | solution.py:456
  17.2 23.5 %collective-permute-start.5 = (bf16[2,96,1920]{2,1,0:T(8,128)(2,1)S(1)}, bf16[2,96,1920]{2,1,0:T(8,128)(2,1)S(1)}, u32[]{:S(2)}, u32[]{:S(2)}) collective-permute-start(bf16[2,96,1920]{2,1,0:T(8,128)(2,1)S(1)} %pad_maximum_fusion.both.a0), channel_id=1, source_target_pairs={{0,96},{1,25},{2,98},{3,27},{4,100},{5,29},{6,102},{7,31},{8,104},... | collective-permute-start | bytes 2211848 | tf_op jit(solution)/shard_map/ppermute | solution.py:456
  19.0 23.2 %copy-start.10 = (s32[4]{0:T(128)S(1)}, s32[4]{0:T(128)}, u32[]{:S(2)}) copy-start(s32[4]{0:T(128)} %positions.1) | copy-start | bytes 52
  19.0 23.3 %copy-start.13 = (f32[1856]{0:T(1024)S(1)}, f32[1856]{0:T(1024)}, u32[]{:S(2)}) copy-start(f32[1856]{0:T(1024)} %param.19) | copy-start | bytes 22276
  19.0 23.3 %copy-start.14 = (f32[1856]{0:T(1024)S(1)}, f32[1856]{0:T(1024)}, u32[]{:S(2)}) copy-start(f32[1856]{0:T(1024)} %param.18) | copy-start | bytes 22276
  19.0 21.7 %collective-permute-start.6 = (bf16[2,96,1920]{2,1,0:T(8,128)(2,1)S(1)}, bf16[2,96,1920]{2,1,0:T(8,128)(2,1)S(1)}, u32[]{:S(2)}, u32[]{:S(2)}) collective-permute-start(bf16[2,96,1920]{2,1,0:T(8,128)(2,1)S(1)} %pad_maximum_fusion.both.a0), channel_id=1, source_target_pairs={{0,64},{1,17},{2,66},{3,19},{4,68},{5,21},{6,70},{7,23},{8,72},{9,... | collective-permute-start | bytes 2211848 | tf_op jit(solution)/shard_map/ppermute | solution.py:456
  20.2 22.4 %copy-start.1 = (bf16[1856,1024]{1,0:T(8,128)(2,1)S(1)}, bf16[1856,1024]{1,0:T(8,128)(2,1)}, u32[]{:S(2)}) copy-start(bf16[1856,1024]{1,0:T(8,128)(2,1)} %weight.2) | copy-start | bytes 11403268
  39.1 3.3 %copy-start.17 = (f32[896]{0:T(1024)S(1)}, f32[896]{0:T(1024)}, u32[]{:S(2)}) copy-start(f32[896]{0:T(1024)} %param.22) | copy-start | bytes 10756
  39.1 3.5 %copy-start.7 = (f32[4,1024]{1,0:T(4,128)S(1)}, f32[4,1024]{1,0:T(4,128)}, u32[]{:S(2)}) copy-start(f32[4,1024]{1,0:T(4,128)} %extra.2) | copy-start | bytes 49156
  39.1 3.5 %copy-start.11 = (f32[1024]{0:T(1024)S(1)}, f32[1024]{0:T(1024)}, u32[]{:S(2)}) copy-start(f32[1024]{0:T(1024)} %param.24) | copy-start | bytes 12292
  39.1 1.6 collective-permute-start.7
  40.8 2.9 %collective-permute-start.10 = (bf16[96,1920]{1,0:T(8,128)(2,1)S(1)}, bf16[96,1920]{1,0:T(8,128)(2,1)S(1)}, u32[]{:S(2)}, u32[]{:S(2)}) collective-permute-start(bf16[96,1920]{1,0:T(8,128)(2,1)S(1)} %slice_bitcast_fusion.1), channel_id=1, source_target_pairs={{0,1},{1,0},{2,3},{3,2},{4,5},{5,4},{6,7},{7,6},{8,9},{9,8},{10,11... | collective-permute-start | bytes 1105928 | tf_op jit(solution)/shard_map/ppermute | solution.py:480
  41.2 2.4 %collective-permute-start.11 = (bf16[96,1920]{1,0:T(8,128)(2,1)S(1)}, bf16[96,1920]{1,0:T(8,128)(2,1)S(1)}, u32[]{:S(2)}, u32[]{:S(2)}) collective-permute-start(bf16[96,1920]{1,0:T(8,128)(2,1)S(1)} %slice_bitcast_fusion), channel_id=1, source_target_pairs={{0,1},{1,0},{2,3},{3,2},{4,5},{5,4},{6,7},{7,6},{8,9},{9,8},{10,11... | collective-permute-start | bytes 1105928 | tf_op jit(solution)/shard_map/ppermute | solution.py:480
  41.5 2.2 %collective-permute-start.8 = (bf16[96,1920]{1,0:T(8,128)(2,1)S(1)}, bf16[96,1920]{1,0:T(8,128)(2,1)S(1)}, u32[]{:S(2)}, u32[]{:S(2)}) collective-permute-start(bf16[96,1920]{1,0:T(8,128)(2,1)S(1)} %slice_bitcast_fusion.3), channel_id=1, source_target_pairs={{0,1},{1,0},{2,3},{3,2},{4,5},{5,4},{6,7},{7,6},{8,9},{9,8},{10,11... | collective-permute-start | bytes 1105928 | tf_op jit(solution)/shard_map/ppermute | solution.py:480
  41.9 2.2 %collective-permute-start.9 = (bf16[96,1920]{1,0:T(8,128)(2,1)S(1)}, bf16[96,1920]{1,0:T(8,128)(2,1)S(1)}, u32[]{:S(2)}, u32[]{:S(2)}) collective-permute-start(bf16[96,1920]{1,0:T(8,128)(2,1)S(1)} %slice_bitcast_fusion.2), channel_id=1, source_target_pairs={{0,1},{1,0},{2,3},{3,2},{4,5},{5,4},{6,7},{7,6},{8,9},{9,8},{10,11... | collective-permute-start | bytes 1105928 | tf_op jit(solution)/shard_map/ppermute | solution.py:480
  42.6 1.9 %copy-start.2 = (bf16[1856,896]{1,0:T(8,128)(2,1)S(1)}, bf16[1856,896]{1,0:T(8,128)(2,1)}, u32[]{:S(2)}) copy-start(bf16[1856,896]{1,0:T(8,128)(2,1)} %weight.3) | copy-start | bytes 9977860
  42.6 1.9 %copy-start.8 = (f32[4,896]{1,0:T(4,128)S(1)}, f32[4,896]{1,0:T(4,128)}, u32[]{:S(2)}) copy-start(f32[4,896]{1,0:T(4,128)} %extra.3) | copy-start | bytes 43012
  43.6 7.2 %copy-start.18 = (s32[3]{0:T(128)S(1)}, s32[3]{0:T(128)}, u32[]{:S(2)}) copy-start(s32[3]{0:T(128)} %lengths.1) | copy-start | bytes 40
  43.6 7.4 %copy-start.16 = (f32[1856]{0:T(1024)S(1)}, f32[1856]{0:T(1024)}, u32[]{:S(2)}) copy-start(f32[1856]{0:T(1024)} %param.32) | copy-start | bytes 22276
  43.6 7.4 %copy-start.19 = (s32[64]{0:T(128)S(1)}, s32[64]{0:T(128)}, u32[]{:S(2)}) copy-start(s32[64]{0:T(128)} %param.30) | copy-start | bytes 772
  50.2 7.8 %copy-start.15 = (f32[4,1856]{1,0:T(4,128)S(1)}, f32[4,1856]{1,0:T(4,128)}, u32[]{:S(2)}) copy-start(f32[4,1856]{1,0:T(4,128)} %param.33) | copy-start | bytes 89092
  50.2 2.6 %collective-permute-start.12 = (bf16[4,112,896]{2,1,0:T(8,128)(2,1)S(1)}, bf16[4,112,896]{2,1,0:T(8,128)(2,1)S(1)}, u32[]{:S(2)}, u32[]{:S(2)}) collective-permute-start(bf16[4,112,896]{2,1,0:T(8,128)(2,1)S(1)} %get-tuple-element.42), channel_id=1, source_target_pairs={{0,1},{1,0},{2,3},{3,2},{4,5},{5,4},{6,7},{7,6},{8,9},{9,8},{10,11... | collective-permute-start | bytes 2408456 | tf_op jit(solution)/shard_map/ppermute | solution.py:498
  53.0 7.6 %collective-permute-start.13 = (bf16[112,896]{1,0:T(8,128)(2,1)S(1)}, bf16[112,896]{1,0:T(8,128)(2,1)S(1)}, u32[]{:S(2)}, u32[]{:S(2)}) collective-permute-start(bf16[112,896]{1,0:T(8,128)(2,1)S(1)} %get-tuple-element.44), channel_id=1, source_target_pairs={{0,2},{1,3},{2,4},{3,5},{4,6},{5,7},{6,0},{7,1},{8,10},{9,11},{10,... | collective-permute-start | bytes 602120 | tf_op jit(solution)/shard_map/ppermute | solution.py:503
  54.4 11.7 %collective-permute-start.14 = (bf16[112,896]{1,0:T(8,128)(2,1)S(1)}, bf16[112,896]{1,0:T(8,128)(2,1)S(1)}, u32[]{:S(2)}, u32[]{:S(2)}) collective-permute-start(bf16[112,896]{1,0:T(8,128)(2,1)S(1)} %get-tuple-element.45), channel_id=1, source_target_pairs={{0,4},{1,5},{2,6},{3,7},{4,0},{5,1},{6,2},{7,3},{8,12},{9,13},{10,... | collective-permute-start | bytes 602120 | tf_op jit(solution)/shard_map/ppermute | solution.py:505
  57.0 9.1 %collective-permute-start.15 = (bf16[112,896]{1,0:T(8,128)(2,1)S(1)}, bf16[112,896]{1,0:T(8,128)(2,1)S(1)}, u32[]{:S(2)}, u32[]{:S(2)}) collective-permute-start(bf16[112,896]{1,0:T(8,128)(2,1)S(1)} %get-tuple-element.46), channel_id=1, source_target_pairs={{0,6},{1,7},{2,0},{3,1},{4,2},{5,3},{6,4},{7,5},{8,14},{9,15},{10,... | collective-permute-start | bytes 602120 | tf_op jit(solution)/shard_map/ppermute | solution.py:504
  67.6 11.8 %all-to-all-start.1 = ((bf16[16,6,896]{2,1,0:T(8,128)(2,1)}), bf16[16,6,896]{2,1,0:T(8,128)(2,1)S(1)}, u32[]{:S(2)}, u32[]{:S(2)}) async-start(bf16[16,6,896]{2,1,0:T(8,128)(2,1)} %get-tuple-element.47), calls=%async_computation.1 | async-start | bytes 458752 | tf_op jit(solution)/shard_map/all_to_all | solution.py:516
  80.0 38.5 %copy-start = (bf16[896,1856]{0,1:T(8,128)(2,1)S(1)}, bf16[896,1856]{0,1:T(8,128)(2,1)}, u32[]{:S(2)}) copy-start(bf16[896,1856]{0,1:T(8,128)(2,1)} %param.31) | copy-start | bytes 9977860
  88.3 11.6 %all-to-all-start.2 = ((bf16[16,6,896]{2,1,0:T(8,128)(2,1)}), bf16[16,6,896]{2,1,0:T(8,128)(2,1)}, u32[]{:S(2)}, u32[]{:S(2)}) async-start(bf16[16,6,896]{2,1,0:T(8,128)(2,1)} %attention.1), calls=%async_computation.2 | async-start | bytes 458752 | tf_op jit(solution)/shard_map/all_to_all | solution.py:550
  100.9 10.5 %collective-permute-start.16 = (bf16[96,896]{1,0:T(8,128)(2,1)S(1)}, bf16[96,896]{1,0:T(8,128)(2,1)S(1)}, u32[]{:S(2)}, u32[]{:S(2)}) collective-permute-start(bf16[96,896]{1,0:T(8,128)(2,1)S(1)} %repack.1.b0), channel_id=1, source_target_pairs={{0,2},{1,3},{2,4},{3,5},{4,6},{5,7},{6,0},{7,1},{8,10},{9,11},{10,... | collective-permute-start | bytes 516104 | tf_op jit(solution)/shard_map/ppermute | solution.py:564
  103.3 13.4 %collective-permute-start.17 = (bf16[96,896]{1,0:T(8,128)(2,1)S(1)}, bf16[96,896]{1,0:T(8,128)(2,1)S(1)}, u32[]{:S(2)}, u32[]{:S(2)}) collective-permute-start(bf16[96,896]{1,0:T(8,128)(2,1)S(1)} %repack.1.b0), channel_id=1, source_target_pairs={{0,4},{1,5},{2,6},{3,7},{4,0},{5,1},{6,2},{7,3},{8,12},{9,13},{10,... | collective-permute-start | bytes 516104 | tf_op jit(solution)/shard_map/ppermute | solution.py:564
  105.5 11.2 %collective-permute-start.18 = (bf16[96,896]{1,0:T(8,128)(2,1)S(1)}, bf16[96,896]{1,0:T(8,128)(2,1)S(1)}, u32[]{:S(2)}, u32[]{:S(2)}) collective-permute-start(bf16[96,896]{1,0:T(8,128)(2,1)S(1)} %repack.1.b0), channel_id=1, source_target_pairs={{0,6},{1,7},{2,0},{3,1},{4,2},{5,3},{6,4},{7,5},{8,14},{9,15},{10,... | collective-permute-start | bytes 516104 | tf_op jit(solution)/shard_map/ppermute | solution.py:564
  107.4 10.1 %collective-permute-start.19 = (bf16[96,896]{1,0:T(8,128)(2,1)S(1)}, bf16[96,896]{1,0:T(8,128)(2,1)S(1)}, u32[]{:S(2)}, u32[]{:S(2)}) collective-permute-start(bf16[96,896]{1,0:T(8,128)(2,1)S(1)} %repack.1.b0), channel_id=1, source_target_pairs={{0,1},{1,0},{2,3},{3,2},{4,5},{5,4},{6,7},{7,6},{8,9},{9,8},{10,11... | collective-permute-start | bytes 516104 | tf_op jit(solution)/shard_map/ppermute | solution.py:565
  111.4 6.3 %collective-permute-start.20 = (bf16[96,896]{1,0:T(8,128)(2,1)S(1)}, bf16[96,896]{1,0:T(8,128)(2,1)S(1)}, u32[]{:S(2)}, u32[]{:S(2)}) collective-permute-start(bf16[96,896]{1,0:T(8,128)(2,1)S(1)} %collective-permute-done.16.b1), channel_id=1, source_target_pairs={{0,1},{1,0},{2,3},{3,2},{4,5},{5,4},{6,7},{7,6},{8,9},{9,8},{10,11... | collective-permute-start | bytes 516104 | tf_op jit(solution)/shard_map/ppermute | solution.py:565
  116.6 1.4 collective-permute-start.21
  116.6 1.9 %collective-permute-start.22 = (bf16[96,896]{1,0:T(8,128)(2,1)S(1)}, bf16[96,896]{1,0:T(8,128)(2,1)S(1)}, u32[]{:S(2)}, u32[]{:S(2)}) collective-permute-start(bf16[96,896]{1,0:T(8,128)(2,1)S(1)} %collective-permute-done.18.b3), channel_id=1, source_target_pairs={{0,1},{1,0},{2,3},{3,2},{4,5},{5,4},{6,7},{7,6},{8,9},{9,8},{10,11... | collective-permute-start | bytes 516104 | tf_op jit(solution)/shard_map/ppermute | solution.py:565
  124.4 4.8 %collective-permute-start.23 = (bf16[4,96,1856]{2,1,0:T(8,128)(2,1)S(1)}, bf16[4,96,1856]{2,1,0:T(8,128)(2,1)S(1)}, u32[]{:S(2)}, u32[]{:S(2)}) collective-permute-start(bf16[4,96,1856]{2,1,0:T(8,128)(2,1)S(1)} %output_sent.1), channel_id=1, source_target_pairs={{0,1},{1,0},{2,3},{3,2},{4,5},{5,4},{6,7},{7,6},{8,9},{9,8},{10,11... | collective-permute-start | bytes 4276232 | tf_op jit(solution)/shard_map/ppermute | solution.py:583
  129.4 12.2 %collective-permute-start.26 = (bf16[2,96,1856]{2,1,0:T(8,128)(2,1)S(1)}, bf16[2,96,1856]{2,1,0:T(8,128)(2,1)S(1)}, u32[]{:S(2)}, u32[]{:S(2)}) collective-permute-start(bf16[2,96,1856]{2,1,0:T(8,128)(2,1)S(1)} %pad_maximum_fusion.3), channel_id=1, source_target_pairs={{0,64},{1,17},{2,66},{3,19},{4,68},{5,21},{6,70},{7,23},{8,72},{9,... | collective-permute-start | bytes 2138120 | tf_op jit(solution)/shard_map/ppermute | solution.py:587
  130.3 17.4 %collective-permute-start.25 = (bf16[2,96,1856]{2,1,0:T(8,128)(2,1)S(1)}, bf16[2,96,1856]{2,1,0:T(8,128)(2,1)S(1)}, u32[]{:S(2)}, u32[]{:S(2)}) collective-permute-start(bf16[2,96,1856]{2,1,0:T(8,128)(2,1)S(1)} %pad_maximum_fusion.2), channel_id=1, source_target_pairs={{0,96},{1,25},{2,98},{3,27},{4,100},{5,29},{6,102},{7,31},{8,104},... | collective-permute-start | bytes 2138120 | tf_op jit(solution)/shard_map/ppermute | solution.py:587
  132.4 17.1 %collective-permute-start.24 = (bf16[2,96,1856]{2,1,0:T(8,128)(2,1)S(1)}, bf16[2,96,1856]{2,1,0:T(8,128)(2,1)S(1)}, u32[]{:S(2)}, u32[]{:S(2)}) collective-permute-start(bf16[2,96,1856]{2,1,0:T(8,128)(2,1)S(1)} %pad_maximum_fusion.1), channel_id=1, source_target_pairs={{0,32},{1,9},{2,34},{3,11},{4,36},{5,13},{6,38},{7,15},{8,40},{9,1... | collective-permute-start | bytes 2138120 | tf_op jit(solution)/shard_map/ppermute | solution.py:587
  149.9 6.0 %collective-permute-start.27 = (bf16[2,24,1856]{2,1,0:T(8,128)(2,1)S(1)}, bf16[2,24,1856]{2,1,0:T(8,128)(2,1)S(1)}, u32[]{:S(2)}, u32[]{:S(2)}) collective-permute-start(bf16[2,24,1856]{2,1,0:T(8,128)(2,1)S(1)} %get-tuple-element.54), channel_id=1, source_target_pairs={{0,8},{1,33},{2,10},{3,35},{4,12},{5,37},{6,14},{7,39},{8,16},{9,4... | collective-permute-start | bytes 534536 | tf_op jit(solution)/shard_map/ppermute | solution.py:599
  149.9 7.1 %collective-permute-start.28 = (bf16[2,24,1856]{2,1,0:T(8,128)(2,1)S(1)}, bf16[2,24,1856]{2,1,0:T(8,128)(2,1)S(1)}, u32[]{:S(2)}, u32[]{:S(2)}) collective-permute-start(bf16[2,24,1856]{2,1,0:T(8,128)(2,1)S(1)} %get-tuple-element.55), channel_id=1, source_target_pairs={{0,24},{1,97},{2,26},{3,99},{4,28},{5,101},{6,30},{7,103},{8,0},{9... | collective-permute-start | bytes 534536 | tf_op jit(solution)/shard_map/ppermute | solution.py:599
  152.6 5.9 %collective-permute-start.29 = (bf16[2,24,1856]{2,1,0:T(8,128)(2,1)S(1)}, bf16[2,24,1856]{2,1,0:T(8,128)(2,1)S(1)}, u32[]{:S(2)}, u32[]{:S(2)}) collective-permute-start(bf16[2,24,1856]{2,1,0:T(8,128)(2,1)S(1)} %get-tuple-element.56), channel_id=1, source_target_pairs={{0,16},{1,65},{2,18},{3,67},{4,20},{5,69},{6,22},{7,71},{8,24},{9,... | collective-permute-start | bytes 534536 | tf_op jit(solution)/shard_map/ppermute | solution.py:599
  158.6 3.7 %collective-permute-start.30 = (bf16[24,1856]{1,0:T(8,128)(2,1)S(1)}, bf16[24,1856]{1,0:T(8,128)(2,1)S(1)}, u32[]{:S(2)}, u32[]{:S(2)}) collective-permute-start(bf16[24,1856]{1,0:T(8,128)(2,1)S(1)} %get-tuple-element.58), channel_id=1, source_target_pairs={{0,1},{1,0},{2,3},{3,2},{4,5},{5,4},{6,7},{7,6},{8,9},{9,8},{10,11... | collective-permute-start | bytes 267272 | tf_op jit(solution)/shard_map/ppermute | solution.py:609
  (5 other events, 3.5 us)

commit v10 on v7

--- a/solution.py
+++ b/solution.py
@@ -120,9 +120,10 @@
         term = term + outlier[:, k : k + 1] * extra[k : k + 1, :]
     for j in range(2 * N_Y):
         rows = slice(6 * j, 6 * j + 6)
-        out[j, 0:6, :] = term[rows, 0:512]
-        out[j, 6:12, :] = term[rows, 512:1024]
-        out[j, 12:16, :] = jnp.zeros((4, 512), F32)
+        out[j, 0:6, :] = term[rows, 0:896]
+        out[j, 6:8, :] = jnp.zeros((2, 896), F32)
+        for t in range(6):
+            out[j, 6:7, 128 * t : 128 * t + 128] = term[6 * j + t : 6 * j + t + 1, 896:1024]
 
 
 def query_kernel(
@@ -161,8 +162,7 @@
             for k in range(6):
                 for n, lanes in lanes_of(896):
                     out[d, 16 * k : 16 * k + 16, lanes] = acc[n, pl.ds(6 * j + k, 16, stride=48), :].astype(BF)
-            out[d, 96:112, 0:512] = pairs[j].astype(BF)
-            out[d, 96:112, 512:896] = jnp.zeros((16, 384), BF)
+            out[d, 96:104, :] = pairs[j].astype(BF)
 
 
 def add_kernel(keep, received, o0, o1, o2, o3):
@@ -172,11 +172,15 @@
 
 def collect_kernel(a, b, c, d, query_out, pair_out, acc):
     total = (a[...].astype(F32) + b[...].astype(F32)) + (c[...].astype(F32) + d[...].astype(F32))
-    put(acc, slice(0, 112), total)
+    put(acc, slice(0, 104), total)
     for i in range(16):
         for n, lanes in lanes_of(896):
             query_out[i, :, lanes] = acc[n, pl.ds(i, 6, stride=16), :].astype(BF)
-    pair_out[...] = total[96:112, 0:512]
+    pair_out[0:6, :] = total[96:102, 0:512]
+    pair_out[6:12, 0:384] = total[96:102, 512:896]
+    for t in range(6):
+        pair_out[6 + t : 7 + t, 384:512] = total[102:103, 128 * t : 128 * t + 128]
+    pair_out[12:16, :] = jnp.zeros((4, 512), F32)
 
 
 def rotate_lanes(values, cosine, sine):
@@ -469,7 +473,7 @@
         pair_kernel,
         in_specs=[vmem] * 10,
         out_specs=vmem,
-        out_shape=jax.ShapeDtypeStruct((2 * N_Y, 16, 512), F32),
+        out_shape=jax.ShapeDtypeStruct((2 * N_Y, 8, columns), F32),
         compiler_params=params(16),
         name="pair_projection",
     )(
@@ -486,7 +490,7 @@
         grid=(1,),
         in_specs=[whole((1, 96, padded))] * 4 + [vmem] * 14,
         out_specs=[vmem] * 2,
-        out_shape=[jax.ShapeDtypeStruct((N_Y, 112, columns), BF)] * 2,
+        out_shape=[jax.ShapeDtypeStruct((N_Y, 104, columns), BF)] * 2,
         scratch_shapes=[pltpu.VMEM((7, tokens, 128), F32)],
         compiler_params=params(24),
         name="query_projection",
@@ -495,7 +499,7 @@
         query_scale[None], query_float, query_int, pairs,
     )
     received = lax.ppermute(send, "gy", SIBLING)
-    piece = jax.ShapeDtypeStruct((112, columns), BF)
+    piece = jax.ShapeDtypeStruct((104, columns), BF)
     mine, to1, to2, to3 = pl.pallas_call(
         add_kernel, out_shape=[piece] * 4, compiler_params=params(8), name="add_cores"
     )(keep, received)
@@ -508,7 +512,7 @@
             jax.ShapeDtypeStruct((16, 6, columns), BF),
             jax.ShapeDtypeStruct((16, 512), F32),
         ],
-        scratch_shapes=[pltpu.VMEM((7, 112, 128), F32)],
+        scratch_shapes=[pltpu.VMEM((7, 104, 128), F32)],
         compiler_params=params(8),
         name="collect",
     )(mine, from1, from2, from3)

time: 159 us -> 161 us (1.013)
  starting transfers between devices: 47 us -> 52.8 us
  Pallas kernels: 29.4 us -> 26 us
    pallas_call x1, Pallas kernels: 9.64 us -> 6.23 us  [on_device(): pl.pallas_call(attend_kernel, in_specs=[smem, vmem, vmem, vmem, vmem, hbm...]
    all_to_all x1, starting transfers between devices: 3.54 us -> 6.84 us  [on_device(): lax.all_to_all(attended, 'gx', split_axis=0, concat_axis=0, tiled=True)]
    ppermute x4, starting transfers between devices: 7.59 us -> 10.7 us  [on_device(): blocks = blocks + [lax.ppermute(b, 'gy', SIBLING) for b in blocks]]
  transfers between devices with their start and end apart: 33 -> 33, of which waited for: 18 -> 18; matrix products, arithmetic and copies ran while one was open for 3% -> 3% of each run, Pallas kernels for 4% -> 3%
where the time goes in v10:
time: 161 us; the launch traced here: 160 us
  starting transfers between devices  52.8 us (33%)
  waiting for transfers between devices  52.5 us (33%)
  Pallas kernels  26 us (16%)
  blocking collectives  18.6 us (12%)
  local copies, waits for them, and re-layouts  7.16 us (4%)
  other arithmetic  2.46 us (2%)
    all_to_all x1, blocking collectives, on_device(): lax.all_to_all(sums, plane, split_axis=0, concat_axis=0, tiled=True, axis...  18.6 us
    ppermute x3, waiting for transfers between devices, on_device(): lax.ppermute(jnp.stack([kept[d], other[d]]), plane, shift_plane(False, d))  17 us
    ppermute x4, starting transfers between devices, on_device(): blocks = blocks + [lax.ppermute(b, 'gy', SIBLING) for b in blocks]  10.7 us
    pallas_call x2, Pallas kernels, project(): pl.pallas_call(functools.partial(output_kernel, sending), in_specs=[vmem]...  8.64 us
    all_to_all x1, starting transfers between devices, on_device(): lax.all_to_all(attended, 'gx', split_axis=0, concat_axis=0, tiled=True)  6.84 us
    pallas_call x1, Pallas kernels, on_device(): pl.pallas_call(attend_kernel, in_specs=[smem, vmem, vmem, vmem, vmem, hbm...  6.23 us
    all_to_all x1, waiting for transfers between devices, on_device(): lax.all_to_all(attended, 'gx', split_axis=0, concat_axis=0, tiled=True)  6.12 us
    all_to_all x1, waiting for transfers between devices, on_device(): lax.all_to_all(summed, 'gx', split_axis=0, concat_axis=0, tiled=True)  5.9 us
  transfers between devices with their start and end apart: 33, of which 18 were waited for; matrix products, arithmetic and copies ran while one was open for 3% of the time, Pallas kernels for 3%

profile of v10, /device:TPU:1, one launch (start us, length us, event | category | flops | bytes accessed | tf_op | source)
XLA Modules:
  0.0 159.9 jit_solution(6541818577828909780)
XLA Ops:
  0.0 0.9 copy-done.3
  1.6 1.8 %prepare.1 = (bf16[48,1920]{1,0:T(8,128)(2,1)S(1)}, bf16[24,1920]{1,0:T(8,128)(2,1)S(1)}, bf16[24,1920]{1,0:T(8,128)(2,1)S(1)}) custom-call(s32[4]{0:T(128)S(1)} %copy-done.8, bf16[48,1856]{1,0:T(8,128)(2,1)S(1)} %copy-done.3), custom_call_target="tpu_custom_call" | custom-call | tf_op jit(solution)/shard_map/prepare/pallas_call | solution.py:442
  3.4 1.5 collective-permute-start
  4.9 0.9 collective-permute-done
  5.9 1.8 %collective-permute-start.1 = (bf16[2,24,1920]{2,1,0:T(8,128)(2,1)S(1)}, bf16[2,24,1920]{2,1,0:T(8,128)(2,1)S(1)}, u32[]{:S(2)}, u32[]{:S(2)}) collective-permute-start(bf16[2,24,1920]{2,1,0:T(8,128)(2,1)S(1)} %pad_maximum_fusion.4), channel_id=1, source_target_pairs={{0,8},{1,33},{2,10},{3,35},{4,12},{5,37},{6,14},{7,39},{8,16},{9,4... | collective-permute-start | bytes 552968 | tf_op jit(solution)/shard_map/ppermute | solution.py:457
  7.7 2.2 %collective-permute-start.2 = (bf16[2,24,1920]{2,1,0:T(8,128)(2,1)S(1)}, bf16[2,24,1920]{2,1,0:T(8,128)(2,1)S(1)}, u32[]{:S(2)}, u32[]{:S(2)}) collective-permute-start(bf16[2,24,1920]{2,1,0:T(8,128)(2,1)S(1)} %pad_maximum_fusion.4), channel_id=1, source_target_pairs={{0,24},{1,97},{2,26},{3,99},{4,28},{5,101},{6,30},{7,103},{8,0},{9... | collective-permute-start | bytes 552968 | tf_op jit(solution)/shard_map/ppermute | solution.py:457
  9.9 1.2 collective-permute-start.3
  11.1 1.6 %collective-permute-done.1 = bf16[2,24,1920]{2,1,0:T(8,128)(2,1)S(1)} collective-permute-done((bf16[2,24,1920]{2,1,0:T(8,128)(2,1)S(1)}, bf16[2,24,1920]{2,1,0:T(8,128)(2,1)S(1)}, u32[]{:S(2)}, u32[]{:S(2)}) %collective-permute-start.1) | collective-permute-done | bytes 184352 | tf_op jit(solution)/shard_map/ppermute | solution.py:457
  12.7 3.4 %collective-permute-done.3 = bf16[2,24,1920]{2,1,0:T(8,128)(2,1)S(1)} collective-permute-done((bf16[2,24,1920]{2,1,0:T(8,128)(2,1)S(1)}, bf16[2,24,1920]{2,1,0:T(8,128)(2,1)S(1)}, u32[]{:S(2)}, u32[]{:S(2)}) %collective-permute-start.3) | collective-permute-done | bytes 184352 | tf_op jit(solution)/shard_map/ppermute | solution.py:457
  16.2 1.0 collective-permute-start.4
  17.2 1.8 %collective-permute-start.5 = (bf16[2,96,1920]{2,1,0:T(8,128)(2,1)S(1)}, bf16[2,96,1920]{2,1,0:T(8,128)(2,1)S(1)}, u32[]{:S(2)}, u32[]{:S(2)}) collective-permute-start(bf16[2,96,1920]{2,1,0:T(8,128)(2,1)S(1)} %pad_maximum_fusion.both.a0), channel_id=1, source_target_pairs={{0,96},{1,25},{2,98},{3,27},{4,100},{5,29},{6,102},{7,31},{8,104},... | collective-permute-start | bytes 2211848 | tf_op jit(solution)/shard_map/ppermute | solution.py:459
  19.0 1.2 collective-permute-start.6
  20.5 18.6 %all_to_all.15 = f32[16,2,96]{2,1,0:T(2,128)S(1)} all-to-all(f32[16,2,96]{2,1,0:T(2,128)S(1)} %row_sums.1), channel_id=1, replica_groups={{0,2,4,6,32,34,36,38,64,66,68,70,96,98,100,102},{8,10,12,14,40,42,44,46..., dimensions={0} | all-to-all | bytes 24576 | tf_op jit(solution)/shard_map/all_to_all | solution.py:466
  39.1 0.8 collective-permute-start.7
  39.9 0.8 collective-permute-done.7.other
  42.6 1.0 pair_projection.1.pairs
  44.5 5.6 %query_projection.1 = (bf16[4,104,896]{2,1,0:T(8,128)(2,1)S(1)}, bf16[4,104,896]{2,1,0:T(8,128)(2,1)S(1)}) custom-call(bf16[2,96,1920]{2,1,0:T(8,128)(2,1)S(1)} %pad_maximum_fusion.both.a0, bf16[2,96,1920]{2,1,0:T(8,128)(2,1)S(1)} %collective-permute-done.4.a1, bf16[2,96,1920]{2,1,0:T(8,128)(2,1)S(1)} %collective-permute-done.6.a2, ...), custom_call_target="tpu_custom_call" | custom-call | tf_op jit(solution)/shard_map/query_projection/pallas_call | solution.py:488
  50.8 1.9 %collective-permute-done.12.received = bf16[4,104,896]{2,1,0:T(8,128)(2,1)S(1)} collective-permute-done((bf16[4,104,896]{2,1,0:T(8,128)(2,1)S(1)}, bf16[4,104,896]{2,1,0:T(8,128)(2,1)S(1)}, u32[]{:S(2)}, u32[]{:S(2)}) %collective-permute-start.12) | collective-permute-done | bytes 745504 | tf_op jit(solution)/shard_map/ppermute | solution.py:501
  52.9 1.4 collective-permute-start.13
  54.2 2.6 %collective-permute-start.14 = (bf16[104,896]{1,0:T(8,128)(2,1)S(1)}, bf16[104,896]{1,0:T(8,128)(2,1)S(1)}, u32[]{:S(2)}, u32[]{:S(2)}) collective-permute-start(bf16[104,896]{1,0:T(8,128)(2,1)S(1)} %get-tuple-element.41), channel_id=1, source_target_pairs={{0,4},{1,5},{2,6},{3,7},{4,0},{5,1},{6,2},{7,3},{8,12},{9,13},{10,... | collective-permute-start | bytes 559112 | tf_op jit(solution)/shard_map/ppermute | solution.py:508
  56.9 1.1 collective-permute-start.15
  58.1 2.1 %collective-permute-done.13.b = bf16[104,896]{1,0:T(8,128)(2,1)S(1)} collective-permute-done((bf16[104,896]{1,0:T(8,128)(2,1)S(1)}, bf16[104,896]{1,0:T(8,128)(2,1)S(1)}, u32[]{:S(2)}, u32[]{:S(2)}) %collective-permute-start.13) | collective-permute-done | bytes 186400 | tf_op jit(solution)/shard_map/ppermute | solution.py:506
  60.2 5.1 %collective-permute-done.14.c = bf16[104,896]{1,0:T(8,128)(2,1)S(1)} collective-permute-done((bf16[104,896]{1,0:T(8,128)(2,1)S(1)}, bf16[104,896]{1,0:T(8,128)(2,1)S(1)}, u32[]{:S(2)}, u32[]{:S(2)}) %collective-permute-start.14) | collective-permute-done | bytes 186400 | tf_op jit(solution)/shard_map/ppermute | solution.py:508
  65.3 1.0 collect.1
  66.9 4.3 %all-to-all-start.1 = ((bf16[16,6,896]{2,1,0:T(8,128)(2,1)}), bf16[16,6,896]{2,1,0:T(8,128)(2,1)S(1)}, u32[]{:S(2)}, u32[]{:S(2)}) async-start(bf16[16,6,896]{2,1,0:T(8,128)(2,1)} %get-tuple-element.43), calls=%async_computation.1 | async-start | bytes 458752 | tf_op jit(solution)/shard_map/all_to_all | solution.py:519
  72.7 5.9 %all-to-all-done.1.queries = bf16[16,6,896]{2,1,0:T(8,128)(2,1)S(1)} async-done(((bf16[16,6,896]{2,1,0:T(8,128)(2,1)}), bf16[16,6,896]{2,1,0:T(8,128)(2,1)S(1)}, u32[]{:S(2)}, u32[]{:S(2)}) %all-to-all-start.1) | async-done | bytes 172064 | tf_op jit(solution)/shard_map/all_to_all | solution.py:519
  79.3 6.2 %attention.1 = bf16[16,6,896]{2,1,0:T(8,128)(2,1)} custom-call(s32[3]{0:T(128)} %lengths.1, bf16[16,6,896]{2,1,0:T(8,128)(2,1)} %copy-done.11, f32[16,512]{1,0:T(8,128)} %copy-done.5, f32[8,128]{1,0:T(8,128)} %pad.13.cosine, f32[8,128]{1,0:T(8,128)} %select_maximum_fusion.sine, bf16[3,2048,512]{2,1,0:T(8,128)(2,1)} %keys.1, bf16[3,2048,512]{2,1,0:T(8,128)(2,1)} %values.1), custom_call_target="tpu_custom_call" | custom-call | tf_op jit(solution)/shard_map/attention/pallas_call | solution.py:532
  85.5 6.8 %all-to-all-start.2 = ((bf16[16,6,896]{2,1,0:T(8,128)(2,1)}), bf16[16,6,896]{2,1,0:T(8,128)(2,1)S(1)}, u32[]{:S(2)}, u32[]{:S(2)}) async-start(bf16[16,6,896]{2,1,0:T(8,128)(2,1)} %attention.1), calls=%async_computation.2 | async-start | bytes 458752 | tf_op jit(solution)/shard_map/all_to_all | solution.py:553
  92.4 1.2 dynamic_slice.3
  93.6 6.1 %all-to-all-done.2.block = bf16[16,6,896]{2,1,0:T(8,128)(2,1)S(1)} async-done(((bf16[16,6,896]{2,1,0:T(8,128)(2,1)}), bf16[16,6,896]{2,1,0:T(8,128)(2,1)S(1)}, u32[]{:S(2)}, u32[]{:S(2)}) %all-to-all-start.2) | async-done | bytes 172064 | tf_op jit(solution)/shard_map/all_to_all | solution.py:553
  100.0 3.5 %collective-permute-start.17 = (bf16[96,896]{1,0:T(8,128)(2,1)S(1)}, bf16[96,896]{1,0:T(8,128)(2,1)S(1)}, u32[]{:S(2)}, u32[]{:S(2)}) collective-permute-start(bf16[96,896]{1,0:T(8,128)(2,1)S(1)} %repack.1.b0), channel_id=1, source_target_pairs={{0,4},{1,5},{2,6},{3,7},{4,0},{5,1},{6,2},{7,3},{8,12},{9,13},{10,... | collective-permute-start | bytes 516104 | tf_op jit(solution)/shard_map/ppermute | solution.py:561
  103.5 0.9 fusion.1
  104.3 5.9 %collective-permute-start.19 = (bf16[96,896]{1,0:T(8,128)(2,1)S(1)}, bf16[96,896]{1,0:T(8,128)(2,1)S(1)}, u32[]{:S(2)}, u32[]{:S(2)}) collective-permute-start(bf16[96,896]{1,0:T(8,128)(2,1)S(1)} %repack.1.b0), channel_id=1, source_target_pairs={{0,1},{1,0},{2,3},{3,2},{4,5},{5,4},{6,7},{7,6},{8,9},{9,8},{10,11... | collective-permute-start | bytes 516104 | tf_op jit(solution)/shard_map/ppermute | solution.py:562
  110.3 3.9 %collective-permute-start.20 = (bf16[96,896]{1,0:T(8,128)(2,1)S(1)}, bf16[96,896]{1,0:T(8,128)(2,1)S(1)}, u32[]{:S(2)}, u32[]{:S(2)}) collective-permute-start(bf16[96,896]{1,0:T(8,128)(2,1)S(1)} %collective-permute-done.16.b1), channel_id=1, source_target_pairs={{0,1},{1,0},{2,3},{3,2},{4,5},{5,4},{6,7},{7,6},{8,9},{9,8},{10,11... | collective-permute-start | bytes 516104 | tf_op jit(solution)/shard_map/ppermute | solution.py:562
  114.2 0.9 collective-permute-start.22
  116.8 4.3 %output_sent.1 = bf16[4,96,1856]{2,1,0:T(8,128)(2,1)S(1)} custom-call(bf16[96,896]{1,0:T(8,128)(2,1)S(1)} %repack.1.b0, bf16[96,896]{1,0:T(8,128)(2,1)S(1)} %collective-permute-done.16.b1, bf16[96,896]{1,0:T(8,128)(2,1)S(1)} %collective-permute-done.17.b2, bf16[96,896]{1,0:T(8,128)(2,1)S(1)} %collective-permute-done.18.b3, ...), custom_call_target="tpu_custom_call" | custom-call | tf_op jit(solution)/shard_map/output_sent/pallas_call | solution.py:571
  121.6 4.3 %output_kept.1.mine = bf16[4,96,1856]{2,1,0:T(8,128)(2,1)S(1)} custom-call(bf16[96,896]{1,0:T(8,128)(2,1)S(1)} %repack.1.b0, bf16[96,896]{1,0:T(8,128)(2,1)S(1)} %collective-permute-done.16.b1, bf16[96,896]{1,0:T(8,128)(2,1)S(1)} %collective-permute-done.17.b2, bf16[96,896]{1,0:T(8,128)(2,1)S(1)} %collective-permute-done.18.b3, ...), custom_call_target="tpu_custom_call" | custom-call | tf_op jit(solution)/shard_map/output_kept/pallas_call | solution.py:571
  126.2 0.8 collective-permute-start.26
  127.1 2.0 %collective-permute-start.25 = (bf16[2,96,1856]{2,1,0:T(8,128)(2,1)S(1)}, bf16[2,96,1856]{2,1,0:T(8,128)(2,1)S(1)}, u32[]{:S(2)}, u32[]{:S(2)}) collective-permute-start(bf16[2,96,1856]{2,1,0:T(8,128)(2,1)S(1)} %pad_maximum_fusion.2), channel_id=1, source_target_pairs={{0,96},{1,25},{2,98},{3,27},{4,100},{5,29},{6,102},{7,31},{8,104},... | collective-permute-start | bytes 2138120 | tf_op jit(solution)/shard_map/ppermute | solution.py:588
  129.3 9.2 %collective-permute-done.26.r2 = bf16[2,96,1856]{2,1,0:T(8,128)(2,1)S(1)} collective-permute-done((bf16[2,96,1856]{2,1,0:T(8,128)(2,1)S(1)}, bf16[2,96,1856]{2,1,0:T(8,128)(2,1)S(1)}, u32[]{:S(2)}, u32[]{:S(2)}) %collective-permute-start.26) | collective-permute-done | bytes 712736 | tf_op jit(solution)/shard_map/ppermute | solution.py:588
  138.5 6.1 %collective-permute-done.25.r3 = bf16[2,96,1856]{2,1,0:T(8,128)(2,1)S(1)} collective-permute-done((bf16[2,96,1856]{2,1,0:T(8,128)(2,1)S(1)}, bf16[2,96,1856]{2,1,0:T(8,128)(2,1)S(1)}, u32[]{:S(2)}, u32[]{:S(2)}) %collective-permute-start.25) | collective-permute-done | bytes 712736 | tf_op jit(solution)/shard_map/ppermute | solution.py:588
  144.5 1.8 %collective-permute-done.24.r1 = bf16[2,96,1856]{2,1,0:T(8,128)(2,1)S(1)} collective-permute-done((bf16[2,96,1856]{2,1,0:T(8,128)(2,1)S(1)}, bf16[2,96,1856]{2,1,0:T(8,128)(2,1)S(1)}, u32[]{:S(2)}, u32[]{:S(2)}) %collective-permute-start.24) | collective-permute-done | bytes 712736 | tf_op jit(solution)/shard_map/ppermute | solution.py:588
  146.8 2.7 %collective-permute-start.28 = (bf16[2,24,1856]{2,1,0:T(8,128)(2,1)S(1)}, bf16[2,24,1856]{2,1,0:T(8,128)(2,1)S(1)}, u32[]{:S(2)}, u32[]{:S(2)}) collective-permute-start(bf16[2,24,1856]{2,1,0:T(8,128)(2,1)S(1)} %get-tuple-element.47), channel_id=1, source_target_pairs={{0,24},{1,97},{2,26},{3,99},{4,28},{5,101},{6,30},{7,103},{8,0},{9... | collective-permute-start | bytes 534536 | tf_op jit(solution)/shard_map/ppermute | solution.py:600
  149.4 3.2 %collective-permute-done.27.r1 = bf16[2,24,1856]{2,1,0:T(8,128)(2,1)S(1)} collective-permute-done((bf16[2,24,1856]{2,1,0:T(8,128)(2,1)S(1)}, bf16[2,24,1856]{2,1,0:T(8,128)(2,1)S(1)}, u32[]{:S(2)}, u32[]{:S(2)}) %collective-permute-start.27) | collective-permute-done | bytes 178208 | tf_op jit(solution)/shard_map/ppermute | solution.py:600
  152.6 1.2 collective-permute-done.28.r3
  153.9 1.4 collective-permute-done.29.r2
  155.4 2.8 %collective-permute-start.30 = (bf16[24,1856]{1,0:T(8,128)(2,1)S(1)}, bf16[24,1856]{1,0:T(8,128)(2,1)S(1)}, u32[]{:S(2)}, u32[]{:S(2)}) collective-permute-start(bf16[24,1856]{1,0:T(8,128)(2,1)S(1)} %get-tuple-element.50), channel_id=1, source_target_pairs={{0,1},{1,0},{2,3},{3,2},{4,5},{5,4},{6,7},{7,6},{8,9},{9,8},{10,11... | collective-permute-start | bytes 267272 | tf_op jit(solution)/shard_map/ppermute | solution.py:610
  158.2 0.9 collective-permute-done.30.other
  (96 shorter events, 11.7 us)
Async XLA Ops:
  0.0 0.9 copy-start.3
  0.9 0.7 copy-start.8
  3.4 2.4 %collective-permute-start = (bf16[24,1920]{1,0:T(8,128)(2,1)S(1)}, bf16[24,1920]{1,0:T(8,128)(2,1)S(1)}, u32[]{:S(2)}, u32[]{:S(2)}) collective-permute-start(bf16[24,1920]{1,0:T(8,128)(2,1)S(1)} %get-tuple-element.29), channel_id=1, source_target_pairs={{0,1},{1,0},{2,3},{3,2},{4,5},{5,4},{6,7},{7,6},{8,9},{9,8},{10,11... | collective-permute-start | bytes 276488 | tf_op jit(solution)/shard_map/ppermute | solution.py:455
  5.9 6.8 %collective-permute-start.1 = (bf16[2,24,1920]{2,1,0:T(8,128)(2,1)S(1)}, bf16[2,24,1920]{2,1,0:T(8,128)(2,1)S(1)}, u32[]{:S(2)}, u32[]{:S(2)}) collective-permute-start(bf16[2,24,1920]{2,1,0:T(8,128)(2,1)S(1)} %pad_maximum_fusion.4), channel_id=1, source_target_pairs={{0,8},{1,33},{2,10},{3,35},{4,12},{5,37},{6,14},{7,39},{8,16},{9,4... | collective-permute-start | bytes 552968 | tf_op jit(solution)/shard_map/ppermute | solution.py:457
  7.7 5.1 %collective-permute-start.2 = (bf16[2,24,1920]{2,1,0:T(8,128)(2,1)S(1)}, bf16[2,24,1920]{2,1,0:T(8,128)(2,1)S(1)}, u32[]{:S(2)}, u32[]{:S(2)}) collective-permute-start(bf16[2,24,1920]{2,1,0:T(8,128)(2,1)S(1)} %pad_maximum_fusion.4), channel_id=1, source_target_pairs={{0,24},{1,97},{2,26},{3,99},{4,28},{5,101},{6,30},{7,103},{8,0},{9... | collective-permute-start | bytes 552968 | tf_op jit(solution)/shard_map/ppermute | solution.py:457
  9.9 6.3 %collective-permute-start.3 = (bf16[2,24,1920]{2,1,0:T(8,128)(2,1)S(1)}, bf16[2,24,1920]{2,1,0:T(8,128)(2,1)S(1)}, u32[]{:S(2)}, u32[]{:S(2)}) collective-permute-start(bf16[2,24,1920]{2,1,0:T(8,128)(2,1)S(1)} %pad_maximum_fusion.4), channel_id=1, source_target_pairs={{0,16},{1,65},{2,18},{3,67},{4,20},{5,69},{6,22},{7,71},{8,24},{9,... | collective-permute-start | bytes 552968 | tf_op jit(solution)/shard_map/ppermute | solution.py:457
  16.2 24.5 %collective-permute-start.4 = (bf16[2,96,1920]{2,1,0:T(8,128)(2,1)S(1)}, bf16[2,96,1920]{2,1,0:T(8,128)(2,1)S(1)}, u32[]{:S(2)}, u32[]{:S(2)}) collective-permute-start(bf16[2,96,1920]{2,1,0:T(8,128)(2,1)S(1)} %pad_maximum_fusion.both.a0), channel_id=1, source_target_pairs={{0,32},{1,9},{2,34},{3,11},{4,36},{5,13},{6,38},{7,15},{8,40},{9,1... | collective-permute-start | bytes 2211848 | tf_op jit(solution)/shard_map/ppermute | solution.py:459
  17.2 23.5 %collective-permute-start.5 = (bf16[2,96,1920]{2,1,0:T(8,128)(2,1)S(1)}, bf16[2,96,1920]{2,1,0:T(8,128)(2,1)S(1)}, u32[]{:S(2)}, u32[]{:S(2)}) collective-permute-start(bf16[2,96,1920]{2,1,0:T(8,128)(2,1)S(1)} %pad_maximum_fusion.both.a0), channel_id=1, source_target_pairs={{0,96},{1,25},{2,98},{3,27},{4,100},{5,29},{6,102},{7,31},{8,104},... | collective-permute-start | bytes 2211848 | tf_op jit(solution)/shard_map/ppermute | solution.py:459
  19.0 23.2 %copy-start.9 = (s32[4]{0:T(128)S(1)}, s32[4]{0:T(128)}, u32[]{:S(2)}) copy-start(s32[4]{0:T(128)} %positions.1) | copy-start | bytes 52
  19.0 23.3 %copy-start.12 = (f32[1856]{0:T(1024)S(1)}, f32[1856]{0:T(1024)}, u32[]{:S(2)}) copy-start(f32[1856]{0:T(1024)} %param.19) | copy-start | bytes 22276
  19.0 23.3 %copy-start.13 = (f32[1856]{0:T(1024)S(1)}, f32[1856]{0:T(1024)}, u32[]{:S(2)}) copy-start(f32[1856]{0:T(1024)} %param.18) | copy-start | bytes 22276
  19.0 21.7 %collective-permute-start.6 = (bf16[2,96,1920]{2,1,0:T(8,128)(2,1)S(1)}, bf16[2,96,1920]{2,1,0:T(8,128)(2,1)S(1)}, u32[]{:S(2)}, u32[]{:S(2)}) collective-permute-start(bf16[2,96,1920]{2,1,0:T(8,128)(2,1)S(1)} %pad_maximum_fusion.both.a0), channel_id=1, source_target_pairs={{0,64},{1,17},{2,66},{3,19},{4,68},{5,21},{6,70},{7,23},{8,72},{9,... | collective-permute-start | bytes 2211848 | tf_op jit(solution)/shard_map/ppermute | solution.py:459
  20.2 22.4 %copy-start.1 = (bf16[1856,1024]{1,0:T(8,128)(2,1)S(1)}, bf16[1856,1024]{1,0:T(8,128)(2,1)}, u32[]{:S(2)}) copy-start(bf16[1856,1024]{1,0:T(8,128)(2,1)} %weight.2) | copy-start | bytes 11403268
  39.1 3.3 %copy-start.14 = (f32[896]{0:T(1024)S(1)}, f32[896]{0:T(1024)}, u32[]{:S(2)}) copy-start(f32[896]{0:T(1024)} %param.22) | copy-start | bytes 10756
  39.1 3.5 %copy-start.6 = (f32[4,1024]{1,0:T(4,128)S(1)}, f32[4,1024]{1,0:T(4,128)}, u32[]{:S(2)}) copy-start(f32[4,1024]{1,0:T(4,128)} %extra.4) | copy-start | bytes 49156
  39.1 3.5 %copy-start.10 = (f32[1024]{0:T(1024)S(1)}, f32[1024]{0:T(1024)}, u32[]{:S(2)}) copy-start(f32[1024]{0:T(1024)} %param.24) | copy-start | bytes 12292
  39.1 1.6 collective-permute-start.7
  40.8 2.9 %collective-permute-start.10 = (bf16[96,1920]{1,0:T(8,128)(2,1)S(1)}, bf16[96,1920]{1,0:T(8,128)(2,1)S(1)}, u32[]{:S(2)}, u32[]{:S(2)}) collective-permute-start(bf16[96,1920]{1,0:T(8,128)(2,1)S(1)} %slice_bitcast_fusion.1), channel_id=1, source_target_pairs={{0,1},{1,0},{2,3},{3,2},{4,5},{5,4},{6,7},{7,6},{8,9},{9,8},{10,11... | collective-permute-start | bytes 1105928 | tf_op jit(solution)/shard_map/ppermute | solution.py:483
  41.2 2.4 %collective-permute-start.11 = (bf16[96,1920]{1,0:T(8,128)(2,1)S(1)}, bf16[96,1920]{1,0:T(8,128)(2,1)S(1)}, u32[]{:S(2)}, u32[]{:S(2)}) collective-permute-start(bf16[96,1920]{1,0:T(8,128)(2,1)S(1)} %slice_bitcast_fusion), channel_id=1, source_target_pairs={{0,1},{1,0},{2,3},{3,2},{4,5},{5,4},{6,7},{7,6},{8,9},{9,8},{10,11... | collective-permute-start | bytes 1105928 | tf_op jit(solution)/shard_map/ppermute | solution.py:483
  41.5 2.1 %collective-permute-start.8 = (bf16[96,1920]{1,0:T(8,128)(2,1)S(1)}, bf16[96,1920]{1,0:T(8,128)(2,1)S(1)}, u32[]{:S(2)}, u32[]{:S(2)}) collective-permute-start(bf16[96,1920]{1,0:T(8,128)(2,1)S(1)} %slice_bitcast_fusion.3), channel_id=1, source_target_pairs={{0,1},{1,0},{2,3},{3,2},{4,5},{5,4},{6,7},{7,6},{8,9},{9,8},{10,11... | collective-permute-start | bytes 1105928 | tf_op jit(solution)/shard_map/ppermute | solution.py:483
  41.9 2.2 %collective-permute-start.9 = (bf16[96,1920]{1,0:T(8,128)(2,1)S(1)}, bf16[96,1920]{1,0:T(8,128)(2,1)S(1)}, u32[]{:S(2)}, u32[]{:S(2)}) collective-permute-start(bf16[96,1920]{1,0:T(8,128)(2,1)S(1)} %slice_bitcast_fusion.2), channel_id=1, source_target_pairs={{0,1},{1,0},{2,3},{3,2},{4,5},{5,4},{6,7},{7,6},{8,9},{9,8},{10,11... | collective-permute-start | bytes 1105928 | tf_op jit(solution)/shard_map/ppermute | solution.py:483
  42.6 1.9 %copy-start.2 = (bf16[1856,896]{1,0:T(8,128)(2,1)S(1)}, bf16[1856,896]{1,0:T(8,128)(2,1)}, u32[]{:S(2)}) copy-start(bf16[1856,896]{1,0:T(8,128)(2,1)} %weight.3) | copy-start | bytes 9977860
  42.6 1.9 %copy-start.7 = (f32[4,896]{1,0:T(4,128)S(1)}, f32[4,896]{1,0:T(4,128)}, u32[]{:S(2)}) copy-start(f32[4,896]{1,0:T(4,128)} %extra.5) | copy-start | bytes 43012
  50.2 7.7 %copy-start.15 = (s32[3]{0:T(128)S(1)}, s32[3]{0:T(128)}, u32[]{:S(2)}) copy-start(s32[3]{0:T(128)} %lengths.1) | copy-start | bytes 40
  50.2 2.5 %collective-permute-start.12 = (bf16[4,104,896]{2,1,0:T(8,128)(2,1)S(1)}, bf16[4,104,896]{2,1,0:T(8,128)(2,1)S(1)}, u32[]{:S(2)}, u32[]{:S(2)}) collective-permute-start(bf16[4,104,896]{2,1,0:T(8,128)(2,1)S(1)} %get-tuple-element.38), channel_id=1, source_target_pairs={{0,1},{1,0},{2,3},{3,2},{4,5},{5,4},{6,7},{7,6},{8,9},{9,8},{10,11... | collective-permute-start | bytes 2236424 | tf_op jit(solution)/shard_map/ppermute | solution.py:501
  52.9 7.3 %collective-permute-start.13 = (bf16[104,896]{1,0:T(8,128)(2,1)S(1)}, bf16[104,896]{1,0:T(8,128)(2,1)S(1)}, u32[]{:S(2)}, u32[]{:S(2)}) collective-permute-start(bf16[104,896]{1,0:T(8,128)(2,1)S(1)} %get-tuple-element.40), channel_id=1, source_target_pairs={{0,2},{1,3},{2,4},{3,5},{4,6},{5,7},{6,0},{7,1},{8,10},{9,11},{10,... | collective-permute-start | bytes 559112 | tf_op jit(solution)/shard_map/ppermute | solution.py:506
  54.2 11.1 %collective-permute-start.14 = (bf16[104,896]{1,0:T(8,128)(2,1)S(1)}, bf16[104,896]{1,0:T(8,128)(2,1)S(1)}, u32[]{:S(2)}, u32[]{:S(2)}) collective-permute-start(bf16[104,896]{1,0:T(8,128)(2,1)S(1)} %get-tuple-element.41), channel_id=1, source_target_pairs={{0,4},{1,5},{2,6},{3,7},{4,0},{5,1},{6,2},{7,3},{8,12},{9,13},{10,... | collective-permute-start | bytes 559112 | tf_op jit(solution)/shard_map/ppermute | solution.py:508
  56.9 8.4 %collective-permute-start.15 = (bf16[104,896]{1,0:T(8,128)(2,1)S(1)}, bf16[104,896]{1,0:T(8,128)(2,1)S(1)}, u32[]{:S(2)}, u32[]{:S(2)}) collective-permute-start(bf16[104,896]{1,0:T(8,128)(2,1)S(1)} %get-tuple-element.42), channel_id=1, source_target_pairs={{0,6},{1,7},{2,0},{3,1},{4,2},{5,3},{6,4},{7,5},{8,14},{9,15},{10,... | collective-permute-start | bytes 559112 | tf_op jit(solution)/shard_map/ppermute | solution.py:507
  66.9 11.7 %all-to-all-start.1 = ((bf16[16,6,896]{2,1,0:T(8,128)(2,1)}), bf16[16,6,896]{2,1,0:T(8,128)(2,1)S(1)}, u32[]{:S(2)}, u32[]{:S(2)}) async-start(bf16[16,6,896]{2,1,0:T(8,128)(2,1)} %get-tuple-element.43), calls=%async_computation.1 | async-start | bytes 458752 | tf_op jit(solution)/shard_map/all_to_all | solution.py:519
  78.6 0.7 copy-start.11
  79.3 36.8 %copy-start = (bf16[896,1856]{0,1:T(8,128)(2,1)S(1)}, bf16[896,1856]{0,1:T(8,128)(2,1)}, u32[]{:S(2)}) copy-start(bf16[896,1856]{0,1:T(8,128)(2,1)} %param.31) | copy-start | bytes 9977860
  85.5 14.2 %all-to-all-start.2 = ((bf16[16,6,896]{2,1,0:T(8,128)(2,1)}), bf16[16,6,896]{2,1,0:T(8,128)(2,1)S(1)}, u32[]{:S(2)}, u32[]{:S(2)}) async-start(bf16[16,6,896]{2,1,0:T(8,128)(2,1)} %attention.1), calls=%async_computation.2 | async-start | bytes 458752 | tf_op jit(solution)/shard_map/all_to_all | solution.py:553
  99.9 10.4 %collective-permute-start.16 = (bf16[96,896]{1,0:T(8,128)(2,1)S(1)}, bf16[96,896]{1,0:T(8,128)(2,1)S(1)}, u32[]{:S(2)}, u32[]{:S(2)}) collective-permute-start(bf16[96,896]{1,0:T(8,128)(2,1)S(1)} %repack.1.b0), channel_id=1, source_target_pairs={{0,2},{1,3},{2,4},{3,5},{4,6},{5,7},{6,0},{7,1},{8,10},{9,11},{10,... | collective-permute-start | bytes 516104 | tf_op jit(solution)/shard_map/ppermute | solution.py:561
  100.0 14.2 %collective-permute-start.17 = (bf16[96,896]{1,0:T(8,128)(2,1)S(1)}, bf16[96,896]{1,0:T(8,128)(2,1)S(1)}, u32[]{:S(2)}, u32[]{:S(2)}) collective-permute-start(bf16[96,896]{1,0:T(8,128)(2,1)S(1)} %repack.1.b0), channel_id=1, source_target_pairs={{0,4},{1,5},{2,6},{3,7},{4,0},{5,1},{6,2},{7,3},{8,12},{9,13},{10,... | collective-permute-start | bytes 516104 | tf_op jit(solution)/shard_map/ppermute | solution.py:561
  103.4 10.7 %collective-permute-start.18 = (bf16[96,896]{1,0:T(8,128)(2,1)S(1)}, bf16[96,896]{1,0:T(8,128)(2,1)S(1)}, u32[]{:S(2)}, u32[]{:S(2)}) collective-permute-start(bf16[96,896]{1,0:T(8,128)(2,1)S(1)} %repack.1.b0), channel_id=1, source_target_pairs={{0,6},{1,7},{2,0},{3,1},{4,2},{5,3},{6,4},{7,5},{8,14},{9,15},{10,... | collective-permute-start | bytes 516104 | tf_op jit(solution)/shard_map/ppermute | solution.py:561
  104.3 11.5 %collective-permute-start.19 = (bf16[96,896]{1,0:T(8,128)(2,1)S(1)}, bf16[96,896]{1,0:T(8,128)(2,1)S(1)}, u32[]{:S(2)}, u32[]{:S(2)}) collective-permute-start(bf16[96,896]{1,0:T(8,128)(2,1)S(1)} %repack.1.b0), channel_id=1, source_target_pairs={{0,1},{1,0},{2,3},{3,2},{4,5},{5,4},{6,7},{7,6},{8,9},{9,8},{10,11... | collective-permute-start | bytes 516104 | tf_op jit(solution)/shard_map/ppermute | solution.py:562
  110.3 5.6 %collective-permute-start.20 = (bf16[96,896]{1,0:T(8,128)(2,1)S(1)}, bf16[96,896]{1,0:T(8,128)(2,1)S(1)}, u32[]{:S(2)}, u32[]{:S(2)}) collective-permute-start(bf16[96,896]{1,0:T(8,128)(2,1)S(1)} %collective-permute-done.16.b1), channel_id=1, source_target_pairs={{0,1},{1,0},{2,3},{3,2},{4,5},{5,4},{6,7},{7,6},{8,9},{9,8},{10,11... | collective-permute-start | bytes 516104 | tf_op jit(solution)/shard_map/ppermute | solution.py:562
  114.1 1.7 %collective-permute-start.21 = (bf16[96,896]{1,0:T(8,128)(2,1)S(1)}, bf16[96,896]{1,0:T(8,128)(2,1)S(1)}, u32[]{:S(2)}, u32[]{:S(2)}) collective-permute-start(bf16[96,896]{1,0:T(8,128)(2,1)S(1)} %collective-permute-done.17.b2), channel_id=1, source_target_pairs={{0,1},{1,0},{2,3},{3,2},{4,5},{5,4},{6,7},{7,6},{8,9},{9,8},{10,11... | collective-permute-start | bytes 516104 | tf_op jit(solution)/shard_map/ppermute | solution.py:562
  114.2 1.9 %collective-permute-start.22 = (bf16[96,896]{1,0:T(8,128)(2,1)S(1)}, bf16[96,896]{1,0:T(8,128)(2,1)S(1)}, u32[]{:S(2)}, u32[]{:S(2)}) collective-permute-start(bf16[96,896]{1,0:T(8,128)(2,1)S(1)} %collective-permute-done.18.b3), channel_id=1, source_target_pairs={{0,1},{1,0},{2,3},{3,2},{4,5},{5,4},{6,7},{7,6},{8,9},{9,8},{10,11... | collective-permute-start | bytes 516104 | tf_op jit(solution)/shard_map/ppermute | solution.py:562
  116.1 0.8 copy-start.4
  121.2 4.9 %collective-permute-start.23 = (bf16[4,96,1856]{2,1,0:T(8,128)(2,1)S(1)}, bf16[4,96,1856]{2,1,0:T(8,128)(2,1)S(1)}, u32[]{:S(2)}, u32[]{:S(2)}) collective-permute-start(bf16[4,96,1856]{2,1,0:T(8,128)(2,1)S(1)} %output_sent.1), channel_id=1, source_target_pairs={{0,1},{1,0},{2,3},{3,2},{4,5},{5,4},{6,7},{7,6},{8,9},{9,8},{10,11... | collective-permute-start | bytes 4276232 | tf_op jit(solution)/shard_map/ppermute | solution.py:584
  126.2 12.2 %collective-permute-start.26 = (bf16[2,96,1856]{2,1,0:T(8,128)(2,1)S(1)}, bf16[2,96,1856]{2,1,0:T(8,128)(2,1)S(1)}, u32[]{:S(2)}, u32[]{:S(2)}) collective-permute-start(bf16[2,96,1856]{2,1,0:T(8,128)(2,1)S(1)} %pad_maximum_fusion.3), channel_id=1, source_target_pairs={{0,64},{1,17},{2,66},{3,19},{4,68},{5,21},{6,70},{7,23},{8,72},{9,... | collective-permute-start | bytes 2138120 | tf_op jit(solution)/shard_map/ppermute | solution.py:588
  127.1 17.4 %collective-permute-start.25 = (bf16[2,96,1856]{2,1,0:T(8,128)(2,1)S(1)}, bf16[2,96,1856]{2,1,0:T(8,128)(2,1)S(1)}, u32[]{:S(2)}, u32[]{:S(2)}) collective-permute-start(bf16[2,96,1856]{2,1,0:T(8,128)(2,1)S(1)} %pad_maximum_fusion.2), channel_id=1, source_target_pairs={{0,96},{1,25},{2,98},{3,27},{4,100},{5,29},{6,102},{7,31},{8,104},... | collective-permute-start | bytes 2138120 | tf_op jit(solution)/shard_map/ppermute | solution.py:588
  129.2 17.1 %collective-permute-start.24 = (bf16[2,96,1856]{2,1,0:T(8,128)(2,1)S(1)}, bf16[2,96,1856]{2,1,0:T(8,128)(2,1)S(1)}, u32[]{:S(2)}, u32[]{:S(2)}) collective-permute-start(bf16[2,96,1856]{2,1,0:T(8,128)(2,1)S(1)} %pad_maximum_fusion.1), channel_id=1, source_target_pairs={{0,32},{1,9},{2,34},{3,11},{4,36},{5,13},{6,38},{7,15},{8,40},{9,1... | collective-permute-start | bytes 2138120 | tf_op jit(solution)/shard_map/ppermute | solution.py:588
  146.7 6.0 %collective-permute-start.27 = (bf16[2,24,1856]{2,1,0:T(8,128)(2,1)S(1)}, bf16[2,24,1856]{2,1,0:T(8,128)(2,1)S(1)}, u32[]{:S(2)}, u32[]{:S(2)}) collective-permute-start(bf16[2,24,1856]{2,1,0:T(8,128)(2,1)S(1)} %get-tuple-element.46), channel_id=1, source_target_pairs={{0,8},{1,33},{2,10},{3,35},{4,12},{5,37},{6,14},{7,39},{8,16},{9,4... | collective-permute-start | bytes 534536 | tf_op jit(solution)/shard_map/ppermute | solution.py:600
  146.8 7.1 %collective-permute-start.28 = (bf16[2,24,1856]{2,1,0:T(8,128)(2,1)S(1)}, bf16[2,24,1856]{2,1,0:T(8,128)(2,1)S(1)}, u32[]{:S(2)}, u32[]{:S(2)}) collective-permute-start(bf16[2,24,1856]{2,1,0:T(8,128)(2,1)S(1)} %get-tuple-element.47), channel_id=1, source_target_pairs={{0,24},{1,97},{2,26},{3,99},{4,28},{5,101},{6,30},{7,103},{8,0},{9... | collective-permute-start | bytes 534536 | tf_op jit(solution)/shard_map/ppermute | solution.py:600
  149.4 5.9 %collective-permute-start.29 = (bf16[2,24,1856]{2,1,0:T(8,128)(2,1)S(1)}, bf16[2,24,1856]{2,1,0:T(8,128)(2,1)S(1)}, u32[]{:S(2)}, u32[]{:S(2)}) collective-permute-start(bf16[2,24,1856]{2,1,0:T(8,128)(2,1)S(1)} %get-tuple-element.48), channel_id=1, source_target_pairs={{0,16},{1,65},{2,18},{3,67},{4,20},{5,69},{6,22},{7,71},{8,24},{9,... | collective-permute-start | bytes 534536 | tf_op jit(solution)/shard_map/ppermute | solution.py:600
  155.4 3.7 %collective-permute-start.30 = (bf16[24,1856]{1,0:T(8,128)(2,1)S(1)}, bf16[24,1856]{1,0:T(8,128)(2,1)S(1)}, u32[]{:S(2)}, u32[]{:S(2)}) collective-permute-start(bf16[24,1856]{1,0:T(8,128)(2,1)S(1)} %get-tuple-element.50), channel_id=1, source_target_pairs={{0,1},{1,0},{2,3},{3,2},{4,5},{5,4},{6,7},{7,6},{8,9},{9,8},{10,11... | collective-permute-start | bytes 267272 | tf_op jit(solution)/shard_map/ppermute | solution.py:610
  (1 other events, 0.6 us)

commit v11 on v10

--- a/solution.py
+++ b/solution.py
@@ -448,7 +448,7 @@
             jax.ShapeDtypeStruct((block_rows // 2, padded), BF),
             jax.ShapeDtypeStruct((block_rows // 2, padded), BF),
         ],
-        compiler_params=params(8),
+        compiler_params=params(60),
         name="prepare",
     )(input_outliers, activations)
     plane = ("gx", "gy")

time: 161 us -> 160 us (level)
  starting transfers between devices: 52.8 us -> 50.8 us
  other arithmetic: 2.46 us -> 4.27 us
    all_to_all x1, starting transfers between devices: 6.84 us -> 4.17 us  [on_device(): lax.all_to_all(attended, 'gx', split_axis=0, concat_axis=0, tiled=True)]
    ppermute x3, starting transfers between devices: 3.59 us -> 6.2 us  [on_device(): blocks = [mine] + [lax.ppermute(mine, 'gy', over_y(d)) for d in (1, 2, 3)]]
    ppermute x4, starting transfers between devices: 10.7 us -> 8.91 us  [on_device(): blocks = blocks + [lax.ppermute(b, 'gy', SIBLING) for b in blocks]]
    unnamed x32 -> x30, local copies, waits for them, and re-layouts: 4.14 us -> 2.57 us
  transfers between devices with their start and end apart: 33 -> 33, of which waited for: 18 -> 19; matrix products, arithmetic and copies ran while one was open for 3% -> 3% of each run, Pallas kernels for 3% -> 3%
where the time goes in v11:
time: 160 us
  waiting for transfers between devices  53 us (33%)
  starting transfers between devices  50.8 us (32%)
  Pallas kernels  27.1 us (17%)
  blocking collectives  18.6 us (12%)
  local copies, waits for them, and re-layouts  5.59 us (3%)
  other arithmetic  4.27 us (3%)
    all_to_all x1, blocking collectives, on_device(): lax.all_to_all(sums, plane, split_axis=0, concat_axis=0, tiled=True, axis...  18.6 us
    ppermute x3, waiting for transfers between devices, on_device(): lax.ppermute(jnp.stack([kept[d], other[d]]), plane, shift_plane(False, d))  17.1 us
    ppermute x4, starting transfers between devices, on_device(): blocks = blocks + [lax.ppermute(b, 'gy', SIBLING) for b in blocks]  8.91 us
    pallas_call x2, Pallas kernels, project(): pl.pallas_call(functools.partial(output_kernel, sending), in_specs=[vmem]...  8.64 us
    pallas_call x1, Pallas kernels, on_device(): pl.pallas_call(attend_kernel, in_specs=[smem, vmem, vmem, vmem, vmem, hbm...  6.22 us
    ppermute x3, starting transfers between devices, on_device(): blocks = [mine] + [lax.ppermute(mine, 'gy', over_y(d)) for d in (1, 2, 3)]  6.2 us
    all_to_all x1, waiting for transfers between devices, on_device(): lax.all_to_all(attended, 'gx', split_axis=0, concat_axis=0, tiled=True)  6.12 us
    all_to_all x1, waiting for transfers between devices, on_device(): lax.all_to_all(summed, 'gx', split_axis=0, concat_axis=0, tiled=True)  5.9 us
  transfers between devices with their start and end apart: 33, of which 19 were waited for; matrix products, arithmetic and copies ran while one was open for 3% of the time, Pallas kernels for 3%

profile of v11, /device:TPU:1, one launch (start us, length us, event | category | flops | bytes accessed | tf_op | source)
XLA Modules:
  0.0 159.7 jit_solution(12977597538813027901)
XLA Ops:
  0.0 3.0 %prepare.1 = (bf16[48,1920]{1,0:T(8,128)(2,1)}, bf16[24,1920]{1,0:T(8,128)(2,1)}, bf16[24,1920]{1,0:T(8,128)(2,1)}) custom-call(s32[4]{0:T(128)} %positions.1, bf16[48,1856]{1,0:T(8,128)(2,1)} %x.7), custom_call_target="tpu_custom_call" | custom-call | tf_op jit(solution)/shard_map/prepare/pallas_call | solution.py:442
  3.0 1.4 collective-permute-start
  4.4 1.1 collective-permute-done
  5.5 0.9 pad_maximum_fusion.4
  6.4 1.8 %collective-permute-start.1 = (bf16[2,24,1920]{2,1,0:T(8,128)(2,1)S(1)}, bf16[2,24,1920]{2,1,0:T(8,128)(2,1)S(1)}, u32[]{:S(2)}, u32[]{:S(2)}) collective-permute-start(bf16[2,24,1920]{2,1,0:T(8,128)(2,1)S(1)} %pad_maximum_fusion.4), channel_id=1, source_target_pairs={{0,8},{1,33},{2,10},{3,35},{4,12},{5,37},{6,14},{7,39},{8,16},{9,4... | collective-permute-start | bytes 552968 | tf_op jit(solution)/shard_map/ppermute | solution.py:457
  8.2 2.2 %collective-permute-start.2 = (bf16[2,24,1920]{2,1,0:T(8,128)(2,1)S(1)}, bf16[2,24,1920]{2,1,0:T(8,128)(2,1)S(1)}, u32[]{:S(2)}, u32[]{:S(2)}) collective-permute-start(bf16[2,24,1920]{2,1,0:T(8,128)(2,1)S(1)} %pad_maximum_fusion.4), channel_id=1, source_target_pairs={{0,24},{1,97},{2,26},{3,99},{4,28},{5,101},{6,30},{7,103},{8,0},{9... | collective-permute-start | bytes 552968 | tf_op jit(solution)/shard_map/ppermute | solution.py:457
  10.4 1.2 collective-permute-start.3
  11.7 1.6 %collective-permute-done.1 = bf16[2,24,1920]{2,1,0:T(8,128)(2,1)S(1)} collective-permute-done((bf16[2,24,1920]{2,1,0:T(8,128)(2,1)S(1)}, bf16[2,24,1920]{2,1,0:T(8,128)(2,1)S(1)}, u32[]{:S(2)}, u32[]{:S(2)}) %collective-permute-start.1) | collective-permute-done | bytes 184352 | tf_op jit(solution)/shard_map/ppermute | solution.py:457
  13.3 3.4 %collective-permute-done.3 = bf16[2,24,1920]{2,1,0:T(8,128)(2,1)S(1)} collective-permute-done((bf16[2,24,1920]{2,1,0:T(8,128)(2,1)S(1)}, bf16[2,24,1920]{2,1,0:T(8,128)(2,1)S(1)}, u32[]{:S(2)}, u32[]{:S(2)}) %collective-permute-start.3) | collective-permute-done | bytes 184352 | tf_op jit(solution)/shard_map/ppermute | solution.py:457
  16.7 1.0 pad_maximum_fusion.both.a0
  17.7 1.0 collective-permute-start.4
  18.7 1.8 %collective-permute-start.5 = (bf16[2,96,1920]{2,1,0:T(8,128)(2,1)S(1)}, bf16[2,96,1920]{2,1,0:T(8,128)(2,1)S(1)}, u32[]{:S(2)}, u32[]{:S(2)}) collective-permute-start(bf16[2,96,1920]{2,1,0:T(8,128)(2,1)S(1)} %pad_maximum_fusion.both.a0), channel_id=1, source_target_pairs={{0,96},{1,25},{2,98},{3,27},{4,100},{5,29},{6,102},{7,31},{8,104},... | collective-permute-start | bytes 2211848 | tf_op jit(solution)/shard_map/ppermute | solution.py:459
  20.5 1.2 collective-permute-start.6
  22.0 18.6 %all_to_all.15 = f32[16,2,96]{2,1,0:T(2,128)S(1)} all-to-all(f32[16,2,96]{2,1,0:T(2,128)S(1)} %row_sums.1), channel_id=1, replica_groups={{0,2,4,6,32,34,36,38,64,66,68,70,96,98,100,102},{8,10,12,14,40,42,44,46..., dimensions={0} | all-to-all | bytes 24576 | tf_op jit(solution)/shard_map/all_to_all | solution.py:466
  41.4 0.8 collective-permute-done.7.other
  44.1 1.0 pair_projection.1.pairs
  46.0 5.6 %query_projection.1 = (bf16[4,104,896]{2,1,0:T(8,128)(2,1)S(1)}, bf16[4,104,896]{2,1,0:T(8,128)(2,1)S(1)}) custom-call(bf16[2,96,1920]{2,1,0:T(8,128)(2,1)S(1)} %pad_maximum_fusion.both.a0, bf16[2,96,1920]{2,1,0:T(8,128)(2,1)S(1)} %collective-permute-done.4.a1, bf16[2,96,1920]{2,1,0:T(8,128)(2,1)S(1)} %collective-permute-done.6.a2, ...), custom_call_target="tpu_custom_call" | custom-call | tf_op jit(solution)/shard_map/query_projection/pallas_call | solution.py:488
  52.3 1.9 %collective-permute-done.12.received = bf16[4,104,896]{2,1,0:T(8,128)(2,1)S(1)} collective-permute-done((bf16[4,104,896]{2,1,0:T(8,128)(2,1)S(1)}, bf16[4,104,896]{2,1,0:T(8,128)(2,1)S(1)}, u32[]{:S(2)}, u32[]{:S(2)}) %collective-permute-start.12) | collective-permute-done | bytes 745504 | tf_op jit(solution)/shard_map/ppermute | solution.py:501
  54.4 1.4 collective-permute-start.13
  55.7 2.6 %collective-permute-start.14 = (bf16[104,896]{1,0:T(8,128)(2,1)S(1)}, bf16[104,896]{1,0:T(8,128)(2,1)S(1)}, u32[]{:S(2)}, u32[]{:S(2)}) collective-permute-start(bf16[104,896]{1,0:T(8,128)(2,1)S(1)} %get-tuple-element.41), channel_id=1, source_target_pairs={{0,4},{1,5},{2,6},{3,7},{4,0},{5,1},{6,2},{7,3},{8,12},{9,13},{10,... | collective-permute-start | bytes 559112 | tf_op jit(solution)/shard_map/ppermute | solution.py:508
  58.4 1.1 collective-permute-start.15
  59.6 2.1 %collective-permute-done.13.b = bf16[104,896]{1,0:T(8,128)(2,1)S(1)} collective-permute-done((bf16[104,896]{1,0:T(8,128)(2,1)S(1)}, bf16[104,896]{1,0:T(8,128)(2,1)S(1)}, u32[]{:S(2)}, u32[]{:S(2)}) %collective-permute-start.13) | collective-permute-done | bytes 186400 | tf_op jit(solution)/shard_map/ppermute | solution.py:506
  61.7 5.1 %collective-permute-done.14.c = bf16[104,896]{1,0:T(8,128)(2,1)S(1)} collective-permute-done((bf16[104,896]{1,0:T(8,128)(2,1)S(1)}, bf16[104,896]{1,0:T(8,128)(2,1)S(1)}, u32[]{:S(2)}, u32[]{:S(2)}) %collective-permute-start.14) | collective-permute-done | bytes 186400 | tf_op jit(solution)/shard_map/ppermute | solution.py:508
  66.8 0.9 collect.1
  68.4 4.3 %all-to-all-start.1 = ((bf16[16,6,896]{2,1,0:T(8,128)(2,1)}), bf16[16,6,896]{2,1,0:T(8,128)(2,1)S(1)}, u32[]{:S(2)}, u32[]{:S(2)}) async-start(bf16[16,6,896]{2,1,0:T(8,128)(2,1)} %get-tuple-element.43), calls=%async_computation.1 | async-start | bytes 458752 | tf_op jit(solution)/shard_map/all_to_all | solution.py:519
  74.2 5.9 %all-to-all-done.1.queries = bf16[16,6,896]{2,1,0:T(8,128)(2,1)S(1)} async-done(((bf16[16,6,896]{2,1,0:T(8,128)(2,1)}), bf16[16,6,896]{2,1,0:T(8,128)(2,1)S(1)}, u32[]{:S(2)}, u32[]{:S(2)}) %all-to-all-start.1) | async-done | bytes 172064 | tf_op jit(solution)/shard_map/all_to_all | solution.py:519
  80.8 6.2 %attention.1 = bf16[16,6,896]{2,1,0:T(8,128)(2,1)} custom-call(s32[3]{0:T(128)} %lengths.1, bf16[16,6,896]{2,1,0:T(8,128)(2,1)} %copy-done.9, f32[16,512]{1,0:T(8,128)} %copy-done.5, f32[8,128]{1,0:T(8,128)} %pad.13.cosine, f32[8,128]{1,0:T(8,128)} %select_maximum_fusion.sine, bf16[3,2048,512]{2,1,0:T(8,128)(2,1)} %keys.1, bf16[3,2048,512]{2,1,0:T(8,128)(2,1)} %values.1), custom_call_target="tpu_custom_call" | custom-call | tf_op jit(solution)/shard_map/attention/pallas_call | solution.py:532
  87.0 4.2 %all-to-all-start.2 = ((bf16[16,6,896]{2,1,0:T(8,128)(2,1)}), bf16[16,6,896]{2,1,0:T(8,128)(2,1)S(1)}, u32[]{:S(2)}, u32[]{:S(2)}) async-start(bf16[16,6,896]{2,1,0:T(8,128)(2,1)} %attention.1), calls=%async_computation.2 | async-start | bytes 458752 | tf_op jit(solution)/shard_map/all_to_all | solution.py:553
  91.2 1.2 dynamic_slice.3
  92.4 6.1 %all-to-all-done.2.block = bf16[16,6,896]{2,1,0:T(8,128)(2,1)S(1)} async-done(((bf16[16,6,896]{2,1,0:T(8,128)(2,1)}), bf16[16,6,896]{2,1,0:T(8,128)(2,1)S(1)}, u32[]{:S(2)}, u32[]{:S(2)}) %all-to-all-start.2) | async-done | bytes 172064 | tf_op jit(solution)/shard_map/all_to_all | solution.py:553
  98.7 2.3 %collective-permute-start.16 = (bf16[96,896]{1,0:T(8,128)(2,1)S(1)}, bf16[96,896]{1,0:T(8,128)(2,1)S(1)}, u32[]{:S(2)}, u32[]{:S(2)}) collective-permute-start(bf16[96,896]{1,0:T(8,128)(2,1)S(1)} %repack.1.b0), channel_id=1, source_target_pairs={{0,2},{1,3},{2,4},{3,5},{4,6},{5,7},{6,0},{7,1},{8,10},{9,11},{10,... | collective-permute-start | bytes 516104 | tf_op jit(solution)/shard_map/ppermute | solution.py:561
  101.0 3.8 %collective-permute-start.17 = (bf16[96,896]{1,0:T(8,128)(2,1)S(1)}, bf16[96,896]{1,0:T(8,128)(2,1)S(1)}, u32[]{:S(2)}, u32[]{:S(2)}) collective-permute-start(bf16[96,896]{1,0:T(8,128)(2,1)S(1)} %repack.1.b0), channel_id=1, source_target_pairs={{0,4},{1,5},{2,6},{3,7},{4,0},{5,1},{6,2},{7,3},{8,12},{9,13},{10,... | collective-permute-start | bytes 516104 | tf_op jit(solution)/shard_map/ppermute | solution.py:561
  104.9 0.9 fusion.1
  105.7 4.3 %collective-permute-start.19 = (bf16[96,896]{1,0:T(8,128)(2,1)S(1)}, bf16[96,896]{1,0:T(8,128)(2,1)S(1)}, u32[]{:S(2)}, u32[]{:S(2)}) collective-permute-start(bf16[96,896]{1,0:T(8,128)(2,1)S(1)} %repack.1.b0), channel_id=1, source_target_pairs={{0,1},{1,0},{2,3},{3,2},{4,5},{5,4},{6,7},{7,6},{8,9},{9,8},{10,11... | collective-permute-start | bytes 516104 | tf_op jit(solution)/shard_map/ppermute | solution.py:562
  110.0 4.1 %collective-permute-start.20 = (bf16[96,896]{1,0:T(8,128)(2,1)S(1)}, bf16[96,896]{1,0:T(8,128)(2,1)S(1)}, u32[]{:S(2)}, u32[]{:S(2)}) collective-permute-start(bf16[96,896]{1,0:T(8,128)(2,1)S(1)} %collective-permute-done.16.b1), channel_id=1, source_target_pairs={{0,1},{1,0},{2,3},{3,2},{4,5},{5,4},{6,7},{7,6},{8,9},{9,8},{10,11... | collective-permute-start | bytes 516104 | tf_op jit(solution)/shard_map/ppermute | solution.py:562
  115.9 0.8 copy-done.4
  116.6 4.3 %output_sent.1 = bf16[4,96,1856]{2,1,0:T(8,128)(2,1)S(1)} custom-call(bf16[96,896]{1,0:T(8,128)(2,1)S(1)} %repack.1.b0, bf16[96,896]{1,0:T(8,128)(2,1)S(1)} %collective-permute-done.16.b1, bf16[96,896]{1,0:T(8,128)(2,1)S(1)} %collective-permute-done.17.b2, bf16[96,896]{1,0:T(8,128)(2,1)S(1)} %collective-permute-done.18.b3, ...), custom_call_target="tpu_custom_call" | custom-call | tf_op jit(solution)/shard_map/output_sent/pallas_call | solution.py:571
  121.2 4.3 %output_kept.1.mine = bf16[4,96,1856]{2,1,0:T(8,128)(2,1)S(1)} custom-call(bf16[96,896]{1,0:T(8,128)(2,1)S(1)} %repack.1.b0, bf16[96,896]{1,0:T(8,128)(2,1)S(1)} %collective-permute-done.16.b1, bf16[96,896]{1,0:T(8,128)(2,1)S(1)} %collective-permute-done.17.b2, bf16[96,896]{1,0:T(8,128)(2,1)S(1)} %collective-permute-done.18.b3, ...), custom_call_target="tpu_custom_call" | custom-call | tf_op jit(solution)/shard_map/output_kept/pallas_call | solution.py:571
  126.6 2.0 %collective-permute-start.25 = (bf16[2,96,1856]{2,1,0:T(8,128)(2,1)S(1)}, bf16[2,96,1856]{2,1,0:T(8,128)(2,1)S(1)}, u32[]{:S(2)}, u32[]{:S(2)}) collective-permute-start(bf16[2,96,1856]{2,1,0:T(8,128)(2,1)S(1)} %pad_maximum_fusion.2), channel_id=1, source_target_pairs={{0,96},{1,25},{2,98},{3,27},{4,100},{5,29},{6,102},{7,31},{8,104},... | collective-permute-start | bytes 2138120 | tf_op jit(solution)/shard_map/ppermute | solution.py:588
  128.8 9.3 %collective-permute-done.26.r2 = bf16[2,96,1856]{2,1,0:T(8,128)(2,1)S(1)} collective-permute-done((bf16[2,96,1856]{2,1,0:T(8,128)(2,1)S(1)}, bf16[2,96,1856]{2,1,0:T(8,128)(2,1)S(1)}, u32[]{:S(2)}, u32[]{:S(2)}) %collective-permute-start.26) | collective-permute-done | bytes 712736 | tf_op jit(solution)/shard_map/ppermute | solution.py:588
  138.1 6.0 %collective-permute-done.25.r3 = bf16[2,96,1856]{2,1,0:T(8,128)(2,1)S(1)} collective-permute-done((bf16[2,96,1856]{2,1,0:T(8,128)(2,1)S(1)}, bf16[2,96,1856]{2,1,0:T(8,128)(2,1)S(1)}, u32[]{:S(2)}, u32[]{:S(2)}) %collective-permute-start.25) | collective-permute-done | bytes 712736 | tf_op jit(solution)/shard_map/ppermute | solution.py:588
  144.0 1.9 %collective-permute-done.24.r1 = bf16[2,96,1856]{2,1,0:T(8,128)(2,1)S(1)} collective-permute-done((bf16[2,96,1856]{2,1,0:T(8,128)(2,1)S(1)}, bf16[2,96,1856]{2,1,0:T(8,128)(2,1)S(1)}, u32[]{:S(2)}, u32[]{:S(2)}) %collective-permute-start.24) | collective-permute-done | bytes 712736 | tf_op jit(solution)/shard_map/ppermute | solution.py:588
  146.4 2.7 %collective-permute-start.28 = (bf16[2,24,1856]{2,1,0:T(8,128)(2,1)S(1)}, bf16[2,24,1856]{2,1,0:T(8,128)(2,1)S(1)}, u32[]{:S(2)}, u32[]{:S(2)}) collective-permute-start(bf16[2,24,1856]{2,1,0:T(8,128)(2,1)S(1)} %get-tuple-element.47), channel_id=1, source_target_pairs={{0,24},{1,97},{2,26},{3,99},{4,28},{5,101},{6,30},{7,103},{8,0},{9... | collective-permute-start | bytes 534536 | tf_op jit(solution)/shard_map/ppermute | solution.py:600
  149.0 3.2 %collective-permute-done.27.r1 = bf16[2,24,1856]{2,1,0:T(8,128)(2,1)S(1)} collective-permute-done((bf16[2,24,1856]{2,1,0:T(8,128)(2,1)S(1)}, bf16[2,24,1856]{2,1,0:T(8,128)(2,1)S(1)}, u32[]{:S(2)}, u32[]{:S(2)}) %collective-permute-start.27) | collective-permute-done | bytes 178208 | tf_op jit(solution)/shard_map/ppermute | solution.py:600
  152.3 1.2 collective-permute-done.28.r3
  153.5 1.4 collective-permute-done.29.r2
  155.0 3.0 %collective-permute-start.30 = (bf16[24,1856]{1,0:T(8,128)(2,1)S(1)}, bf16[24,1856]{1,0:T(8,128)(2,1)S(1)}, u32[]{:S(2)}, u32[]{:S(2)}) collective-permute-start(bf16[24,1856]{1,0:T(8,128)(2,1)S(1)} %get-tuple-element.50), channel_id=1, source_target_pairs={{0,1},{1,0},{2,3},{3,2},{4,5},{5,4},{6,7},{7,6},{8,9},{9,8},{10,11... | collective-permute-start | bytes 267272 | tf_op jit(solution)/shard_map/ppermute | solution.py:610
  158.0 0.9 collective-permute-done.30.other
  (94 shorter events, 12.1 us)
Async XLA Ops:
  3.0 2.6 %collective-permute-start = (bf16[24,1920]{1,0:T(8,128)(2,1)}, bf16[24,1920]{1,0:T(8,128)(2,1)S(1)}, u32[]{:S(2)}, u32[]{:S(2)}) collective-permute-start(bf16[24,1920]{1,0:T(8,128)(2,1)} %get-tuple-element.29), channel_id=1, source_target_pairs={{0,1},{1,0},{2,3},{3,2},{4,5},{5,4},{6,7},{7,6},{8,9},{9,8},{10,11... | collective-permute-start | bytes 276488 | tf_op jit(solution)/shard_map/ppermute | solution.py:455
  6.4 6.8 %collective-permute-start.1 = (bf16[2,24,1920]{2,1,0:T(8,128)(2,1)S(1)}, bf16[2,24,1920]{2,1,0:T(8,128)(2,1)S(1)}, u32[]{:S(2)}, u32[]{:S(2)}) collective-permute-start(bf16[2,24,1920]{2,1,0:T(8,128)(2,1)S(1)} %pad_maximum_fusion.4), channel_id=1, source_target_pairs={{0,8},{1,33},{2,10},{3,35},{4,12},{5,37},{6,14},{7,39},{8,16},{9,4... | collective-permute-start | bytes 552968 | tf_op jit(solution)/shard_map/ppermute | solution.py:457
  8.2 5.0 %collective-permute-start.2 = (bf16[2,24,1920]{2,1,0:T(8,128)(2,1)S(1)}, bf16[2,24,1920]{2,1,0:T(8,128)(2,1)S(1)}, u32[]{:S(2)}, u32[]{:S(2)}) collective-permute-start(bf16[2,24,1920]{2,1,0:T(8,128)(2,1)S(1)} %pad_maximum_fusion.4), channel_id=1, source_target_pairs={{0,24},{1,97},{2,26},{3,99},{4,28},{5,101},{6,30},{7,103},{8,0},{9... | collective-permute-start | bytes 552968 | tf_op jit(solution)/shard_map/ppermute | solution.py:457
  10.4 6.3 %collective-permute-start.3 = (bf16[2,24,1920]{2,1,0:T(8,128)(2,1)S(1)}, bf16[2,24,1920]{2,1,0:T(8,128)(2,1)S(1)}, u32[]{:S(2)}, u32[]{:S(2)}) collective-permute-start(bf16[2,24,1920]{2,1,0:T(8,128)(2,1)S(1)} %pad_maximum_fusion.4), channel_id=1, source_target_pairs={{0,16},{1,65},{2,18},{3,67},{4,20},{5,69},{6,22},{7,71},{8,24},{9,... | collective-permute-start | bytes 552968 | tf_op jit(solution)/shard_map/ppermute | solution.py:457
  16.7 27.3 %copy-start.3 = (bf16[48,1920]{1,0:T(8,128)(2,1)S(1)}, bf16[48,1920]{1,0:T(8,128)(2,1)}, u32[]{:S(2)}) copy-start(bf16[48,1920]{1,0:T(8,128)(2,1)} %get-tuple-element.36.own) | copy-start | bytes 552964
  17.7 24.5 %collective-permute-start.4 = (bf16[2,96,1920]{2,1,0:T(8,128)(2,1)S(1)}, bf16[2,96,1920]{2,1,0:T(8,128)(2,1)S(1)}, u32[]{:S(2)}, u32[]{:S(2)}) collective-permute-start(bf16[2,96,1920]{2,1,0:T(8,128)(2,1)S(1)} %pad_maximum_fusion.both.a0), channel_id=1, source_target_pairs={{0,32},{1,9},{2,34},{3,11},{4,36},{5,13},{6,38},{7,15},{8,40},{9,1... | collective-permute-start | bytes 2211848 | tf_op jit(solution)/shard_map/ppermute | solution.py:459
  18.7 23.5 %collective-permute-start.5 = (bf16[2,96,1920]{2,1,0:T(8,128)(2,1)S(1)}, bf16[2,96,1920]{2,1,0:T(8,128)(2,1)S(1)}, u32[]{:S(2)}, u32[]{:S(2)}) collective-permute-start(bf16[2,96,1920]{2,1,0:T(8,128)(2,1)S(1)} %pad_maximum_fusion.both.a0), channel_id=1, source_target_pairs={{0,96},{1,25},{2,98},{3,27},{4,100},{5,29},{6,102},{7,31},{8,104},... | collective-permute-start | bytes 2211848 | tf_op jit(solution)/shard_map/ppermute | solution.py:459
  20.5 23.2 %copy-start.12 = (s32[4]{0:T(128)S(1)}, s32[4]{0:T(128)}, u32[]{:S(2)}) copy-start(s32[4]{0:T(128)} %positions.1) | copy-start | bytes 52
  20.5 23.3 %copy-start.10 = (f32[1856]{0:T(1024)S(1)}, f32[1856]{0:T(1024)}, u32[]{:S(2)}) copy-start(f32[1856]{0:T(1024)} %param.19) | copy-start | bytes 22276
  20.5 23.3 %copy-start.11 = (f32[1856]{0:T(1024)S(1)}, f32[1856]{0:T(1024)}, u32[]{:S(2)}) copy-start(f32[1856]{0:T(1024)} %param.18) | copy-start | bytes 22276
  20.5 21.7 %collective-permute-start.6 = (bf16[2,96,1920]{2,1,0:T(8,128)(2,1)S(1)}, bf16[2,96,1920]{2,1,0:T(8,128)(2,1)S(1)}, u32[]{:S(2)}, u32[]{:S(2)}) collective-permute-start(bf16[2,96,1920]{2,1,0:T(8,128)(2,1)S(1)} %pad_maximum_fusion.both.a0), channel_id=1, source_target_pairs={{0,64},{1,17},{2,66},{3,19},{4,68},{5,21},{6,70},{7,23},{8,72},{9,... | collective-permute-start | bytes 2211848 | tf_op jit(solution)/shard_map/ppermute | solution.py:459
  21.7 22.4 %copy-start.1 = (bf16[1856,1024]{1,0:T(8,128)(2,1)S(1)}, bf16[1856,1024]{1,0:T(8,128)(2,1)}, u32[]{:S(2)}) copy-start(bf16[1856,1024]{1,0:T(8,128)(2,1)} %weight.2) | copy-start | bytes 11403268
  40.6 3.3 %copy-start.13 = (f32[896]{0:T(1024)S(1)}, f32[896]{0:T(1024)}, u32[]{:S(2)}) copy-start(f32[896]{0:T(1024)} %param.22) | copy-start | bytes 10756
  40.6 3.5 %copy-start.6 = (f32[4,1024]{1,0:T(4,128)S(1)}, f32[4,1024]{1,0:T(4,128)}, u32[]{:S(2)}) copy-start(f32[4,1024]{1,0:T(4,128)} %extra.4) | copy-start | bytes 49156
  40.6 3.5 %copy-start.8 = (f32[1024]{0:T(1024)S(1)}, f32[1024]{0:T(1024)}, u32[]{:S(2)}) copy-start(f32[1024]{0:T(1024)} %param.24) | copy-start | bytes 12292
  40.6 1.6 collective-permute-start.7
  42.2 2.9 %collective-permute-start.10 = (bf16[96,1920]{1,0:T(8,128)(2,1)S(1)}, bf16[96,1920]{1,0:T(8,128)(2,1)S(1)}, u32[]{:S(2)}, u32[]{:S(2)}) collective-permute-start(bf16[96,1920]{1,0:T(8,128)(2,1)S(1)} %slice_bitcast_fusion.1), channel_id=1, source_target_pairs={{0,1},{1,0},{2,3},{3,2},{4,5},{5,4},{6,7},{7,6},{8,9},{9,8},{10,11... | collective-permute-start | bytes 1105928 | tf_op jit(solution)/shard_map/ppermute | solution.py:483
  42.7 2.4 %collective-permute-start.11 = (bf16[96,1920]{1,0:T(8,128)(2,1)S(1)}, bf16[96,1920]{1,0:T(8,128)(2,1)S(1)}, u32[]{:S(2)}, u32[]{:S(2)}) collective-permute-start(bf16[96,1920]{1,0:T(8,128)(2,1)S(1)} %slice_bitcast_fusion), channel_id=1, source_target_pairs={{0,1},{1,0},{2,3},{3,2},{4,5},{5,4},{6,7},{7,6},{8,9},{9,8},{10,11... | collective-permute-start | bytes 1105928 | tf_op jit(solution)/shard_map/ppermute | solution.py:483
  43.0 2.2 %collective-permute-start.8 = (bf16[96,1920]{1,0:T(8,128)(2,1)S(1)}, bf16[96,1920]{1,0:T(8,128)(2,1)S(1)}, u32[]{:S(2)}, u32[]{:S(2)}) collective-permute-start(bf16[96,1920]{1,0:T(8,128)(2,1)S(1)} %slice_bitcast_fusion.3), channel_id=1, source_target_pairs={{0,1},{1,0},{2,3},{3,2},{4,5},{5,4},{6,7},{7,6},{8,9},{9,8},{10,11... | collective-permute-start | bytes 1105928 | tf_op jit(solution)/shard_map/ppermute | solution.py:483
  43.4 2.2 %collective-permute-start.9 = (bf16[96,1920]{1,0:T(8,128)(2,1)S(1)}, bf16[96,1920]{1,0:T(8,128)(2,1)S(1)}, u32[]{:S(2)}, u32[]{:S(2)}) collective-permute-start(bf16[96,1920]{1,0:T(8,128)(2,1)S(1)} %slice_bitcast_fusion.2), channel_id=1, source_target_pairs={{0,1},{1,0},{2,3},{3,2},{4,5},{5,4},{6,7},{7,6},{8,9},{9,8},{10,11... | collective-permute-start | bytes 1105928 | tf_op jit(solution)/shard_map/ppermute | solution.py:483
  44.1 1.9 %copy-start.2 = (bf16[1856,896]{1,0:T(8,128)(2,1)S(1)}, bf16[1856,896]{1,0:T(8,128)(2,1)}, u32[]{:S(2)}) copy-start(bf16[1856,896]{1,0:T(8,128)(2,1)} %weight.3) | copy-start | bytes 9977860
  44.1 1.9 %copy-start.7 = (f32[4,896]{1,0:T(4,128)S(1)}, f32[4,896]{1,0:T(4,128)}, u32[]{:S(2)}) copy-start(f32[4,896]{1,0:T(4,128)} %extra.5) | copy-start | bytes 43012
  51.7 7.7 %copy-start.14 = (s32[3]{0:T(128)S(1)}, s32[3]{0:T(128)}, u32[]{:S(2)}) copy-start(s32[3]{0:T(128)} %lengths.1) | copy-start | bytes 40
  51.7 2.5 %collective-permute-start.12 = (bf16[4,104,896]{2,1,0:T(8,128)(2,1)S(1)}, bf16[4,104,896]{2,1,0:T(8,128)(2,1)S(1)}, u32[]{:S(2)}, u32[]{:S(2)}) collective-permute-start(bf16[4,104,896]{2,1,0:T(8,128)(2,1)S(1)} %get-tuple-element.38), channel_id=1, source_target_pairs={{0,1},{1,0},{2,3},{3,2},{4,5},{5,4},{6,7},{7,6},{8,9},{9,8},{10,11... | collective-permute-start | bytes 2236424 | tf_op jit(solution)/shard_map/ppermute | solution.py:501
  54.4 7.3 %collective-permute-start.13 = (bf16[104,896]{1,0:T(8,128)(2,1)S(1)}, bf16[104,896]{1,0:T(8,128)(2,1)S(1)}, u32[]{:S(2)}, u32[]{:S(2)}) collective-permute-start(bf16[104,896]{1,0:T(8,128)(2,1)S(1)} %get-tuple-element.40), channel_id=1, source_target_pairs={{0,2},{1,3},{2,4},{3,5},{4,6},{5,7},{6,0},{7,1},{8,10},{9,11},{10,... | collective-permute-start | bytes 559112 | tf_op jit(solution)/shard_map/ppermute | solution.py:506
  55.7 11.1 %collective-permute-start.14 = (bf16[104,896]{1,0:T(8,128)(2,1)S(1)}, bf16[104,896]{1,0:T(8,128)(2,1)S(1)}, u32[]{:S(2)}, u32[]{:S(2)}) collective-permute-start(bf16[104,896]{1,0:T(8,128)(2,1)S(1)} %get-tuple-element.41), channel_id=1, source_target_pairs={{0,4},{1,5},{2,6},{3,7},{4,0},{5,1},{6,2},{7,3},{8,12},{9,13},{10,... | collective-permute-start | bytes 559112 | tf_op jit(solution)/shard_map/ppermute | solution.py:508
  58.4 8.5 %collective-permute-start.15 = (bf16[104,896]{1,0:T(8,128)(2,1)S(1)}, bf16[104,896]{1,0:T(8,128)(2,1)S(1)}, u32[]{:S(2)}, u32[]{:S(2)}) collective-permute-start(bf16[104,896]{1,0:T(8,128)(2,1)S(1)} %get-tuple-element.42), channel_id=1, source_target_pairs={{0,6},{1,7},{2,0},{3,1},{4,2},{5,3},{6,4},{7,5},{8,14},{9,15},{10,... | collective-permute-start | bytes 559112 | tf_op jit(solution)/shard_map/ppermute | solution.py:507
  67.8 0.6 copy-start.5
  68.4 11.7 %all-to-all-start.1 = ((bf16[16,6,896]{2,1,0:T(8,128)(2,1)}), bf16[16,6,896]{2,1,0:T(8,128)(2,1)S(1)}, u32[]{:S(2)}, u32[]{:S(2)}) async-start(bf16[16,6,896]{2,1,0:T(8,128)(2,1)} %get-tuple-element.43), calls=%async_computation.1 | async-start | bytes 458752 | tf_op jit(solution)/shard_map/all_to_all | solution.py:519
  80.1 0.7 copy-start.9
  80.8 35.1 %copy-start = (bf16[896,1856]{0,1:T(8,128)(2,1)S(1)}, bf16[896,1856]{0,1:T(8,128)(2,1)}, u32[]{:S(2)}) copy-start(bf16[896,1856]{0,1:T(8,128)(2,1)} %param.31) | copy-start | bytes 9977860
  87.0 11.5 %all-to-all-start.2 = ((bf16[16,6,896]{2,1,0:T(8,128)(2,1)}), bf16[16,6,896]{2,1,0:T(8,128)(2,1)S(1)}, u32[]{:S(2)}, u32[]{:S(2)}) async-start(bf16[16,6,896]{2,1,0:T(8,128)(2,1)} %attention.1), calls=%async_computation.2 | async-start | bytes 458752 | tf_op jit(solution)/shard_map/all_to_all | solution.py:553
  98.7 11.4 %collective-permute-start.16 = (bf16[96,896]{1,0:T(8,128)(2,1)S(1)}, bf16[96,896]{1,0:T(8,128)(2,1)S(1)}, u32[]{:S(2)}, u32[]{:S(2)}) collective-permute-start(bf16[96,896]{1,0:T(8,128)(2,1)S(1)} %repack.1.b0), channel_id=1, source_target_pairs={{0,2},{1,3},{2,4},{3,5},{4,6},{5,7},{6,0},{7,1},{8,10},{9,11},{10,... | collective-permute-start | bytes 516104 | tf_op jit(solution)/shard_map/ppermute | solution.py:561
  101.0 13.1 %collective-permute-start.17 = (bf16[96,896]{1,0:T(8,128)(2,1)S(1)}, bf16[96,896]{1,0:T(8,128)(2,1)S(1)}, u32[]{:S(2)}, u32[]{:S(2)}) collective-permute-start(bf16[96,896]{1,0:T(8,128)(2,1)S(1)} %repack.1.b0), channel_id=1, source_target_pairs={{0,4},{1,5},{2,6},{3,7},{4,0},{5,1},{6,2},{7,3},{8,12},{9,13},{10,... | collective-permute-start | bytes 516104 | tf_op jit(solution)/shard_map/ppermute | solution.py:561
  104.8 9.4 %collective-permute-start.18 = (bf16[96,896]{1,0:T(8,128)(2,1)S(1)}, bf16[96,896]{1,0:T(8,128)(2,1)S(1)}, u32[]{:S(2)}, u32[]{:S(2)}) collective-permute-start(bf16[96,896]{1,0:T(8,128)(2,1)S(1)} %repack.1.b0), channel_id=1, source_target_pairs={{0,6},{1,7},{2,0},{3,1},{4,2},{5,3},{6,4},{7,5},{8,14},{9,15},{10,... | collective-permute-start | bytes 516104 | tf_op jit(solution)/shard_map/ppermute | solution.py:561
  105.7 9.7 %collective-permute-start.19 = (bf16[96,896]{1,0:T(8,128)(2,1)S(1)}, bf16[96,896]{1,0:T(8,128)(2,1)S(1)}, u32[]{:S(2)}, u32[]{:S(2)}) collective-permute-start(bf16[96,896]{1,0:T(8,128)(2,1)S(1)} %repack.1.b0), channel_id=1, source_target_pairs={{0,1},{1,0},{2,3},{3,2},{4,5},{5,4},{6,7},{7,6},{8,9},{9,8},{10,11... | collective-permute-start | bytes 516104 | tf_op jit(solution)/shard_map/ppermute | solution.py:562
  110.0 5.4 %collective-permute-start.20 = (bf16[96,896]{1,0:T(8,128)(2,1)S(1)}, bf16[96,896]{1,0:T(8,128)(2,1)S(1)}, u32[]{:S(2)}, u32[]{:S(2)}) collective-permute-start(bf16[96,896]{1,0:T(8,128)(2,1)S(1)} %collective-permute-done.16.b1), channel_id=1, source_target_pairs={{0,1},{1,0},{2,3},{3,2},{4,5},{5,4},{6,7},{7,6},{8,9},{9,8},{10,11... | collective-permute-start | bytes 516104 | tf_op jit(solution)/shard_map/ppermute | solution.py:562
  114.1 1.4 collective-permute-start.21
  114.1 1.7 %collective-permute-start.22 = (bf16[96,896]{1,0:T(8,128)(2,1)S(1)}, bf16[96,896]{1,0:T(8,128)(2,1)S(1)}, u32[]{:S(2)}, u32[]{:S(2)}) collective-permute-start(bf16[96,896]{1,0:T(8,128)(2,1)S(1)} %collective-permute-done.18.b3), channel_id=1, source_target_pairs={{0,1},{1,0},{2,3},{3,2},{4,5},{5,4},{6,7},{7,6},{8,9},{9,8},{10,11... | collective-permute-start | bytes 516104 | tf_op jit(solution)/shard_map/ppermute | solution.py:562
  115.9 0.8 copy-start.4
  120.9 4.7 %collective-permute-start.23 = (bf16[4,96,1856]{2,1,0:T(8,128)(2,1)S(1)}, bf16[4,96,1856]{2,1,0:T(8,128)(2,1)S(1)}, u32[]{:S(2)}, u32[]{:S(2)}) collective-permute-start(bf16[4,96,1856]{2,1,0:T(8,128)(2,1)S(1)} %output_sent.1), channel_id=1, source_target_pairs={{0,1},{1,0},{2,3},{3,2},{4,5},{5,4},{6,7},{7,6},{8,9},{9,8},{10,11... | collective-permute-start | bytes 4276232 | tf_op jit(solution)/shard_map/ppermute | solution.py:584
  125.8 12.2 %collective-permute-start.26 = (bf16[2,96,1856]{2,1,0:T(8,128)(2,1)S(1)}, bf16[2,96,1856]{2,1,0:T(8,128)(2,1)S(1)}, u32[]{:S(2)}, u32[]{:S(2)}) collective-permute-start(bf16[2,96,1856]{2,1,0:T(8,128)(2,1)S(1)} %pad_maximum_fusion.3), channel_id=1, source_target_pairs={{0,64},{1,17},{2,66},{3,19},{4,68},{5,21},{6,70},{7,23},{8,72},{9,... | collective-permute-start | bytes 2138120 | tf_op jit(solution)/shard_map/ppermute | solution.py:588
  126.6 17.4 %collective-permute-start.25 = (bf16[2,96,1856]{2,1,0:T(8,128)(2,1)S(1)}, bf16[2,96,1856]{2,1,0:T(8,128)(2,1)S(1)}, u32[]{:S(2)}, u32[]{:S(2)}) collective-permute-start(bf16[2,96,1856]{2,1,0:T(8,128)(2,1)S(1)} %pad_maximum_fusion.2), channel_id=1, source_target_pairs={{0,96},{1,25},{2,98},{3,27},{4,100},{5,29},{6,102},{7,31},{8,104},... | collective-permute-start | bytes 2138120 | tf_op jit(solution)/shard_map/ppermute | solution.py:588
  128.7 17.2 %collective-permute-start.24 = (bf16[2,96,1856]{2,1,0:T(8,128)(2,1)S(1)}, bf16[2,96,1856]{2,1,0:T(8,128)(2,1)S(1)}, u32[]{:S(2)}, u32[]{:S(2)}) collective-permute-start(bf16[2,96,1856]{2,1,0:T(8,128)(2,1)S(1)} %pad_maximum_fusion.1), channel_id=1, source_target_pairs={{0,32},{1,9},{2,34},{3,11},{4,36},{5,13},{6,38},{7,15},{8,40},{9,1... | collective-permute-start | bytes 2138120 | tf_op jit(solution)/shard_map/ppermute | solution.py:588
  146.3 6.0 %collective-permute-start.27 = (bf16[2,24,1856]{2,1,0:T(8,128)(2,1)S(1)}, bf16[2,24,1856]{2,1,0:T(8,128)(2,1)S(1)}, u32[]{:S(2)}, u32[]{:S(2)}) collective-permute-start(bf16[2,24,1856]{2,1,0:T(8,128)(2,1)S(1)} %get-tuple-element.46), channel_id=1, source_target_pairs={{0,8},{1,33},{2,10},{3,35},{4,12},{5,37},{6,14},{7,39},{8,16},{9,4... | collective-permute-start | bytes 534536 | tf_op jit(solution)/shard_map/ppermute | solution.py:600
  146.4 7.1 %collective-permute-start.28 = (bf16[2,24,1856]{2,1,0:T(8,128)(2,1)S(1)}, bf16[2,24,1856]{2,1,0:T(8,128)(2,1)S(1)}, u32[]{:S(2)}, u32[]{:S(2)}) collective-permute-start(bf16[2,24,1856]{2,1,0:T(8,128)(2,1)S(1)} %get-tuple-element.47), channel_id=1, source_target_pairs={{0,24},{1,97},{2,26},{3,99},{4,28},{5,101},{6,30},{7,103},{8,0},{9... | collective-permute-start | bytes 534536 | tf_op jit(solution)/shard_map/ppermute | solution.py:600
  149.0 5.9 %collective-permute-start.29 = (bf16[2,24,1856]{2,1,0:T(8,128)(2,1)S(1)}, bf16[2,24,1856]{2,1,0:T(8,128)(2,1)S(1)}, u32[]{:S(2)}, u32[]{:S(2)}) collective-permute-start(bf16[2,24,1856]{2,1,0:T(8,128)(2,1)S(1)} %get-tuple-element.48), channel_id=1, source_target_pairs={{0,16},{1,65},{2,18},{3,67},{4,20},{5,69},{6,22},{7,71},{8,24},{9,... | collective-permute-start | bytes 534536 | tf_op jit(solution)/shard_map/ppermute | solution.py:600
  155.0 3.9 %collective-permute-start.30 = (bf16[24,1856]{1,0:T(8,128)(2,1)S(1)}, bf16[24,1856]{1,0:T(8,128)(2,1)S(1)}, u32[]{:S(2)}, u32[]{:S(2)}) collective-permute-start(bf16[24,1856]{1,0:T(8,128)(2,1)S(1)} %get-tuple-element.50), channel_id=1, source_target_pairs={{0,1},{1,0},{2,3},{3,2},{4,5},{5,4},{6,7},{7,6},{8,9},{9,8},{10,11... | collective-permute-start | bytes 267272 | tf_op jit(solution)/shard_map/ppermute | solution.py:610
